TPU v7x, 32 devices: a whole 2x2x4 slice. The times are simulated.
32 devices in a mesh: mp: 8 (over y, x, core), tokens: 4 (over z).
Axes of the slice: x: 2, y: 2, z: 4, core: 2. Of those that a mesh axis runs over, the one named last changes fastest.
Arguments:
- tokens_in: bfloat16 [128, 5120], P(('tokens', 'mp')), may hold values from -6 to 6
- grad_out: bfloat16 [128, 5120], P(('tokens', 'mp')), may hold values from -6 to 6
- pre_act: bfloat16 [128, 13824], P('tokens', 'mp'), may hold values from -6 to 6
- w_in: bfloat16 [5120, 13824], P(None, 'mp'), may hold values from -0.078125 to 0.078125
- w_out: bfloat16 [13824, 5120], P('mp'), may hold values from -0.0546875 to 0.0546875
Outputs:
- grad_in: bfloat16 [128, 5120], P(('tokens', 'mp'))
- grad_w_in: bfloat16 [5120, 13824], P('tokens', 'mp')
- grad_w_out: bfloat16 [13824, 5120], P('mp', 'tokens')
All inputs are finite; a program needn't handle non-finite values.
Results may differ from a plain program's by a relative error of at most 0.023.
Values may be sent and summed in bfloat16 or wider, within the bound.
No kernel may reach another device: no remote copies, remote signals or barrier semaphores. Data moves between devices by JAX's collectives and lax.ppermute only.
A program may use at most 128 MiB of HBM per device.

v0:
```python
import math

import jax
import jax.numpy as jnp
from jax import lax
from jax.sharding import PartitionSpec as P

root_two_pi = math.sqrt(2.0 / math.pi)
cubic = 0.044715


def gelu_value(pre):
    inner = root_two_pi * (pre + cubic * pre * pre * pre)
    return 0.5 * pre * (1.0 + jnp.tanh(inner))


def gelu_slope(pre):
    tanh_val = jnp.tanh(root_two_pi * (pre + cubic * pre * pre * pre))
    return 0.5 * (1.0 + tanh_val) + 0.5 * pre * (1.0 - tanh_val * tanh_val) * root_two_pi * (
        1.0 + 3.0 * cubic * pre * pre
    )


def shards(tokens_in, grad_out, pre_act, w_in, w_out):
    rows_in, rows_grad = (
        lax.all_gather(tokens_in, "mp", axis=0, tiled=True),
        lax.all_gather(grad_out, "mp", axis=0, tiled=True),
    )
    pre = pre_act.astype(jnp.float32)
    activated = gelu_value(pre).astype(jnp.bfloat16)
    slope = gelu_slope(pre)
    grad_act = lax.dot_general(
        rows_grad, w_out, (((1,), (1,)), ((), ())), preferred_element_type=jnp.float32
    )
    grad_pre = (grad_act * slope).astype(jnp.bfloat16)
    grad_in = lax.psum_scatter(
        lax.dot_general(
            grad_pre, w_in, (((1,), (1,)), ((), ())), preferred_element_type=jnp.float32
        ),
        "mp",
        scatter_dimension=0,
        tiled=True,
    ).astype(jnp.bfloat16)
    group_count = lax.axis_size("tokens")
    total = rows_in.shape[0] * group_count
    scale_back = 1.0 / math.sqrt(total)
    part_in = (
        lax.dot_general(
            rows_in, grad_pre, (((0,), (0,)), ((), ())), preferred_element_type=jnp.float32
        )
        * scale_back
    )
    part_out = (
        lax.dot_general(
            activated, rows_grad, (((0,), (0,)), ((), ())), preferred_element_type=jnp.float32
        )
        * scale_back
    )
    sum_in, sum_out = (
        lax.psum_scatter(
            part_in.astype(jnp.bfloat16), "tokens", scatter_dimension=0, tiled=True
        ).astype(jnp.float32),
        lax.psum_scatter(
            part_out.astype(jnp.bfloat16), "tokens", scatter_dimension=1, tiled=True
        ).astype(jnp.float32),
    )
    grad_w_in = sum_in.astype(jnp.bfloat16)
    grad_w_out = sum_out.astype(jnp.bfloat16)
    return (grad_in, grad_w_in, grad_w_out)


def solution(mesh):
    placed = (
        P(("tokens", "mp"), None),
        P(("tokens", "mp"), None),
        P("tokens", "mp"),
        P(None, "mp"),
        P("mp", None),
    )
    return jax.shard_map(
        shards,
        mesh=mesh,
        in_specs=placed,
        out_specs=(P(("tokens", "mp"), None), P("tokens", "mp"), P("mp", "tokens")),
        check_vma=False,
    )
```

profile of v0, /device:TPU:0, one launch (start us, length us, event | category | flops | bytes accessed | tf_op | source)
XLA Modules:
  0.0 648.9 jit_solution(12997321926167509431)
XLA Ops:
  7.2 0.0 reduce-scatter.3.cloned.1.call-start
  7.2 11.1 %all-gather.1 = bf16[8,4,5120]{2,1,0:T(4,128)(2,1)S(1)} all-gather(bf16[1,4,5120]{2,1,0:T(4,128)(2,1)} %bitcast.12), channel_id=1, replica_groups=mesh['mp'=8,'tokens'=4] {'mp'}, dimensions={0}, use_global_device_ids=true | all-gather | bytes 368640 | tf_op jit(solution)/shard_map/all_gather | solution.py:26
  18.3 0.1 reshape.9
  18.4 9.2 %all-gather = bf16[8,4,5120]{2,1,0:T(4,128)(2,1)S(1)} all-gather(bf16[1,4,5120]{2,1,0:T(4,128)(2,1)} %bitcast.13), channel_id=1, replica_groups=mesh['mp'=8,'tokens'=4] {'mp'}, dimensions={0}, use_global_device_ids=true | all-gather | bytes 368640 | tf_op jit(solution)/shard_map/all_gather | solution.py:27
  27.6 0.1 reshape.7
  27.7 11.2 %fusion.1 = bf16[32,1728]{1,0:T(8,128)(2,1)S(1)} fusion(bf16[32,5120]{1,0:T(8,128)(2,1)S(1)} %reshape.7, bf16[1728,5120]{1,0:T(8,128)(2,1)} %param.9, bf16[32,1728]{1,0:T(8,128)(2,1)} %param.7), kind=kOutput, calls=%fused_computation.4 | convolution fusion | flops 567336960 | bytes 18243584 | tf_op jit(solution)/shard_map/dot_general | solution.py:32
  38.9 0.0 copy-start
  39.0 8.7 %fusion = bf16[5120,1728]{0,1:T(8,128)(2,1)} fusion(bf16[32,1728]{1,0:T(8,128)(2,1)S(1)} %fusion.1, bf16[32,5120]{1,0:T(8,128)(2,1)S(1)} %reshape.9), kind=kOutput, calls=%fused_computation.2 | convolution fusion | flops 583925760 | bytes 18132992 | tf_op jit(solution)/shard_map/dot_general | solution.py:48
  47.7 0.0 reduce-scatter.3.cloned.1.call-update
  47.7 0.2 reduce-scatter.5.cloned.1.call-start
  48.0 0.0 copy-done
  48.0 8.9 %multiply_convert_fusion = bf16[1728,5120]{1,0:T(8,128)(2,1)} fusion(bf16[32,5120]{1,0:T(8,128)(2,1)S(1)} %reshape.7, bf16[32,1728]{1,0:T(8,128)(2,1)S(1)} %copy-done), kind=kOutput, calls=%fused_computation | convolution fusion | flops 584478720 | bytes 18132992 | tf_op jit(solution)/shard_map/dot_general | solution.py:54
  56.9 0.0 copy-start.1
  56.9 0.0 reduce-scatter.5.cloned.1.call-update
  56.9 9.2 %fusion.20 = f32[32,5120]{1,0:T(8,128)S(1)} fusion(bf16[32,1728]{1,0:T(8,128)(2,1)S(1)} %fusion.1, bf16[5120,1728]{0,1:T(8,128)(2,1)} %param.8), kind=kOutput, calls=%fused_computation.30 | convolution fusion | flops 566231040 | bytes 18460672 | tf_op jit(solution)/shard_map/dot_general | solution.py:37
  66.1 0.0 copy-done.1
  66.1 0.6 dynamic-slice
  67.4 29.9 %all-reduce.2 = bf16[32,5120]{1,0:T(8,128)(2,1)S(1)} all-reduce(f32[32,5120]{1,0:T(8,128)S(1)} %fusion.20), channel_id=2, replica_groups=mesh['mp'=8,'tokens'=4] {'mp'}, use_global_device_ids=true, to_apply=%region_0.0.clone | all-reduce | flops 163840 | bytes 983040
  97.3 0.6 dynamic-slice_convert_fusion
  97.9 245.2 %reduce-scatter.3.cloned.1.call-done = bf16[1280,1728]{0,1:T(8,128)(2,1)} async-done(((bf16[5120,1728]{0,1:T(8,128)(2,1)}), bf16[1280,1728]{0,1:T(8,128)(2,1)}) %reduce-scatter.3.cloned.1.call-update) | async-done | bytes 4423696 | tf_op jit(solution)/shard_map/reduce_scatter | solution.py:60
  343.1 299.0 %reduce-scatter.5.cloned.1.call-done = bf16[1728,1280]{1,0:T(8,128)(2,1)} async-done(((bf16[1728,5120]{1,0:T(8,128)(2,1)}), bf16[1728,1280]{1,0:T(8,128)(2,1)}) %reduce-scatter.5.cloned.1.call-update) | async-done | bytes 4423696 | tf_op jit(solution)/shard_map/reduce_scatter | solution.py:63
Async XLA Ops:
  7.2 336.0 %reduce-scatter.3.cloned.1.call-start = ((), (), s32[]{:S(2)}) async-start(), calls=%async_computation.2 | async-start | bytes 22118400 | tf_op jit(solution)/shard_map/reduce_scatter | solution.py:60
  38.9 9.0 %copy-start = (bf16[32,1728]{1,0:T(8,128)(2,1)S(1)}, bf16[32,1728]{1,0:T(8,128)(2,1)}, u32[]{:S(2)}) copy-start(bf16[32,1728]{1,0:T(8,128)(2,1)} %param.7) | copy-start | bytes 331780
  47.7 594.3 %reduce-scatter.5.cloned.1.call-start = ((), (), s32[]{:S(2)}) async-start(), calls=%async_computation.3 | async-start | bytes 22118400 | tf_op jit(solution)/shard_map/reduce_scatter | solution.py:63
  56.9 9.2 %copy-start.1 = (u32[32]{0:T(128)S(1)}, u32[32]{0:T(128)}, u32[]{:S(2)}) copy-start(u32[32]{0:T(128)} %constant.17) | copy-start | bytes 388
Sparse Core Ops, SparseCore 0:
  47.8 295.2 reduce-scatter.2
  346.2 295.8 reduce-scatter.4
where the time goes:
time: 649 us
  waiting for transfers between devices  544 us (84%)
  blocking collectives  50.2 us (8%)
  matrix products  38.1 us (6%)
  between operations  14.7 us (2%)
    reduce_scatter x1, waiting for transfers between devices, shards(): lax.psum_scatter(part_out.astype(jnp.bfloat16), 'tokens', scatter_dimensi...  299 us
    reduce_scatter x1, waiting for transfers between devices, shards(): lax.psum_scatter(part_in.astype(jnp.bfloat16), 'tokens', scatter_dimensio...  245 us
    unnamed x1, blocking collectives  29.9 us
  transfers between devices with their start and end apart: 2, of which 2 were waited for; matrix products, arithmetic and copies ran while one was open for 3% of the time, Pallas kernels for 0%

commit v1 on v0

v1 whole, which is shorter than its diff:
```python
import math

import jax
import jax.numpy as jnp
from jax import lax
from jax.sharding import PartitionSpec as P

root_two_pi = math.sqrt(2.0 / math.pi)
cubic = 0.044715


def gelu_value(pre):
    inner = root_two_pi * (pre + cubic * pre * pre * pre)
    return 0.5 * pre * (1.0 + jnp.tanh(inner))


def gelu_slope(pre):
    tanh_val = jnp.tanh(root_two_pi * (pre + cubic * pre * pre * pre))
    return 0.5 * (1.0 + tanh_val) + 0.5 * pre * (1.0 - tanh_val * tanh_val) * root_two_pi * (
        1.0 + 3.0 * cubic * pre * pre
    )


def swap(x, axis):
    return lax.all_to_all(x, axis, 0, 0)


def gather(x, axis):
    return swap(jnp.broadcast_to(x, (lax.axis_size(axis),) + x.shape), axis)


def shards(tokens_in, grad_out, pre_act, w_in, w_out):
    n_mp, n_tok = lax.axis_size("mp"), lax.axis_size("tokens")
    rows, width = tokens_in.shape
    group, hidden = pre_act.shape
    part = width // n_tok
    total = group * n_tok
    scale_back = 1.0 / math.sqrt(total)

    rows_grad = gather(grad_out, "mp").reshape(group, width)
    pre_all = gather(pre_act, "tokens").reshape(total, hidden)

    both = jnp.stack([tokens_in, grad_out]).reshape(2, rows, n_tok, part)
    cols = swap(both.transpose(2, 0, 1, 3), "tokens")
    cols = gather(cols, "mp")
    cols_in, cols_grad = cols.transpose(2, 1, 0, 3, 4).reshape(2, total, part)

    pre = pre_act.astype(jnp.float32)
    grad_act = lax.dot_general(
        rows_grad, w_out, (((1,), (1,)), ((), ())), preferred_element_type=jnp.float32
    )
    grad_pre = (grad_act * gelu_slope(pre)).astype(jnp.bfloat16)
    grad_pre_all = gather(grad_pre, "tokens").reshape(total, hidden)

    part_grad_in = lax.dot_general(
        grad_pre, w_in, (((1,), (1,)), ((), ())), preferred_element_type=jnp.float32
    )
    blocks = swap(part_grad_in.astype(jnp.bfloat16).reshape(n_mp, rows, width), "mp")
    grad_in = jnp.sum(blocks.astype(jnp.float32), axis=0).astype(jnp.bfloat16)

    activated = gelu_value(pre_all.astype(jnp.float32)).astype(jnp.bfloat16)
    grad_w_out = (
        lax.dot_general(
            activated, cols_grad, (((0,), (0,)), ((), ())), preferred_element_type=jnp.float32
        )
        * scale_back
    ).astype(jnp.bfloat16)
    grad_w_in = (
        lax.dot_general(
            cols_in, grad_pre_all, (((0,), (0,)), ((), ())), preferred_element_type=jnp.float32
        )
        * scale_back
    ).astype(jnp.bfloat16)
    return (grad_in, grad_w_in, grad_w_out)


def solution(mesh):
    placed = (
        P(("tokens", "mp"), None),
        P(("tokens", "mp"), None),
        P("tokens", "mp"),
        P(None, "mp"),
        P("mp", None),
    )
    return jax.shard_map(
        shards,
        mesh=mesh,
        in_specs=placed,
        out_specs=(P(("tokens", "mp"), None), P("tokens", "mp"), P("mp", "tokens")),
        check_vma=False,
    )
```

time: 649 us -> 105 us (0.16)
  waiting for transfers between devices: 544 us -> 35.5 us
  blocking collectives: 50.2 us -> 10 us
  starting transfers between devices: 0.26 us -> 22.1 us
  between operations: 14.7 us -> 0.72 us
  matrix products: 38.1 us -> 27.4 us
    reduce_scatter x2 -> x0, waiting for transfers between devices: 544 us -> none  [the longest x1 299 us: shards(): lax.psum_scatter(part_out.astype(jnp.bfloat16), 'tokens', scatter_dimensi...]
    all_to_all x0 -> x5, waiting for transfers between devices: none -> 35.5 us  [swap(): return lax.all_to_all(x, axis, 0, 0)]
    unnamed x1 -> x0, blocking collectives: 29.9 us -> none
    all_to_all x0 -> x5, starting transfers between devices: none -> 22.1 us  [swap(): return lax.all_to_all(x, axis, 0, 0)]
    all_gather x2 -> x0, blocking collectives: 20.3 us -> none  [the longest x1 11.1 us: shards(): lax.all_gather(tokens_in, 'mp', axis=0, tiled=True)]
    dot_general x2, matrix products: 17.7 us -> 6.88 us  [the longest x1 3.45 us: shards(): lax.dot_general(cols_in, grad_pre_all, (((0,), (0,)), ((), ())), preferre...]
    all_to_all x0 -> x1, blocking collectives: none -> 10 us  [swap(): return lax.all_to_all(x, axis, 0, 0)]
  transfers between devices with their start and end apart: 2 -> 5, of which waited for: 2 -> 4; matrix products, arithmetic and copies ran while one was open for 3% -> 26% of each run, Pallas kernels for 0% -> 0%
where the time goes in v1:
time: 105 us; the launch traced here: 103 us
  waiting for transfers between devices  35.5 us (34%)
  matrix products  27.4 us (26%)
  starting transfers between devices  22.1 us (21%)
  blocking collectives  10 us (10%)
  local copies, waits for them, and re-layouts  5.06 us (5%)
  other arithmetic  2.57 us (2%)
    all_to_all x5, waiting for transfers between devices, swap(): return lax.all_to_all(x, axis, 0, 0)  35.5 us
    all_to_all x5, starting transfers between devices, swap(): return lax.all_to_all(x, axis, 0, 0)  22.1 us
    dot_general x1, matrix products, shards(): lax.dot_general(rows_grad, w_out, (((1,), (1,)), ((), ())), preferred_ele...  11.2 us
    all_to_all x1, blocking collectives, swap(): return lax.all_to_all(x, axis, 0, 0)  10 us
    dot_general x1, matrix products, shards(): lax.dot_general(grad_pre, w_in, (((1,), (1,)), ((), ())), preferred_eleme...  9.23 us
    broadcast_in_dim x4, local copies, waits for them, and re-layouts, gather(): return swap(jnp.broadcast_to(x, (lax.axis_size(axis),) + x.shape), axis)  4.19 us
    dot_general x1, matrix products, shards(): lax.dot_general(cols_in, grad_pre_all, (((0,), (0,)), ((), ())), preferre...  3.45 us
    dot_general x1, matrix products, shards(): lax.dot_general(activated, cols_grad, (((0,), (0,)), ((), ())), preferred...  3.44 us
  transfers between devices with their start and end apart: 5, of which 4 were waited for; matrix products, arithmetic and copies ran while one was open for 26% of the time, Pallas kernels for 0%

profile of v1, /device:TPU:0, one launch (start us, length us, event | category | flops | bytes accessed | tf_op | source)
XLA Modules:
  0.0 103.4 jit_solution(8698531138973894682)
XLA Ops:
  0.6 1.6 %broadcast_in_dim.12 = bf16[8,4,5120]{2,1,0:T(4,128)(2,1)} broadcast(bf16[4,5120]{1,0:T(4,128)(2,1)} %param.6), dimensions={1,2} | broadcast | bytes 368640 | tf_op jit(solution)/shard_map/broadcast_in_dim | solution.py:29
  2.2 5.2 %all-to-all-start = ((bf16[8,4,5120]{2,1,0:T(4,128)(2,1)}), bf16[8,4,5120]{2,1,0:T(4,128)(2,1)S(1)}, u32[]{:S(2)}, u32[]{:S(2)}) async-start(bf16[8,4,5120]{2,1,0:T(4,128)(2,1)} %broadcast_in_dim.12), calls=%async_computation | async-start | bytes 655360 | tf_op jit(solution)/shard_map/all_to_all | solution.py:25
  7.4 1.5 %maximum_bitcast_fusion = bf16[4,2,4,1280]{3,2,1,0:T(4,128)(2,1)} fusion(bf16[1,4,4,1280]{3,1,0,2:T(4,128)(2,1)} %bitcast.18, bf16[1,4,4,1280]{3,1,0,2:T(4,128)(2,1)} %bitcast.19), kind=kLoop, calls=%fused_computation.31 | loop fusion | flops 40960 | bytes 163840 | tf_op jit(solution)/shard_map/transpose | solution.py:44
  8.9 6.1 %all-to-all-done = bf16[8,4,5120]{2,1,0:T(4,128)(2,1)S(1)} async-done(((bf16[8,4,5120]{2,1,0:T(4,128)(2,1)}), bf16[8,4,5120]{2,1,0:T(4,128)(2,1)S(1)}, u32[]{:S(2)}, u32[]{:S(2)}) %all-to-all-start) | async-done | bytes 327712 | tf_op jit(solution)/shard_map/all_to_all | solution.py:25
  15.0 4.9 %all-to-all-start.2 = ((bf16[4,2,4,1280]{3,2,1,0:T(4,128)(2,1)}), bf16[4,2,4,1280]{3,2,1,0:T(4,128)(2,1)S(1)}, u32[]{:S(2)}, u32[]{:S(2)}) async-start(bf16[4,2,4,1280]{3,2,1,0:T(4,128)(2,1)} %maximum_bitcast_fusion), calls=%async_computation.2 | async-start | bytes 163840 | tf_op jit(solution)/shard_map/all_to_all | solution.py:25
  20.0 11.2 %fusion.2 = bf16[32,1728]{1,0:T(8,128)(2,1)S(1)} fusion(bf16[32,5120]{1,0:T(8,128)(2,1)S(1)} %reshape.27, bf16[1728,5120]{1,0:T(8,128)(2,1)} %param.9, bf16[32,1728]{1,0:T(8,128)(2,1)} %param.7), kind=kOutput, calls=%fused_computation.6 | convolution fusion | flops 567336960 | bytes 18243584 | tf_op jit(solution)/shard_map/dot_general | solution.py:49
  31.2 9.2 %convolution_convert_fusion = bf16[32,5120]{1,0:T(8,128)(2,1)S(1)} fusion(bf16[32,1728]{1,0:T(8,128)(2,1)S(1)} %fusion.2, bf16[5120,1728]{0,1:T(8,128)(2,1)} %param.8), kind=kOutput, calls=%fused_computation.4 | convolution fusion | flops 566394880 | bytes 18132992 | tf_op jit(solution)/shard_map/dot_general | solution.py:55
  40.5 0.1 reshape.28
  40.6 10.0 %all_to_all.30 = bf16[8,4,5120]{2,1,0:T(4,128)(2,1)S(1)} all-to-all(bf16[8,4,5120]{2,1,0:T(4,128)(2,1)S(1)} %reshape.28), channel_id=1, replica_groups=mesh['mp'=8,'tokens'=4] {'mp'}, dimensions={0} | all-to-all | bytes 655360 | tf_op jit(solution)/shard_map/all_to_all | solution.py:25
  50.6 0.8 broadcast_in_dim.15
  51.4 5.1 %all-to-all-start.5 = ((bf16[4,32,1728]{2,1,0:T(8,128)(2,1)}), bf16[4,32,1728]{2,1,0:T(8,128)(2,1)S(1)}, u32[]{:S(2)}, u32[]{:S(2)}) async-start(bf16[4,32,1728]{2,1,0:T(8,128)(2,1)} %broadcast_in_dim.15), calls=%async_computation.5 | async-start | bytes 917504 | tf_op jit(solution)/shard_map/all_to_all | solution.py:25
  56.6 13.0 %all-to-all-done.5 = bf16[4,32,1728]{2,1,0:T(8,128)(2,1)S(1)} async-done(((bf16[4,32,1728]{2,1,0:T(8,128)(2,1)}), bf16[4,32,1728]{2,1,0:T(8,128)(2,1)S(1)}, u32[]{:S(2)}, u32[]{:S(2)}) %all-to-all-start.5) | async-done | bytes 442400 | tf_op jit(solution)/shard_map/all_to_all | solution.py:25
  69.5 1.0 broadcast_in_dim.13
  70.6 3.5 %all-to-all-start.3 = ((bf16[8,4,2,4,1280]{4,3,1,2,0:T(4,128)(2,1)}), bf16[8,4,2,4,1280]{4,3,1,2,0:T(4,128)(2,1)S(1)}, u32[]{:S(2)}, u32[]{:S(2)}) async-start(bf16[8,4,2,4,1280]{4,3,1,2,0:T(4,128)(2,1)} %broadcast_in_dim.13), calls=%async_computation.3 | async-start | bytes 1310720 | tf_op jit(solution)/shard_map/all_to_all | solution.py:25
  74.1 0.8 reduce_sum.12
  74.9 0.3 fusion.4
  75.2 10.0 %all-to-all-done.3 = bf16[8,4,2,4,1280]{4,3,1,2,0:T(4,128)(2,1)S(1)} async-done(((bf16[8,4,2,4,1280]{4,3,1,2,0:T(4,128)(2,1)}), bf16[8,4,2,4,1280]{4,3,1,2,0:T(4,128)(2,1)S(1)}, u32[]{:S(2)}, u32[]{:S(2)}) %all-to-all-start.3) | async-done | bytes 655392 | tf_op jit(solution)/shard_map/all_to_all | solution.py:25
  85.2 0.8 broadcast_in_dim.14
  86.0 3.5 %all-to-all-start.4 = ((bf16[4,32,1728]{2,1,0:T(8,128)(2,1)}), bf16[4,32,1728]{2,1,0:T(8,128)(2,1)S(1)}, u32[]{:S(2)}, u32[]{:S(2)}) async-start(bf16[4,32,1728]{2,1,0:T(8,128)(2,1)} %broadcast_in_dim.14), calls=%async_computation.4 | async-start | bytes 917504 | tf_op jit(solution)/shard_map/all_to_all | solution.py:25
  89.5 0.2 fusion.15
  89.7 0.1 copy.12
  90.1 3.4 %fusion.1 = bf16[1728,1280]{1,0:T(8,128)(2,1)} fusion(bf16[128,1728]{1,0:T(8,128)(2,1)S(1)} %bitcast.15, bf16[128,1280]{1,0:T(8,128)(2,1)S(1)} %unstack.15), kind=kOutput, calls=%fused_computation.3 | convolution fusion | flops 570654720 | bytes 5193728 | tf_op jit(solution)/shard_map/dot_general | solution.py:63
  93.5 6.4 %all-to-all-done.4 = bf16[4,32,1728]{2,1,0:T(8,128)(2,1)S(1)} async-done(((bf16[4,32,1728]{2,1,0:T(8,128)(2,1)}), bf16[4,32,1728]{2,1,0:T(8,128)(2,1)S(1)}, u32[]{:S(2)}, u32[]{:S(2)}) %all-to-all-start.4) | async-done | bytes 442400 | tf_op jit(solution)/shard_map/all_to_all | solution.py:25
  99.9 3.4 %fusion = bf16[1280,1728]{0,1:T(8,128)(2,1)} fusion(bf16[128,1280]{1,0:T(8,128)(2,1)S(1)} %unstack.13, bf16[128,1728]{1,0:T(8,128)(2,1)S(1)} %bitcast.17), kind=kOutput, calls=%fused_computation.2 | convolution fusion | flops 570654720 | bytes 5193728 | tf_op jit(solution)/shard_map/dot_general | solution.py:69
  (8 shorter events, 0.4 us)
Async XLA Ops:
  2.2 12.8 %all-to-all-start = ((bf16[8,4,5120]{2,1,0:T(4,128)(2,1)}), bf16[8,4,5120]{2,1,0:T(4,128)(2,1)S(1)}, u32[]{:S(2)}, u32[]{:S(2)}) async-start(bf16[8,4,5120]{2,1,0:T(4,128)(2,1)} %broadcast_in_dim.12), calls=%async_computation | async-start | bytes 655360 | tf_op jit(solution)/shard_map/all_to_all | solution.py:25
  15.0 25.6 %all-to-all-start.2 = ((bf16[4,2,4,1280]{3,2,1,0:T(4,128)(2,1)}), bf16[4,2,4,1280]{3,2,1,0:T(4,128)(2,1)S(1)}, u32[]{:S(2)}, u32[]{:S(2)}) async-start(bf16[4,2,4,1280]{3,2,1,0:T(4,128)(2,1)} %maximum_bitcast_fusion), calls=%async_computation.2 | async-start | bytes 163840 | tf_op jit(solution)/shard_map/all_to_all | solution.py:25
  31.2 19.4 %copy-start = (bf16[32,1728]{1,0:T(8,128)(2,1)S(1)}, bf16[32,1728]{1,0:T(8,128)(2,1)}, u32[]{:S(2)}) copy-start(bf16[32,1728]{1,0:T(8,128)(2,1)} %param.7) | copy-start | bytes 331780
  51.4 18.1 %all-to-all-start.5 = ((bf16[4,32,1728]{2,1,0:T(8,128)(2,1)}), bf16[4,32,1728]{2,1,0:T(8,128)(2,1)S(1)}, u32[]{:S(2)}, u32[]{:S(2)}) async-start(bf16[4,32,1728]{2,1,0:T(8,128)(2,1)} %broadcast_in_dim.15), calls=%async_computation.5 | async-start | bytes 917504 | tf_op jit(solution)/shard_map/all_to_all | solution.py:25
  70.6 14.6 %all-to-all-start.3 = ((bf16[8,4,2,4,1280]{4,3,1,2,0:T(4,128)(2,1)}), bf16[8,4,2,4,1280]{4,3,1,2,0:T(4,128)(2,1)S(1)}, u32[]{:S(2)}, u32[]{:S(2)}) async-start(bf16[8,4,2,4,1280]{4,3,1,2,0:T(4,128)(2,1)} %broadcast_in_dim.13), calls=%async_computation.3 | async-start | bytes 1310720 | tf_op jit(solution)/shard_map/all_to_all | solution.py:25
  86.0 13.9 %all-to-all-start.4 = ((bf16[4,32,1728]{2,1,0:T(8,128)(2,1)}), bf16[4,32,1728]{2,1,0:T(8,128)(2,1)S(1)}, u32[]{:S(2)}, u32[]{:S(2)}) async-start(bf16[4,32,1728]{2,1,0:T(8,128)(2,1)} %broadcast_in_dim.14), calls=%async_computation.4 | async-start | bytes 917504 | tf_op jit(solution)/shard_map/all_to_all | solution.py:25

commit v2 on v1

v2 whole, which is shorter than its diff:
```python
import functools
import math

import jax
import jax.numpy as jnp
from jax import lax
from jax.experimental import pallas as pl
from jax.experimental.pallas import tpu as pltpu
from jax.sharding import PartitionSpec as P

root_two_pi = math.sqrt(2.0 / math.pi)
cubic = 0.044715


def gelu_value(pre):
    inner = root_two_pi * (pre + cubic * pre * pre * pre)
    return 0.5 * pre * (1.0 + jnp.tanh(inner))


def gelu_slope(pre):
    tanh_val = jnp.tanh(root_two_pi * (pre + cubic * pre * pre * pre))
    return 0.5 * (1.0 + tanh_val) + 0.5 * pre * (1.0 - tanh_val * tanh_val) * root_two_pi * (
        1.0 + 3.0 * cubic * pre * pre
    )


def partner(i, k, n):
    return i ^ k if n & (n - 1) == 0 else (i + k) % n


def fetch(x, axis, k):
    n = lax.axis_size(axis)
    return lax.ppermute(x, axis, [(partner(i, k, n), i) for i in range(n)])


def swap(x, axis):
    return lax.all_to_all(x, axis, 0, 0)


def block_of(width, most):
    return max([b for b in range(128, most + 1, 128) if width % b == 0], default=width)


def grad_pre_body(steps, rows_ref, pre_ref, w_ref, out_ref, total_ref):
    step = pl.program_id(0)
    term = lax.dot_general(
        rows_ref[...], w_ref[...], (((1,), (1,)), ((), ())), preferred_element_type=jnp.float32
    )

    @pl.when(step == 0)
    def _():
        total_ref[...] = term

    @pl.when(step > 0)
    def _():
        total_ref[...] += term

    @pl.when(step == steps - 1)
    def _():
        slope = gelu_slope(pre_ref[...].astype(jnp.float32))
        out_ref[...] = (total_ref[...] * slope).astype(jnp.bfloat16)


def grad_pre_of(rows_grad, pre_act, w_out):
    group, width = rows_grad.shape
    hidden = w_out.shape[0]
    block = block_of(width, 1024)
    return pl.pallas_call(
        functools.partial(grad_pre_body, width // block),
        grid=(width // block,),
        in_specs=[
            pl.BlockSpec((group, block), lambda i: (0, i)),
            pl.BlockSpec((group, hidden), lambda i: (0, 0)),
            pl.BlockSpec((hidden, block), lambda i: (0, i)),
        ],
        out_specs=pl.BlockSpec((group, hidden), lambda i: (0, 0)),
        out_shape=jax.ShapeDtypeStruct((group, hidden), jnp.bfloat16),
        scratch_shapes=[pltpu.VMEM((group, hidden), jnp.float32)],
        compiler_params=pltpu.CompilerParams(vmem_limit_bytes=32 << 20),
        cost_estimate=pl.CostEstimate(
            flops=2 * group * width * hidden, bytes_accessed=2 * hidden * width, transcendentals=0
        ),
        name="grad_pre",
    )(rows_grad, pre_act, w_out)


def grad_in_body(grad_pre_ref, w_ref, out_ref):
    out_ref[...] = jnp.dot(
        grad_pre_ref[...], w_ref[...], preferred_element_type=jnp.float32
    ).astype(jnp.bfloat16)


def grad_in_part(grad_pre, w_in_t):
    group, hidden = grad_pre.shape
    width = w_in_t.shape[1]
    block = block_of(width, 1024)
    return pl.pallas_call(
        grad_in_body,
        grid=(width // block,),
        in_specs=[
            pl.BlockSpec((group, hidden), lambda i: (0, 0)),
            pl.BlockSpec((hidden, block), lambda i: (0, i)),
        ],
        out_specs=pl.BlockSpec((group, block), lambda i: (0, i)),
        out_shape=jax.ShapeDtypeStruct((group, width), jnp.bfloat16),
        compiler_params=pltpu.CompilerParams(vmem_limit_bytes=32 << 20),
        cost_estimate=pl.CostEstimate(
            flops=2 * group * width * hidden, bytes_accessed=2 * hidden * width, transcendentals=0
        ),
        name="grad_in_part",
    )(grad_pre, w_in_t)


def shards(tokens_in, grad_out, pre_act, w_in, w_out):
    n_mp, n_tok = lax.axis_size("mp"), lax.axis_size("tokens")
    t = lax.axis_index("tokens")
    rows, width = tokens_in.shape
    group, hidden = pre_act.shape
    part = width // n_tok
    total = group * n_tok
    scale_back = 1.0 / math.sqrt(total)

    both = jnp.concatenate([tokens_in, grad_out], axis=0)
    wide = max(hidden, part)
    own_pre = jnp.pad(pre_act, ((0, 0), (0, wide - hidden)))
    pre, cols = [], []
    for k in range(n_tok):
        taker = t ^ k if n_tok & (n_tok - 1) == 0 else (t - k) % n_tok
        piece = lax.dynamic_slice_in_dim(both, taker * part, part, axis=1)
        if k == 0:
            pre.append(pre_act)
            cols.append(piece)
        else:
            piece = jnp.pad(piece, ((0, 0), (0, wide - part)))
            packed = fetch(jnp.concatenate([own_pre, piece], axis=0), "tokens", k)
            pre.append(packed[:group, :hidden])
            cols.append(packed[group:, :part])
    pre_all = jnp.concatenate(pre, axis=0)
    cols = jnp.stack(cols).reshape(n_tok, 2, rows, part).transpose(1, 0, 2, 3)
    cols = swap(jnp.broadcast_to(cols, (n_mp,) + cols.shape), "mp")
    cols = cols.transpose(1, 2, 0, 3, 4)
    cols_in, cols_grad = cols.reshape(2, total, part)

    rows_grad = lax.all_gather(grad_out, "mp", axis=0, tiled=True)
    grad_pre = grad_pre_of(rows_grad, pre_act, w_out)
    grad_pre_all = jnp.concatenate(
        [grad_pre] + [fetch(grad_pre, "tokens", k) for k in range(1, n_tok)], axis=0
    )

    blocks = swap(grad_in_part(grad_pre, w_in.T).reshape(n_mp, rows, width), "mp")
    grad_in = jnp.sum(blocks.astype(jnp.float32), axis=0).astype(jnp.bfloat16)

    activated = gelu_value(pre_all.astype(jnp.float32)).astype(jnp.bfloat16)
    grad_w_out = (
        lax.dot_general(
            activated, cols_grad, (((0,), (0,)), ((), ())), preferred_element_type=jnp.float32
        )
        * scale_back
    ).astype(jnp.bfloat16)
    grad_w_in = (
        lax.dot_general(
            cols_in, grad_pre_all, (((0,), (0,)), ((), ())), preferred_element_type=jnp.float32
        )
        * scale_back
    ).astype(jnp.bfloat16)
    return (grad_in, grad_w_in, grad_w_out)


def solution(mesh):
    placed = (
        P(("tokens", "mp"), None),
        P(("tokens", "mp"), None),
        P("tokens", "mp"),
        P(None, "mp"),
        P("mp", None),
    )
    return jax.shard_map(
        shards,
        mesh=mesh,
        in_specs=placed,
        out_specs=(P(("tokens", "mp"), None), P("tokens", "mp"), P("mp", "tokens")),
        check_vma=False,
    )
```

time: 105 us -> 78.9 us (0.75); the launches traced: 103 us -> 78.4 us
  waiting for transfers between devices: 35.5 us -> 13.2 us
  matrix products: 27.4 us -> 7.02 us
  Pallas kernels: 0 us -> 12 us
  local copies, waits for them, and re-layouts: 5.06 us -> 15.6 us
  starting transfers between devices: 22.1 us -> 17.1 us
    all_to_all x5 -> x2, waiting for transfers between devices: 35.5 us -> 13.2 us  [swap(): return lax.all_to_all(x, axis, 0, 0)]
    dot_general x2 -> x0, matrix products: 20.5 us -> none  [the longest x1 11.2 us: shards(): lax.dot_general(rows_grad, w_out, (((1,), (1,)), ((), ())), preferred_ele...]
    all_to_all x5 -> x2, starting transfers between devices: 22.1 us -> 6.97 us  [swap(): return lax.all_to_all(x, axis, 0, 0)]
    unnamed x2 -> x9, local copies, waits for them, and re-layouts: 0.01 us -> 13 us
    pallas_call x0 -> x2, Pallas kernels: none -> 12 us  [the longest x1 7.21 us: grad_pre_of(): pl.pallas_call(functools.partial(grad_pre_body, width // block), grid=(wi...]
    ppermute x0 -> x6, starting transfers between devices: none -> 10.1 us  [fetch(): return lax.ppermute(x, axis, [(partner(i, k, n), i) for i in range(n)])]
    all_to_all x1 -> x0, blocking collectives: 10 us -> none  [swap(): return lax.all_to_all(x, axis, 0, 0)]
    all_gather x0 -> x1, blocking collectives: none -> 9.89 us  [shards(): rows_grad = lax.all_gather(grad_out, 'mp', axis=0, tiled=True)]
  transfers between devices with their start and end apart: 5 -> 8, of which waited for: 4 -> 2; matrix products, arithmetic and copies ran while one was open for 26% -> 8% of each run, Pallas kernels for 0% -> 15%
where the time goes in v2:
time: 78.9 us; the launch traced here: 78.4 us
  starting transfers between devices  17.1 us (22%)
  local copies, waits for them, and re-layouts  15.6 us (20%)
  waiting for transfers between devices  13.2 us (17%)
  Pallas kernels  12 us (15%)
  blocking collectives  9.89 us (13%)
  matrix products  7.02 us (9%)
  other arithmetic  2.7 us (3%)
  between operations  0.88 us (1%)
    all_to_all x2, waiting for transfers between devices, swap(): return lax.all_to_all(x, axis, 0, 0)  13.2 us
    unnamed x9, local copies, waits for them, and re-layouts  13 us
    ppermute x6, starting transfers between devices, fetch(): return lax.ppermute(x, axis, [(partner(i, k, n), i) for i in range(n)])  10.1 us
    all_gather x1, blocking collectives, shards(): rows_grad = lax.all_gather(grad_out, 'mp', axis=0, tiled=True)  9.89 us
    pallas_call x1, Pallas kernels, grad_pre_of(): pl.pallas_call(functools.partial(grad_pre_body, width // block), grid=(wi...  7.21 us
    all_to_all x2, starting transfers between devices, swap(): return lax.all_to_all(x, axis, 0, 0)  6.97 us
    pallas_call x1, Pallas kernels, grad_in_part(): pl.pallas_call(grad_in_body, grid=(width // block,), in_specs=[pl.BlockSp...  4.77 us
    dot_general x1, matrix products, shards(): lax.dot_general(activated, cols_grad, (((0,), (0,)), ((), ())), preferred...  3.57 us
  transfers between devices with their start and end apart: 8, of which 2 were waited for; matrix products, arithmetic and copies ran while one was open for 8% of the time, Pallas kernels for 15%

profile of v2, /device:TPU:0, one launch (start us, length us, event | category | flops | bytes accessed | tf_op | source)
XLA Modules:
  0.0 78.4 jit_solution(7734766377279457303)
XLA Ops:
  0.7 0.9 %fusion.33 = (bf16[8,1280]{1,0:T(8,128)(2,1)S(1)}, bf16[8,1280]{1,0:T(8,128)(2,1)S(1)}, bf16[8,1280]{1,0:T(8,128)(2,1)S(1)}, bf16[8,1280]{1,0:T(8,128)(2,1)S(1)}) fusion(s32[]{:T(128)S(6)} %select_n.12, bf16[4,5120]{1,0:T(4,128)(2,1)} %param.5, bf16[4,5120]{1,0:T(4,128)(2,1)} %param.6, s32[]{:T(128)S(6)} %select_n.13, s32[]{:T(128)S(6)} %select_n.14, ...), kind=kLoop, calls=%fused_computation.49 | loop fusion | flops 163840 | bytes 163856 | tf_op jit(solution)/shard_map/concatenate | solution.py:123
  1.6 0.9 %fusion.29 = (bf16[40,1728]{1,0:T(8,128)(2,1)S(1)}, bf16[40,1728]{1,0:T(8,128)(2,1)S(1)}, bf16[40,1728]{1,0:T(8,128)(2,1)S(1)}) fusion(bf16[8,1280]{1,0:T(8,128)(2,1)S(1)} %get-tuple-element.9, bf16[32,1728]{1,0:T(8,128)(2,1)} %pre_ref.1, bf16[8,1280]{1,0:T(8,128)(2,1)S(1)} %get-tuple-element.10, bf16[8,1280]{1,0:T(8,128)(2,1)S(1)} %get-tuple-element.11), kind=kLoop, calls=%fused_computation.36 | loop fusion | flops 967680 | bytes 586752 | tf_op jit(solution)/shard_map/concatenate | solution.py:135
  2.5 3.1 %collective-permute-start = (bf16[40,1728]{1,0:T(8,128)(2,1)S(1)}, bf16[40,1728]{1,0:T(8,128)(2,1)S(1)}, u32[]{:S(2)}, u32[]{:S(2)}) collective-permute-start(bf16[40,1728]{1,0:T(8,128)(2,1)S(1)} %get-tuple-element.5), channel_id=1, source_target_pairs={{1,0},{0,1},{3,2},{2,3},{5,4},{4,5},{7,6},{6,7},{9,8},{8,9},{11,10... | collective-permute-start | bytes 414728 | tf_op jit(solution)/shard_map/ppermute | solution.py:33
  5.6 2.6 %collective-permute-start.1 = (bf16[40,1728]{1,0:T(8,128)(2,1)S(1)}, bf16[40,1728]{1,0:T(8,128)(2,1)S(1)}, u32[]{:S(2)}, u32[]{:S(2)}) collective-permute-start(bf16[40,1728]{1,0:T(8,128)(2,1)S(1)} %get-tuple-element.6), channel_id=1, source_target_pairs={{2,0},{3,1},{0,2},{1,3},{6,4},{7,5},{4,6},{5,7},{10,8},{11,9},{8,1... | collective-permute-start | bytes 414728 | tf_op jit(solution)/shard_map/ppermute | solution.py:33
  8.2 9.9 %all-gather = bf16[8,4,5120]{2,1,0:T(4,128)(2,1)S(1)} all-gather(bf16[1,4,5120]{2,1,0:T(4,128)(2,1)} %bitcast.12), channel_id=1, replica_groups=mesh['mp'=8,'tokens'=4] {'mp'}, dimensions={0}, use_global_device_ids=true | all-gather | bytes 368640 | tf_op jit(solution)/shard_map/all_gather | solution.py:144
  18.2 6.0 %copy-done.1 = bf16[1728,5120]{1,0:T(8,128)(2,1)S(1)} copy-done((bf16[1728,5120]{1,0:T(8,128)(2,1)S(1)}, bf16[1728,5120]{1,0:T(8,128)(2,1)}, u32[]{:S(2)}) %copy-start.1) | copy-done | bytes 17694744
  24.2 0.9 %copy-done.2 = bf16[32,1728]{1,0:T(8,128)(2,1)S(1)} copy-done((bf16[32,1728]{1,0:T(8,128)(2,1)S(1)}, bf16[32,1728]{1,0:T(8,128)(2,1)}, u32[]{:S(2)}) %copy-start.2) | copy-done | bytes 110616
  25.1 7.2 %grad_pre.1.grad_pre_ref = bf16[32,1728]{1,0:T(8,128)(2,1)S(1)} custom-call(bf16[32,5120]{1,0:T(8,128)(2,1)S(1)} %reshape.25.rows_ref, bf16[32,1728]{1,0:T(8,128)(2,1)S(1)} %copy-done.2, bf16[1728,5120]{1,0:T(8,128)(2,1)S(1)} %copy-done.1), custom_call_target="tpu_custom_call" | custom-call | flops 566231040 | bytes 17694720 | tf_op jit(solution)/shard_map/grad_pre/pallas_call | solution.py:68
  32.3 6.0 %copy-done = bf16[5120,1728]{0,1:T(8,128)(2,1)S(1)} copy-done((bf16[5120,1728]{0,1:T(8,128)(2,1)S(1)}, bf16[5120,1728]{0,1:T(8,128)(2,1)}, u32[]{:S(2)}) %copy-start) | copy-done | bytes 17694744
  38.4 4.8 %grad_in_part.1 = bf16[32,5120]{1,0:T(8,128)(2,1)S(1)} custom-call(bf16[32,1728]{1,0:T(8,128)(2,1)S(1)} %grad_pre.1.grad_pre_ref, bf16[1728,5120]{1,0:T(8,128)(2,1)S(1)} %bitcast.10), custom_call_target="tpu_custom_call" | custom-call | flops 566231040 | bytes 17694720 | tf_op jit(solution)/shard_map/grad_in_part/pallas_call | solution.py:97
  43.2 0.9 %reshape.23 = bf16[8,4,5120]{2,1,0:T(4,128)(2,1)} reshape(bf16[32,5120]{1,0:T(8,128)(2,1)S(1)} %grad_in_part.1) | data formatting | bytes 655360 | tf_op jit(solution)/shard_map/reshape | solution.py:150
  44.0 3.4 %all-to-all-start = ((bf16[8,4,5120]{2,1,0:T(4,128)(2,1)}), bf16[8,4,5120]{2,1,0:T(4,128)(2,1)S(1)}, u32[]{:S(2)}, u32[]{:S(2)}) async-start(bf16[8,4,5120]{2,1,0:T(4,128)(2,1)} %reshape.23), calls=%async_computation | async-start | bytes 655360 | tf_op jit(solution)/shard_map/all_to_all | solution.py:37
  47.7 7.4 %all-to-all-done = bf16[8,4,5120]{2,1,0:T(4,128)(2,1)S(1)} async-done(((bf16[8,4,5120]{2,1,0:T(4,128)(2,1)}), bf16[8,4,5120]{2,1,0:T(4,128)(2,1)S(1)}, u32[]{:S(2)}, u32[]{:S(2)}) %all-to-all-start) | async-done | bytes 327712 | tf_op jit(solution)/shard_map/all_to_all | solution.py:37
  55.0 1.0 %broadcast_in_dim.3 = bf16[8,2,4,4,1280]{4,3,2,1,0:T(4,128)(2,1)} broadcast(bf16[2,4,4,1280]{3,2,1,0:T(4,128)(2,1)S(1)} %maximum_bitcast_fusion), dimensions={1,2,3,4} | broadcast | bytes 737280 | tf_op jit(solution)/shard_map/broadcast_in_dim | solution.py:140
  56.0 3.5 %all-to-all-start.1 = ((bf16[8,2,4,4,1280]{4,3,2,1,0:T(4,128)(2,1)}), bf16[8,2,4,4,1280]{4,3,2,1,0:T(4,128)(2,1)S(1)}, u32[]{:S(2)}, u32[]{:S(2)}) async-start(bf16[8,2,4,4,1280]{4,3,2,1,0:T(4,128)(2,1)} %broadcast_in_dim.3), calls=%async_computation.1 | async-start | bytes 1310720 | tf_op jit(solution)/shard_map/all_to_all | solution.py:37
  59.6 3.7 %collective-permute-start.5 = (bf16[32,1728]{1,0:T(8,128)(2,1)S(1)}, bf16[32,1728]{1,0:T(8,128)(2,1)S(1)}, u32[]{:S(2)}, u32[]{:S(2)}) collective-permute-start(bf16[32,1728]{1,0:T(8,128)(2,1)S(1)} %grad_pre.1.grad_pre_ref), channel_id=1, source_target_pairs={{3,0},{2,1},{1,2},{0,3},{7,4},{6,5},{5,6},{4,7},{11,8},{10,9},{9,1... | collective-permute-start | bytes 331784 | tf_op jit(solution)/shard_map/ppermute | solution.py:33
  63.3 0.8 collective-permute-start.3
  64.1 0.8 reduce_sum.12
  64.8 5.8 %all-to-all-done.1 = bf16[8,2,4,4,1280]{4,3,2,1,0:T(4,128)(2,1)S(1)} async-done(((bf16[8,2,4,4,1280]{4,3,2,1,0:T(4,128)(2,1)}), bf16[8,2,4,4,1280]{4,3,2,1,0:T(4,128)(2,1)S(1)}, u32[]{:S(2)}, u32[]{:S(2)}) %all-to-all-start.1) | async-done | bytes 655392 | tf_op jit(solution)/shard_map/all_to_all | solution.py:37
  70.7 0.2 fusion.42
  70.9 0.1 copy.14
  71.1 3.6 %fusion.1 = bf16[1728,1280]{1,0:T(8,128)(2,1)} fusion(bf16[128,1280]{1,0:T(8,128)(2,1)S(1)} %unstack.15, bf16[32,1728]{1,0:T(8,128)(2,1)S(1)} %slice.31, bf16[32,1728]{1,0:T(8,128)(2,1)S(1)} %slice.30, bf16[32,1728]{1,0:T(8,128)(2,1)S(1)} %slice.29, bf16[32,1728]{1,0:T(8,128)(2,1)S(1)} %copy-done.3), kind=kOutput, calls=%fused_computation.3 | convolution fusion | flops 574414848 | bytes 5193728 | tf_op jit(solution)/shard_map/dot_general | solution.py:155
  74.7 0.1 copy.13
  74.9 3.5 %fusion = bf16[1280,1728]{0,1:T(8,128)(2,1)} fusion(bf16[128,1280]{1,0:T(8,128)(2,1)S(1)} %unstack.13, bf16[32,1728]{1,0:T(8,128)(2,1)S(1)} %collective-permute-done.5, bf16[32,1728]{1,0:T(8,128)(2,1)S(1)} %collective-permute-done.4, bf16[32,1728]{1,0:T(8,128)(2,1)S(1)} %collective-permute-done.3, bf16[32,1728]{1,0:T(8,128)(2,1)S(1)} %grad_pre.1.grad_pre_ref), kind=kOutput, calls=%fused_computation.2 | convolution fusion | flops 572424192 | bytes 5193728 | tf_op jit(solution)/shard_map/dot_general | solution.py:161
  (27 shorter events, 0.4 us)
Async XLA Ops:
  2.5 45.0 %collective-permute-start = (bf16[40,1728]{1,0:T(8,128)(2,1)S(1)}, bf16[40,1728]{1,0:T(8,128)(2,1)S(1)}, u32[]{:S(2)}, u32[]{:S(2)}) collective-permute-start(bf16[40,1728]{1,0:T(8,128)(2,1)S(1)} %get-tuple-element.5), channel_id=1, source_target_pairs={{1,0},{0,1},{3,2},{2,3},{5,4},{4,5},{7,6},{6,7},{9,8},{8,9},{11,10... | collective-permute-start | bytes 414728 | tf_op jit(solution)/shard_map/ppermute | solution.py:33
  5.6 41.9 %collective-permute-start.1 = (bf16[40,1728]{1,0:T(8,128)(2,1)S(1)}, bf16[40,1728]{1,0:T(8,128)(2,1)S(1)}, u32[]{:S(2)}, u32[]{:S(2)}) collective-permute-start(bf16[40,1728]{1,0:T(8,128)(2,1)S(1)} %get-tuple-element.6), channel_id=1, source_target_pairs={{2,0},{3,1},{0,2},{1,3},{6,4},{7,5},{4,6},{5,7},{10,8},{11,9},{8,1... | collective-permute-start | bytes 414728 | tf_op jit(solution)/shard_map/ppermute | solution.py:33
  8.2 39.4 %collective-permute-start.2 = (bf16[40,1728]{1,0:T(8,128)(2,1)S(1)}, bf16[40,1728]{1,0:T(8,128)(2,1)S(1)}, u32[]{:S(2)}, u32[]{:S(2)}) collective-permute-start(bf16[40,1728]{1,0:T(8,128)(2,1)S(1)} %get-tuple-element.7), channel_id=1, source_target_pairs={{3,0},{2,1},{1,2},{0,3},{7,4},{6,5},{5,6},{4,7},{11,8},{10,9},{9,1... | collective-permute-start | bytes 414728 | tf_op jit(solution)/shard_map/ppermute | solution.py:33
  18.2 6.0 %copy-start.1 = (bf16[1728,5120]{1,0:T(8,128)(2,1)S(1)}, bf16[1728,5120]{1,0:T(8,128)(2,1)}, u32[]{:S(2)}) copy-start(bf16[1728,5120]{1,0:T(8,128)(2,1)} %w_ref.1) | copy-start | bytes 53084164
  24.2 0.9 %copy-start.2 = (bf16[32,1728]{1,0:T(8,128)(2,1)S(1)}, bf16[32,1728]{1,0:T(8,128)(2,1)}, u32[]{:S(2)}) copy-start(bf16[32,1728]{1,0:T(8,128)(2,1)} %pre_ref.1) | copy-start | bytes 331780
  32.3 6.0 %copy-start = (bf16[5120,1728]{0,1:T(8,128)(2,1)S(1)}, bf16[5120,1728]{0,1:T(8,128)(2,1)}, u32[]{:S(2)}) copy-start(bf16[5120,1728]{0,1:T(8,128)(2,1)} %param.8) | copy-start | bytes 53084164
  38.4 32.7 %copy-start.3 = (bf16[32,1728]{1,0:T(8,128)(2,1)S(1)}, bf16[32,1728]{1,0:T(8,128)(2,1)}, u32[]{:S(2)}) copy-start(bf16[32,1728]{1,0:T(8,128)(2,1)} %pre_ref.1) | copy-start | bytes 331780
  44.0 11.0 %all-to-all-start = ((bf16[8,4,5120]{2,1,0:T(4,128)(2,1)}), bf16[8,4,5120]{2,1,0:T(4,128)(2,1)S(1)}, u32[]{:S(2)}, u32[]{:S(2)}) async-start(bf16[8,4,5120]{2,1,0:T(4,128)(2,1)} %reshape.23), calls=%async_computation | async-start | bytes 655360 | tf_op jit(solution)/shard_map/all_to_all | solution.py:37
  56.0 14.6 %all-to-all-start.1 = ((bf16[8,2,4,4,1280]{4,3,2,1,0:T(4,128)(2,1)}), bf16[8,2,4,4,1280]{4,3,2,1,0:T(4,128)(2,1)S(1)}, u32[]{:S(2)}, u32[]{:S(2)}) async-start(bf16[8,2,4,4,1280]{4,3,2,1,0:T(4,128)(2,1)} %broadcast_in_dim.3), calls=%async_computation.1 | async-start | bytes 1310720 | tf_op jit(solution)/shard_map/all_to_all | solution.py:37
  59.6 15.3 %collective-permute-start.5 = (bf16[32,1728]{1,0:T(8,128)(2,1)S(1)}, bf16[32,1728]{1,0:T(8,128)(2,1)S(1)}, u32[]{:S(2)}, u32[]{:S(2)}) collective-permute-start(bf16[32,1728]{1,0:T(8,128)(2,1)S(1)} %grad_pre.1.grad_pre_ref), channel_id=1, source_target_pairs={{3,0},{2,1},{1,2},{0,3},{7,4},{6,5},{5,6},{4,7},{11,8},{10,9},{9,1... | collective-permute-start | bytes 331784 | tf_op jit(solution)/shard_map/ppermute | solution.py:33
  63.3 11.6 %collective-permute-start.4 = (bf16[32,1728]{1,0:T(8,128)(2,1)S(1)}, bf16[32,1728]{1,0:T(8,128)(2,1)S(1)}, u32[]{:S(2)}, u32[]{:S(2)}) collective-permute-start(bf16[32,1728]{1,0:T(8,128)(2,1)S(1)} %grad_pre.1.grad_pre_ref), channel_id=1, source_target_pairs={{2,0},{3,1},{0,2},{1,3},{6,4},{7,5},{4,6},{5,7},{10,8},{11,9},{8,1... | collective-permute-start | bytes 331784 | tf_op jit(solution)/shard_map/ppermute | solution.py:33
  63.3 11.7 %collective-permute-start.3 = (bf16[32,1728]{1,0:T(8,128)(2,1)S(1)}, bf16[32,1728]{1,0:T(8,128)(2,1)S(1)}, u32[]{:S(2)}, u32[]{:S(2)}) collective-permute-start(bf16[32,1728]{1,0:T(8,128)(2,1)S(1)} %grad_pre.1.grad_pre_ref), channel_id=1, source_target_pairs={{1,0},{0,1},{3,2},{2,3},{5,4},{4,5},{7,6},{6,7},{9,8},{8,9},{11,10... | collective-permute-start | bytes 331784 | tf_op jit(solution)/shard_map/ppermute | solution.py:33

commit v3 on v2

--- a/solution.py
+++ b/solution.py
@@ -37,46 +37,40 @@
     return lax.all_to_all(x, axis, 0, 0)
 
 
-def block_of(width, most):
-    return max([b for b in range(128, most + 1, 128) if width % b == 0], default=width)
+def block_of(size, most, unit):
+    return max([b for b in range(unit, most + 1, unit) if size % b == 0], default=size)
 
 
 def grad_pre_body(steps, rows_ref, pre_ref, w_ref, out_ref, total_ref):
     step = pl.program_id(0)
-    term = lax.dot_general(
-        rows_ref[...], w_ref[...], (((1,), (1,)), ((), ())), preferred_element_type=jnp.float32
-    )
-
-    @pl.when(step == 0)
-    def _():
-        total_ref[...] = term
-
-    @pl.when(step > 0)
-    def _():
-        total_ref[...] += term
+    block = w_ref.shape[0]
+    here = pl.ds(pl.multiple_of(step * block, block), block)
+    total_ref[here, :] = lax.dot_general(
+        w_ref[...], rows_ref[...], (((1,), (1,)), ((), ())), preferred_element_type=jnp.float32
+    )
 
     @pl.when(step == steps - 1)
     def _():
         slope = gelu_slope(pre_ref[...].astype(jnp.float32))
-        out_ref[...] = (total_ref[...] * slope).astype(jnp.bfloat16)
+        out_ref[...] = (total_ref[...].T * slope).astype(jnp.bfloat16)
 
 
 def grad_pre_of(rows_grad, pre_act, w_out):
     group, width = rows_grad.shape
     hidden = w_out.shape[0]
-    block = block_of(width, 1024)
+    block = block_of(hidden, 192, 16)
     return pl.pallas_call(
-        functools.partial(grad_pre_body, width // block),
-        grid=(width // block,),
+        functools.partial(grad_pre_body, hidden // block),
+        grid=(hidden // block,),
         in_specs=[
-            pl.BlockSpec((group, block), lambda i: (0, i)),
+            pl.BlockSpec((group, width), lambda i: (0, 0)),
             pl.BlockSpec((group, hidden), lambda i: (0, 0)),
-            pl.BlockSpec((hidden, block), lambda i: (0, i)),
+            pl.BlockSpec((block, width), lambda i: (i, 0)),
         ],
         out_specs=pl.BlockSpec((group, hidden), lambda i: (0, 0)),
         out_shape=jax.ShapeDtypeStruct((group, hidden), jnp.bfloat16),
-        scratch_shapes=[pltpu.VMEM((group, hidden), jnp.float32)],
-        compiler_params=pltpu.CompilerParams(vmem_limit_bytes=32 << 20),
+        scratch_shapes=[pltpu.VMEM((hidden, group), jnp.float32)],
+        compiler_params=pltpu.CompilerParams(vmem_limit_bytes=56 << 20),
         cost_estimate=pl.CostEstimate(
             flops=2 * group * width * hidden, bytes_accessed=2 * hidden * width, transcendentals=0
         ),
@@ -93,7 +87,7 @@
 def grad_in_part(grad_pre, w_in_t):
     group, hidden = grad_pre.shape
     width = w_in_t.shape[1]
-    block = block_of(width, 1024)
+    block = block_of(width, 512, 128)
     return pl.pallas_call(
         grad_in_body,
         grid=(width // block,),
@@ -103,12 +97,54 @@
         ],
         out_specs=pl.BlockSpec((group, block), lambda i: (0, i)),
         out_shape=jax.ShapeDtypeStruct((group, width), jnp.bfloat16),
-        compiler_params=pltpu.CompilerParams(vmem_limit_bytes=32 << 20),
+        compiler_params=pltpu.CompilerParams(vmem_limit_bytes=56 << 20),
         cost_estimate=pl.CostEstimate(
             flops=2 * group * width * hidden, bytes_accessed=2 * hidden * width, transcendentals=0
         ),
         name="grad_in_part",
     )(grad_pre, w_in_t)
+
+
+def grad_w_body(places, scale_back, *refs):
+    pre_refs, grad_pre_refs = refs[:places], refs[places : 2 * places]
+    cols_ref, in_ref, out_ref, act_t, grad_pre_t = refs[2 * places :]
+    group, hidden = grad_pre_refs[0].shape
+
+    @pl.when(pl.program_id(0) == 0)
+    def _():
+        for k in range(places):
+            here = slice(k * group, (k + 1) * group)
+            pre = pre_refs[k][:group, :hidden].astype(jnp.float32)
+            act_t[:, here] = gelu_value(pre).T.astype(jnp.bfloat16)
+            grad_pre_t[:, here] = grad_pre_refs[k][...].astype(jnp.float32).T.astype(jnp.bfloat16)
+
+    for left, right, to_ref in ((grad_pre_t, 0, in_ref), (act_t, 1, out_ref)):
+        term = jnp.dot(left[...], cols_ref[right], preferred_element_type=jnp.float32)
+        to_ref[...] = (term * scale_back).astype(jnp.bfloat16)
+
+
+def grad_w_of(pre, grad_pre, cols, scale_back):
+    places = len(pre)
+    group, hidden = grad_pre[0].shape
+    total, part = cols.shape[1:]
+    block = block_of(part, 256, 128)
+    whole = [pl.BlockSpec(x.shape, lambda i: (0, 0)) for x in (*pre, *grad_pre)]
+    shape = jax.ShapeDtypeStruct((hidden, part), jnp.bfloat16)
+    return pl.pallas_call(
+        functools.partial(grad_w_body, places, scale_back),
+        grid=(part // block,),
+        in_specs=[*whole, pl.BlockSpec((2, total, block), lambda i: (0, 0, i))],
+        out_specs=[pl.BlockSpec((hidden, block), lambda i: (0, i))] * 2,
+        out_shape=[shape, shape],
+        scratch_shapes=[pltpu.VMEM((hidden, total), jnp.bfloat16)] * 2,
+        compiler_params=pltpu.CompilerParams(vmem_limit_bytes=56 << 20),
+        cost_estimate=pl.CostEstimate(
+            flops=4 * total * part * hidden,
+            bytes_accessed=4 * hidden * part,
+            transcendentals=total * hidden,
+        ),
+        name="grad_w",
+    )(*pre, *grad_pre, cols)
 
 
 def shards(tokens_in, grad_out, pre_act, w_in, w_out):
@@ -133,37 +169,21 @@
         else:
             piece = jnp.pad(piece, ((0, 0), (0, wide - part)))
             packed = fetch(jnp.concatenate([own_pre, piece], axis=0), "tokens", k)
-            pre.append(packed[:group, :hidden])
+            pre.append(packed)
             cols.append(packed[group:, :part])
-    pre_all = jnp.concatenate(pre, axis=0)
     cols = jnp.stack(cols).reshape(n_tok, 2, rows, part).transpose(1, 0, 2, 3)
     cols = swap(jnp.broadcast_to(cols, (n_mp,) + cols.shape), "mp")
-    cols = cols.transpose(1, 2, 0, 3, 4)
-    cols_in, cols_grad = cols.reshape(2, total, part)
+    cols = cols.transpose(1, 2, 0, 3, 4).reshape(2, total, part)
 
     rows_grad = lax.all_gather(grad_out, "mp", axis=0, tiled=True)
     grad_pre = grad_pre_of(rows_grad, pre_act, w_out)
-    grad_pre_all = jnp.concatenate(
-        [grad_pre] + [fetch(grad_pre, "tokens", k) for k in range(1, n_tok)], axis=0
-    )
+    grad_pre_all = [grad_pre] + [fetch(grad_pre, "tokens", k) for k in range(1, n_tok)]
 
     blocks = swap(grad_in_part(grad_pre, w_in.T).reshape(n_mp, rows, width), "mp")
     grad_in = jnp.sum(blocks.astype(jnp.float32), axis=0).astype(jnp.bfloat16)
 
-    activated = gelu_value(pre_all.astype(jnp.float32)).astype(jnp.bfloat16)
-    grad_w_out = (
-        lax.dot_general(
-            activated, cols_grad, (((0,), (0,)), ((), ())), preferred_element_type=jnp.float32
-        )
-        * scale_back
-    ).astype(jnp.bfloat16)
-    grad_w_in = (
-        lax.dot_general(
-            cols_in, grad_pre_all, (((0,), (0,)), ((), ())), preferred_element_type=jnp.float32
-        )
-        * scale_back
-    ).astype(jnp.bfloat16)
-    return (grad_in, grad_w_in, grad_w_out)
+    grad_w_in_t, grad_w_out = grad_w_of(pre, grad_pre_all, cols, scale_back)
+    return (grad_in, grad_w_in_t.T, grad_w_out)
 
 
 def solution(mesh):

time: 78.9 us -> 84.4 us (1.070)
  Pallas kernels: 12 us -> 33 us
  local copies, waits for them, and re-layouts: 15.6 us -> 6.22 us
  matrix products: 7.02 us -> 0 us
    pallas_call x1 -> x2, Pallas kernels: 7.21 us -> 21.3 us  [the longest x1 12.2 us: grad_pre_of(): pl.pallas_call(functools.partial(grad_pre_body, hidden // block), grid=(h...]
    unnamed x9 -> x15, local copies, waits for them, and re-layouts: 13 us -> 2.08 us
    dot_general x2 -> x0, matrix products: 7.02 us -> none  [the longest x1 3.57 us: shards(): lax.dot_general(activated, cols_grad, (((0,), (0,)), ((), ())), preferred...]
    pallas_call x1, Pallas kernels: 4.77 us -> 11.6 us  [grad_in_part(): pl.pallas_call(grad_in_body, grid=(width // block,), in_specs=[pl.BlockSp...]
    reshape x0 -> x1, local copies, waits for them, and re-layouts: none -> 0.99 us  [shards(): cols = cols.transpose(1, 2, 0, 3, 4).reshape(2, total, part)]
    reshape x1, local copies, waits for them, and re-layouts: 0.86 us -> 1.82 us  [shards(): grad_in_part(grad_pre, w_in.T).reshape(n_mp, rows, width)]
  transfers between devices with their start and end apart: 8 -> 8, of which waited for: 2 -> 3; matrix products, arithmetic and copies ran while one was open for 8% -> 6% of each run, Pallas kernels for 15% -> 28%
where the time goes in v3:
time: 84.4 us; the launch traced here: 83.7 us
  Pallas kernels  33 us (39%)
  starting transfers between devices  17.1 us (20%)
  waiting for transfers between devices  14 us (17%)
  blocking collectives  9.89 us (12%)
  local copies, waits for them, and re-layouts  6.22 us (7%)
  other arithmetic  2.7 us (3%)
    all_to_all x2, waiting for transfers between devices, swap(): return lax.all_to_all(x, axis, 0, 0)  13.1 us
    pallas_call x1, Pallas kernels, grad_pre_of(): pl.pallas_call(functools.partial(grad_pre_body, hidden // block), grid=(h...  12.2 us
    pallas_call x1, Pallas kernels, grad_in_part(): pl.pallas_call(grad_in_body, grid=(width // block,), in_specs=[pl.BlockSp...  11.6 us
    ppermute x6, starting transfers between devices, fetch(): return lax.ppermute(x, axis, [(partner(i, k, n), i) for i in range(n)])  10.1 us
    all_gather x1, blocking collectives, shards(): rows_grad = lax.all_gather(grad_out, 'mp', axis=0, tiled=True)  9.89 us
    pallas_call x1, Pallas kernels, grad_w_of(): pl.pallas_call(functools.partial(grad_w_body, places, scale_back), grid=(...  9.17 us
    all_to_all x2, starting transfers between devices, swap(): return lax.all_to_all(x, axis, 0, 0)  6.97 us
    unnamed x15, local copies, waits for them, and re-layouts  2.08 us
  transfers between devices with their start and end apart: 8, of which 3 were waited for; matrix products, arithmetic and copies ran while one was open for 6% of the time, Pallas kernels for 28%

profile of v3, /device:TPU:0, one launch (start us, length us, event | category | flops | bytes accessed | tf_op | source)
XLA Modules:
  0.0 83.7 jit_solution(18268713393358863963)
XLA Ops:
  0.7 0.9 %fusion.6 = (bf16[8,1280]{1,0:T(8,128)(2,1)S(1)}, bf16[8,1280]{1,0:T(8,128)(2,1)S(1)}, bf16[8,1280]{1,0:T(8,128)(2,1)S(1)}, bf16[8,1280]{1,0:T(8,128)(2,1)S(1)}) fusion(s32[]{:T(128)S(6)} %select_n.15, bf16[4,5120]{1,0:T(4,128)(2,1)} %param.5, bf16[4,5120]{1,0:T(4,128)(2,1)} %param.6, s32[]{:T(128)S(6)} %select_n.12, s32[]{:T(128)S(6)} %select_n.13, ...), kind=kLoop, calls=%fused_computation.16 | loop fusion | flops 163840 | bytes 163856 | tf_op jit(solution)/shard_map/concatenate | solution.py:159
  1.6 0.9 %fusion.5 = (bf16[40,1728]{1,0:T(8,128)(2,1)S(1)}, bf16[40,1728]{1,0:T(8,128)(2,1)S(1)}, bf16[40,1728]{1,0:T(8,128)(2,1)S(1)}) fusion(bf16[8,1280]{1,0:T(8,128)(2,1)S(1)} %get-tuple-element.13, bf16[32,1728]{1,0:T(8,128)(2,1)} %refs_0_.1, bf16[8,1280]{1,0:T(8,128)(2,1)S(1)} %get-tuple-element.12, bf16[8,1280]{1,0:T(8,128)(2,1)S(1)} %get-tuple-element.11), kind=kLoop, calls=%fused_computation.6 | loop fusion | flops 967680 | bytes 586752 | tf_op jit(solution)/shard_map/concatenate | solution.py:171
  2.5 3.1 %collective-permute-start = (bf16[40,1728]{1,0:T(8,128)(2,1)S(1)}, bf16[40,1728]{1,0:T(8,128)(2,1)S(1)}, u32[]{:S(2)}, u32[]{:S(2)}) collective-permute-start(bf16[40,1728]{1,0:T(8,128)(2,1)S(1)} %get-tuple-element.9), channel_id=1, source_target_pairs={{1,0},{0,1},{3,2},{2,3},{5,4},{4,5},{7,6},{6,7},{9,8},{8,9},{11,10... | collective-permute-start | bytes 414728 | tf_op jit(solution)/shard_map/ppermute | solution.py:33
  5.6 2.6 %collective-permute-start.1 = (bf16[40,1728]{1,0:T(8,128)(2,1)S(1)}, bf16[40,1728]{1,0:T(8,128)(2,1)S(1)}, u32[]{:S(2)}, u32[]{:S(2)}) collective-permute-start(bf16[40,1728]{1,0:T(8,128)(2,1)S(1)} %get-tuple-element.8), channel_id=1, source_target_pairs={{2,0},{3,1},{0,2},{1,3},{6,4},{7,5},{4,6},{5,7},{10,8},{11,9},{8,1... | collective-permute-start | bytes 414728 | tf_op jit(solution)/shard_map/ppermute | solution.py:33
  8.2 9.9 %all-gather = bf16[8,4,5120]{2,1,0:T(4,128)(2,1)S(1)} all-gather(bf16[1,4,5120]{2,1,0:T(4,128)(2,1)} %bitcast.8), channel_id=1, replica_groups=mesh['mp'=8,'tokens'=4] {'mp'}, dimensions={0}, use_global_device_ids=true | all-gather | bytes 368640 | tf_op jit(solution)/shard_map/all_gather | solution.py:178
  18.1 0.8 reshape.24.rows_ref
  18.9 12.2 %grad_pre.1.grad_pre_ref.refs_4_ = bf16[32,1728]{1,0:T(8,128)(2,1)} custom-call(bf16[32,5120]{1,0:T(8,128)(2,1)} %reshape.24.rows_ref, bf16[32,1728]{1,0:T(8,128)(2,1)} %refs_0_.1, bf16[1728,5120]{1,0:T(8,128)(2,1)} %w_ref.1), custom_call_target="tpu_custom_call" | custom-call | flops 566231040 | bytes 17694720 | tf_op jit(solution)/shard_map/grad_pre/pallas_call | solution.py:62
  31.1 11.6 %grad_in_part.1 = bf16[32,5120]{1,0:T(8,128)(2,1)} custom-call(bf16[32,1728]{1,0:T(8,128)(2,1)} %grad_pre.1.grad_pre_ref.refs_4_, bf16[1728,5120]{1,0:T(8,128)(2,1)} %bitcast.6), custom_call_target="tpu_custom_call" | custom-call | flops 566231040 | bytes 17694720 | tf_op jit(solution)/shard_map/grad_in_part/pallas_call | solution.py:91
  42.7 1.8 %reshape.21 = bf16[8,4,5120]{2,1,0:T(4,128)(2,1)} reshape(bf16[32,5120]{1,0:T(8,128)(2,1)} %grad_in_part.1) | data formatting | bytes 655360 | tf_op jit(solution)/shard_map/reshape | solution.py:182
  44.5 3.4 %all-to-all-start = ((bf16[8,4,5120]{2,1,0:T(4,128)(2,1)}), bf16[8,4,5120]{2,1,0:T(4,128)(2,1)S(1)}, u32[]{:S(2)}, u32[]{:S(2)}) async-start(bf16[8,4,5120]{2,1,0:T(4,128)(2,1)} %reshape.21), calls=%async_computation | async-start | bytes 655360 | tf_op jit(solution)/shard_map/all_to_all | solution.py:37
  48.2 7.3 %all-to-all-done = bf16[8,4,5120]{2,1,0:T(4,128)(2,1)S(1)} async-done(((bf16[8,4,5120]{2,1,0:T(4,128)(2,1)}), bf16[8,4,5120]{2,1,0:T(4,128)(2,1)S(1)}, u32[]{:S(2)}, u32[]{:S(2)}) %all-to-all-start) | async-done | bytes 327712 | tf_op jit(solution)/shard_map/all_to_all | solution.py:37
  55.5 1.0 %broadcast_in_dim.3 = bf16[8,2,4,4,1280]{4,3,2,1,0:T(4,128)(2,1)} broadcast(bf16[2,4,4,1280]{3,2,1,0:T(4,128)(2,1)S(1)} %copy.9), dimensions={1,2,3,4} | broadcast | bytes 737280 | tf_op jit(solution)/shard_map/broadcast_in_dim | solution.py:175
  56.5 3.5 %all-to-all-start.1 = ((bf16[8,2,4,4,1280]{4,3,2,1,0:T(4,128)(2,1)}), bf16[8,2,4,4,1280]{4,3,2,1,0:T(4,128)(2,1)S(1)}, u32[]{:S(2)}, u32[]{:S(2)}) async-start(bf16[8,2,4,4,1280]{4,3,2,1,0:T(4,128)(2,1)} %broadcast_in_dim.3), calls=%async_computation.1 | async-start | bytes 1310720 | tf_op jit(solution)/shard_map/all_to_all | solution.py:37
  60.1 0.7 collective-permute-start.3
  60.8 3.5 %collective-permute-start.4 = (bf16[32,1728]{1,0:T(8,128)(2,1)S(1)}, bf16[32,1728]{1,0:T(8,128)(2,1)S(1)}, u32[]{:S(2)}, u32[]{:S(2)}) collective-permute-start(bf16[32,1728]{1,0:T(8,128)(2,1)S(1)} %copy-done), channel_id=1, source_target_pairs={{2,0},{3,1},{0,2},{1,3},{6,4},{7,5},{4,6},{5,7},{10,8},{11,9},{8,1... | collective-permute-start | bytes 331784 | tf_op jit(solution)/shard_map/ppermute | solution.py:33
  64.3 0.2 collective-permute-start.5
  64.5 0.8 reduce_sum.12
  65.3 5.9 %all-to-all-done.1 = bf16[8,2,4,4,1280]{4,3,2,1,0:T(4,128)(2,1)S(1)} async-done(((bf16[8,2,4,4,1280]{4,3,2,1,0:T(4,128)(2,1)}), bf16[8,2,4,4,1280]{4,3,2,1,0:T(4,128)(2,1)S(1)}, u32[]{:S(2)}, u32[]{:S(2)}) %all-to-all-start.1) | async-done | bytes 655392 | tf_op jit(solution)/shard_map/all_to_all | solution.py:37
  71.2 0.2 copy.10
  71.4 1.0 %reshape.22.refs_8_ = bf16[2,128,1280]{2,1,0:T(8,128)(2,1)} reshape(bf16[2,4,8,4,1280]{4,3,2,1,0:T(4,128)(2,1)S(1)} %copy.10) | data formatting | bytes 1310720 | tf_op jit(solution)/shard_map/reshape | solution.py:176
  72.4 0.8 collective-permute-done.4.refs_6_
  73.3 0.6 copy-done.5
  73.9 0.7 copy-done.6
  74.5 9.2 %grad_w.1 = (bf16[1728,1280]{1,0:T(8,128)(2,1)}, bf16[1728,1280]{1,0:T(8,128)(2,1)}) custom-call(bf16[32,1728]{1,0:T(8,128)(2,1)} %refs_0_.1, bf16[40,1728]{1,0:T(8,128)(2,1)} %copy-done.1, bf16[40,1728]{1,0:T(8,128)(2,1)} %copy-done.2, bf16[40,1728]{1,0:T(8,128)(2,1)} %copy-done.3, bf16[32,1728]{1,0:T(8,128)(2,1)} %grad_pre.1.grad_pre_ref.refs_4_, ...), custom_call_target="tpu_custom_call" | custom-call | flops 1132462080 | bytes 8847360 | tf_op jit(solution)/shard_map/grad_w/pallas_call | solution.py:133
  (27 shorter events, 0.2 us)
Async XLA Ops:
  2.5 45.4 %collective-permute-start = (bf16[40,1728]{1,0:T(8,128)(2,1)S(1)}, bf16[40,1728]{1,0:T(8,128)(2,1)S(1)}, u32[]{:S(2)}, u32[]{:S(2)}) collective-permute-start(bf16[40,1728]{1,0:T(8,128)(2,1)S(1)} %get-tuple-element.9), channel_id=1, source_target_pairs={{1,0},{0,1},{3,2},{2,3},{5,4},{4,5},{7,6},{6,7},{9,8},{8,9},{11,10... | collective-permute-start | bytes 414728 | tf_op jit(solution)/shard_map/ppermute | solution.py:33
  5.6 42.4 %collective-permute-start.1 = (bf16[40,1728]{1,0:T(8,128)(2,1)S(1)}, bf16[40,1728]{1,0:T(8,128)(2,1)S(1)}, u32[]{:S(2)}, u32[]{:S(2)}) collective-permute-start(bf16[40,1728]{1,0:T(8,128)(2,1)S(1)} %get-tuple-element.8), channel_id=1, source_target_pairs={{2,0},{3,1},{0,2},{1,3},{6,4},{7,5},{4,6},{5,7},{10,8},{11,9},{8,1... | collective-permute-start | bytes 414728 | tf_op jit(solution)/shard_map/ppermute | solution.py:33
  8.2 39.9 %collective-permute-start.2 = (bf16[40,1728]{1,0:T(8,128)(2,1)S(1)}, bf16[40,1728]{1,0:T(8,128)(2,1)S(1)}, u32[]{:S(2)}, u32[]{:S(2)}) collective-permute-start(bf16[40,1728]{1,0:T(8,128)(2,1)S(1)} %get-tuple-element.7), channel_id=1, source_target_pairs={{3,0},{2,1},{1,2},{0,3},{7,4},{6,5},{5,6},{4,7},{11,8},{10,9},{9,1... | collective-permute-start | bytes 414728 | tf_op jit(solution)/shard_map/ppermute | solution.py:33
  31.1 29.0 %copy-start = (bf16[32,1728]{1,0:T(8,128)(2,1)S(1)}, bf16[32,1728]{1,0:T(8,128)(2,1)}, u32[]{:S(2)}) copy-start(bf16[32,1728]{1,0:T(8,128)(2,1)} %grad_pre.1.grad_pre_ref.refs_4_) | copy-start | bytes 331780
  44.5 11.0 %all-to-all-start = ((bf16[8,4,5120]{2,1,0:T(4,128)(2,1)}), bf16[8,4,5120]{2,1,0:T(4,128)(2,1)S(1)}, u32[]{:S(2)}, u32[]{:S(2)}) async-start(bf16[8,4,5120]{2,1,0:T(4,128)(2,1)} %reshape.21), calls=%async_computation | async-start | bytes 655360 | tf_op jit(solution)/shard_map/all_to_all | solution.py:37
  48.0 25.2 %copy-start.1 = (bf16[40,1728]{1,0:T(8,128)(2,1)}, bf16[40,1728]{1,0:T(8,128)(2,1)S(1)}, u32[]{:S(2)}) copy-start(bf16[40,1728]{1,0:T(8,128)(2,1)S(1)} %collective-permute-done.refs_1_) | copy-start | bytes 414724
  48.0 25.2 %copy-start.2 = (bf16[40,1728]{1,0:T(8,128)(2,1)}, bf16[40,1728]{1,0:T(8,128)(2,1)S(1)}, u32[]{:S(2)}) copy-start(bf16[40,1728]{1,0:T(8,128)(2,1)S(1)} %collective-permute-done.1.refs_2_) | copy-start | bytes 414724
  48.1 25.2 %copy-start.3 = (bf16[40,1728]{1,0:T(8,128)(2,1)}, bf16[40,1728]{1,0:T(8,128)(2,1)S(1)}, u32[]{:S(2)}) copy-start(bf16[40,1728]{1,0:T(8,128)(2,1)S(1)} %collective-permute-done.2.refs_3_) | copy-start | bytes 414724
  56.5 14.6 %all-to-all-start.1 = ((bf16[8,2,4,4,1280]{4,3,2,1,0:T(4,128)(2,1)}), bf16[8,2,4,4,1280]{4,3,2,1,0:T(4,128)(2,1)S(1)}, u32[]{:S(2)}, u32[]{:S(2)}) async-start(bf16[8,2,4,4,1280]{4,3,2,1,0:T(4,128)(2,1)} %broadcast_in_dim.3), calls=%async_computation.1 | async-start | bytes 1310720 | tf_op jit(solution)/shard_map/all_to_all | solution.py:37
  60.1 12.3 %collective-permute-start.3 = (bf16[32,1728]{1,0:T(8,128)(2,1)S(1)}, bf16[32,1728]{1,0:T(8,128)(2,1)S(1)}, u32[]{:S(2)}, u32[]{:S(2)}) collective-permute-start(bf16[32,1728]{1,0:T(8,128)(2,1)S(1)} %copy-done), channel_id=1, source_target_pairs={{1,0},{0,1},{3,2},{2,3},{5,4},{4,5},{7,6},{6,7},{9,8},{8,9},{11,10... | collective-permute-start | bytes 331784 | tf_op jit(solution)/shard_map/ppermute | solution.py:33
  60.8 12.4 %collective-permute-start.4 = (bf16[32,1728]{1,0:T(8,128)(2,1)S(1)}, bf16[32,1728]{1,0:T(8,128)(2,1)S(1)}, u32[]{:S(2)}, u32[]{:S(2)}) collective-permute-start(bf16[32,1728]{1,0:T(8,128)(2,1)S(1)} %copy-done), channel_id=1, source_target_pairs={{2,0},{3,1},{0,2},{1,3},{6,4},{7,5},{4,6},{5,7},{10,8},{11,9},{8,1... | collective-permute-start | bytes 331784 | tf_op jit(solution)/shard_map/ppermute | solution.py:33
  64.3 8.9 %collective-permute-start.5 = (bf16[32,1728]{1,0:T(8,128)(2,1)S(1)}, bf16[32,1728]{1,0:T(8,128)(2,1)S(1)}, u32[]{:S(2)}, u32[]{:S(2)}) collective-permute-start(bf16[32,1728]{1,0:T(8,128)(2,1)S(1)} %copy-done), channel_id=1, source_target_pairs={{3,0},{2,1},{1,2},{0,3},{7,4},{6,5},{5,6},{4,7},{11,8},{10,9},{9,1... | collective-permute-start | bytes 331784 | tf_op jit(solution)/shard_map/ppermute | solution.py:33
  72.4 0.9 %copy-start.4 = (bf16[32,1728]{1,0:T(8,128)(2,1)}, bf16[32,1728]{1,0:T(8,128)(2,1)S(1)}, u32[]{:S(2)}) copy-start(bf16[32,1728]{1,0:T(8,128)(2,1)S(1)} %collective-permute-done.3.refs_5_) | copy-start | bytes 331780
  73.2 0.6 copy-start.5
  73.9 0.7 copy-start.6

commit v4 on v3

v4 whole, which is shorter than its diff:
```python
import functools
import math

import jax
import jax.numpy as jnp
from jax import lax
from jax.experimental import pallas as pl
from jax.experimental.pallas import tpu as pltpu
from jax.sharding import PartitionSpec as P

root_two_pi = math.sqrt(2.0 / math.pi)
cubic = 0.044715


def gelu_value(pre):
    inner = root_two_pi * (pre + cubic * pre * pre * pre)
    return 0.5 * pre * (1.0 + jnp.tanh(inner))


def gelu_slope(pre):
    tanh_val = jnp.tanh(root_two_pi * (pre + cubic * pre * pre * pre))
    return 0.5 * (1.0 + tanh_val) + 0.5 * pre * (1.0 - tanh_val * tanh_val) * root_two_pi * (
        1.0 + 3.0 * cubic * pre * pre
    )


def partner(i, k, n):
    return i ^ k if n & (n - 1) == 0 else (i + k) % n


def fetch(x, axis, k):
    n = lax.axis_size(axis)
    return lax.ppermute(x, axis, [(partner(i, k, n), i) for i in range(n)])


def swap(x, axis):
    return lax.all_to_all(x, axis, 0, 0)


def block_of(size, most, unit):
    return max([b for b in range(unit, most + 1, unit) if size % b == 0], default=size)


def stream(source, held, sems, block, depth, work):
    steps = source.shape[1] // block

    def copy(i):
        here = pl.ds(pl.multiple_of(i * block, block), block)
        return pltpu.make_async_copy(source.at[:, here], held.at[:, here], sems.at[i])

    depth = min(depth, steps)
    for i in range(depth):
        copy(i).start()

    def step(i, carry):
        copy(i).wait()

        @pl.when(i + depth < steps)
        def _():
            copy(i + depth).start()

        work(pl.ds(pl.multiple_of(i * block, block), block))
        return carry

    lax.fori_loop(0, steps, step, 0)


def grad_pre_body(block, depth, rows_ref, pre_ref, w_ref, out_ref, held, rows, total, sems):
    places, each, _ = rows_ref.shape
    for k in range(places):
        rows[k * each : (k + 1) * each, :] = rows_ref[k].astype(jnp.float32)
    total[...] = jnp.zeros_like(total)

    def work(here):
        total[...] += lax.dot_general(
            held[:, here],
            rows[:, here].astype(jnp.bfloat16),
            (((1,), (1,)), ((), ())),
            preferred_element_type=jnp.float32,
        )

    stream(w_ref, held, sems, block, depth, work)
    slope = gelu_slope(pre_ref[...].astype(jnp.float32))
    out_ref[...] = (total[...].T * slope).astype(jnp.bfloat16)


def grad_pre_of(rows_grad, pre_act, w_out):
    group, hidden = pre_act.shape
    width = w_out.shape[1]
    block = block_of(width, 512, 128)
    return pl.pallas_call(
        functools.partial(grad_pre_body, block, 4),
        in_specs=[
            pl.BlockSpec(memory_space=pltpu.VMEM),
            pl.BlockSpec(memory_space=pltpu.VMEM),
            pl.BlockSpec(memory_space=pltpu.HBM),
        ],
        out_specs=pl.BlockSpec(memory_space=pltpu.VMEM),
        out_shape=jax.ShapeDtypeStruct((group, hidden), jnp.bfloat16),
        scratch_shapes=[
            pltpu.VMEM((hidden, width), jnp.bfloat16),
            pltpu.VMEM((group, width), jnp.float32),
            pltpu.VMEM((hidden, group), jnp.float32),
            pltpu.SemaphoreType.DMA((width // block,)),
        ],
        compiler_params=pltpu.CompilerParams(vmem_limit_bytes=28 << 20),
        cost_estimate=pl.CostEstimate(
            flops=2 * group * width * hidden, bytes_accessed=2 * hidden * width, transcendentals=0
        ),
        name="grad_pre",
    )(rows_grad, pre_act, w_out)


def grad_in_body(block, depth, grad_pre_ref, w_ref, out_ref, held, sems):
    places, each, _ = out_ref.shape

    def work(here):
        term = jnp.dot(grad_pre_ref[...], held[:, here], preferred_element_type=jnp.float32)
        for k in range(places):
            out_ref[k, :, here] = term[k * each : (k + 1) * each].astype(jnp.bfloat16)

    stream(w_ref, held, sems, block, depth, work)


def grad_in_part(grad_pre, w_in_t, places):
    group, hidden = grad_pre.shape
    width = w_in_t.shape[1]
    block = block_of(width, 512, 128)
    return pl.pallas_call(
        functools.partial(grad_in_body, block, 4),
        in_specs=[
            pl.BlockSpec(memory_space=pltpu.VMEM),
            pl.BlockSpec(memory_space=pltpu.HBM),
        ],
        out_specs=pl.BlockSpec(memory_space=pltpu.VMEM),
        out_shape=jax.ShapeDtypeStruct((places, group // places, width), jnp.bfloat16),
        scratch_shapes=[
            pltpu.VMEM((hidden, width), jnp.bfloat16),
            pltpu.SemaphoreType.DMA((width // block,)),
        ],
        compiler_params=pltpu.CompilerParams(vmem_limit_bytes=28 << 20),
        cost_estimate=pl.CostEstimate(
            flops=2 * group * width * hidden, bytes_accessed=2 * hidden * width, transcendentals=0
        ),
        name="grad_in_part",
    )(grad_pre, w_in_t)


def turn(x_ref, to_ref, unit):
    hidden = x_ref.shape[1]
    for low in range(0, hidden, unit):
        size = min(unit, hidden - low)
        eye = lax.broadcasted_iota(jnp.int32, (size, size), 0) == lax.broadcasted_iota(
            jnp.int32, (size, size), 1
        )
        to_ref[low : low + size, :] = lax.dot_general(
            eye.astype(jnp.float32).astype(jnp.bfloat16),
            x_ref[:, low : low + size],
            (((1,), (1,)), ((), ())),
            preferred_element_type=jnp.float32,
        ).astype(jnp.bfloat16)


def grad_w_body(places, scale_back, block, *refs):
    pre_refs, grad_pre_refs = refs[:places], refs[places : 2 * places]
    cols_ref, in_ref, out_ref, flat, act_t, grad_pre_t, held_in, held_out, sems = refs[2 * places :]
    group, hidden = grad_pre_refs[0].shape
    part = cols_ref.shape[2]
    copies = []

    def product(left, right, held, to_ref):
        for low in range(0, part, block):
            here = slice(low, low + block)
            term = jnp.dot(left[...], cols_ref[right, :, here], preferred_element_type=jnp.float32)
            held[:, here] = (term * scale_back).astype(jnp.bfloat16)
            copies.append(
                pltpu.make_async_copy(held.at[:, here], to_ref.at[:, here], sems.at[len(copies)])
            )
            copies[-1].start()

    for k in range(places):
        pre = pre_refs[k][:group, :hidden].astype(jnp.float32)
        flat[k * group : (k + 1) * group, :] = gelu_value(pre).astype(jnp.bfloat16)
    turn(flat, act_t, 256)
    product(act_t, 1, held_out, out_ref)
    for k in range(places):
        flat[k * group : (k + 1) * group, :] = grad_pre_refs[k][...]
    turn(flat, grad_pre_t, 256)
    product(grad_pre_t, 0, held_in, in_ref)
    for copy in copies:
        copy.wait()


def grad_w_of(pre, grad_pre, cols, scale_back):
    places = len(pre)
    group, hidden = grad_pre[0].shape
    total, part = cols.shape[1:]
    block = block_of(part, 256, 128)
    shape = jax.ShapeDtypeStruct((hidden, part), jnp.bfloat16)
    return pl.pallas_call(
        functools.partial(grad_w_body, places, scale_back, block),
        in_specs=[pl.BlockSpec(memory_space=pltpu.VMEM)] * (2 * places + 1),
        out_specs=[pl.BlockSpec(memory_space=pltpu.HBM)] * 2,
        out_shape=[shape, shape],
        scratch_shapes=[
            pltpu.VMEM((total, hidden), jnp.bfloat16),
            pltpu.VMEM((hidden, total), jnp.bfloat16),
            pltpu.VMEM((hidden, total), jnp.bfloat16),
            pltpu.VMEM((hidden, part), jnp.bfloat16),
            pltpu.VMEM((hidden, part), jnp.bfloat16),
            pltpu.SemaphoreType.DMA((2 * (part // block),)),
        ],
        compiler_params=pltpu.CompilerParams(vmem_limit_bytes=28 << 20),
        cost_estimate=pl.CostEstimate(
            flops=4 * total * part * hidden,
            bytes_accessed=4 * hidden * part,
            transcendentals=total * hidden,
        ),
        name="grad_w",
    )(*pre, *grad_pre, cols)


def shards(tokens_in, grad_out, pre_act, w_in, w_out):
    n_mp, n_tok = lax.axis_size("mp"), lax.axis_size("tokens")
    t = lax.axis_index("tokens")
    rows, width = tokens_in.shape
    group, hidden = pre_act.shape
    part = width // n_tok
    total = group * n_tok
    scale_back = 1.0 / math.sqrt(total)

    both = jnp.concatenate([tokens_in, grad_out], axis=0)
    wide = max(hidden, part)
    own_pre = jnp.pad(pre_act, ((0, 0), (0, wide - hidden)))
    pre, cols = [], []
    for k in range(n_tok):
        taker = t ^ k if n_tok & (n_tok - 1) == 0 else (t - k) % n_tok
        piece = lax.dynamic_slice_in_dim(both, taker * part, part, axis=1)
        if k == 0:
            pre.append(pre_act)
            cols.append(piece)
        else:
            piece = jnp.pad(piece, ((0, 0), (0, wide - part)))
            packed = fetch(jnp.concatenate([own_pre, piece], axis=0), "tokens", k)
            pre.append(packed)
            cols.append(packed[group:, :part])
    rows_grad = swap(jnp.broadcast_to(grad_out, (n_mp,) + grad_out.shape), "mp")
    grad_pre = grad_pre_of(rows_grad, pre_act, w_out)
    grad_pre_all = [grad_pre] + [fetch(grad_pre, "tokens", k) for k in range(1, n_tok)]

    cols = jnp.stack(cols).reshape(n_tok, 2, rows, part).transpose(1, 0, 2, 3)
    cols, grad_pre = lax.optimization_barrier((cols, grad_pre))
    cols = swap(jnp.broadcast_to(cols, (n_mp,) + cols.shape), "mp")

    blocks = grad_in_part(grad_pre, w_in.T, n_mp)
    cols, blocks = lax.optimization_barrier((cols, blocks))
    blocks = swap(blocks, "mp")
    cols = cols.transpose(1, 2, 0, 3, 4).reshape(2, total, part)
    grad_w_in_t, grad_w_out = grad_w_of(pre, grad_pre_all, cols, scale_back)
    grad_in = jnp.sum(blocks.astype(jnp.float32), axis=0).astype(jnp.bfloat16)
    return (grad_in, grad_w_in_t.T, grad_w_out)


def solution(mesh):
    placed = (
        P(("tokens", "mp"), None),
        P(("tokens", "mp"), None),
        P("tokens", "mp"),
        P(None, "mp"),
        P("mp", None),
    )
    return jax.shard_map(
        shards,
        mesh=mesh,
        in_specs=placed,
        out_specs=(P(("tokens", "mp"), None), P("tokens", "mp"), P("mp", "tokens")),
        check_vma=False,
    )
```

time: 84.4 us -> 78.5 us (0.930)
  Pallas kernels: 33 us -> 21 us
  blocking collectives: 9.89 us -> 0 us
  local copies, waits for them, and re-layouts: 6.22 us -> 16 us
  starting transfers between devices: 17.1 us -> 21.7 us
  waiting for transfers between devices: 14 us -> 15.7 us
    ppermute x6, waiting for transfers between devices: 0.85 us -> 13.8 us  [fetch(): return lax.ppermute(x, axis, [(partner(i, k, n), i) for i in range(n)])]
    pallas_call x3, Pallas kernels: 33 us -> 21 us  [the longest x1 9.02 us: grad_pre_of(): pl.pallas_call(functools.partial(grad_pre_body, block, 4), in_specs=[pl.B...]
    all_to_all x2 -> x3, waiting for transfers between devices: 13.1 us -> 1.9 us  [swap(): return lax.all_to_all(x, axis, 0, 0)]
    unnamed x15 -> x8, local copies, waits for them, and re-layouts: 2.08 us -> 13 us
    all_gather x1 -> x0, blocking collectives: 9.89 us -> none  [shards(): rows_grad = lax.all_gather(grad_out, 'mp', axis=0, tiled=True)]
    all_to_all x2 -> x3, starting transfers between devices: 6.97 us -> 11.6 us  [swap(): return lax.all_to_all(x, axis, 0, 0)]
    reshape x1 -> x0, local copies, waits for them, and re-layouts: 1.82 us -> none  [shards(): grad_in_part(grad_pre, w_in.T).reshape(n_mp, rows, width)]
    broadcast_in_dim x0 -> x1, local copies, waits for them, and re-layouts: none -> 1.59 us  [shards(): rows_grad = swap(jnp.broadcast_to(grad_out, (n_mp,) + grad_out.shape), 'mp')]
  transfers between devices with their start and end apart: 8 -> 9, of which waited for: 3 -> 4; matrix products, arithmetic and copies ran while one was open for 6% -> 3% of each run, Pallas kernels for 28% -> 15%
where the time goes in v4:
time: 78.5 us; the launch traced here: 77.9 us
  starting transfers between devices  21.7 us (28%)
  Pallas kernels  21 us (27%)
  local copies, waits for them, and re-layouts  16 us (20%)
  waiting for transfers between devices  15.7 us (20%)
  other arithmetic  2.7 us (3%)
  between operations  0.79 us (1%)
    ppermute x6, waiting for transfers between devices, fetch(): return lax.ppermute(x, axis, [(partner(i, k, n), i) for i in range(n)])  13.8 us
    unnamed x8, local copies, waits for them, and re-layouts  13 us
    all_to_all x3, starting transfers between devices, swap(): return lax.all_to_all(x, axis, 0, 0)  11.6 us
    ppermute x6, starting transfers between devices, fetch(): return lax.ppermute(x, axis, [(partner(i, k, n), i) for i in range(n)])  10.1 us
    pallas_call x1, Pallas kernels, grad_pre_of(): pl.pallas_call(functools.partial(grad_pre_body, block, 4), in_specs=[pl.B...  9.02 us
    pallas_call x1, Pallas kernels, grad_in_part(): pl.pallas_call(functools.partial(grad_in_body, block, 4), in_specs=[pl.Bl...  7.32 us
    pallas_call x1, Pallas kernels, grad_w_of(): pl.pallas_call(functools.partial(grad_w_body, places, scale_back, block),...  4.64 us
    all_to_all x3, waiting for transfers between devices, swap(): return lax.all_to_all(x, axis, 0, 0)  1.9 us
  transfers between devices with their start and end apart: 9, of which 4 were waited for; matrix products, arithmetic and copies ran while one was open for 3% of the time, Pallas kernels for 15%

profile of v4, /device:TPU:0, one launch (start us, length us, event | category | flops | bytes accessed | tf_op | source)
XLA Modules:
  0.0 77.9 jit_solution(15296989867111938299)
XLA Ops:
  0.7 0.9 %fusion.7 = (bf16[8,1280]{1,0:T(8,128)(2,1)S(1)}, bf16[8,1280]{1,0:T(8,128)(2,1)S(1)}, bf16[8,1280]{1,0:T(8,128)(2,1)S(1)}, bf16[8,1280]{1,0:T(8,128)(2,1)S(1)}) fusion(s32[]{:T(128)S(6)} %select_n.12, bf16[4,5120]{1,0:T(4,128)(2,1)} %param.5, bf16[4,5120]{1,0:T(4,128)(2,1)} %param.6, s32[]{:T(128)S(6)} %select_n.13, s32[]{:T(128)S(6)} %select_n.14, ...), kind=kLoop, calls=%fused_computation.17 | loop fusion | flops 163840 | bytes 163856 | tf_op jit(solution)/shard_map/concatenate | solution.py:232
  1.6 0.9 %fusion.3 = (bf16[40,1728]{1,0:T(8,128)(2,1)S(1)}, bf16[40,1728]{1,0:T(8,128)(2,1)S(1)}, bf16[40,1728]{1,0:T(8,128)(2,1)S(1)}) fusion(bf16[8,1280]{1,0:T(8,128)(2,1)S(1)} %get-tuple-element.19, bf16[32,1728]{1,0:T(8,128)(2,1)} %refs_0_.1, bf16[8,1280]{1,0:T(8,128)(2,1)S(1)} %get-tuple-element.20, bf16[8,1280]{1,0:T(8,128)(2,1)S(1)} %get-tuple-element.21), kind=kLoop, calls=%fused_computation.4 | loop fusion | flops 967680 | bytes 586752 | tf_op jit(solution)/shard_map/concatenate | solution.py:244
  2.5 3.1 %collective-permute-start = (bf16[40,1728]{1,0:T(8,128)(2,1)S(1)}, bf16[40,1728]{1,0:T(8,128)(2,1)S(1)}, u32[]{:S(2)}, u32[]{:S(2)}) collective-permute-start(bf16[40,1728]{1,0:T(8,128)(2,1)S(1)} %get-tuple-element.15), channel_id=1, source_target_pairs={{1,0},{0,1},{3,2},{2,3},{5,4},{4,5},{7,6},{6,7},{9,8},{8,9},{11,10... | collective-permute-start | bytes 414728 | tf_op jit(solution)/shard_map/ppermute | solution.py:33
  5.6 2.6 %collective-permute-start.1 = (bf16[40,1728]{1,0:T(8,128)(2,1)S(1)}, bf16[40,1728]{1,0:T(8,128)(2,1)S(1)}, u32[]{:S(2)}, u32[]{:S(2)}) collective-permute-start(bf16[40,1728]{1,0:T(8,128)(2,1)S(1)} %get-tuple-element.16), channel_id=1, source_target_pairs={{2,0},{3,1},{0,2},{1,3},{6,4},{7,5},{4,6},{5,7},{10,8},{11,9},{8,1... | collective-permute-start | bytes 414728 | tf_op jit(solution)/shard_map/ppermute | solution.py:33
  8.2 1.6 %broadcast_in_dim.6 = bf16[8,4,5120]{2,1,0:T(4,128)(2,1)} broadcast(bf16[4,5120]{1,0:T(4,128)(2,1)} %param.6), dimensions={1,2} | broadcast | bytes 368640 | tf_op jit(solution)/shard_map/broadcast_in_dim | solution.py:247
  9.8 3.9 %all-to-all-start = ((bf16[8,4,5120]{2,1,0:T(4,128)(2,1)}), bf16[8,4,5120]{2,1,0:T(4,128)(2,1)S(1)}, u32[]{:S(2)}, u32[]{:S(2)}) async-start(bf16[8,4,5120]{2,1,0:T(4,128)(2,1)} %broadcast_in_dim.6), calls=%async_computation | async-start | bytes 655360 | tf_op jit(solution)/shard_map/all_to_all | solution.py:37
  13.8 5.6 %collective-permute-done.1.refs_2_ = bf16[40,1728]{1,0:T(8,128)(2,1)S(1)} collective-permute-done((bf16[40,1728]{1,0:T(8,128)(2,1)S(1)}, bf16[40,1728]{1,0:T(8,128)(2,1)S(1)}, u32[]{:S(2)}, u32[]{:S(2)}) %collective-permute-start.1) | collective-permute-done | bytes 138272 | tf_op jit(solution)/shard_map/ppermute | solution.py:33
  19.5 1.9 %all-to-all-done.rows_ref = bf16[8,4,5120]{2,1,0:T(4,128)(2,1)S(1)} async-done(((bf16[8,4,5120]{2,1,0:T(4,128)(2,1)}), bf16[8,4,5120]{2,1,0:T(4,128)(2,1)S(1)}, u32[]{:S(2)}, u32[]{:S(2)}) %all-to-all-start) | async-done | bytes 327712 | tf_op jit(solution)/shard_map/all_to_all | solution.py:37
  21.4 6.0 %copy-done.1 = bf16[1728,5120]{1,0:T(8,128)(2,1)S(1)} copy-done((bf16[1728,5120]{1,0:T(8,128)(2,1)S(1)}, bf16[1728,5120]{1,0:T(8,128)(2,1)}, u32[]{:S(2)}) %copy-start.1) | copy-done | bytes 17694744
  27.4 0.9 %copy-done.2 = bf16[32,1728]{1,0:T(8,128)(2,1)S(1)} copy-done((bf16[32,1728]{1,0:T(8,128)(2,1)S(1)}, bf16[32,1728]{1,0:T(8,128)(2,1)}, u32[]{:S(2)}) %copy-start.2) | copy-done | bytes 110616
  28.3 9.0 %grad_pre.1.grad_pre_ref.refs_4_ = bf16[32,1728]{1,0:T(8,128)(2,1)S(1)} custom-call(bf16[8,4,5120]{2,1,0:T(4,128)(2,1)S(1)} %all-to-all-done.rows_ref, bf16[32,1728]{1,0:T(8,128)(2,1)S(1)} %copy-done.2, bf16[1728,5120]{1,0:T(8,128)(2,1)S(1)} %copy-done.1), custom_call_target="tpu_custom_call" | custom-call | flops 566231040 | bytes 17694720 | tf_op jit(solution)/shard_map/grad_pre/pallas_call | solution.py:91
  37.4 1.0 %broadcast_in_dim.7 = bf16[8,2,4,4,1280]{4,3,2,1,0:T(4,128)(2,1)} broadcast(bf16[2,4,4,1280]{3,2,1,0:T(4,128)(2,1)S(1)} %copy.9), dimensions={1,2,3,4} | broadcast | bytes 737280 | tf_op jit(solution)/shard_map/broadcast_in_dim | solution.py:253
  38.4 3.5 %all-to-all-start.1 = ((bf16[8,2,4,4,1280]{4,3,2,1,0:T(4,128)(2,1)}), bf16[8,2,4,4,1280]{4,3,2,1,0:T(4,128)(2,1)S(1)}, u32[]{:S(2)}, u32[]{:S(2)}) async-start(bf16[8,2,4,4,1280]{4,3,2,1,0:T(4,128)(2,1)} %broadcast_in_dim.7), calls=%async_computation.1 | async-start | bytes 1310720 | tf_op jit(solution)/shard_map/all_to_all | solution.py:37
  41.9 6.0 %copy-done = bf16[5120,1728]{0,1:T(8,128)(2,1)S(1)} copy-done((bf16[5120,1728]{0,1:T(8,128)(2,1)S(1)}, bf16[5120,1728]{0,1:T(8,128)(2,1)}, u32[]{:S(2)}) %copy-start) | copy-done | bytes 17694744
  48.0 7.3 %grad_in_part.1 = bf16[8,4,5120]{2,1,0:T(4,128)(2,1)} custom-call(bf16[32,1728]{1,0:T(8,128)(2,1)S(1)} %grad_pre.1.grad_pre_ref.refs_4_, bf16[1728,5120]{1,0:T(8,128)(2,1)S(1)} %bitcast.5), custom_call_target="tpu_custom_call" | custom-call | flops 566231040 | bytes 17694720 | tf_op jit(solution)/shard_map/grad_in_part/pallas_call | solution.py:129
  55.3 4.1 %all-to-all-start.2 = ((bf16[8,4,5120]{2,1,0:T(4,128)(2,1)}), bf16[8,4,5120]{2,1,0:T(4,128)(2,1)S(1)}, u32[]{:S(2)}, u32[]{:S(2)}) async-start(bf16[8,4,5120]{2,1,0:T(4,128)(2,1)} %grad_in_part.1), calls=%async_computation.2 | async-start | bytes 655360 | tf_op jit(solution)/shard_map/all_to_all | solution.py:37
  59.4 3.6 %collective-permute-start.5 = (bf16[32,1728]{1,0:T(8,128)(2,1)S(1)}, bf16[32,1728]{1,0:T(8,128)(2,1)S(1)}, u32[]{:S(2)}, u32[]{:S(2)}) collective-permute-start(bf16[32,1728]{1,0:T(8,128)(2,1)S(1)} %grad_pre.1.grad_pre_ref.refs_4_), channel_id=1, source_target_pairs={{3,0},{2,1},{1,2},{0,3},{7,4},{6,5},{5,6},{4,7},{11,8},{10,9},{9,1... | collective-permute-start | bytes 331784 | tf_op jit(solution)/shard_map/ppermute | solution.py:33
  63.1 0.8 %collective-permute-start.3 = (bf16[32,1728]{1,0:T(8,128)(2,1)S(1)}, bf16[32,1728]{1,0:T(8,128)(2,1)S(1)}, u32[]{:S(2)}, u32[]{:S(2)}) collective-permute-start(bf16[32,1728]{1,0:T(8,128)(2,1)S(1)} %grad_pre.1.grad_pre_ref.refs_4_), channel_id=1, source_target_pairs={{1,0},{0,1},{3,2},{2,3},{5,4},{4,5},{7,6},{6,7},{9,8},{8,9},{11,10... | collective-permute-start | bytes 331784 | tf_op jit(solution)/shard_map/ppermute | solution.py:33
  63.8 0.2 copy.10
  64.1 0.2 reshape.18.refs_8_
  64.2 3.1 %collective-permute-done.5.refs_7_ = bf16[32,1728]{1,0:T(8,128)(2,1)S(1)} collective-permute-done((bf16[32,1728]{1,0:T(8,128)(2,1)S(1)}, bf16[32,1728]{1,0:T(8,128)(2,1)S(1)}, u32[]{:S(2)}, u32[]{:S(2)}) %collective-permute-start.5) | collective-permute-done | bytes 110624 | tf_op jit(solution)/shard_map/ppermute | solution.py:33
  67.3 5.2 %collective-permute-done.4.refs_6_ = bf16[32,1728]{1,0:T(8,128)(2,1)S(1)} collective-permute-done((bf16[32,1728]{1,0:T(8,128)(2,1)S(1)}, bf16[32,1728]{1,0:T(8,128)(2,1)S(1)}, u32[]{:S(2)}, u32[]{:S(2)}) %collective-permute-start.4) | collective-permute-done | bytes 110624 | tf_op jit(solution)/shard_map/ppermute | solution.py:33
  72.5 4.6 %grad_w.1 = (bf16[1728,1280]{1,0:T(8,128)(2,1)}, bf16[1728,1280]{1,0:T(8,128)(2,1)}) custom-call(bf16[32,1728]{1,0:T(8,128)(2,1)S(1)} %copy-done.3, bf16[40,1728]{1,0:T(8,128)(2,1)S(1)} %collective-permute-done.refs_1_, bf16[40,1728]{1,0:T(8,128)(2,1)S(1)} %collective-permute-done.1.refs_2_, bf16[40,1728]{1,0:T(8,128)(2,1)S(1)} %collective-permute-done.2.refs_3_, ...), custom_call_target="tpu_custom_call" | custom-call | flops 1132462080 | bytes 8847360 | tf_op jit(solution)/shard_map/grad_w/pallas_call | solution.py:200
  77.2 0.8 reduce_sum.12
  (21 shorter events, 0.2 us)
Async XLA Ops:
  2.5 11.2 %collective-permute-start = (bf16[40,1728]{1,0:T(8,128)(2,1)S(1)}, bf16[40,1728]{1,0:T(8,128)(2,1)S(1)}, u32[]{:S(2)}, u32[]{:S(2)}) collective-permute-start(bf16[40,1728]{1,0:T(8,128)(2,1)S(1)} %get-tuple-element.15), channel_id=1, source_target_pairs={{1,0},{0,1},{3,2},{2,3},{5,4},{4,5},{7,6},{6,7},{9,8},{8,9},{11,10... | collective-permute-start | bytes 414728 | tf_op jit(solution)/shard_map/ppermute | solution.py:33
  5.6 13.7 %collective-permute-start.1 = (bf16[40,1728]{1,0:T(8,128)(2,1)S(1)}, bf16[40,1728]{1,0:T(8,128)(2,1)S(1)}, u32[]{:S(2)}, u32[]{:S(2)}) collective-permute-start(bf16[40,1728]{1,0:T(8,128)(2,1)S(1)} %get-tuple-element.16), channel_id=1, source_target_pairs={{2,0},{3,1},{0,2},{1,3},{6,4},{7,5},{4,6},{5,7},{10,8},{11,9},{8,1... | collective-permute-start | bytes 414728 | tf_op jit(solution)/shard_map/ppermute | solution.py:33
  8.2 11.2 %collective-permute-start.2 = (bf16[40,1728]{1,0:T(8,128)(2,1)S(1)}, bf16[40,1728]{1,0:T(8,128)(2,1)S(1)}, u32[]{:S(2)}, u32[]{:S(2)}) collective-permute-start(bf16[40,1728]{1,0:T(8,128)(2,1)S(1)} %get-tuple-element.17), channel_id=1, source_target_pairs={{3,0},{2,1},{1,2},{0,3},{7,4},{6,5},{5,6},{4,7},{11,8},{10,9},{9,1... | collective-permute-start | bytes 414728 | tf_op jit(solution)/shard_map/ppermute | solution.py:33
  9.8 11.6 %all-to-all-start = ((bf16[8,4,5120]{2,1,0:T(4,128)(2,1)}), bf16[8,4,5120]{2,1,0:T(4,128)(2,1)S(1)}, u32[]{:S(2)}, u32[]{:S(2)}) async-start(bf16[8,4,5120]{2,1,0:T(4,128)(2,1)} %broadcast_in_dim.6), calls=%async_computation | async-start | bytes 655360 | tf_op jit(solution)/shard_map/all_to_all | solution.py:37
  21.4 6.0 %copy-start.1 = (bf16[1728,5120]{1,0:T(8,128)(2,1)S(1)}, bf16[1728,5120]{1,0:T(8,128)(2,1)}, u32[]{:S(2)}) copy-start(bf16[1728,5120]{1,0:T(8,128)(2,1)} %w_ref.1) | copy-start | bytes 53084164
  27.4 0.9 %copy-start.2 = (bf16[32,1728]{1,0:T(8,128)(2,1)S(1)}, bf16[32,1728]{1,0:T(8,128)(2,1)}, u32[]{:S(2)}) copy-start(bf16[32,1728]{1,0:T(8,128)(2,1)} %refs_0_.1) | copy-start | bytes 331780
  28.3 44.2 %copy-start.3 = (bf16[32,1728]{1,0:T(8,128)(2,1)S(1)}, bf16[32,1728]{1,0:T(8,128)(2,1)}, u32[]{:S(2)}) copy-start(bf16[32,1728]{1,0:T(8,128)(2,1)} %refs_0_.1) | copy-start | bytes 331780
  38.4 16.9 %all-to-all-start.1 = ((bf16[8,2,4,4,1280]{4,3,2,1,0:T(4,128)(2,1)}), bf16[8,2,4,4,1280]{4,3,2,1,0:T(4,128)(2,1)S(1)}, u32[]{:S(2)}, u32[]{:S(2)}) async-start(bf16[8,2,4,4,1280]{4,3,2,1,0:T(4,128)(2,1)} %broadcast_in_dim.7), calls=%async_computation.1 | async-start | bytes 1310720 | tf_op jit(solution)/shard_map/all_to_all | solution.py:37
  41.9 6.0 %copy-start = (bf16[5120,1728]{0,1:T(8,128)(2,1)S(1)}, bf16[5120,1728]{0,1:T(8,128)(2,1)}, u32[]{:S(2)}) copy-start(bf16[5120,1728]{0,1:T(8,128)(2,1)} %param.8) | copy-start | bytes 53084164
  55.3 21.8 %all-to-all-start.2 = ((bf16[8,4,5120]{2,1,0:T(4,128)(2,1)}), bf16[8,4,5120]{2,1,0:T(4,128)(2,1)S(1)}, u32[]{:S(2)}, u32[]{:S(2)}) async-start(bf16[8,4,5120]{2,1,0:T(4,128)(2,1)} %grad_in_part.1), calls=%async_computation.2 | async-start | bytes 655360 | tf_op jit(solution)/shard_map/all_to_all | solution.py:37
  59.4 7.8 %collective-permute-start.5 = (bf16[32,1728]{1,0:T(8,128)(2,1)S(1)}, bf16[32,1728]{1,0:T(8,128)(2,1)S(1)}, u32[]{:S(2)}, u32[]{:S(2)}) collective-permute-start(bf16[32,1728]{1,0:T(8,128)(2,1)S(1)} %grad_pre.1.grad_pre_ref.refs_4_), channel_id=1, source_target_pairs={{3,0},{2,1},{1,2},{0,3},{7,4},{6,5},{5,6},{4,7},{11,8},{10,9},{9,1... | collective-permute-start | bytes 331784 | tf_op jit(solution)/shard_map/ppermute | solution.py:33
  63.1 9.4 %collective-permute-start.4 = (bf16[32,1728]{1,0:T(8,128)(2,1)S(1)}, bf16[32,1728]{1,0:T(8,128)(2,1)S(1)}, u32[]{:S(2)}, u32[]{:S(2)}) collective-permute-start(bf16[32,1728]{1,0:T(8,128)(2,1)S(1)} %grad_pre.1.grad_pre_ref.refs_4_), channel_id=1, source_target_pairs={{2,0},{3,1},{0,2},{1,3},{6,4},{7,5},{4,6},{5,7},{10,8},{11,9},{8,1... | collective-permute-start | bytes 331784 | tf_op jit(solution)/shard_map/ppermute | solution.py:33
  63.1 9.4 %collective-permute-start.3 = (bf16[32,1728]{1,0:T(8,128)(2,1)S(1)}, bf16[32,1728]{1,0:T(8,128)(2,1)S(1)}, u32[]{:S(2)}, u32[]{:S(2)}) collective-permute-start(bf16[32,1728]{1,0:T(8,128)(2,1)S(1)} %grad_pre.1.grad_pre_ref.refs_4_), channel_id=1, source_target_pairs={{1,0},{0,1},{3,2},{2,3},{5,4},{4,5},{7,6},{6,7},{9,8},{8,9},{11,10... | collective-permute-start | bytes 331784 | tf_op jit(solution)/shard_map/ppermute | solution.py:33

commit v5 on v4

--- a/solution.py
+++ b/solution.py
@@ -65,7 +65,9 @@
     lax.fori_loop(0, steps, step, 0)
 
 
-def grad_pre_body(block, depth, rows_ref, pre_ref, w_ref, out_ref, held, rows, total, sems):
+def grad_pre_body(block, depth, rows_ref, pre_ref, w_ref, out_ref, held, pre, rows, total, sems, sem):
+    pre_copy = pltpu.make_async_copy(pre_ref, pre, sem)
+    pre_copy.start()
     places, each, _ = rows_ref.shape
     for k in range(places):
         rows[k * each : (k + 1) * each, :] = rows_ref[k].astype(jnp.float32)
@@ -80,7 +82,8 @@
         )
 
     stream(w_ref, held, sems, block, depth, work)
-    slope = gelu_slope(pre_ref[...].astype(jnp.float32))
+    pre_copy.wait()
+    slope = gelu_slope(pre[...].astype(jnp.float32))
     out_ref[...] = (total[...].T * slope).astype(jnp.bfloat16)
 
 
@@ -92,18 +95,20 @@
         functools.partial(grad_pre_body, block, 4),
         in_specs=[
             pl.BlockSpec(memory_space=pltpu.VMEM),
-            pl.BlockSpec(memory_space=pltpu.VMEM),
+            pl.BlockSpec(memory_space=pltpu.HBM),
             pl.BlockSpec(memory_space=pltpu.HBM),
         ],
         out_specs=pl.BlockSpec(memory_space=pltpu.VMEM),
         out_shape=jax.ShapeDtypeStruct((group, hidden), jnp.bfloat16),
         scratch_shapes=[
             pltpu.VMEM((hidden, width), jnp.bfloat16),
+            pltpu.VMEM((group, hidden), jnp.bfloat16),
             pltpu.VMEM((group, width), jnp.float32),
             pltpu.VMEM((hidden, group), jnp.float32),
             pltpu.SemaphoreType.DMA((width // block,)),
-        ],
-        compiler_params=pltpu.CompilerParams(vmem_limit_bytes=28 << 20),
+            pltpu.SemaphoreType.DMA,
+        ],
+        compiler_params=pltpu.CompilerParams(vmem_limit_bytes=56 << 20),
         cost_estimate=pl.CostEstimate(
             flops=2 * group * width * hidden, bytes_accessed=2 * hidden * width, transcendentals=0
         ),
@@ -138,7 +143,7 @@
             pltpu.VMEM((hidden, width), jnp.bfloat16),
             pltpu.SemaphoreType.DMA((width // block,)),
         ],
-        compiler_params=pltpu.CompilerParams(vmem_limit_bytes=28 << 20),
+        compiler_params=pltpu.CompilerParams(vmem_limit_bytes=56 << 20),
         cost_estimate=pl.CostEstimate(
             flops=2 * group * width * hidden, bytes_accessed=2 * hidden * width, transcendentals=0
         ),
@@ -210,10 +215,10 @@
             pltpu.VMEM((hidden, part), jnp.bfloat16),
             pltpu.SemaphoreType.DMA((2 * (part // block),)),
         ],
-        compiler_params=pltpu.CompilerParams(vmem_limit_bytes=28 << 20),
+        compiler_params=pltpu.CompilerParams(vmem_limit_bytes=20 << 20),
         cost_estimate=pl.CostEstimate(
-            flops=4 * total * part * hidden,
-            bytes_accessed=4 * hidden * part,
+            flops=80 * total * part * hidden,
+            bytes_accessed=40 * hidden * part,
             transcendentals=total * hidden,
         ),
         name="grad_w",
@@ -229,27 +234,30 @@
     total = group * n_tok
     scale_back = 1.0 / math.sqrt(total)
 
+    rows_grad = jnp.broadcast_to(grad_out, (n_mp,) + grad_out.shape)
+    rows_grad, tokens_in, grad_out = lax.optimization_barrier((rows_grad, tokens_in, grad_out))
+    rows_grad = swap(rows_grad, "mp")
+
     both = jnp.concatenate([tokens_in, grad_out], axis=0)
     wide = max(hidden, part)
     own_pre = jnp.pad(pre_act, ((0, 0), (0, wide - hidden)))
-    pre, cols = [], []
+    packed = []
     for k in range(n_tok):
         taker = t ^ k if n_tok & (n_tok - 1) == 0 else (t - k) % n_tok
         piece = lax.dynamic_slice_in_dim(both, taker * part, part, axis=1)
         if k == 0:
-            pre.append(pre_act)
-            cols.append(piece)
+            own_piece = piece
         else:
             piece = jnp.pad(piece, ((0, 0), (0, wide - part)))
-            packed = fetch(jnp.concatenate([own_pre, piece], axis=0), "tokens", k)
-            pre.append(packed)
-            cols.append(packed[group:, :part])
-    rows_grad = swap(jnp.broadcast_to(grad_out, (n_mp,) + grad_out.shape), "mp")
+            packed.append(fetch(jnp.concatenate([own_pre, piece], axis=0), "tokens", k))
+
     grad_pre = grad_pre_of(rows_grad, pre_act, w_out)
     grad_pre_all = [grad_pre] + [fetch(grad_pre, "tokens", k) for k in range(1, n_tok)]
 
-    cols = jnp.stack(cols).reshape(n_tok, 2, rows, part).transpose(1, 0, 2, 3)
-    cols, grad_pre = lax.optimization_barrier((cols, grad_pre))
+    packed, grad_pre = lax.optimization_barrier((packed, grad_pre))
+    pre = [pre_act] + packed
+    cols = jnp.stack([own_piece] + [x[group:, :part] for x in packed])
+    cols = cols.reshape(n_tok, 2, rows, part).transpose(1, 0, 2, 3)
     cols = swap(jnp.broadcast_to(cols, (n_mp,) + cols.shape), "mp")
 
     blocks = grad_in_part(grad_pre, w_in.T, n_mp)

time: 78.5 us -> 57.4 us (0.73)
  local copies, waits for them, and re-layouts: 16 us -> 3.81 us
  waiting for transfers between devices: 15.7 us -> 4.45 us
  Pallas kernels: 21 us -> 23 us
    ppermute x6, waiting for transfers between devices: 13.8 us -> 0.24 us  [fetch(): return lax.ppermute(x, axis, [(partner(i, k, n), i) for i in range(n)])]
    unnamed x8 -> x6, local copies, waits for them, and re-layouts: 13 us -> 0.74 us
    all_to_all x3, waiting for transfers between devices: 1.9 us -> 4.22 us  [swap(): return lax.all_to_all(x, axis, 0, 0)]
    all_to_all x3, starting transfers between devices: 11.6 us -> 13.2 us  [swap(): return lax.all_to_all(x, axis, 0, 0)]
    pallas_call x1, Pallas kernels: 7.32 us -> 8.6 us  [grad_in_part(): pl.pallas_call(functools.partial(grad_in_body, block, 4), in_specs=[pl.Bl...]
    ppermute x6, starting transfers between devices: 10.1 us -> 8.85 us  [fetch(): return lax.ppermute(x, axis, [(partner(i, k, n), i) for i in range(n)])]
  transfers between devices with their start and end apart: 9 -> 9, of which waited for: 4 -> 3; matrix products, arithmetic and copies ran while one was open for 3% -> 4% of each run, Pallas kernels for 15% -> 40%
where the time goes in v5:
time: 57.4 us; the launch traced here: 56.8 us
  Pallas kernels  23 us (40%)
  starting transfers between devices  22.1 us (39%)
  waiting for transfers between devices  4.45 us (8%)
  local copies, waits for them, and re-layouts  3.81 us (7%)
  other arithmetic  2.69 us (5%)
  between operations  0.79 us (1%)
    all_to_all x3, starting transfers between devices, swap(): return lax.all_to_all(x, axis, 0, 0)  13.2 us
    pallas_call x1, Pallas kernels, grad_pre_of(): pl.pallas_call(functools.partial(grad_pre_body, block, 4), in_specs=[pl.B...  9.71 us
    ppermute x6, starting transfers between devices, fetch(): return lax.ppermute(x, axis, [(partner(i, k, n), i) for i in range(n)])  8.85 us
    pallas_call x1, Pallas kernels, grad_in_part(): pl.pallas_call(functools.partial(grad_in_body, block, 4), in_specs=[pl.Bl...  8.6 us
    pallas_call x1, Pallas kernels, grad_w_of(): pl.pallas_call(functools.partial(grad_w_body, places, scale_back, block),...  4.65 us
    all_to_all x3, waiting for transfers between devices, swap(): return lax.all_to_all(x, axis, 0, 0)  4.22 us
    broadcast_in_dim x1, local copies, waits for them, and re-layouts, shards(): rows_grad = jnp.broadcast_to(grad_out, (n_mp,) + grad_out.shape)  1.59 us
  transfers between devices with their start and end apart: 9, of which 3 were waited for; matrix products, arithmetic and copies ran while one was open for 4% of the time, Pallas kernels for 40%

profile of v5, /device:TPU:0, one launch (start us, length us, event | category | flops | bytes accessed | tf_op | source)
XLA Modules:
  0.0 56.8 jit_solution(1609178457158350203)
XLA Ops:
  0.6 1.6 %broadcast_in_dim.6 = bf16[8,4,5120]{2,1,0:T(4,128)(2,1)} broadcast(bf16[4,5120]{1,0:T(4,128)(2,1)} %param.6), dimensions={1,2} | broadcast | bytes 368640 | tf_op jit(solution)/shard_map/broadcast_in_dim | solution.py:237
  2.2 5.2 %all-to-all-start = ((bf16[8,4,5120]{2,1,0:T(4,128)(2,1)}), bf16[8,4,5120]{2,1,0:T(4,128)(2,1)S(1)}, u32[]{:S(2)}, u32[]{:S(2)}) async-start(bf16[8,4,5120]{2,1,0:T(4,128)(2,1)} %broadcast_in_dim.6), calls=%async_computation | async-start | bytes 655360 | tf_op jit(solution)/shard_map/all_to_all | solution.py:37
  7.4 0.9 %fusion.7 = (bf16[8,1280]{1,0:T(8,128)(2,1)S(1)}, bf16[8,1280]{1,0:T(8,128)(2,1)S(1)}, bf16[8,1280]{1,0:T(8,128)(2,1)S(1)}, bf16[8,1280]{1,0:T(8,128)(2,1)S(1)}) fusion(s32[]{:T(128)S(6)} %select_n.12, bf16[4,5120]{1,0:T(4,128)(2,1)} %param.5, bf16[4,5120]{1,0:T(4,128)(2,1)} %param.6, s32[]{:T(128)S(6)} %select_n.13, s32[]{:T(128)S(6)} %select_n.14, ...), kind=kLoop, calls=%fused_computation.17 | loop fusion | flops 163840 | bytes 163856 | tf_op jit(solution)/shard_map/concatenate | solution.py:241
  8.3 0.9 %fusion.5 = (bf16[40,1728]{1,0:T(8,128)(2,1)S(1)}, bf16[40,1728]{1,0:T(8,128)(2,1)S(1)}, bf16[40,1728]{1,0:T(8,128)(2,1)S(1)}) fusion(bf16[8,1280]{1,0:T(8,128)(2,1)S(1)} %get-tuple-element.31, bf16[32,1728]{1,0:T(8,128)(2,1)} %refs_0_.1, bf16[8,1280]{1,0:T(8,128)(2,1)S(1)} %get-tuple-element.30, bf16[8,1280]{1,0:T(8,128)(2,1)S(1)} %get-tuple-element.29), kind=kLoop, calls=%fused_computation.6 | loop fusion | flops 967680 | bytes 586752 | tf_op jit(solution)/shard_map/concatenate | solution.py:252
  9.3 3.7 %collective-permute-start.2 = (bf16[40,1728]{1,0:T(8,128)(2,1)S(1)}, bf16[40,1728]{1,0:T(8,128)(2,1)S(1)}, u32[]{:S(2)}, u32[]{:S(2)}) collective-permute-start(bf16[40,1728]{1,0:T(8,128)(2,1)S(1)} %get-tuple-element.25), channel_id=1, source_target_pairs={{3,0},{2,1},{1,2},{0,3},{7,4},{6,5},{5,6},{4,7},{11,8},{10,9},{9,1... | collective-permute-start | bytes 414728 | tf_op jit(solution)/shard_map/ppermute | solution.py:33
  12.9 0.8 %collective-permute-start = (bf16[40,1728]{1,0:T(8,128)(2,1)S(1)}, bf16[40,1728]{1,0:T(8,128)(2,1)S(1)}, u32[]{:S(2)}, u32[]{:S(2)}) collective-permute-start(bf16[40,1728]{1,0:T(8,128)(2,1)S(1)} %get-tuple-element.27), channel_id=1, source_target_pairs={{1,0},{0,1},{3,2},{2,3},{5,4},{4,5},{7,6},{6,7},{9,8},{8,9},{11,10... | collective-permute-start | bytes 414728 | tf_op jit(solution)/shard_map/ppermute | solution.py:33
  13.7 0.0 copy-start.1
  13.7 1.3 %all-to-all-done.rows_ref = bf16[8,4,5120]{2,1,0:T(4,128)(2,1)S(1)} async-done(((bf16[8,4,5120]{2,1,0:T(4,128)(2,1)}), bf16[8,4,5120]{2,1,0:T(4,128)(2,1)S(1)}, u32[]{:S(2)}, u32[]{:S(2)}) %all-to-all-start) | async-done | bytes 327712 | tf_op jit(solution)/shard_map/all_to_all | solution.py:37
  15.0 0.7 %copy-done.2 = bf16[8,4,5120]{2,1,0:T(4,128)(2,1)} copy-done((bf16[8,4,5120]{2,1,0:T(4,128)(2,1)}, bf16[8,4,5120]{2,1,0:T(4,128)(2,1)S(1)}, u32[]{:S(2)}) %copy-start.2) | copy-done | bytes 327704
  15.8 9.7 %grad_pre.1.grad_pre_ref.refs_4_ = bf16[32,1728]{1,0:T(8,128)(2,1)} custom-call(bf16[8,4,5120]{2,1,0:T(4,128)(2,1)} %copy-done.2, bf16[32,1728]{1,0:T(8,128)(2,1)} %refs_0_.1, bf16[1728,5120]{1,0:T(8,128)(2,1)} %w_ref.1), custom_call_target="tpu_custom_call" | custom-call | flops 566231040 | bytes 17694720 | tf_op jit(solution)/shard_map/grad_pre/pallas_call | solution.py:94
  25.5 0.0 copy-start
  25.5 0.2 collective-permute-done.1.refs_2_
  25.8 0.1 maximum_bitcast_fusion
  25.9 1.0 %broadcast_in_dim.7 = bf16[8,2,4,4,1280]{4,3,2,1,0:T(4,128)(2,1)} broadcast(bf16[2,4,4,1280]{3,2,1,0:T(4,128)(2,1)S(1)} %copy.9), dimensions={1,2,3,4} | broadcast | bytes 737280 | tf_op jit(solution)/shard_map/broadcast_in_dim | solution.py:261
  26.9 3.8 %all-to-all-start.1 = ((bf16[8,2,4,4,1280]{4,3,2,1,0:T(4,128)(2,1)}), bf16[8,2,4,4,1280]{4,3,2,1,0:T(4,128)(2,1)S(1)}, u32[]{:S(2)}, u32[]{:S(2)}) async-start(bf16[8,2,4,4,1280]{4,3,2,1,0:T(4,128)(2,1)} %broadcast_in_dim.7), calls=%async_computation.1 | async-start | bytes 1310720 | tf_op jit(solution)/shard_map/all_to_all | solution.py:37
  30.8 3.2 %collective-permute-start.5 = (bf16[32,1728]{1,0:T(8,128)(2,1)}, bf16[32,1728]{1,0:T(8,128)(2,1)S(1)}, u32[]{:S(2)}, u32[]{:S(2)}) collective-permute-start(bf16[32,1728]{1,0:T(8,128)(2,1)} %grad_pre.1.grad_pre_ref.refs_4_), channel_id=1, source_target_pairs={{3,0},{2,1},{1,2},{0,3},{7,4},{6,5},{5,6},{4,7},{11,8},{10,9},{9,1... | collective-permute-start | bytes 331784 | tf_op jit(solution)/shard_map/ppermute | solution.py:33
  34.0 1.2 %collective-permute-start.3 = (bf16[32,1728]{1,0:T(8,128)(2,1)}, bf16[32,1728]{1,0:T(8,128)(2,1)S(1)}, u32[]{:S(2)}, u32[]{:S(2)}) collective-permute-start(bf16[32,1728]{1,0:T(8,128)(2,1)} %grad_pre.1.grad_pre_ref.refs_4_), channel_id=1, source_target_pairs={{1,0},{0,1},{3,2},{2,3},{5,4},{4,5},{7,6},{6,7},{9,8},{8,9},{11,10... | collective-permute-start | bytes 331784 | tf_op jit(solution)/shard_map/ppermute | solution.py:33
  35.2 8.6 %grad_in_part.1 = bf16[8,4,5120]{2,1,0:T(4,128)(2,1)} custom-call(bf16[32,1728]{1,0:T(8,128)(2,1)} %grad_pre.1.grad_pre_ref.refs_4_, bf16[1728,5120]{1,0:T(8,128)(2,1)} %bitcast.5), custom_call_target="tpu_custom_call" | custom-call | flops 566231040 | bytes 17694720 | tf_op jit(solution)/shard_map/grad_in_part/pallas_call | solution.py:134
  43.8 0.2 copy.10
  44.0 0.2 reshape.18.refs_8_
  44.2 4.2 %all-to-all-start.2 = ((bf16[8,4,5120]{2,1,0:T(4,128)(2,1)}), bf16[8,4,5120]{2,1,0:T(4,128)(2,1)S(1)}, u32[]{:S(2)}, u32[]{:S(2)}) async-start(bf16[8,4,5120]{2,1,0:T(4,128)(2,1)} %grad_in_part.1), calls=%async_computation.2 | async-start | bytes 655360 | tf_op jit(solution)/shard_map/all_to_all | solution.py:37
  48.4 4.7 %grad_w.1 = (bf16[1728,1280]{1,0:T(8,128)(2,1)}, bf16[1728,1280]{1,0:T(8,128)(2,1)}) custom-call(bf16[32,1728]{1,0:T(8,128)(2,1)S(1)} %copy-done.1, bf16[40,1728]{1,0:T(8,128)(2,1)S(1)} %collective-permute-done.refs_1_, bf16[40,1728]{1,0:T(8,128)(2,1)S(1)} %collective-permute-done.1.refs_2_, bf16[40,1728]{1,0:T(8,128)(2,1)S(1)} %collective-permute-done.2.refs_3_, ...), custom_call_target="tpu_custom_call" | custom-call | flops 22649241600 | bytes 88473600 | tf_op jit(solution)/shard_map/grad_w/pallas_call | solution.py:205
  53.1 2.9 %all-to-all-done.2 = bf16[8,4,5120]{2,1,0:T(4,128)(2,1)S(1)} async-done(((bf16[8,4,5120]{2,1,0:T(4,128)(2,1)}), bf16[8,4,5120]{2,1,0:T(4,128)(2,1)S(1)}, u32[]{:S(2)}, u32[]{:S(2)}) %all-to-all-start.2) | async-done | bytes 327712 | tf_op jit(solution)/shard_map/all_to_all | solution.py:37
  56.0 0.8 %reduce_sum.12 = bf16[4,5120]{1,0:T(4,128)(2,1)} reduce(bf16[8,4,5120]{2,1,0:T(4,128)(2,1)S(1)} %all-to-all-done.2, bf16[]{:T(256)} %constant.7.clone.1), dimensions={0}, to_apply=%region_0.1 | reduce | flops 143360 | bytes 368642 | tf_op jit(solution)/shard_map/reduce_sum | solution.py:268
  (19 shorter events, 0.1 us)
Async XLA Ops:
  2.2 12.8 %all-to-all-start = ((bf16[8,4,5120]{2,1,0:T(4,128)(2,1)}), bf16[8,4,5120]{2,1,0:T(4,128)(2,1)S(1)}, u32[]{:S(2)}, u32[]{:S(2)}) async-start(bf16[8,4,5120]{2,1,0:T(4,128)(2,1)} %broadcast_in_dim.6), calls=%async_computation | async-start | bytes 655360 | tf_op jit(solution)/shard_map/all_to_all | solution.py:37
  9.3 16.2 %collective-permute-start.2 = (bf16[40,1728]{1,0:T(8,128)(2,1)S(1)}, bf16[40,1728]{1,0:T(8,128)(2,1)S(1)}, u32[]{:S(2)}, u32[]{:S(2)}) collective-permute-start(bf16[40,1728]{1,0:T(8,128)(2,1)S(1)} %get-tuple-element.25), channel_id=1, source_target_pairs={{3,0},{2,1},{1,2},{0,3},{7,4},{6,5},{5,6},{4,7},{11,8},{10,9},{9,1... | collective-permute-start | bytes 414728 | tf_op jit(solution)/shard_map/ppermute | solution.py:33
  12.9 12.8 %collective-permute-start.1 = (bf16[40,1728]{1,0:T(8,128)(2,1)S(1)}, bf16[40,1728]{1,0:T(8,128)(2,1)S(1)}, u32[]{:S(2)}, u32[]{:S(2)}) collective-permute-start(bf16[40,1728]{1,0:T(8,128)(2,1)S(1)} %get-tuple-element.26), channel_id=1, source_target_pairs={{2,0},{3,1},{0,2},{1,3},{6,4},{7,5},{4,6},{5,7},{10,8},{11,9},{8,1... | collective-permute-start | bytes 414728 | tf_op jit(solution)/shard_map/ppermute | solution.py:33
  12.9 12.8 %collective-permute-start = (bf16[40,1728]{1,0:T(8,128)(2,1)S(1)}, bf16[40,1728]{1,0:T(8,128)(2,1)S(1)}, u32[]{:S(2)}, u32[]{:S(2)}) collective-permute-start(bf16[40,1728]{1,0:T(8,128)(2,1)S(1)} %get-tuple-element.27), channel_id=1, source_target_pairs={{1,0},{0,1},{3,2},{2,3},{5,4},{4,5},{7,6},{6,7},{9,8},{8,9},{11,10... | collective-permute-start | bytes 414728 | tf_op jit(solution)/shard_map/ppermute | solution.py:33
  13.7 34.7 %copy-start.1 = (bf16[32,1728]{1,0:T(8,128)(2,1)S(1)}, bf16[32,1728]{1,0:T(8,128)(2,1)}, u32[]{:S(2)}) copy-start(bf16[32,1728]{1,0:T(8,128)(2,1)} %refs_0_.1) | copy-start | bytes 331780
  15.0 0.7 %copy-start.2 = (bf16[8,4,5120]{2,1,0:T(4,128)(2,1)}, bf16[8,4,5120]{2,1,0:T(4,128)(2,1)S(1)}, u32[]{:S(2)}) copy-start(bf16[8,4,5120]{2,1,0:T(4,128)(2,1)S(1)} %all-to-all-done.rows_ref) | copy-start | bytes 983044
  25.5 22.9 %copy-start = (bf16[32,1728]{1,0:T(8,128)(2,1)S(1)}, bf16[32,1728]{1,0:T(8,128)(2,1)}, u32[]{:S(2)}) copy-start(bf16[32,1728]{1,0:T(8,128)(2,1)} %grad_pre.1.grad_pre_ref.refs_4_) | copy-start | bytes 331780
  26.9 16.8 %all-to-all-start.1 = ((bf16[8,2,4,4,1280]{4,3,2,1,0:T(4,128)(2,1)}), bf16[8,2,4,4,1280]{4,3,2,1,0:T(4,128)(2,1)S(1)}, u32[]{:S(2)}, u32[]{:S(2)}) async-start(bf16[8,2,4,4,1280]{4,3,2,1,0:T(4,128)(2,1)} %broadcast_in_dim.7), calls=%async_computation.1 | async-start | bytes 1310720 | tf_op jit(solution)/shard_map/all_to_all | solution.py:37
  30.8 17.6 %collective-permute-start.5 = (bf16[32,1728]{1,0:T(8,128)(2,1)}, bf16[32,1728]{1,0:T(8,128)(2,1)S(1)}, u32[]{:S(2)}, u32[]{:S(2)}) collective-permute-start(bf16[32,1728]{1,0:T(8,128)(2,1)} %grad_pre.1.grad_pre_ref.refs_4_), channel_id=1, source_target_pairs={{3,0},{2,1},{1,2},{0,3},{7,4},{6,5},{5,6},{4,7},{11,8},{10,9},{9,1... | collective-permute-start | bytes 331784 | tf_op jit(solution)/shard_map/ppermute | solution.py:33
  34.0 14.4 %collective-permute-start.4 = (bf16[32,1728]{1,0:T(8,128)(2,1)}, bf16[32,1728]{1,0:T(8,128)(2,1)S(1)}, u32[]{:S(2)}, u32[]{:S(2)}) collective-permute-start(bf16[32,1728]{1,0:T(8,128)(2,1)} %grad_pre.1.grad_pre_ref.refs_4_), channel_id=1, source_target_pairs={{2,0},{3,1},{0,2},{1,3},{6,4},{7,5},{4,6},{5,7},{10,8},{11,9},{8,1... | collective-permute-start | bytes 331784 | tf_op jit(solution)/shard_map/ppermute | solution.py:33
  34.0 14.4 %collective-permute-start.3 = (bf16[32,1728]{1,0:T(8,128)(2,1)}, bf16[32,1728]{1,0:T(8,128)(2,1)S(1)}, u32[]{:S(2)}, u32[]{:S(2)}) collective-permute-start(bf16[32,1728]{1,0:T(8,128)(2,1)} %grad_pre.1.grad_pre_ref.refs_4_), channel_id=1, source_target_pairs={{1,0},{0,1},{3,2},{2,3},{5,4},{4,5},{7,6},{6,7},{9,8},{8,9},{11,10... | collective-permute-start | bytes 331784 | tf_op jit(solution)/shard_map/ppermute | solution.py:33
  44.2 11.9 %all-to-all-start.2 = ((bf16[8,4,5120]{2,1,0:T(4,128)(2,1)}), bf16[8,4,5120]{2,1,0:T(4,128)(2,1)S(1)}, u32[]{:S(2)}, u32[]{:S(2)}) async-start(bf16[8,4,5120]{2,1,0:T(4,128)(2,1)} %grad_in_part.1), calls=%async_computation.2 | async-start | bytes 655360 | tf_op jit(solution)/shard_map/all_to_all | solution.py:37

commit v6 on v5

--- a/solution.py
+++ b/solution.py
@@ -41,12 +41,15 @@
     return max([b for b in range(unit, most + 1, unit) if size % b == 0], default=size)
 
 
-def stream(source, held, sems, block, depth, work):
-    steps = source.shape[1] // block
+def stream(source, held, sems, axis, block, depth, work):
+    steps = source.shape[axis] // block
+
+    def place(i):
+        here = pl.ds(pl.multiple_of(i * block, block), block)
+        return (here, slice(None)) if axis == 0 else (slice(None), here)
 
     def copy(i):
-        here = pl.ds(pl.multiple_of(i * block, block), block)
-        return pltpu.make_async_copy(source.at[:, here], held.at[:, here], sems.at[i])
+        return pltpu.make_async_copy(source.at[place(i)], held.at[place(i)], sems.at[i])
 
     depth = min(depth, steps)
     for i in range(depth):
@@ -68,20 +71,17 @@
 def grad_pre_body(block, depth, rows_ref, pre_ref, w_ref, out_ref, held, pre, rows, total, sems, sem):
     pre_copy = pltpu.make_async_copy(pre_ref, pre, sem)
     pre_copy.start()
-    places, each, _ = rows_ref.shape
-    for k in range(places):
-        rows[k * each : (k + 1) * each, :] = rows_ref[k].astype(jnp.float32)
-    total[...] = jnp.zeros_like(total)
+    places = rows_ref.shape[0]
+    rows[...] = jnp.concatenate(
+        [rows_ref[k].astype(jnp.float32) for k in range(places)], axis=0
+    ).astype(jnp.bfloat16)
 
     def work(here):
-        total[...] += lax.dot_general(
-            held[:, here],
-            rows[:, here].astype(jnp.bfloat16),
-            (((1,), (1,)), ((), ())),
-            preferred_element_type=jnp.float32,
+        total[here, :] = lax.dot_general(
+            held[here, :], rows[...], (((1,), (1,)), ((), ())), preferred_element_type=jnp.float32
         )
 
-    stream(w_ref, held, sems, block, depth, work)
+    stream(w_ref, held, sems, 0, block, depth, work)
     pre_copy.wait()
     slope = gelu_slope(pre[...].astype(jnp.float32))
     out_ref[...] = (total[...].T * slope).astype(jnp.bfloat16)
@@ -90,7 +90,7 @@
 def grad_pre_of(rows_grad, pre_act, w_out):
     group, hidden = pre_act.shape
     width = w_out.shape[1]
-    block = block_of(width, 512, 128)
+    block = block_of(hidden, 96, 16)
     return pl.pallas_call(
         functools.partial(grad_pre_body, block, 4),
         in_specs=[
@@ -103,12 +103,12 @@
         scratch_shapes=[
             pltpu.VMEM((hidden, width), jnp.bfloat16),
             pltpu.VMEM((group, hidden), jnp.bfloat16),
-            pltpu.VMEM((group, width), jnp.float32),
+            pltpu.VMEM((group, width), jnp.bfloat16),
             pltpu.VMEM((hidden, group), jnp.float32),
-            pltpu.SemaphoreType.DMA((width // block,)),
+            pltpu.SemaphoreType.DMA((hidden // block,)),
             pltpu.SemaphoreType.DMA,
         ],
-        compiler_params=pltpu.CompilerParams(vmem_limit_bytes=56 << 20),
+        compiler_params=pltpu.CompilerParams(vmem_limit_bytes=48 << 20),
         cost_estimate=pl.CostEstimate(
             flops=2 * group * width * hidden, bytes_accessed=2 * hidden * width, transcendentals=0
         ),
@@ -124,13 +124,13 @@
         for k in range(places):
             out_ref[k, :, here] = term[k * each : (k + 1) * each].astype(jnp.bfloat16)
 
-    stream(w_ref, held, sems, block, depth, work)
+    stream(w_ref, held, sems, 1, block, depth, work)
 
 
 def grad_in_part(grad_pre, w_in_t, places):
     group, hidden = grad_pre.shape
     width = w_in_t.shape[1]
-    block = block_of(width, 512, 128)
+    block = block_of(width, 256, 128)
     return pl.pallas_call(
         functools.partial(grad_in_body, block, 4),
         in_specs=[
@@ -143,7 +143,7 @@
             pltpu.VMEM((hidden, width), jnp.bfloat16),
             pltpu.SemaphoreType.DMA((width // block,)),
         ],
-        compiler_params=pltpu.CompilerParams(vmem_limit_bytes=56 << 20),
+        compiler_params=pltpu.CompilerParams(vmem_limit_bytes=48 << 20),
         cost_estimate=pl.CostEstimate(
             flops=2 * group * width * hidden, bytes_accessed=2 * hidden * width, transcendentals=0
         ),

time: 57.4 us -> 57.4 us (level)
  Pallas kernels: 23 us -> 22.1 us
  waiting for transfers between devices: 4.45 us -> 5.26 us
    pallas_call x1, Pallas kernels: 9.71 us -> 8.77 us  [grad_pre_of(): pl.pallas_call(functools.partial(grad_pre_body, block, 4), in_specs=[pl.B...]
    ppermute x6, waiting for transfers between devices: 0.24 us -> 1.01 us  [fetch(): return lax.ppermute(x, axis, [(partner(i, k, n), i) for i in range(n)])]
  transfers between devices with their start and end apart: 9 -> 9, of which waited for: 3 -> 3; matrix products, arithmetic and copies ran while one was open for 4% -> 4% of each run, Pallas kernels for 40% -> 39%
where the time goes in v6:
time: 57.4 us; the launch traced here: 56.9 us
  starting transfers between devices  22.1 us (39%)
  Pallas kernels  22.1 us (39%)
  waiting for transfers between devices  5.26 us (9%)
  local copies, waits for them, and re-layouts  3.97 us (7%)
  other arithmetic  2.69 us (5%)
  between operations  0.77 us (1%)
    all_to_all x3, starting transfers between devices, swap(): return lax.all_to_all(x, axis, 0, 0)  13.2 us
    ppermute x6, starting transfers between devices, fetch(): return lax.ppermute(x, axis, [(partner(i, k, n), i) for i in range(n)])  8.85 us
    pallas_call x1, Pallas kernels, grad_pre_of(): pl.pallas_call(functools.partial(grad_pre_body, block, 4), in_specs=[pl.B...  8.77 us
    pallas_call x1, Pallas kernels, grad_in_part(): pl.pallas_call(functools.partial(grad_in_body, block, 4), in_specs=[pl.Bl...  8.67 us
    pallas_call x1, Pallas kernels, grad_w_of(): pl.pallas_call(functools.partial(grad_w_body, places, scale_back, block),...  4.64 us
    all_to_all x3, waiting for transfers between devices, swap(): return lax.all_to_all(x, axis, 0, 0)  4.25 us
    broadcast_in_dim x1, local copies, waits for them, and re-layouts, shards(): rows_grad = jnp.broadcast_to(grad_out, (n_mp,) + grad_out.shape)  1.59 us
  transfers between devices with their start and end apart: 9, of which 3 were waited for; matrix products, arithmetic and copies ran while one was open for 4% of the time, Pallas kernels for 39%

profile of v6, /device:TPU:0, one launch (start us, length us, event | category | flops | bytes accessed | tf_op | source)
XLA Modules:
  0.0 56.9 jit_solution(6558658880499405099)
XLA Ops:
  0.6 1.6 %broadcast_in_dim.6 = bf16[8,4,5120]{2,1,0:T(4,128)(2,1)} broadcast(bf16[4,5120]{1,0:T(4,128)(2,1)} %param.6), dimensions={1,2} | broadcast | bytes 368640 | tf_op jit(solution)/shard_map/broadcast_in_dim | solution.py:237
  2.2 5.2 %all-to-all-start = ((bf16[8,4,5120]{2,1,0:T(4,128)(2,1)}), bf16[8,4,5120]{2,1,0:T(4,128)(2,1)S(1)}, u32[]{:S(2)}, u32[]{:S(2)}) async-start(bf16[8,4,5120]{2,1,0:T(4,128)(2,1)} %broadcast_in_dim.6), calls=%async_computation | async-start | bytes 655360 | tf_op jit(solution)/shard_map/all_to_all | solution.py:37
  7.4 0.9 %fusion.7 = (bf16[8,1280]{1,0:T(8,128)(2,1)S(1)}, bf16[8,1280]{1,0:T(8,128)(2,1)S(1)}, bf16[8,1280]{1,0:T(8,128)(2,1)S(1)}, bf16[8,1280]{1,0:T(8,128)(2,1)S(1)}) fusion(s32[]{:T(128)S(6)} %select_n.12, bf16[4,5120]{1,0:T(4,128)(2,1)} %param.5, bf16[4,5120]{1,0:T(4,128)(2,1)} %param.6, s32[]{:T(128)S(6)} %select_n.13, s32[]{:T(128)S(6)} %select_n.14, ...), kind=kLoop, calls=%fused_computation.17 | loop fusion | flops 163840 | bytes 163856 | tf_op jit(solution)/shard_map/concatenate | solution.py:241
  8.3 0.9 %fusion.5 = (bf16[40,1728]{1,0:T(8,128)(2,1)S(1)}, bf16[40,1728]{1,0:T(8,128)(2,1)S(1)}, bf16[40,1728]{1,0:T(8,128)(2,1)S(1)}) fusion(bf16[8,1280]{1,0:T(8,128)(2,1)S(1)} %get-tuple-element.31, bf16[32,1728]{1,0:T(8,128)(2,1)} %refs_0_.1, bf16[8,1280]{1,0:T(8,128)(2,1)S(1)} %get-tuple-element.30, bf16[8,1280]{1,0:T(8,128)(2,1)S(1)} %get-tuple-element.29), kind=kLoop, calls=%fused_computation.6 | loop fusion | flops 967680 | bytes 586752 | tf_op jit(solution)/shard_map/concatenate | solution.py:252
  9.3 3.7 %collective-permute-start.2 = (bf16[40,1728]{1,0:T(8,128)(2,1)S(1)}, bf16[40,1728]{1,0:T(8,128)(2,1)S(1)}, u32[]{:S(2)}, u32[]{:S(2)}) collective-permute-start(bf16[40,1728]{1,0:T(8,128)(2,1)S(1)} %get-tuple-element.25), channel_id=1, source_target_pairs={{3,0},{2,1},{1,2},{0,3},{7,4},{6,5},{5,6},{4,7},{11,8},{10,9},{9,1... | collective-permute-start | bytes 414728 | tf_op jit(solution)/shard_map/ppermute | solution.py:33
  12.9 0.0 collective-permute-start.1
  12.9 0.8 %collective-permute-start = (bf16[40,1728]{1,0:T(8,128)(2,1)S(1)}, bf16[40,1728]{1,0:T(8,128)(2,1)S(1)}, u32[]{:S(2)}, u32[]{:S(2)}) collective-permute-start(bf16[40,1728]{1,0:T(8,128)(2,1)S(1)} %get-tuple-element.27), channel_id=1, source_target_pairs={{1,0},{0,1},{3,2},{2,3},{5,4},{4,5},{7,6},{6,7},{9,8},{8,9},{11,10... | collective-permute-start | bytes 414728 | tf_op jit(solution)/shard_map/ppermute | solution.py:33
  13.7 1.3 %all-to-all-done.rows_ref = bf16[8,4,5120]{2,1,0:T(4,128)(2,1)S(1)} async-done(((bf16[8,4,5120]{2,1,0:T(4,128)(2,1)}), bf16[8,4,5120]{2,1,0:T(4,128)(2,1)S(1)}, u32[]{:S(2)}, u32[]{:S(2)}) %all-to-all-start) | async-done | bytes 327712 | tf_op jit(solution)/shard_map/all_to_all | solution.py:37
  15.0 0.9 %copy-done = bf16[32,1728]{1,0:T(8,128)(2,1)S(1)} copy-done((bf16[32,1728]{1,0:T(8,128)(2,1)S(1)}, bf16[32,1728]{1,0:T(8,128)(2,1)}, u32[]{:S(2)}) %copy-start) | copy-done | bytes 110616
  15.9 8.8 %grad_pre.1.grad_pre_ref.refs_4_ = bf16[32,1728]{1,0:T(8,128)(2,1)S(1)} custom-call(bf16[8,4,5120]{2,1,0:T(4,128)(2,1)S(1)} %all-to-all-done.rows_ref, bf16[32,1728]{1,0:T(8,128)(2,1)S(1)} %copy-done, bf16[1728,5120]{1,0:T(8,128)(2,1)} %w_ref.1), custom_call_target="tpu_custom_call" | custom-call | flops 566231040 | bytes 17694720 | tf_op jit(solution)/shard_map/grad_pre/pallas_call | solution.py:94
  24.7 1.0 %collective-permute-done.1.refs_2_ = bf16[40,1728]{1,0:T(8,128)(2,1)S(1)} collective-permute-done((bf16[40,1728]{1,0:T(8,128)(2,1)S(1)}, bf16[40,1728]{1,0:T(8,128)(2,1)S(1)}, u32[]{:S(2)}, u32[]{:S(2)}) %collective-permute-start.1) | collective-permute-done | bytes 138272 | tf_op jit(solution)/shard_map/ppermute | solution.py:33
  25.7 0.0 collective-permute-done.refs_1_
  25.8 0.1 maximum_bitcast_fusion
  25.9 1.0 %broadcast_in_dim.7 = bf16[8,2,4,4,1280]{4,3,2,1,0:T(4,128)(2,1)} broadcast(bf16[2,4,4,1280]{3,2,1,0:T(4,128)(2,1)S(1)} %copy.9), dimensions={1,2,3,4} | broadcast | bytes 737280 | tf_op jit(solution)/shard_map/broadcast_in_dim | solution.py:261
  26.9 3.8 %all-to-all-start.1 = ((bf16[8,2,4,4,1280]{4,3,2,1,0:T(4,128)(2,1)}), bf16[8,2,4,4,1280]{4,3,2,1,0:T(4,128)(2,1)S(1)}, u32[]{:S(2)}, u32[]{:S(2)}) async-start(bf16[8,2,4,4,1280]{4,3,2,1,0:T(4,128)(2,1)} %broadcast_in_dim.7), calls=%async_computation.1 | async-start | bytes 1310720 | tf_op jit(solution)/shard_map/all_to_all | solution.py:37
  30.8 2.5 %collective-permute-start.5 = (bf16[32,1728]{1,0:T(8,128)(2,1)S(1)}, bf16[32,1728]{1,0:T(8,128)(2,1)S(1)}, u32[]{:S(2)}, u32[]{:S(2)}) collective-permute-start(bf16[32,1728]{1,0:T(8,128)(2,1)S(1)} %grad_pre.1.grad_pre_ref.refs_4_), channel_id=1, source_target_pairs={{3,0},{2,1},{1,2},{0,3},{7,4},{6,5},{5,6},{4,7},{11,8},{10,9},{9,1... | collective-permute-start | bytes 331784 | tf_op jit(solution)/shard_map/ppermute | solution.py:33
  33.2 1.9 %collective-permute-start.3 = (bf16[32,1728]{1,0:T(8,128)(2,1)S(1)}, bf16[32,1728]{1,0:T(8,128)(2,1)S(1)}, u32[]{:S(2)}, u32[]{:S(2)}) collective-permute-start(bf16[32,1728]{1,0:T(8,128)(2,1)S(1)} %grad_pre.1.grad_pre_ref.refs_4_), channel_id=1, source_target_pairs={{1,0},{0,1},{3,2},{2,3},{5,4},{4,5},{7,6},{6,7},{9,8},{8,9},{11,10... | collective-permute-start | bytes 331784 | tf_op jit(solution)/shard_map/ppermute | solution.py:33
  35.2 8.7 %grad_in_part.1 = bf16[8,4,5120]{2,1,0:T(4,128)(2,1)} custom-call(bf16[32,1728]{1,0:T(8,128)(2,1)S(1)} %grad_pre.1.grad_pre_ref.refs_4_, bf16[1728,5120]{1,0:T(8,128)(2,1)} %bitcast.5), custom_call_target="tpu_custom_call" | custom-call | flops 566231040 | bytes 17694720 | tf_op jit(solution)/shard_map/grad_in_part/pallas_call | solution.py:134
  43.8 0.2 copy.10
  44.1 0.2 reshape.18.refs_8_
  44.2 4.2 %all-to-all-start.2 = ((bf16[8,4,5120]{2,1,0:T(4,128)(2,1)}), bf16[8,4,5120]{2,1,0:T(4,128)(2,1)S(1)}, u32[]{:S(2)}, u32[]{:S(2)}) async-start(bf16[8,4,5120]{2,1,0:T(4,128)(2,1)} %grad_in_part.1), calls=%async_computation.2 | async-start | bytes 655360 | tf_op jit(solution)/shard_map/all_to_all | solution.py:37
  48.5 4.6 %grad_w.1 = (bf16[1728,1280]{1,0:T(8,128)(2,1)}, bf16[1728,1280]{1,0:T(8,128)(2,1)}) custom-call(bf16[32,1728]{1,0:T(8,128)(2,1)S(1)} %copy-done.1, bf16[40,1728]{1,0:T(8,128)(2,1)S(1)} %collective-permute-done.refs_1_, bf16[40,1728]{1,0:T(8,128)(2,1)S(1)} %collective-permute-done.1.refs_2_, bf16[40,1728]{1,0:T(8,128)(2,1)S(1)} %collective-permute-done.2.refs_3_, ...), custom_call_target="tpu_custom_call" | custom-call | flops 22649241600 | bytes 88473600 | tf_op jit(solution)/shard_map/grad_w/pallas_call | solution.py:205
  53.1 2.9 %all-to-all-done.2 = bf16[8,4,5120]{2,1,0:T(4,128)(2,1)S(1)} async-done(((bf16[8,4,5120]{2,1,0:T(4,128)(2,1)}), bf16[8,4,5120]{2,1,0:T(4,128)(2,1)S(1)}, u32[]{:S(2)}, u32[]{:S(2)}) %all-to-all-start.2) | async-done | bytes 327712 | tf_op jit(solution)/shard_map/all_to_all | solution.py:37
  56.1 0.8 %reduce_sum.12 = bf16[4,5120]{1,0:T(4,128)(2,1)} reduce(bf16[8,4,5120]{2,1,0:T(4,128)(2,1)S(1)} %all-to-all-done.2, bf16[]{:T(256)} %constant.7.clone.1), dimensions={0}, to_apply=%region_0.1 | reduce | flops 143360 | bytes 368642 | tf_op jit(solution)/shard_map/reduce_sum | solution.py:268
  (17 shorter events, 0.1 us)
Async XLA Ops:
  2.2 12.8 %all-to-all-start = ((bf16[8,4,5120]{2,1,0:T(4,128)(2,1)}), bf16[8,4,5120]{2,1,0:T(4,128)(2,1)S(1)}, u32[]{:S(2)}, u32[]{:S(2)}) async-start(bf16[8,4,5120]{2,1,0:T(4,128)(2,1)} %broadcast_in_dim.6), calls=%async_computation | async-start | bytes 655360 | tf_op jit(solution)/shard_map/all_to_all | solution.py:37
  9.3 15.5 %collective-permute-start.2 = (bf16[40,1728]{1,0:T(8,128)(2,1)S(1)}, bf16[40,1728]{1,0:T(8,128)(2,1)S(1)}, u32[]{:S(2)}, u32[]{:S(2)}) collective-permute-start(bf16[40,1728]{1,0:T(8,128)(2,1)S(1)} %get-tuple-element.25), channel_id=1, source_target_pairs={{3,0},{2,1},{1,2},{0,3},{7,4},{6,5},{5,6},{4,7},{11,8},{10,9},{9,1... | collective-permute-start | bytes 414728 | tf_op jit(solution)/shard_map/ppermute | solution.py:33
  12.9 12.8 %collective-permute-start.1 = (bf16[40,1728]{1,0:T(8,128)(2,1)S(1)}, bf16[40,1728]{1,0:T(8,128)(2,1)S(1)}, u32[]{:S(2)}, u32[]{:S(2)}) collective-permute-start(bf16[40,1728]{1,0:T(8,128)(2,1)S(1)} %get-tuple-element.26), channel_id=1, source_target_pairs={{2,0},{3,1},{0,2},{1,3},{6,4},{7,5},{4,6},{5,7},{10,8},{11,9},{8,1... | collective-permute-start | bytes 414728 | tf_op jit(solution)/shard_map/ppermute | solution.py:33
  12.9 12.8 %collective-permute-start = (bf16[40,1728]{1,0:T(8,128)(2,1)S(1)}, bf16[40,1728]{1,0:T(8,128)(2,1)S(1)}, u32[]{:S(2)}, u32[]{:S(2)}) collective-permute-start(bf16[40,1728]{1,0:T(8,128)(2,1)S(1)} %get-tuple-element.27), channel_id=1, source_target_pairs={{1,0},{0,1},{3,2},{2,3},{5,4},{4,5},{7,6},{6,7},{9,8},{8,9},{11,10... | collective-permute-start | bytes 414728 | tf_op jit(solution)/shard_map/ppermute | solution.py:33
  15.0 0.9 %copy-start = (bf16[32,1728]{1,0:T(8,128)(2,1)S(1)}, bf16[32,1728]{1,0:T(8,128)(2,1)}, u32[]{:S(2)}) copy-start(bf16[32,1728]{1,0:T(8,128)(2,1)} %refs_0_.1) | copy-start | bytes 331780
  15.9 32.6 %copy-start.1 = (bf16[32,1728]{1,0:T(8,128)(2,1)S(1)}, bf16[32,1728]{1,0:T(8,128)(2,1)}, u32[]{:S(2)}) copy-start(bf16[32,1728]{1,0:T(8,128)(2,1)} %refs_0_.1) | copy-start | bytes 331780
  26.9 16.9 %all-to-all-start.1 = ((bf16[8,2,4,4,1280]{4,3,2,1,0:T(4,128)(2,1)}), bf16[8,2,4,4,1280]{4,3,2,1,0:T(4,128)(2,1)S(1)}, u32[]{:S(2)}, u32[]{:S(2)}) async-start(bf16[8,2,4,4,1280]{4,3,2,1,0:T(4,128)(2,1)} %broadcast_in_dim.7), calls=%async_computation.1 | async-start | bytes 1310720 | tf_op jit(solution)/shard_map/all_to_all | solution.py:37
  30.8 17.7 %collective-permute-start.5 = (bf16[32,1728]{1,0:T(8,128)(2,1)S(1)}, bf16[32,1728]{1,0:T(8,128)(2,1)S(1)}, u32[]{:S(2)}, u32[]{:S(2)}) collective-permute-start(bf16[32,1728]{1,0:T(8,128)(2,1)S(1)} %grad_pre.1.grad_pre_ref.refs_4_), channel_id=1, source_target_pairs={{3,0},{2,1},{1,2},{0,3},{7,4},{6,5},{5,6},{4,7},{11,8},{10,9},{9,1... | collective-permute-start | bytes 331784 | tf_op jit(solution)/shard_map/ppermute | solution.py:33
  33.2 15.2 %collective-permute-start.4 = (bf16[32,1728]{1,0:T(8,128)(2,1)S(1)}, bf16[32,1728]{1,0:T(8,128)(2,1)S(1)}, u32[]{:S(2)}, u32[]{:S(2)}) collective-permute-start(bf16[32,1728]{1,0:T(8,128)(2,1)S(1)} %grad_pre.1.grad_pre_ref.refs_4_), channel_id=1, source_target_pairs={{2,0},{3,1},{0,2},{1,3},{6,4},{7,5},{4,6},{5,7},{10,8},{11,9},{8,1... | collective-permute-start | bytes 331784 | tf_op jit(solution)/shard_map/ppermute | solution.py:33
  33.2 15.2 %collective-permute-start.3 = (bf16[32,1728]{1,0:T(8,128)(2,1)S(1)}, bf16[32,1728]{1,0:T(8,128)(2,1)S(1)}, u32[]{:S(2)}, u32[]{:S(2)}) collective-permute-start(bf16[32,1728]{1,0:T(8,128)(2,1)S(1)} %grad_pre.1.grad_pre_ref.refs_4_), channel_id=1, source_target_pairs={{1,0},{0,1},{3,2},{2,3},{5,4},{4,5},{7,6},{6,7},{9,8},{8,9},{11,10... | collective-permute-start | bytes 331784 | tf_op jit(solution)/shard_map/ppermute | solution.py:33
  44.2 11.9 %all-to-all-start.2 = ((bf16[8,4,5120]{2,1,0:T(4,128)(2,1)}), bf16[8,4,5120]{2,1,0:T(4,128)(2,1)S(1)}, u32[]{:S(2)}, u32[]{:S(2)}) async-start(bf16[8,4,5120]{2,1,0:T(4,128)(2,1)} %grad_in_part.1), calls=%async_computation.2 | async-start | bytes 655360 | tf_op jit(solution)/shard_map/all_to_all | solution.py:37

commit v7 on v6

--- a/solution.py
+++ b/solution.py
@@ -41,74 +41,80 @@
     return max([b for b in range(unit, most + 1, unit) if size % b == 0], default=size)
 
 
-def stream(source, held, sems, axis, block, depth, work):
-    steps = source.shape[axis] // block
-
-    def place(i):
-        here = pl.ds(pl.multiple_of(i * block, block), block)
-        return (here, slice(None)) if axis == 0 else (slice(None), here)
-
-    def copy(i):
-        return pltpu.make_async_copy(source.at[place(i)], held.at[place(i)], sems.at[i])
-
-    depth = min(depth, steps)
-    for i in range(depth):
-        copy(i).start()
-
-    def step(i, carry):
-        copy(i).wait()
-
-        @pl.when(i + depth < steps)
-        def _():
-            copy(i + depth).start()
-
-        work(pl.ds(pl.multiple_of(i * block, block), block))
-        return carry
-
-    lax.fori_loop(0, steps, step, 0)
-
-
-def grad_pre_body(block, depth, rows_ref, pre_ref, w_ref, out_ref, held, pre, rows, total, sems, sem):
-    pre_copy = pltpu.make_async_copy(pre_ref, pre, sem)
-    pre_copy.start()
+def pack_body(takers, tokens_ref, grad_ref, pre_ref, *refs):
+    *packed, own, pre_copy, slabs = refs
+    places, rows, part = slabs.shape
+    hidden = pre_ref.shape[1]
+    both = jnp.concatenate(
+        [tokens_ref[...].astype(jnp.float32), grad_ref[...].astype(jnp.float32)], axis=0
+    )
+    for p in range(places):
+        slabs[p] = both[:, p * part : (p + 1) * part]
+    t = lax.axis_index("tokens")
+    own[...] = slabs[t].astype(jnp.bfloat16)
+    pre_copy[...] = pre_ref[...]
+    pre = pre_ref[...].astype(jnp.float32)
+    for k, ref in enumerate(packed):
+        piece = slabs[takers(t, k + 1)]
+        wide = ref.shape[1]
+        ref[...] = jnp.concatenate(
+            [
+                jnp.pad(pre, ((0, 0), (0, wide - hidden))),
+                jnp.pad(piece, ((0, 0), (0, wide - part))),
+            ],
+            axis=0,
+        ).astype(jnp.bfloat16)
+
+
+def pack(tokens_in, grad_out, pre_act, n_tok):
+    def takers(t, k):
+        return t ^ k if n_tok & (n_tok - 1) == 0 else lax.rem(t - k + n_tok, n_tok)
+
+    rows, width = tokens_in.shape
+    group, hidden = pre_act.shape
+    part = width // n_tok
+    shapes = [(group + 2 * rows, max(hidden, part))] * (n_tok - 1) + [(2 * rows, part), pre_act.shape]
+    return pl.pallas_call(
+        functools.partial(pack_body, takers),
+        in_specs=[pl.BlockSpec(memory_space=pltpu.VMEM)] * 3,
+        out_specs=[pl.BlockSpec(memory_space=pltpu.VMEM)] * (n_tok + 1),
+        out_shape=[jax.ShapeDtypeStruct(shape, jnp.bfloat16) for shape in shapes],
+        scratch_shapes=[pltpu.VMEM((n_tok, 2 * rows, part), jnp.float32)],
+        compiler_params=pltpu.CompilerParams(vmem_limit_bytes=8 << 20),
+        cost_estimate=pl.CostEstimate(flops=10**10, bytes_accessed=36 * 10**6, transcendentals=0),
+        name="pack",
+    )(tokens_in, grad_out, pre_act)
+
+
+def grad_pre_body(block, rows_ref, pre_ref, w_ref, out_ref, rows, total):
     places = rows_ref.shape[0]
+    hidden = w_ref.shape[0]
     rows[...] = jnp.concatenate(
         [rows_ref[k].astype(jnp.float32) for k in range(places)], axis=0
     ).astype(jnp.bfloat16)
-
-    def work(here):
+    for low in range(0, hidden, block):
+        here = slice(low, low + block)
         total[here, :] = lax.dot_general(
-            held[here, :], rows[...], (((1,), (1,)), ((), ())), preferred_element_type=jnp.float32
+            w_ref[here, :], rows[...], (((1,), (1,)), ((), ())), preferred_element_type=jnp.float32
         )
-
-    stream(w_ref, held, sems, 0, block, depth, work)
-    pre_copy.wait()
-    slope = gelu_slope(pre[...].astype(jnp.float32))
+    slope = gelu_slope(pre_ref[...].astype(jnp.float32))
     out_ref[...] = (total[...].T * slope).astype(jnp.bfloat16)
 
 
 def grad_pre_of(rows_grad, pre_act, w_out):
     group, hidden = pre_act.shape
     width = w_out.shape[1]
-    block = block_of(hidden, 96, 16)
-    return pl.pallas_call(
-        functools.partial(grad_pre_body, block, 4),
-        in_specs=[
-            pl.BlockSpec(memory_space=pltpu.VMEM),
-            pl.BlockSpec(memory_space=pltpu.HBM),
-            pl.BlockSpec(memory_space=pltpu.HBM),
-        ],
+    block = block_of(hidden, 432, 16)
+    return pl.pallas_call(
+        functools.partial(grad_pre_body, block),
+        in_specs=[pl.BlockSpec(memory_space=pltpu.VMEM)] * 3,
         out_specs=pl.BlockSpec(memory_space=pltpu.VMEM),
         out_shape=jax.ShapeDtypeStruct((group, hidden), jnp.bfloat16),
         scratch_shapes=[
-            pltpu.VMEM((hidden, width), jnp.bfloat16),
-            pltpu.VMEM((group, hidden), jnp.bfloat16),
             pltpu.VMEM((group, width), jnp.bfloat16),
             pltpu.VMEM((hidden, group), jnp.float32),
-            pltpu.SemaphoreType.DMA((hidden // block,)),
-            pltpu.SemaphoreType.DMA,
         ],
-        compiler_params=pltpu.CompilerParams(vmem_limit_bytes=48 << 20),
+        compiler_params=pltpu.CompilerParams(vmem_limit_bytes=8 << 20),
         cost_estimate=pl.CostEstimate(
             flops=2 * group * width * hidden, bytes_accessed=2 * hidden * width, transcendentals=0
         ),
@@ -116,34 +122,25 @@
     )(rows_grad, pre_act, w_out)
 
 
-def grad_in_body(block, depth, grad_pre_ref, w_ref, out_ref, held, sems):
-    places, each, _ = out_ref.shape
-
-    def work(here):
-        term = jnp.dot(grad_pre_ref[...], held[:, here], preferred_element_type=jnp.float32)
+def grad_in_body(block, grad_pre_ref, w_ref, out_ref):
+    places, each, width = out_ref.shape
+    for low in range(0, width, block):
+        here = slice(low, low + block)
+        term = jnp.dot(grad_pre_ref[...], w_ref[:, here], preferred_element_type=jnp.float32)
         for k in range(places):
             out_ref[k, :, here] = term[k * each : (k + 1) * each].astype(jnp.bfloat16)
-
-    stream(w_ref, held, sems, 1, block, depth, work)
 
 
 def grad_in_part(grad_pre, w_in_t, places):
     group, hidden = grad_pre.shape
     width = w_in_t.shape[1]
-    block = block_of(width, 256, 128)
-    return pl.pallas_call(
-        functools.partial(grad_in_body, block, 4),
-        in_specs=[
-            pl.BlockSpec(memory_space=pltpu.VMEM),
-            pl.BlockSpec(memory_space=pltpu.HBM),
-        ],
+    block = block_of(width, 1024, 128)
+    return pl.pallas_call(
+        functools.partial(grad_in_body, block),
+        in_specs=[pl.BlockSpec(memory_space=pltpu.VMEM)] * 2,
         out_specs=pl.BlockSpec(memory_space=pltpu.VMEM),
         out_shape=jax.ShapeDtypeStruct((places, group // places, width), jnp.bfloat16),
-        scratch_shapes=[
-            pltpu.VMEM((hidden, width), jnp.bfloat16),
-            pltpu.SemaphoreType.DMA((width // block,)),
-        ],
-        compiler_params=pltpu.CompilerParams(vmem_limit_bytes=48 << 20),
+        compiler_params=pltpu.CompilerParams(vmem_limit_bytes=8 << 20),
         cost_estimate=pl.CostEstimate(
             flops=2 * group * width * hidden, bytes_accessed=2 * hidden * width, transcendentals=0
         ),
@@ -227,7 +224,6 @@
 
 def shards(tokens_in, grad_out, pre_act, w_in, w_out):
     n_mp, n_tok = lax.axis_size("mp"), lax.axis_size("tokens")
-    t = lax.axis_index("tokens")
     rows, width = tokens_in.shape
     group, hidden = pre_act.shape
     part = width // n_tok
@@ -238,18 +234,8 @@
     rows_grad, tokens_in, grad_out = lax.optimization_barrier((rows_grad, tokens_in, grad_out))
     rows_grad = swap(rows_grad, "mp")
 
-    both = jnp.concatenate([tokens_in, grad_out], axis=0)
-    wide = max(hidden, part)
-    own_pre = jnp.pad(pre_act, ((0, 0), (0, wide - hidden)))
-    packed = []
-    for k in range(n_tok):
-        taker = t ^ k if n_tok & (n_tok - 1) == 0 else (t - k) % n_tok
-        piece = lax.dynamic_slice_in_dim(both, taker * part, part, axis=1)
-        if k == 0:
-            own_piece = piece
-        else:
-            piece = jnp.pad(piece, ((0, 0), (0, wide - part)))
-            packed.append(fetch(jnp.concatenate([own_pre, piece], axis=0), "tokens", k))
+    *packed, own_piece, pre_act = pack(tokens_in, grad_out, pre_act, n_tok)
+    packed = [fetch(x, "tokens", k + 1) for k, x in enumerate(packed)]
 
     grad_pre = grad_pre_of(rows_grad, pre_act, w_out)
     grad_pre_all = [grad_pre] + [fetch(grad_pre, "tokens", k) for k in range(1, n_tok)]

time: 57.4 us -> 58.7 us (1.023)
  local copies, waits for them, and re-layouts: 3.97 us -> 17.6 us
  Pallas kernels: 22.1 us -> 13.5 us
  other arithmetic: 2.69 us -> 0.83 us
  waiting for transfers between devices: 5.26 us -> 3.63 us
    unnamed x4 -> x10, local copies, waits for them, and re-layouts: 0.9 us -> 14.5 us
    pallas_call x2 -> x3, Pallas kernels: 17.4 us -> 8.84 us  [the longest x1 4.9 us: grad_pre_of(): pl.pallas_call(functools.partial(grad_pre_body, block), in_specs=[pl.Bloc...]
    concatenate x2 -> x0, other arithmetic: 1.86 us -> none  [the longest x1 0.93 us: shards(): packed.append(fetch(jnp.concatenate([own_pre, piece], axis=0), 'tokens', k))]
    ppermute x6, waiting for transfers between devices: 1.01 us -> 0.02 us  [fetch(): return lax.ppermute(x, axis, [(partner(i, k, n), i) for i in range(n)])]
    all_to_all x3, waiting for transfers between devices: 4.25 us -> 3.62 us  [swap(): return lax.all_to_all(x, axis, 0, 0)]
  transfers between devices with their start and end apart: 9 -> 9, of which waited for: 3 -> 2; matrix products, arithmetic and copies ran while one was open for 4% -> 1% of each run, Pallas kernels for 39% -> 23%
where the time goes in v7:
time: 58.7 us; the launch traced here: 58.1 us
  starting transfers between devices  21.8 us (37%)
  local copies, waits for them, and re-layouts  17.6 us (30%)
  Pallas kernels  13.5 us (23%)
  waiting for transfers between devices  3.63 us (6%)
  other arithmetic  0.83 us (1%)
  between operations  0.77 us (1%)
    unnamed x10, local copies, waits for them, and re-layouts  14.5 us
    all_to_all x3, starting transfers between devices, swap(): return lax.all_to_all(x, axis, 0, 0)  12.9 us
    ppermute x6, starting transfers between devices, fetch(): return lax.ppermute(x, axis, [(partner(i, k, n), i) for i in range(n)])  8.9 us
    pallas_call x1, Pallas kernels, grad_pre_of(): pl.pallas_call(functools.partial(grad_pre_body, block), in_specs=[pl.Bloc...  4.9 us
    pallas_call x1, Pallas kernels, grad_w_of(): pl.pallas_call(functools.partial(grad_w_body, places, scale_back, block),...  4.65 us
    pallas_call x1, Pallas kernels, grad_in_part(): pl.pallas_call(functools.partial(grad_in_body, block), in_specs=[pl.Block...  3.88 us
    all_to_all x3, waiting for transfers between devices, swap(): return lax.all_to_all(x, axis, 0, 0)  3.62 us
    broadcast_in_dim x1, local copies, waits for them, and re-layouts, shards(): rows_grad = jnp.broadcast_to(grad_out, (n_mp,) + grad_out.shape)  1.59 us
  transfers between devices with their start and end apart: 9, of which 2 were waited for; matrix products, arithmetic and copies ran while one was open for 1% of the time, Pallas kernels for 23%

profile of v7, /device:TPU:0, one launch (start us, length us, event | category | flops | bytes accessed | tf_op | source)
XLA Modules:
  0.0 58.1 jit_solution(8404252652728075395)
XLA Ops:
  0.6 1.6 %broadcast_in_dim.6 = bf16[8,4,5120]{2,1,0:T(4,128)(2,1)} broadcast(bf16[4,5120]{1,0:T(4,128)(2,1)} %grad_ref), dimensions={1,2} | broadcast | bytes 368640 | tf_op jit(solution)/shard_map/broadcast_in_dim | solution.py:233
  2.2 5.2 %all-to-all-start = ((bf16[8,4,5120]{2,1,0:T(4,128)(2,1)}), bf16[8,4,5120]{2,1,0:T(4,128)(2,1)S(1)}, u32[]{:S(2)}, u32[]{:S(2)}) async-start(bf16[8,4,5120]{2,1,0:T(4,128)(2,1)} %broadcast_in_dim.6), calls=%async_computation | async-start | bytes 655360 | tf_op jit(solution)/shard_map/all_to_all | solution.py:37
  7.4 0.8 %copy-done.2 = bf16[4,5120]{1,0:T(4,128)(2,1)S(1)} copy-done((bf16[4,5120]{1,0:T(4,128)(2,1)S(1)}, bf16[4,5120]{1,0:T(4,128)(2,1)}, u32[]{:S(2)}) %copy-start.2) | copy-done | bytes 40984
  8.2 0.9 %copy-done.3 = bf16[32,1728]{1,0:T(8,128)(2,1)S(1)} copy-done((bf16[32,1728]{1,0:T(8,128)(2,1)S(1)}, bf16[32,1728]{1,0:T(8,128)(2,1)}, u32[]{:S(2)}) %copy-start.3) | copy-done | bytes 110616
  9.1 0.8 %copy-done.4 = bf16[4,5120]{1,0:T(4,128)(2,1)S(1)} copy-done((bf16[4,5120]{1,0:T(4,128)(2,1)S(1)}, bf16[4,5120]{1,0:T(4,128)(2,1)}, u32[]{:S(2)}) %copy-start.4) | copy-done | bytes 40984
  9.9 1.6 %collective-permute-start = (bf16[40,1728]{1,0:T(8,128)(2,1)S(1)}, bf16[40,1728]{1,0:T(8,128)(2,1)S(1)}, u32[]{:S(2)}, u32[]{:S(2)}) collective-permute-start(bf16[40,1728]{1,0:T(8,128)(2,1)S(1)} %get-tuple-element.22), channel_id=1, source_target_pairs={{1,0},{0,1},{3,2},{2,3},{5,4},{4,5},{7,6},{6,7},{9,8},{8,9},{11,10... | collective-permute-start | bytes 414728 | tf_op jit(solution)/shard_map/ppermute | solution.py:33
  11.6 2.6 %collective-permute-start.1 = (bf16[40,1728]{1,0:T(8,128)(2,1)S(1)}, bf16[40,1728]{1,0:T(8,128)(2,1)S(1)}, u32[]{:S(2)}, u32[]{:S(2)}) collective-permute-start(bf16[40,1728]{1,0:T(8,128)(2,1)S(1)} %get-tuple-element.23), channel_id=1, source_target_pairs={{2,0},{3,1},{0,2},{1,3},{6,4},{7,5},{4,6},{5,7},{10,8},{11,9},{8,1... | collective-permute-start | bytes 414728 | tf_op jit(solution)/shard_map/ppermute | solution.py:33
  14.1 0.2 collective-permute-start.2
  14.4 0.7 %all-to-all-done.rows_ref = bf16[8,4,5120]{2,1,0:T(4,128)(2,1)S(1)} async-done(((bf16[8,4,5120]{2,1,0:T(4,128)(2,1)}), bf16[8,4,5120]{2,1,0:T(4,128)(2,1)S(1)}, u32[]{:S(2)}, u32[]{:S(2)}) %all-to-all-start) | async-done | bytes 327712 | tf_op jit(solution)/shard_map/all_to_all | solution.py:37
  15.0 6.0 %copy-done.1 = bf16[1728,5120]{1,0:T(8,128)(2,1)S(1)} copy-done((bf16[1728,5120]{1,0:T(8,128)(2,1)S(1)}, bf16[1728,5120]{1,0:T(8,128)(2,1)}, u32[]{:S(2)}) %copy-start.1) | copy-done | bytes 17694744
  21.1 4.9 %grad_pre.1.grad_pre_ref.refs_4_ = bf16[32,1728]{1,0:T(8,128)(2,1)S(1)} custom-call(bf16[8,4,5120]{2,1,0:T(4,128)(2,1)S(1)} %all-to-all-done.rows_ref, bf16[32,1728]{1,0:T(8,128)(2,1)S(1)} %get-tuple-element.26.pre_ref.refs_0_, bf16[1728,5120]{1,0:T(8,128)(2,1)S(1)} %copy-done.1), custom_call_target="tpu_custom_call" | custom-call | flops 566231040 | bytes 17694720 | tf_op jit(solution)/shard_map/grad_pre/pallas_call | solution.py:108
  26.2 1.0 %broadcast_in_dim.7 = bf16[8,2,4,4,1280]{4,3,2,1,0:T(4,128)(2,1)} broadcast(bf16[2,4,4,1280]{3,2,1,0:T(4,128)(2,1)S(1)} %copy.9), dimensions={1,2,3,4} | broadcast | bytes 737280 | tf_op jit(solution)/shard_map/broadcast_in_dim | solution.py:247
  27.2 3.6 %all-to-all-start.1 = ((bf16[8,2,4,4,1280]{4,3,2,1,0:T(4,128)(2,1)}), bf16[8,2,4,4,1280]{4,3,2,1,0:T(4,128)(2,1)S(1)}, u32[]{:S(2)}, u32[]{:S(2)}) async-start(bf16[8,2,4,4,1280]{4,3,2,1,0:T(4,128)(2,1)} %broadcast_in_dim.7), calls=%async_computation.1 | async-start | bytes 1310720 | tf_op jit(solution)/shard_map/all_to_all | solution.py:37
  30.8 3.7 %collective-permute-start.5 = (bf16[32,1728]{1,0:T(8,128)(2,1)S(1)}, bf16[32,1728]{1,0:T(8,128)(2,1)S(1)}, u32[]{:S(2)}, u32[]{:S(2)}) collective-permute-start(bf16[32,1728]{1,0:T(8,128)(2,1)S(1)} %grad_pre.1.grad_pre_ref.refs_4_), channel_id=1, source_target_pairs={{3,0},{2,1},{1,2},{0,3},{7,4},{6,5},{5,6},{4,7},{11,8},{10,9},{9,1... | collective-permute-start | bytes 331784 | tf_op jit(solution)/shard_map/ppermute | solution.py:33
  34.4 0.2 collective-permute-start.4
  34.7 0.5 collective-permute-start.3
  35.2 6.0 %copy-done = bf16[5120,1728]{0,1:T(8,128)(2,1)S(1)} copy-done((bf16[5120,1728]{0,1:T(8,128)(2,1)S(1)}, bf16[5120,1728]{0,1:T(8,128)(2,1)}, u32[]{:S(2)}) %copy-start) | copy-done | bytes 17694744
  41.3 3.9 %grad_in_part.1 = bf16[8,4,5120]{2,1,0:T(4,128)(2,1)} custom-call(bf16[32,1728]{1,0:T(8,128)(2,1)S(1)} %grad_pre.1.grad_pre_ref.refs_4_, bf16[1728,5120]{1,0:T(8,128)(2,1)S(1)} %bitcast.5), custom_call_target="tpu_custom_call" | custom-call | flops 566231040 | bytes 17694720 | tf_op jit(solution)/shard_map/grad_in_part/pallas_call | solution.py:138
  45.1 0.2 copy.10
  45.4 0.2 reshape.18.refs_8_
  45.5 4.2 %all-to-all-start.2 = ((bf16[8,4,5120]{2,1,0:T(4,128)(2,1)}), bf16[8,4,5120]{2,1,0:T(4,128)(2,1)S(1)}, u32[]{:S(2)}, u32[]{:S(2)}) async-start(bf16[8,4,5120]{2,1,0:T(4,128)(2,1)} %grad_in_part.1), calls=%async_computation.2 | async-start | bytes 655360 | tf_op jit(solution)/shard_map/all_to_all | solution.py:37
  49.7 4.6 %grad_w.1 = (bf16[1728,1280]{1,0:T(8,128)(2,1)}, bf16[1728,1280]{1,0:T(8,128)(2,1)}) custom-call(bf16[32,1728]{1,0:T(8,128)(2,1)S(1)} %get-tuple-element.26.pre_ref.refs_0_, bf16[40,1728]{1,0:T(8,128)(2,1)S(1)} %collective-permute-done.refs_1_, bf16[40,1728]{1,0:T(8,128)(2,1)S(1)} %collective-permute-done.1.refs_2_, ...), custom_call_target="tpu_custom_call" | custom-call | flops 22649241600 | bytes 88473600 | tf_op jit(solution)/shard_map/grad_w/pallas_call | solution.py:202
  54.4 3.0 %all-to-all-done.2 = bf16[8,4,5120]{2,1,0:T(4,128)(2,1)S(1)} async-done(((bf16[8,4,5120]{2,1,0:T(4,128)(2,1)}), bf16[8,4,5120]{2,1,0:T(4,128)(2,1)S(1)}, u32[]{:S(2)}, u32[]{:S(2)}) %all-to-all-start.2) | async-done | bytes 327712 | tf_op jit(solution)/shard_map/all_to_all | solution.py:37
  57.3 0.8 %reduce_sum.12 = bf16[4,5120]{1,0:T(4,128)(2,1)} reduce(bf16[8,4,5120]{2,1,0:T(4,128)(2,1)S(1)} %all-to-all-done.2, bf16[]{:T(256)} %constant.2.clone.1), dimensions={0}, to_apply=%region_0.0 | reduce | flops 143360 | bytes 368642 | tf_op jit(solution)/shard_map/reduce_sum | solution.py:254
  (22 shorter events, 0.2 us)
Async XLA Ops:
  2.2 12.8 %all-to-all-start = ((bf16[8,4,5120]{2,1,0:T(4,128)(2,1)}), bf16[8,4,5120]{2,1,0:T(4,128)(2,1)S(1)}, u32[]{:S(2)}, u32[]{:S(2)}) async-start(bf16[8,4,5120]{2,1,0:T(4,128)(2,1)} %broadcast_in_dim.6), calls=%async_computation | async-start | bytes 655360 | tf_op jit(solution)/shard_map/all_to_all | solution.py:37
  7.4 0.8 %copy-start.2 = (bf16[4,5120]{1,0:T(4,128)(2,1)S(1)}, bf16[4,5120]{1,0:T(4,128)(2,1)}, u32[]{:S(2)}) copy-start(bf16[4,5120]{1,0:T(4,128)(2,1)} %grad_ref) | copy-start | bytes 122884
  8.2 0.9 %copy-start.3 = (bf16[32,1728]{1,0:T(8,128)(2,1)S(1)}, bf16[32,1728]{1,0:T(8,128)(2,1)}, u32[]{:S(2)}) copy-start(bf16[32,1728]{1,0:T(8,128)(2,1)} %pre_ref.1) | copy-start | bytes 331780
  9.1 0.8 %copy-start.4 = (bf16[4,5120]{1,0:T(4,128)(2,1)S(1)}, bf16[4,5120]{1,0:T(4,128)(2,1)}, u32[]{:S(2)}) copy-start(bf16[4,5120]{1,0:T(4,128)(2,1)} %tokens_ref) | copy-start | bytes 122884
  9.9 16.1 %collective-permute-start = (bf16[40,1728]{1,0:T(8,128)(2,1)S(1)}, bf16[40,1728]{1,0:T(8,128)(2,1)S(1)}, u32[]{:S(2)}, u32[]{:S(2)}) collective-permute-start(bf16[40,1728]{1,0:T(8,128)(2,1)S(1)} %get-tuple-element.22), channel_id=1, source_target_pairs={{1,0},{0,1},{3,2},{2,3},{5,4},{4,5},{7,6},{6,7},{9,8},{8,9},{11,10... | collective-permute-start | bytes 414728 | tf_op jit(solution)/shard_map/ppermute | solution.py:33
  11.6 14.4 %collective-permute-start.1 = (bf16[40,1728]{1,0:T(8,128)(2,1)S(1)}, bf16[40,1728]{1,0:T(8,128)(2,1)S(1)}, u32[]{:S(2)}, u32[]{:S(2)}) collective-permute-start(bf16[40,1728]{1,0:T(8,128)(2,1)S(1)} %get-tuple-element.23), channel_id=1, source_target_pairs={{2,0},{3,1},{0,2},{1,3},{6,4},{7,5},{4,6},{5,7},{10,8},{11,9},{8,1... | collective-permute-start | bytes 414728 | tf_op jit(solution)/shard_map/ppermute | solution.py:33
  14.1 11.9 %collective-permute-start.2 = (bf16[40,1728]{1,0:T(8,128)(2,1)S(1)}, bf16[40,1728]{1,0:T(8,128)(2,1)S(1)}, u32[]{:S(2)}, u32[]{:S(2)}) collective-permute-start(bf16[40,1728]{1,0:T(8,128)(2,1)S(1)} %get-tuple-element.24), channel_id=1, source_target_pairs={{3,0},{2,1},{1,2},{0,3},{7,4},{6,5},{5,6},{4,7},{11,8},{10,9},{9,1... | collective-permute-start | bytes 414728 | tf_op jit(solution)/shard_map/ppermute | solution.py:33
  15.0 6.0 %copy-start.1 = (bf16[1728,5120]{1,0:T(8,128)(2,1)S(1)}, bf16[1728,5120]{1,0:T(8,128)(2,1)}, u32[]{:S(2)}) copy-start(bf16[1728,5120]{1,0:T(8,128)(2,1)} %w_ref.1) | copy-start | bytes 53084164
  27.2 17.9 %all-to-all-start.1 = ((bf16[8,2,4,4,1280]{4,3,2,1,0:T(4,128)(2,1)}), bf16[8,2,4,4,1280]{4,3,2,1,0:T(4,128)(2,1)S(1)}, u32[]{:S(2)}, u32[]{:S(2)}) async-start(bf16[8,2,4,4,1280]{4,3,2,1,0:T(4,128)(2,1)} %broadcast_in_dim.7), calls=%async_computation.1 | async-start | bytes 1310720 | tf_op jit(solution)/shard_map/all_to_all | solution.py:37
  30.8 18.9 %collective-permute-start.5 = (bf16[32,1728]{1,0:T(8,128)(2,1)S(1)}, bf16[32,1728]{1,0:T(8,128)(2,1)S(1)}, u32[]{:S(2)}, u32[]{:S(2)}) collective-permute-start(bf16[32,1728]{1,0:T(8,128)(2,1)S(1)} %grad_pre.1.grad_pre_ref.refs_4_), channel_id=1, source_target_pairs={{3,0},{2,1},{1,2},{0,3},{7,4},{6,5},{5,6},{4,7},{11,8},{10,9},{9,1... | collective-permute-start | bytes 331784 | tf_op jit(solution)/shard_map/ppermute | solution.py:33
  34.4 15.2 %collective-permute-start.4 = (bf16[32,1728]{1,0:T(8,128)(2,1)S(1)}, bf16[32,1728]{1,0:T(8,128)(2,1)S(1)}, u32[]{:S(2)}, u32[]{:S(2)}) collective-permute-start(bf16[32,1728]{1,0:T(8,128)(2,1)S(1)} %grad_pre.1.grad_pre_ref.refs_4_), channel_id=1, source_target_pairs={{2,0},{3,1},{0,2},{1,3},{6,4},{7,5},{4,6},{5,7},{10,8},{11,9},{8,1... | collective-permute-start | bytes 331784 | tf_op jit(solution)/shard_map/ppermute | solution.py:33
  34.7 15.0 %collective-permute-start.3 = (bf16[32,1728]{1,0:T(8,128)(2,1)S(1)}, bf16[32,1728]{1,0:T(8,128)(2,1)S(1)}, u32[]{:S(2)}, u32[]{:S(2)}) collective-permute-start(bf16[32,1728]{1,0:T(8,128)(2,1)S(1)} %grad_pre.1.grad_pre_ref.refs_4_), channel_id=1, source_target_pairs={{1,0},{0,1},{3,2},{2,3},{5,4},{4,5},{7,6},{6,7},{9,8},{8,9},{11,10... | collective-permute-start | bytes 331784 | tf_op jit(solution)/shard_map/ppermute | solution.py:33
  35.2 6.0 %copy-start = (bf16[5120,1728]{0,1:T(8,128)(2,1)S(1)}, bf16[5120,1728]{0,1:T(8,128)(2,1)}, u32[]{:S(2)}) copy-start(bf16[5120,1728]{0,1:T(8,128)(2,1)} %param.8) | copy-start | bytes 53084164
  45.5 11.8 %all-to-all-start.2 = ((bf16[8,4,5120]{2,1,0:T(4,128)(2,1)}), bf16[8,4,5120]{2,1,0:T(4,128)(2,1)S(1)}, u32[]{:S(2)}, u32[]{:S(2)}) async-start(bf16[8,4,5120]{2,1,0:T(4,128)(2,1)} %grad_in_part.1), calls=%async_computation.2 | async-start | bytes 655360 | tf_op jit(solution)/shard_map/all_to_all | solution.py:37

commit v8 on v7

v8 whole, which is shorter than its diff:
```python
import functools
import math

import jax
import jax.numpy as jnp
from jax import lax
from jax.experimental import pallas as pl
from jax.experimental.pallas import tpu as pltpu
from jax.sharding import PartitionSpec as P

root_two_pi = math.sqrt(2.0 / math.pi)
cubic = 0.044715


def gelu_value(pre):
    inner = root_two_pi * (pre + cubic * pre * pre * pre)
    return 0.5 * pre * (1.0 + jnp.tanh(inner))


def gelu_slope(pre):
    tanh_val = jnp.tanh(root_two_pi * (pre + cubic * pre * pre * pre))
    return 0.5 * (1.0 + tanh_val) + 0.5 * pre * (1.0 - tanh_val * tanh_val) * root_two_pi * (
        1.0 + 3.0 * cubic * pre * pre
    )


def partner(i, k, n):
    if n & (n - 1) == 0:
        return i ^ k
    return (i + k) % n if isinstance(i, int) else lax.rem(i + k, n)


def fetch(x, axis, k):
    n = lax.axis_size(axis)
    return lax.ppermute(x, axis, [(partner(i, k, n), i) for i in range(n)])


def other_core(x):
    return lax.ppermute(x, "mp", [(i ^ 1, i) for i in range(lax.axis_size("mp"))])


def chip_pairs(k):
    n = lax.axis_size("mp")
    return [(i, partner(i // 2, k, n // 2) * 2 + i % 2) for i in range(n)]


def fetch_chip(x, k):
    return lax.ppermute(x, "mp", [(there, here) for here, there in chip_pairs(k)])


def give_chip(x, k):
    return lax.ppermute(x, "mp", chip_pairs(k))


def block_of(size, most, unit):
    return max([b for b in range(unit, most + 1, unit) if size % b == 0], default=size)


def call(body, shapes, args, name, scratch=(), limit=8, flops=10**6, bytes_accessed=10**5, out_space=pltpu.VMEM):
    return pl.pallas_call(
        body,
        in_specs=[pl.BlockSpec(memory_space=pltpu.VMEM)] * len(args),
        out_specs=[pl.BlockSpec(memory_space=out_space)] * len(shapes),
        out_shape=[jax.ShapeDtypeStruct(*shape) for shape in shapes],
        scratch_shapes=list(scratch),
        compiler_params=pltpu.CompilerParams(vmem_limit_bytes=limit << 20),
        cost_estimate=pl.CostEstimate(
            flops=flops, bytes_accessed=bytes_accessed, transcendentals=0
        ),
        name=name,
    )(*args)


def place_of(block, chips):
    m = lax.axis_index("mp")
    core, k = divmod(block, chips)
    return 2 * partner(lax.shift_right_logical(m, 1), k, chips) + ((m & 1) ^ core)


def pack_body(tokens_ref, grad_ref, pre_ref, *refs):
    *packed, own, pre_copy, grad_copy, slabs = refs
    places, rows, part = slabs.shape
    hidden = pre_ref.shape[1]
    grad_copy[...] = grad_ref[...]
    both = jnp.concatenate(
        [tokens_ref[...].astype(jnp.float32), grad_ref[...].astype(jnp.float32)], axis=0
    )
    for p in range(places):
        slabs[p] = both[:, p * part : (p + 1) * part]
    t = lax.axis_index("tokens")
    own[...] = slabs[t].astype(jnp.bfloat16)
    pre_copy[...] = pre_ref[...]
    pre = pre_ref[...].astype(jnp.float32)
    for k, ref in enumerate(packed, 1):
        taker = t ^ k if places & (places - 1) == 0 else lax.rem(t - k + places, places)
        wide = ref.shape[1]
        ref[...] = jnp.concatenate(
            [
                jnp.pad(pre, ((0, 0), (0, wide - hidden))),
                jnp.pad(slabs[taker], ((0, 0), (0, wide - part))),
            ],
            axis=0,
        ).astype(jnp.bfloat16)


def pack(tokens_in, grad_out, pre_act, n_tok):
    rows, width = tokens_in.shape
    group, hidden = pre_act.shape
    part = width // n_tok
    shapes = [(group + 2 * rows, max(hidden, part))] * (n_tok - 1)
    shapes += [(2 * rows, part), pre_act.shape, grad_out.shape]
    return call(
        pack_body,
        [(shape, jnp.bfloat16) for shape in shapes],
        [tokens_in, grad_out, pre_act],
        "pack",
        [pltpu.VMEM((n_tok, 2 * rows, part), jnp.float32)],
        flops=10**10,
        bytes_accessed=36 * 10**6,
    )


def join_body(*refs):
    *pieces, out = refs
    out[...] = jnp.concatenate([x[...].astype(jnp.float32) for x in pieces], axis=0).astype(
        jnp.bfloat16
    )


def join(pieces):
    shape = (sum(x.shape[0] for x in pieces), pieces[0].shape[1])
    return call(join_body, [(shape, jnp.bfloat16)], pieces, "join")[0]


def sort_body(own, *refs):
    *packed, out = refs
    rows, part = own.shape[0] // 2, own.shape[1]
    pieces = [own[...].astype(jnp.float32)]
    for ref in packed:
        group = ref.shape[0] - 2 * rows
        pieces.append(ref[...].astype(jnp.float32)[group:, :part])
    for a in range(2):
        out[a] = jnp.concatenate([x[a * rows : (a + 1) * rows] for x in pieces], axis=0).astype(
            jnp.bfloat16
        )


def sort(own, packed):
    shape = (2, own.shape[0] // 2 * (len(packed) + 1), own.shape[1])
    return call(sort_body, [(shape, jnp.bfloat16)], [own, *packed], "sort")[0]


def stack_body(*refs):
    *pieces, out = refs
    for k, x in enumerate(pieces):
        out[k] = x[...]


def stack(pieces):
    shape = (len(pieces),) + pieces[0].shape
    return call(stack_body, [(shape, jnp.bfloat16)], pieces, "stack")[0]


def grad_pre_body(block, own_ref, other_ref, pre_ref, w_ref, out_ref, rows, total):
    hidden, group = total.shape
    half = own_ref.shape[0]
    rows[:half, :] = own_ref[...]
    rows[half:, :] = other_ref[...]
    for low in range(0, hidden, block):
        here = slice(low, low + block)
        total[here, :] = lax.dot_general(
            w_ref[here, :], rows[...], (((1,), (1,)), ((), ())), preferred_element_type=jnp.float32
        )
    each = group // lax.axis_size("mp")
    chips = half // each
    row = lax.broadcasted_iota(jnp.int32, (group, 1), 0)
    from_row = row
    for b in range(group // each):
        inside = (row >= b * each) & (row < (b + 1) * each)
        from_row = jnp.where(inside, row + (place_of(b, chips) - b) * each, from_row)
    pick = from_row == lax.broadcasted_iota(jnp.int32, (group, group), 1)
    pre = jnp.dot(
        pick.astype(jnp.float32).astype(jnp.bfloat16), pre_ref[...], preferred_element_type=jnp.float32
    )
    out_ref[...] = (total[...].T * gelu_slope(pre)).astype(jnp.bfloat16)


def grad_pre_of(own, other, pre_act, w_out):
    group, hidden = pre_act.shape
    width = w_out.shape[1]
    return call(
        functools.partial(grad_pre_body, block_of(hidden, 432, 16)),
        [((group, hidden), jnp.bfloat16)],
        [own, other, pre_act, w_out],
        "grad_pre",
        [pltpu.VMEM((group, width), jnp.bfloat16), pltpu.VMEM((hidden, group), jnp.float32)],
        flops=2 * group * width * hidden,
        bytes_accessed=2 * hidden * width,
    )[0]


def grad_in_body(block, grad_pre_ref, w_ref, own_ref, other_ref):
    half, width = own_ref.shape
    for low in range(0, width, block):
        here = slice(low, low + block)
        term = jnp.dot(grad_pre_ref[...], w_ref[:, here], preferred_element_type=jnp.float32)
        own_ref[:, here] = term[:half]
        other_ref[:, here] = term[half:].astype(jnp.bfloat16)


def grad_in_part(grad_pre, w_in_t):
    group, hidden = grad_pre.shape
    width = w_in_t.shape[1]
    half = (group // 2, width)
    return call(
        functools.partial(grad_in_body, block_of(width, 1024, 128)),
        [(half, jnp.float32), (half, jnp.bfloat16)],
        [grad_pre, w_in_t],
        "grad_in_part",
        flops=2 * group * width * hidden,
        bytes_accessed=2 * hidden * width,
    )


def pair_body(own_ref, other_ref, first_ref, *rest):
    rows = first_ref.shape[0]
    total = own_ref[...] + other_ref[...].astype(jnp.float32)
    first_ref[...] = total[:rows]
    for k, ref in enumerate(rest, 1):
        ref[...] = total[k * rows : (k + 1) * rows].astype(jnp.bfloat16)


def pair(own, other, chips):
    shape = (own.shape[0] // chips, own.shape[1])
    shapes = [(shape, jnp.float32)] + [(shape, jnp.bfloat16)] * (chips - 1)
    return call(pair_body, shapes, [own, other], "pair")


def finish_body(first_ref, *refs):
    *rest, out = refs
    total = first_ref[...]
    for ref in rest:
        total = total + ref[...].astype(jnp.float32)
    out[...] = total.astype(jnp.bfloat16)


def finish(first, rest):
    return call(finish_body, [(first.shape, jnp.bfloat16)], [first, *rest], "finish")[0]


def turn(x_ref, to_ref, unit):
    hidden = x_ref.shape[1]
    for low in range(0, hidden, unit):
        size = min(unit, hidden - low)
        eye = lax.broadcasted_iota(jnp.int32, (size, size), 0) == lax.broadcasted_iota(
            jnp.int32, (size, size), 1
        )
        to_ref[low : low + size, :] = lax.dot_general(
            eye.astype(jnp.float32).astype(jnp.bfloat16),
            x_ref[:, low : low + size],
            (((1,), (1,)), ((), ())),
            preferred_element_type=jnp.float32,
        ).astype(jnp.bfloat16)


def grad_w_body(places, scale_back, block, *refs):
    pre_refs, grad_pre_refs = refs[:places], refs[places : 2 * places]
    own_ref, other_ref, in_ref, out_ref, flat, sorted_rows, turned, held_in, held_out, sems = refs[
        2 * places :
    ]
    group, hidden = grad_pre_refs[0].shape
    chips, _, each, part = own_ref.shape
    rows = each // places
    total = places * group
    copies = []

    def arrange(place):
        size = block_of(total, 128, each)
        for low in range(0, total, size):
            row = low + lax.broadcasted_iota(jnp.int32, (size, 1), 0)
            from_row = row
            for b in range(low // each, (low + size) // each):
                for k in range(places):
                    first = b * each + k * rows
                    inside = (row >= first) & (row < first + rows)
                    shift = k * group + place(b) * rows - first
                    from_row = jnp.where(inside, row + shift, from_row)
            pick = from_row == lax.broadcasted_iota(jnp.int32, (size, total), 1)
            sorted_rows[low : low + size, :] = jnp.dot(
                pick.astype(jnp.float32).astype(jnp.bfloat16),
                flat[...],
                preferred_element_type=jnp.float32,
            ).astype(jnp.bfloat16)
        turn(sorted_rows, turned, 256)

    def product(right, held, to_ref):
        for low in range(0, part, block):
            here = slice(low, low + block)
            cols = jnp.concatenate(
                [ref[k, right, :, here] for ref in (own_ref, other_ref) for k in range(chips)], axis=0
            )
            term = jnp.dot(turned[...], cols, preferred_element_type=jnp.float32)
            held[:, here] = (term * scale_back).astype(jnp.bfloat16)
            copies.append(
                pltpu.make_async_copy(held.at[:, here], to_ref.at[:, here], sems.at[len(copies)])
            )
            copies[-1].start()

    for k in range(places):
        pre = pre_refs[k][:group, :hidden].astype(jnp.float32)
        flat[k * group : (k + 1) * group, :] = gelu_value(pre).astype(jnp.bfloat16)
    arrange(lambda b: place_of(b, chips))
    product(1, held_out, out_ref)
    for k in range(places):
        flat[k * group : (k + 1) * group, :] = grad_pre_refs[k][...]
    arrange(lambda b: b)
    product(0, held_in, in_ref)
    for copy in copies:
        copy.wait()


def grad_w_of(pre, grad_pre, own, other, scale_back):
    places = len(pre)
    group, hidden = grad_pre[0].shape
    total, part = places * group, own.shape[3]
    block = block_of(part, 256, 128)
    return call(
        functools.partial(grad_w_body, places, scale_back, block),
        [((hidden, part), jnp.bfloat16)] * 2,
        [*pre, *grad_pre, own, other],
        "grad_w",
        [
            pltpu.VMEM((total, hidden), jnp.bfloat16),
            pltpu.VMEM((total, hidden), jnp.bfloat16),
            pltpu.VMEM((hidden, total), jnp.bfloat16),
            pltpu.VMEM((hidden, part), jnp.bfloat16),
            pltpu.VMEM((hidden, part), jnp.bfloat16),
            pltpu.SemaphoreType.DMA((2 * (part // block),)),
        ],
        limit=20,
        flops=80 * total * part * hidden,
        bytes_accessed=40 * hidden * part,
        out_space=pltpu.HBM,
    )


def shards(tokens_in, grad_out, pre_act, w_in, w_out):
    n_mp, n_tok = lax.axis_size("mp"), lax.axis_size("tokens")
    chips = n_mp // 2
    scale_back = 1.0 / math.sqrt(pre_act.shape[0] * n_tok)

    rows_grad = [fetch_chip(grad_out, k) for k in range(1, chips)]
    *packed, own_piece, pre_act, grad_out = pack(tokens_in, grad_out, pre_act, n_tok)
    own_rows = join([grad_out, *rows_grad])
    other_rows = other_core(own_rows)
    packed = [fetch(x, "tokens", k) for k, x in enumerate(packed, 1)]

    grad_pre = grad_pre_of(own_rows, other_rows, pre_act, w_out)
    grad_pre_all = [grad_pre] + [fetch(grad_pre, "tokens", k) for k in range(1, n_tok)]

    packed, own_piece, grad_pre = lax.optimization_barrier((packed, own_piece, grad_pre))
    cols = sort(own_piece, packed)
    cols_chips = [fetch_chip(cols, k) for k in range(1, chips)]

    own, other = grad_in_part(grad_pre, w_in.T)
    first, *rest = pair(own, other_core(other), chips)
    rest = [give_chip(x, k) for k, x in enumerate(rest, 1)]

    own_cols = stack([cols, *cols_chips])
    other_cols = other_core(own_cols)
    grad_w_in_t, grad_w_out = grad_w_of(
        [pre_act] + packed, grad_pre_all, own_cols, other_cols, scale_back
    )
    return (finish(first, rest), grad_w_in_t.T, grad_w_out)


def solution(mesh):
    placed = (
        P(("tokens", "mp"), None),
        P(("tokens", "mp"), None),
        P("tokens", "mp"),
        P(None, "mp"),
        P("mp", None),
    )
    return jax.shard_map(
        shards,
        mesh=mesh,
        in_specs=placed,
        out_specs=(P(("tokens", "mp"), None), P("tokens", "mp"), P("mp", "tokens")),
        check_vma=False,
    )
```

time: 58.7 us -> 59.5 us (1.014)
  waiting for transfers between devices: 3.63 us -> 20.3 us
  local copies, waits for them, and re-layouts: 17.6 us -> 2.96 us
  other arithmetic: 0.83 us -> 0.01 us
    ppermute x0 -> x12, waiting for transfers between devices: none -> 13.6 us  [the longest x3 6.96 us: give_chip(): return lax.ppermute(x, 'mp', chip_pairs(k))]
    all_to_all x3 -> x0, starting transfers between devices: 12.9 us -> none  [swap(): return lax.all_to_all(x, axis, 0, 0)]
    ppermute x0 -> x12, starting transfers between devices: none -> 11.7 us  [the longest x6 8.1 us: fetch_chip(): lax.ppermute(x, 'mp', [(there, here) for here, there in chip_pairs(k)])]
    unnamed x10 -> x18, local copies, waits for them, and re-layouts: 14.5 us -> 2.96 us
    ppermute x6, waiting for transfers between devices: 0.02 us -> 6.66 us  [fetch(): return lax.ppermute(x, axis, [(partner(i, k, n), i) for i in range(n)])]
    all_to_all x3 -> x0, waiting for transfers between devices: 3.62 us -> none  [swap(): return lax.all_to_all(x, axis, 0, 0)]
    broadcast_in_dim x2 -> x0, local copies, waits for them, and re-layouts: 2.6 us -> none  [the longest x1 1.59 us: shards(): rows_grad = jnp.broadcast_to(grad_out, (n_mp,) + grad_out.shape)]
    ppermute x6, starting transfers between devices: 8.9 us -> 9.78 us  [fetch(): return lax.ppermute(x, axis, [(partner(i, k, n), i) for i in range(n)])]
  transfers between devices with their start and end apart: 9 -> 18, of which waited for: 2 -> 9; matrix products, arithmetic and copies ran while one was open for 1% -> 0% of each run, Pallas kernels for 23% -> 15%
where the time goes in v8:
time: 59.5 us; the launch traced here: 59.3 us
  starting transfers between devices  21.4 us (36%)
  waiting for transfers between devices  20.3 us (34%)
  Pallas kernels  13.9 us (23%)
  local copies, waits for them, and re-layouts  2.96 us (5%)
  between operations  0.78 us (1%)
    pallas_call x9, Pallas kernels, call(): pl.pallas_call(body, in_specs=[pl.BlockSpec(memory_space=pltpu.VMEM)] * l...  13.9 us
    ppermute x6, starting transfers between devices, fetch(): return lax.ppermute(x, axis, [(partner(i, k, n), i) for i in range(n)])  9.78 us
    ppermute x6, starting transfers between devices, fetch_chip(): lax.ppermute(x, 'mp', [(there, here) for here, there in chip_pairs(k)])  8.1 us
    ppermute x3, waiting for transfers between devices, give_chip(): return lax.ppermute(x, 'mp', chip_pairs(k))  6.96 us
    ppermute x6, waiting for transfers between devices, fetch(): return lax.ppermute(x, axis, [(partner(i, k, n), i) for i in range(n)])  6.66 us
    ppermute x6, waiting for transfers between devices, fetch_chip(): lax.ppermute(x, 'mp', [(there, here) for here, there in chip_pairs(k)])  5.61 us
    unnamed x18, local copies, waits for them, and re-layouts  2.96 us
    ppermute x3, starting transfers between devices, give_chip(): return lax.ppermute(x, 'mp', chip_pairs(k))  2.91 us
  transfers between devices with their start and end apart: 18, of which 9 were waited for; matrix products, arithmetic and copies ran while one was open for 0% of the time, Pallas kernels for 15%

profile of v8, /device:TPU:0, one launch (start us, length us, event | category | flops | bytes accessed | tf_op | source)
XLA Modules:
  0.0 59.3 jit_solution(11030342324396103389)
XLA Ops:
  0.6 3.0 %collective-permute-start.3 = (bf16[4,5120]{1,0:T(4,128)(2,1)}, bf16[4,5120]{1,0:T(4,128)(2,1)S(1)}, u32[]{:S(2)}, u32[]{:S(2)}) collective-permute-start(bf16[4,5120]{1,0:T(4,128)(2,1)} %grad_ref.1), channel_id=1, source_target_pairs={{8,0},{12,4},{0,8},{4,12},{24,16},{28,20},{16,24},{20,28},{9,1},{1... | collective-permute-start | bytes 122888 | tf_op jit(solution)/shard_map/ppermute | solution.py:48
  3.6 1.5 %collective-permute-start.4 = (bf16[4,5120]{1,0:T(4,128)(2,1)}, bf16[4,5120]{1,0:T(4,128)(2,1)S(1)}, u32[]{:S(2)}, u32[]{:S(2)}) collective-permute-start(bf16[4,5120]{1,0:T(4,128)(2,1)} %grad_ref.1), channel_id=1, source_target_pairs={{16,0},{20,4},{24,8},{28,12},{0,16},{4,20},{8,24},{12,28},{17,1},{... | collective-permute-start | bytes 122888 | tf_op jit(solution)/shard_map/ppermute | solution.py:48
  5.2 1.4 %copy-done.1 = bf16[32,1728]{1,0:T(8,128)(2,1)S(1)} copy-done((bf16[32,1728]{1,0:T(8,128)(2,1)S(1)}, bf16[32,1728]{1,0:T(8,128)(2,1)}, u32[]{:S(2)}) %copy-start.1) | copy-done | bytes 110616
  6.6 0.8 %copy-done.2 = bf16[4,5120]{1,0:T(4,128)(2,1)S(1)} copy-done((bf16[4,5120]{1,0:T(4,128)(2,1)S(1)}, bf16[4,5120]{1,0:T(4,128)(2,1)}, u32[]{:S(2)}) %copy-start.2) | copy-done | bytes 40984
  7.3 0.8 %copy-done.3 = bf16[4,5120]{1,0:T(4,128)(2,1)S(1)} copy-done((bf16[4,5120]{1,0:T(4,128)(2,1)S(1)}, bf16[4,5120]{1,0:T(4,128)(2,1)}, u32[]{:S(2)}) %copy-start.3) | copy-done | bytes 40984
  8.2 2.1 %collective-permute-done.5.refs_3_ = bf16[4,5120]{1,0:T(4,128)(2,1)S(1)} collective-permute-done((bf16[4,5120]{1,0:T(4,128)(2,1)}, bf16[4,5120]{1,0:T(4,128)(2,1)S(1)}, u32[]{:S(2)}, u32[]{:S(2)}) %collective-permute-start.5) | collective-permute-done | bytes 40992 | tf_op jit(solution)/shard_map/ppermute | solution.py:48
  10.4 1.6 %collective-permute-start = (bf16[40,1728]{1,0:T(8,128)(2,1)S(1)}, bf16[40,1728]{1,0:T(8,128)(2,1)S(1)}, u32[]{:S(2)}, u32[]{:S(2)}) collective-permute-start(bf16[40,1728]{1,0:T(8,128)(2,1)S(1)} %get-tuple-element.22), channel_id=1, source_target_pairs={{1,0},{0,1},{3,2},{2,3},{5,4},{4,5},{7,6},{6,7},{9,8},{8,9},{11,10... | collective-permute-start | bytes 414728 | tf_op jit(solution)/shard_map/ppermute | solution.py:35
  12.0 2.6 %collective-permute-start.1 = (bf16[40,1728]{1,0:T(8,128)(2,1)S(1)}, bf16[40,1728]{1,0:T(8,128)(2,1)S(1)}, u32[]{:S(2)}, u32[]{:S(2)}) collective-permute-start(bf16[40,1728]{1,0:T(8,128)(2,1)S(1)} %get-tuple-element.23), channel_id=1, source_target_pairs={{2,0},{3,1},{0,2},{1,3},{6,4},{7,5},{4,6},{5,7},{10,8},{11,9},{8,1... | collective-permute-start | bytes 414728 | tf_op jit(solution)/shard_map/ppermute | solution.py:35
  14.9 4.9 %grad_pre.1.grad_pre_ref.refs_4_ = bf16[32,1728]{1,0:T(8,128)(2,1)S(1)} custom-call(bf16[16,5120]{1,0:T(8,128)(2,1)S(1)} %join.1.own_ref, bf16[16,5120]{1,0:T(8,128)(2,1)S(1)} %collective-permute-done.6.other_ref, bf16[32,1728]{1,0:T(8,128)(2,1)S(1)} %get-tuple-element.27.pre_ref.refs_0_, bf16[1728,5120]{1,0:T(8,128)(2,1)S(1)} %copy-done), custom_call_target="tpu_custom_call" | custom-call | flops 566231040 | bytes 17694720 | tf_op jit(solution)/shard_map/grad_pre/pallas_call | solution.py:60
  19.8 5.9 %collective-permute-done.1.refs_1_.refs_2_ = bf16[40,1728]{1,0:T(8,128)(2,1)S(1)} collective-permute-done((bf16[40,1728]{1,0:T(8,128)(2,1)S(1)}, bf16[40,1728]{1,0:T(8,128)(2,1)S(1)}, u32[]{:S(2)}, u32[]{:S(2)}) %collective-permute-start.1) | collective-permute-done | bytes 138272 | tf_op jit(solution)/shard_map/ppermute | solution.py:35
  26.4 1.2 %collective-permute-start.15 = (bf16[2,16,1280]{2,1,0:T(8,128)(2,1)S(1)}, bf16[2,16,1280]{2,1,0:T(8,128)(2,1)S(1)}, u32[]{:S(2)}, u32[]{:S(2)}) collective-permute-start(bf16[2,16,1280]{2,1,0:T(8,128)(2,1)S(1)} %sort.1.refs_0_), channel_id=1, source_target_pairs={{16,0},{20,4},{24,8},{28,12},{0,16},{4,20},{8,24},{12,28},{17,1},{... | collective-permute-start | bytes 245768 | tf_op jit(solution)/shard_map/ppermute | solution.py:48
  27.5 1.8 %collective-permute-start.16 = (bf16[2,16,1280]{2,1,0:T(8,128)(2,1)S(1)}, bf16[2,16,1280]{2,1,0:T(8,128)(2,1)S(1)}, u32[]{:S(2)}, u32[]{:S(2)}) collective-permute-start(bf16[2,16,1280]{2,1,0:T(8,128)(2,1)S(1)} %sort.1.refs_0_), channel_id=1, source_target_pairs={{24,0},{28,4},{16,8},{20,12},{8,16},{12,20},{0,24},{4,28},{25,1},{... | collective-permute-start | bytes 245768 | tf_op jit(solution)/shard_map/ppermute | solution.py:48
  29.3 1.0 %collective-permute-done.14.refs_1_ = bf16[2,16,1280]{2,1,0:T(8,128)(2,1)S(1)} collective-permute-done((bf16[2,16,1280]{2,1,0:T(8,128)(2,1)S(1)}, bf16[2,16,1280]{2,1,0:T(8,128)(2,1)S(1)}, u32[]{:S(2)}, u32[]{:S(2)}) %collective-permute-start.14) | collective-permute-done | bytes 81952 | tf_op jit(solution)/shard_map/ppermute | solution.py:48
  30.3 0.9 %collective-permute-done.15.refs_2_ = bf16[2,16,1280]{2,1,0:T(8,128)(2,1)S(1)} collective-permute-done((bf16[2,16,1280]{2,1,0:T(8,128)(2,1)S(1)}, bf16[2,16,1280]{2,1,0:T(8,128)(2,1)S(1)}, u32[]{:S(2)}, u32[]{:S(2)}) %collective-permute-start.15) | collective-permute-done | bytes 81952 | tf_op jit(solution)/shard_map/ppermute | solution.py:48
  31.2 1.6 %collective-permute-done.16.refs_3_ = bf16[2,16,1280]{2,1,0:T(8,128)(2,1)S(1)} collective-permute-done((bf16[2,16,1280]{2,1,0:T(8,128)(2,1)S(1)}, bf16[2,16,1280]{2,1,0:T(8,128)(2,1)S(1)}, u32[]{:S(2)}, u32[]{:S(2)}) %collective-permute-start.16) | collective-permute-done | bytes 81952 | tf_op jit(solution)/shard_map/ppermute | solution.py:48
  33.0 3.2 %grad_in_part.1 = (f32[16,5120]{1,0:T(8,128)S(1)}, bf16[16,5120]{1,0:T(8,128)(2,1)S(1)}) custom-call(bf16[32,1728]{1,0:T(8,128)(2,1)S(1)} %grad_pre.1.grad_pre_ref.refs_4_, bf16[1728,5120]{1,0:T(8,128)(2,1)S(1)} %bitcast.4), custom_call_target="tpu_custom_call" | custom-call | flops 566231040 | bytes 17694720 | tf_op jit(solution)/shard_map/grad_in_part/pallas_call | solution.py:60
  36.7 1.0 %collective-permute-done.7.other_ref = bf16[16,5120]{1,0:T(8,128)(2,1)S(1)} collective-permute-done((bf16[16,5120]{1,0:T(8,128)(2,1)S(1)}, bf16[16,5120]{1,0:T(8,128)(2,1)S(1)}, u32[]{:S(2)}, u32[]{:S(2)}) %collective-permute-start.7) | collective-permute-done | bytes 163872 | tf_op jit(solution)/shard_map/ppermute | solution.py:39
  37.8 1.9 %collective-permute-start.10 = (bf16[4,5120]{1,0:T(4,128)(2,1)S(1)}, bf16[4,5120]{1,0:T(4,128)(2,1)S(1)}, u32[]{:S(2)}, u32[]{:S(2)}) collective-permute-start(bf16[4,5120]{1,0:T(4,128)(2,1)S(1)} %get-tuple-element.34), channel_id=1, source_target_pairs={{0,24},{4,28},{8,16},{12,20},{16,8},{20,12},{24,0},{28,4},{1,25},{... | collective-permute-start | bytes 122888 | tf_op jit(solution)/shard_map/ppermute | solution.py:52
  39.6 2.9 %collective-permute-start.11 = (bf16[32,1728]{1,0:T(8,128)(2,1)S(1)}, bf16[32,1728]{1,0:T(8,128)(2,1)S(1)}, u32[]{:S(2)}, u32[]{:S(2)}) collective-permute-start(bf16[32,1728]{1,0:T(8,128)(2,1)S(1)} %grad_pre.1.grad_pre_ref.refs_4_), channel_id=1, source_target_pairs={{1,0},{0,1},{3,2},{2,3},{5,4},{4,5},{7,6},{6,7},{9,8},{8,9},{11,10... | collective-permute-start | bytes 331784 | tf_op jit(solution)/shard_map/ppermute | solution.py:35
  42.5 1.0 %collective-permute-start.12 = (bf16[32,1728]{1,0:T(8,128)(2,1)S(1)}, bf16[32,1728]{1,0:T(8,128)(2,1)S(1)}, u32[]{:S(2)}, u32[]{:S(2)}) collective-permute-start(bf16[32,1728]{1,0:T(8,128)(2,1)S(1)} %grad_pre.1.grad_pre_ref.refs_4_), channel_id=1, source_target_pairs={{2,0},{3,1},{0,2},{1,3},{6,4},{7,5},{4,6},{5,7},{10,8},{11,9},{8,1... | collective-permute-start | bytes 331784 | tf_op jit(solution)/shard_map/ppermute | solution.py:35
  43.5 1.5 %collective-permute-start.13 = (bf16[32,1728]{1,0:T(8,128)(2,1)S(1)}, bf16[32,1728]{1,0:T(8,128)(2,1)S(1)}, u32[]{:S(2)}, u32[]{:S(2)}) collective-permute-start(bf16[32,1728]{1,0:T(8,128)(2,1)S(1)} %grad_pre.1.grad_pre_ref.refs_4_), channel_id=1, source_target_pairs={{3,0},{2,1},{1,2},{0,3},{7,4},{6,5},{5,6},{4,7},{11,8},{10,9},{9,1... | collective-permute-start | bytes 331784 | tf_op jit(solution)/shard_map/ppermute | solution.py:35
  45.5 3.5 %collective-permute-done.8.refs_0_ = bf16[4,5120]{1,0:T(4,128)(2,1)S(1)} collective-permute-done((bf16[4,5120]{1,0:T(4,128)(2,1)S(1)}, bf16[4,5120]{1,0:T(4,128)(2,1)S(1)}, u32[]{:S(2)}, u32[]{:S(2)}) %collective-permute-start.8) | collective-permute-done | bytes 40992 | tf_op jit(solution)/shard_map/ppermute | solution.py:52
  49.5 3.5 %collective-permute-done.9.refs_1_ = bf16[4,5120]{1,0:T(4,128)(2,1)S(1)} collective-permute-done((bf16[4,5120]{1,0:T(4,128)(2,1)S(1)}, bf16[4,5120]{1,0:T(4,128)(2,1)S(1)}, u32[]{:S(2)}, u32[]{:S(2)}) %collective-permute-start.9) | collective-permute-done | bytes 40992 | tf_op jit(solution)/shard_map/ppermute | solution.py:52
  54.4 4.9 %grad_w.1 = (bf16[1728,1280]{1,0:T(8,128)(2,1)}, bf16[1728,1280]{1,0:T(8,128)(2,1)}) custom-call(bf16[32,1728]{1,0:T(8,128)(2,1)S(1)} %get-tuple-element.27.pre_ref.refs_0_, bf16[40,1728]{1,0:T(8,128)(2,1)S(1)} %collective-permute-done.refs_0_.refs_1_, bf16[40,1728]{1,0:T(8,128)(2,1)S(1)} %collective-permute-done.1.refs_1_.refs_2_, ...), custom_call_target="tpu_custom_call" | custom-call | flops 22649241600 | bytes 88473600 | tf_op jit(solution)/shard_map/grad_w/pallas_call | solution.py:60
  (40 shorter events, 4.1 us)
Async XLA Ops:
  0.6 14.2 %copy-start = (bf16[1728,5120]{1,0:T(8,128)(2,1)S(1)}, bf16[1728,5120]{1,0:T(8,128)(2,1)}, u32[]{:S(2)}) copy-start(bf16[1728,5120]{1,0:T(8,128)(2,1)} %w_ref.1) | copy-start | bytes 53084164
  0.6 7.6 %collective-permute-start.3 = (bf16[4,5120]{1,0:T(4,128)(2,1)}, bf16[4,5120]{1,0:T(4,128)(2,1)S(1)}, u32[]{:S(2)}, u32[]{:S(2)}) collective-permute-start(bf16[4,5120]{1,0:T(4,128)(2,1)} %grad_ref.1), channel_id=1, source_target_pairs={{8,0},{12,4},{0,8},{4,12},{24,16},{28,20},{16,24},{20,28},{9,1},{1... | collective-permute-start | bytes 122888 | tf_op jit(solution)/shard_map/ppermute | solution.py:48
  3.6 4.6 %collective-permute-start.4 = (bf16[4,5120]{1,0:T(4,128)(2,1)}, bf16[4,5120]{1,0:T(4,128)(2,1)S(1)}, u32[]{:S(2)}, u32[]{:S(2)}) collective-permute-start(bf16[4,5120]{1,0:T(4,128)(2,1)} %grad_ref.1), channel_id=1, source_target_pairs={{16,0},{20,4},{24,8},{28,12},{0,16},{4,20},{8,24},{12,28},{17,1},{... | collective-permute-start | bytes 122888 | tf_op jit(solution)/shard_map/ppermute | solution.py:48
  5.2 5.1 %collective-permute-start.5 = (bf16[4,5120]{1,0:T(4,128)(2,1)}, bf16[4,5120]{1,0:T(4,128)(2,1)S(1)}, u32[]{:S(2)}, u32[]{:S(2)}) collective-permute-start(bf16[4,5120]{1,0:T(4,128)(2,1)} %grad_ref.1), channel_id=1, source_target_pairs={{24,0},{28,4},{16,8},{20,12},{8,16},{12,20},{0,24},{4,28},{25,1},{... | collective-permute-start | bytes 122888 | tf_op jit(solution)/shard_map/ppermute | solution.py:48
  8.1 24.9 %slice-start = ((s8[17694720]{0:T(1024)(128)(4,1)}), s8[4194304]{0:T(1024)(128)(4,1)S(1)}, s32[]{:S(2)}) async-start(s8[17694720]{0:T(1024)(128)(4,1)} %bitcast.2), calls=%async_computation | async-start | bytes 8388608
  8.1 24.9 %slice-start.1 = ((s8[17694720]{0:T(1024)(128)(4,1)}), s8[4194304]{0:T(1024)(128)(4,1)S(1)}, s32[]{:S(2)}) async-start(s8[17694720]{0:T(1024)(128)(4,1)} %bitcast.2), calls=%async_computation.1 | async-start | bytes 8388608
  8.1 24.9 %slice-start.2 = ((s8[17694720]{0:T(1024)(128)(4,1)}), s8[4194304]{0:T(1024)(128)(4,1)S(1)}, s32[]{:S(2)}) async-start(s8[17694720]{0:T(1024)(128)(4,1)} %bitcast.2), calls=%async_computation.2 | async-start | bytes 8388608
  8.1 24.9 %slice-start.3 = ((s8[17694720]{0:T(1024)(128)(4,1)}), s8[4194304]{0:T(1024)(128)(4,1)S(1)}, s32[]{:S(2)}) async-start(s8[17694720]{0:T(1024)(128)(4,1)} %bitcast.2), calls=%async_computation.3 | async-start | bytes 8388608
  10.3 4.5 %collective-permute-start.6 = (bf16[16,5120]{1,0:T(8,128)(2,1)S(1)}, bf16[16,5120]{1,0:T(8,128)(2,1)S(1)}, u32[]{:S(2)}, u32[]{:S(2)}) collective-permute-start(bf16[16,5120]{1,0:T(8,128)(2,1)S(1)} %join.1.own_ref), channel_id=1, source_target_pairs={{4,0},{0,4},{12,8},{8,12},{20,16},{16,20},{28,24},{24,28},{5,1},{1... | collective-permute-start | bytes 491528 | tf_op jit(solution)/shard_map/ppermute | solution.py:39
  10.4 9.4 %collective-permute-start = (bf16[40,1728]{1,0:T(8,128)(2,1)S(1)}, bf16[40,1728]{1,0:T(8,128)(2,1)S(1)}, u32[]{:S(2)}, u32[]{:S(2)}) collective-permute-start(bf16[40,1728]{1,0:T(8,128)(2,1)S(1)} %get-tuple-element.22), channel_id=1, source_target_pairs={{1,0},{0,1},{3,2},{2,3},{5,4},{4,5},{7,6},{6,7},{9,8},{8,9},{11,10... | collective-permute-start | bytes 414728 | tf_op jit(solution)/shard_map/ppermute | solution.py:35
  12.0 13.7 %collective-permute-start.1 = (bf16[40,1728]{1,0:T(8,128)(2,1)S(1)}, bf16[40,1728]{1,0:T(8,128)(2,1)S(1)}, u32[]{:S(2)}, u32[]{:S(2)}) collective-permute-start(bf16[40,1728]{1,0:T(8,128)(2,1)S(1)} %get-tuple-element.23), channel_id=1, source_target_pairs={{2,0},{3,1},{0,2},{1,3},{6,4},{7,5},{4,6},{5,7},{10,8},{11,9},{8,1... | collective-permute-start | bytes 414728 | tf_op jit(solution)/shard_map/ppermute | solution.py:35
  14.6 11.1 %collective-permute-start.2 = (bf16[40,1728]{1,0:T(8,128)(2,1)S(1)}, bf16[40,1728]{1,0:T(8,128)(2,1)S(1)}, u32[]{:S(2)}, u32[]{:S(2)}) collective-permute-start(bf16[40,1728]{1,0:T(8,128)(2,1)S(1)} %get-tuple-element.24), channel_id=1, source_target_pairs={{3,0},{2,1},{1,2},{0,3},{7,4},{6,5},{5,6},{4,7},{11,8},{10,9},{9,1... | collective-permute-start | bytes 414728 | tf_op jit(solution)/shard_map/ppermute | solution.py:35
  14.9 18.2 %slice-start.4 = ((s8[17694720]{0:T(1024)(128)(4,1)}), s8[917504]{0:T(1024)(128)(4,1)S(1)}, s32[]{:S(2)}) async-start(s8[17694720]{0:T(1024)(128)(4,1)} %bitcast.2), calls=%async_computation.4 | async-start | bytes 1835008
  25.8 4.6 %collective-permute-start.14 = (bf16[2,16,1280]{2,1,0:T(8,128)(2,1)S(1)}, bf16[2,16,1280]{2,1,0:T(8,128)(2,1)S(1)}, u32[]{:S(2)}, u32[]{:S(2)}) collective-permute-start(bf16[2,16,1280]{2,1,0:T(8,128)(2,1)S(1)} %sort.1.refs_0_), channel_id=1, source_target_pairs={{8,0},{12,4},{0,8},{4,12},{24,16},{28,20},{16,24},{20,28},{9,1},{1... | collective-permute-start | bytes 245768 | tf_op jit(solution)/shard_map/ppermute | solution.py:48
  26.4 4.9 %collective-permute-start.15 = (bf16[2,16,1280]{2,1,0:T(8,128)(2,1)S(1)}, bf16[2,16,1280]{2,1,0:T(8,128)(2,1)S(1)}, u32[]{:S(2)}, u32[]{:S(2)}) collective-permute-start(bf16[2,16,1280]{2,1,0:T(8,128)(2,1)S(1)} %sort.1.refs_0_), channel_id=1, source_target_pairs={{16,0},{20,4},{24,8},{28,12},{0,16},{4,20},{8,24},{12,28},{17,1},{... | collective-permute-start | bytes 245768 | tf_op jit(solution)/shard_map/ppermute | solution.py:48
  27.5 5.3 %collective-permute-start.16 = (bf16[2,16,1280]{2,1,0:T(8,128)(2,1)S(1)}, bf16[2,16,1280]{2,1,0:T(8,128)(2,1)S(1)}, u32[]{:S(2)}, u32[]{:S(2)}) collective-permute-start(bf16[2,16,1280]{2,1,0:T(8,128)(2,1)S(1)} %sort.1.refs_0_), channel_id=1, source_target_pairs={{24,0},{28,4},{16,8},{20,12},{8,16},{12,20},{0,24},{4,28},{25,1},{... | collective-permute-start | bytes 245768 | tf_op jit(solution)/shard_map/ppermute | solution.py:48
  32.9 21.5 %collective-permute-start.17 = (bf16[4,2,16,1280]{3,2,1,0:T(8,128)(2,1)S(1)}, bf16[4,2,16,1280]{3,2,1,0:T(8,128)(2,1)S(1)}, u32[]{:S(2)}, u32[]{:S(2)}) collective-permute-start(bf16[4,2,16,1280]{3,2,1,0:T(8,128)(2,1)S(1)} %stack.1.refs_8_), channel_id=1, source_target_pairs={{4,0},{0,4},{12,8},{8,12},{20,16},{16,20},{28,24},{24,28},{5,1},{1... | collective-permute-start | bytes 983048 | tf_op jit(solution)/shard_map/ppermute | solution.py:39
  36.2 1.5 %collective-permute-start.7 = (bf16[16,5120]{1,0:T(8,128)(2,1)S(1)}, bf16[16,5120]{1,0:T(8,128)(2,1)S(1)}, u32[]{:S(2)}, u32[]{:S(2)}) collective-permute-start(bf16[16,5120]{1,0:T(8,128)(2,1)S(1)} %get-tuple-element.30), channel_id=1, source_target_pairs={{4,0},{0,4},{12,8},{8,12},{20,16},{16,20},{28,24},{24,28},{5,1},{1... | collective-permute-start | bytes 491528 | tf_op jit(solution)/shard_map/ppermute | solution.py:39
  37.8 7.2 %collective-permute-start.10 = (bf16[4,5120]{1,0:T(4,128)(2,1)S(1)}, bf16[4,5120]{1,0:T(4,128)(2,1)S(1)}, u32[]{:S(2)}, u32[]{:S(2)}) collective-permute-start(bf16[4,5120]{1,0:T(4,128)(2,1)S(1)} %get-tuple-element.34), channel_id=1, source_target_pairs={{0,24},{4,28},{8,16},{12,20},{16,8},{20,12},{24,0},{28,4},{1,25},{... | collective-permute-start | bytes 122888 | tf_op jit(solution)/shard_map/ppermute | solution.py:52
  39.6 14.0 %collective-permute-start.11 = (bf16[32,1728]{1,0:T(8,128)(2,1)S(1)}, bf16[32,1728]{1,0:T(8,128)(2,1)S(1)}, u32[]{:S(2)}, u32[]{:S(2)}) collective-permute-start(bf16[32,1728]{1,0:T(8,128)(2,1)S(1)} %grad_pre.1.grad_pre_ref.refs_4_), channel_id=1, source_target_pairs={{1,0},{0,1},{3,2},{2,3},{5,4},{4,5},{7,6},{6,7},{9,8},{8,9},{11,10... | collective-permute-start | bytes 331784 | tf_op jit(solution)/shard_map/ppermute | solution.py:35
  42.5 11.9 %collective-permute-start.12 = (bf16[32,1728]{1,0:T(8,128)(2,1)S(1)}, bf16[32,1728]{1,0:T(8,128)(2,1)S(1)}, u32[]{:S(2)}, u32[]{:S(2)}) collective-permute-start(bf16[32,1728]{1,0:T(8,128)(2,1)S(1)} %grad_pre.1.grad_pre_ref.refs_4_), channel_id=1, source_target_pairs={{2,0},{3,1},{0,2},{1,3},{6,4},{7,5},{4,6},{5,7},{10,8},{11,9},{8,1... | collective-permute-start | bytes 331784 | tf_op jit(solution)/shard_map/ppermute | solution.py:35
  43.5 10.8 %collective-permute-start.13 = (bf16[32,1728]{1,0:T(8,128)(2,1)S(1)}, bf16[32,1728]{1,0:T(8,128)(2,1)S(1)}, u32[]{:S(2)}, u32[]{:S(2)}) collective-permute-start(bf16[32,1728]{1,0:T(8,128)(2,1)S(1)} %grad_pre.1.grad_pre_ref.refs_4_), channel_id=1, source_target_pairs={{3,0},{2,1},{1,2},{0,3},{7,4},{6,5},{5,6},{4,7},{11,8},{10,9},{9,1... | collective-permute-start | bytes 331784 | tf_op jit(solution)/shard_map/ppermute | solution.py:35
  45.0 4.0 %collective-permute-start.8 = (bf16[4,5120]{1,0:T(4,128)(2,1)S(1)}, bf16[4,5120]{1,0:T(4,128)(2,1)S(1)}, u32[]{:S(2)}, u32[]{:S(2)}) collective-permute-start(bf16[4,5120]{1,0:T(4,128)(2,1)S(1)} %get-tuple-element.32), channel_id=1, source_target_pairs={{0,8},{4,12},{8,0},{12,4},{16,24},{20,28},{24,16},{28,20},{1,9},{5... | collective-permute-start | bytes 122888 | tf_op jit(solution)/shard_map/ppermute | solution.py:52
  49.0 4.0 %collective-permute-start.9 = (bf16[4,5120]{1,0:T(4,128)(2,1)S(1)}, bf16[4,5120]{1,0:T(4,128)(2,1)S(1)}, u32[]{:S(2)}, u32[]{:S(2)}) collective-permute-start(bf16[4,5120]{1,0:T(4,128)(2,1)S(1)} %get-tuple-element.33), channel_id=1, source_target_pairs={{0,16},{4,20},{8,24},{12,28},{16,0},{20,4},{24,8},{28,12},{1,17},{... | collective-permute-start | bytes 122888 | tf_op jit(solution)/shard_map/ppermute | solution.py:52
  (3 other events, 2.9 us)

commit v9 on v8

--- a/solution.py
+++ b/solution.py
@@ -56,10 +56,11 @@
     return max([b for b in range(unit, most + 1, unit) if size % b == 0], default=size)
 
 
-def call(body, shapes, args, name, scratch=(), limit=8, flops=10**6, bytes_accessed=10**5, out_space=pltpu.VMEM):
+def call(body, shapes, args, name, scratch=(), limit=8, flops=10**6, bytes_accessed=10**5,
+         in_space=pltpu.VMEM, out_space=pltpu.VMEM):
     return pl.pallas_call(
         body,
-        in_specs=[pl.BlockSpec(memory_space=pltpu.VMEM)] * len(args),
+        in_specs=[pl.BlockSpec(memory_space=in_space)] * len(args),
         out_specs=[pl.BlockSpec(memory_space=out_space)] * len(shapes),
         out_shape=[jax.ShapeDtypeStruct(*shape) for shape in shapes],
         scratch_shapes=list(scratch),
@@ -77,11 +78,30 @@
     return 2 * partner(lax.shift_right_logical(m, 1), k, chips) + ((m & 1) ^ core)
 
 
-def pack_body(tokens_ref, grad_ref, pre_ref, *refs):
-    *packed, own, pre_copy, grad_copy, slabs = refs
+def lead_body(out):
+    out[...] = jnp.zeros_like(out)
+
+
+def lead():
+    return call(
+        lead_body, [((8, 128), jnp.float32)], [], "lead", flops=10**10, bytes_accessed=36 * 10**6
+    )[0]
+
+
+def pack_body(tokens_in, grad_in, pre_in, after, *refs):
+    *packed, own, pre_ref, grad_ref, slabs, tokens_ref, sems = refs
+    copies = [
+        pltpu.make_async_copy(source, target, sems.at[i])
+        for i, (source, target) in enumerate(
+            ((tokens_in, tokens_ref), (grad_in, grad_ref), (pre_in, pre_ref))
+        )
+    ]
+    for copy in copies:
+        copy.start()
+    for copy in copies:
+        copy.wait()
     places, rows, part = slabs.shape
     hidden = pre_ref.shape[1]
-    grad_copy[...] = grad_ref[...]
     both = jnp.concatenate(
         [tokens_ref[...].astype(jnp.float32), grad_ref[...].astype(jnp.float32)], axis=0
     )
@@ -89,7 +109,6 @@
         slabs[p] = both[:, p * part : (p + 1) * part]
     t = lax.axis_index("tokens")
     own[...] = slabs[t].astype(jnp.bfloat16)
-    pre_copy[...] = pre_ref[...]
     pre = pre_ref[...].astype(jnp.float32)
     for k, ref in enumerate(packed, 1):
         taker = t ^ k if places & (places - 1) == 0 else lax.rem(t - k + places, places)
@@ -103,7 +122,7 @@
         ).astype(jnp.bfloat16)
 
 
-def pack(tokens_in, grad_out, pre_act, n_tok):
+def pack(tokens_in, grad_out, pre_act, n_tok, after):
     rows, width = tokens_in.shape
     group, hidden = pre_act.shape
     part = width // n_tok
@@ -112,24 +131,29 @@
     return call(
         pack_body,
         [(shape, jnp.bfloat16) for shape in shapes],
-        [tokens_in, grad_out, pre_act],
+        [tokens_in, grad_out, pre_act, after],
         "pack",
-        [pltpu.VMEM((n_tok, 2 * rows, part), jnp.float32)],
+        [
+            pltpu.VMEM((n_tok, 2 * rows, part), jnp.float32),
+            pltpu.VMEM(tokens_in.shape, jnp.bfloat16),
+            pltpu.SemaphoreType.DMA((3,)),
+        ],
         flops=10**10,
         bytes_accessed=36 * 10**6,
-    )
-
-
-def join_body(*refs):
+        in_space=pltpu.HBM,
+    )
+
+
+def join_body(after, *refs):
     *pieces, out = refs
     out[...] = jnp.concatenate([x[...].astype(jnp.float32) for x in pieces], axis=0).astype(
         jnp.bfloat16
     )
 
 
-def join(pieces):
+def join(pieces, after):
     shape = (sum(x.shape[0] for x in pieces), pieces[0].shape[1])
-    return call(join_body, [(shape, jnp.bfloat16)], pieces, "join")[0]
+    return call(join_body, [(shape, jnp.bfloat16)], [after, *pieces], "join")[0]
 
 
 def sort_body(own, *refs):
@@ -194,58 +218,42 @@
         [own, other, pre_act, w_out],
         "grad_pre",
         [pltpu.VMEM((group, width), jnp.bfloat16), pltpu.VMEM((hidden, group), jnp.float32)],
+    )[0]
+
+
+def grad_in_body(block, grad_pre_ref, w_ref, after, out_ref):
+    places, rows, width = out_ref.shape
+    for low in range(0, width, block):
+        here = slice(low, low + block)
+        term = jnp.dot(grad_pre_ref[...], w_ref[:, here], preferred_element_type=jnp.float32)
+        for b in range(places):
+            out_ref[place_of(b, places // 2), :, here] = term[b * rows : (b + 1) * rows].astype(
+                jnp.bfloat16
+            )
+
+
+def grad_in_part(grad_pre, w_in_t, places, after):
+    group, hidden = grad_pre.shape
+    width = w_in_t.shape[1]
+    return call(
+        functools.partial(grad_in_body, block_of(width, 1024, 128)),
+        [((places, group // places, width), jnp.bfloat16)],
+        [grad_pre, w_in_t, after],
+        "grad_in_part",
         flops=2 * group * width * hidden,
         bytes_accessed=2 * hidden * width,
     )[0]
 
 
-def grad_in_body(block, grad_pre_ref, w_ref, own_ref, other_ref):
-    half, width = own_ref.shape
-    for low in range(0, width, block):
-        here = slice(low, low + block)
-        term = jnp.dot(grad_pre_ref[...], w_ref[:, here], preferred_element_type=jnp.float32)
-        own_ref[:, here] = term[:half]
-        other_ref[:, here] = term[half:].astype(jnp.bfloat16)
-
-
-def grad_in_part(grad_pre, w_in_t):
-    group, hidden = grad_pre.shape
-    width = w_in_t.shape[1]
-    half = (group // 2, width)
-    return call(
-        functools.partial(grad_in_body, block_of(width, 1024, 128)),
-        [(half, jnp.float32), (half, jnp.bfloat16)],
-        [grad_pre, w_in_t],
-        "grad_in_part",
-        flops=2 * group * width * hidden,
-        bytes_accessed=2 * hidden * width,
-    )
-
-
-def pair_body(own_ref, other_ref, first_ref, *rest):
-    rows = first_ref.shape[0]
-    total = own_ref[...] + other_ref[...].astype(jnp.float32)
-    first_ref[...] = total[:rows]
-    for k, ref in enumerate(rest, 1):
-        ref[...] = total[k * rows : (k + 1) * rows].astype(jnp.bfloat16)
-
-
-def pair(own, other, chips):
-    shape = (own.shape[0] // chips, own.shape[1])
-    shapes = [(shape, jnp.float32)] + [(shape, jnp.bfloat16)] * (chips - 1)
-    return call(pair_body, shapes, [own, other], "pair")
-
-
-def finish_body(first_ref, *refs):
-    *rest, out = refs
-    total = first_ref[...]
-    for ref in rest:
-        total = total + ref[...].astype(jnp.float32)
+def finish_body(terms_ref, out):
+    total = terms_ref[0].astype(jnp.float32)
+    for k in range(1, terms_ref.shape[0]):
+        total = total + terms_ref[k].astype(jnp.float32)
     out[...] = total.astype(jnp.bfloat16)
 
 
-def finish(first, rest):
-    return call(finish_body, [(first.shape, jnp.bfloat16)], [first, *rest], "finish")[0]
+def finish(terms):
+    return call(finish_body, [(terms.shape[1:], jnp.bfloat16)], [terms], "finish")[0]
 
 
 def turn(x_ref, to_ref, unit):
@@ -350,10 +358,10 @@
     scale_back = 1.0 / math.sqrt(pre_act.shape[0] * n_tok)
 
     rows_grad = [fetch_chip(grad_out, k) for k in range(1, chips)]
-    *packed, own_piece, pre_act, grad_out = pack(tokens_in, grad_out, pre_act, n_tok)
-    own_rows = join([grad_out, *rows_grad])
+    *packed, own_piece, pre_act, grad_out = pack(tokens_in, grad_out, pre_act, n_tok, lead())
+    packed = [fetch(x, "tokens", k) for k, x in enumerate(packed, 1)]
+    own_rows = join([grad_out, *rows_grad], packed[0])
     other_rows = other_core(own_rows)
-    packed = [fetch(x, "tokens", k) for k, x in enumerate(packed, 1)]
 
     grad_pre = grad_pre_of(own_rows, other_rows, pre_act, w_out)
     grad_pre_all = [grad_pre] + [fetch(grad_pre, "tokens", k) for k in range(1, n_tok)]
@@ -362,16 +370,14 @@
     cols = sort(own_piece, packed)
     cols_chips = [fetch_chip(cols, k) for k in range(1, chips)]
 
-    own, other = grad_in_part(grad_pre, w_in.T)
-    first, *rest = pair(own, other_core(other), chips)
-    rest = [give_chip(x, k) for k, x in enumerate(rest, 1)]
+    terms = lax.all_to_all(grad_in_part(grad_pre, w_in.T, n_mp, grad_pre_all[1]), "mp", 0, 0)
 
     own_cols = stack([cols, *cols_chips])
     other_cols = other_core(own_cols)
     grad_w_in_t, grad_w_out = grad_w_of(
         [pre_act] + packed, grad_pre_all, own_cols, other_cols, scale_back
     )
-    return (finish(first, rest), grad_w_in_t.T, grad_w_out)
+    return (finish(terms), grad_w_in_t.T, grad_w_out)
 
 
 def solution(mesh):

time: 59.5 us -> 59.4 us (level)
  local copies, waits for them, and re-layouts: 2.96 us -> 0.93 us
  starting transfers between devices: 21.4 us -> 23.4 us
  waiting for transfers between devices: 20.3 us -> 19.1 us
  Pallas kernels: 13.9 us -> 14.9 us
    ppermute x3 -> x0, waiting for transfers between devices: 6.96 us -> none  [give_chip(): return lax.ppermute(x, 'mp', chip_pairs(k))]
    all_to_all x0 -> x1, starting transfers between devices: none -> 3.59 us  [shards(): lax.all_to_all(grad_in_part(grad_pre, w_in.T, n_mp, grad_pre_all[1]), 'mp...]
    ppermute x6, waiting for transfers between devices: 6.66 us -> 9.85 us  [fetch(): return lax.ppermute(x, axis, [(partner(i, k, n), i) for i in range(n)])]
    ppermute x3 -> x0, starting transfers between devices: 2.91 us -> none  [give_chip(): return lax.ppermute(x, 'mp', chip_pairs(k))]
    ppermute x6, starting transfers between devices: 9.78 us -> 12.6 us  [fetch(): return lax.ppermute(x, axis, [(partner(i, k, n), i) for i in range(n)])]
    unnamed x18 -> x26, local copies, waits for them, and re-layouts: 2.96 us -> 0.93 us
    ppermute x6, waiting for transfers between devices: 5.61 us -> 7.53 us  [fetch_chip(): lax.ppermute(x, 'mp', [(there, here) for here, there in chip_pairs(k)])]
    all_to_all x0 -> x1, waiting for transfers between devices: none -> 1.7 us  [shards(): lax.all_to_all(grad_in_part(grad_pre, w_in.T, n_mp, grad_pre_all[1]), 'mp...]
  transfers between devices with their start and end apart: 18 -> 15, of which waited for: 9 -> 8; matrix products, arithmetic and copies ran while one was open for 0% -> 0% of each run, Pallas kernels for 15% -> 16%
where the time goes in v9:
time: 59.4 us; the launch traced here: 59.2 us
  starting transfers between devices  23.4 us (39%)
  waiting for transfers between devices  19.1 us (32%)
  Pallas kernels  14.9 us (25%)
  local copies, waits for them, and re-layouts  0.93 us (2%)
  between operations  0.87 us (1%)
    pallas_call x9, Pallas kernels, call(): pl.pallas_call(body, in_specs=[pl.BlockSpec(memory_space=in_space)] * len...  14.9 us
    ppermute x6, starting transfers between devices, fetch(): return lax.ppermute(x, axis, [(partner(i, k, n), i) for i in range(n)])  12.6 us
    ppermute x6, waiting for transfers between devices, fetch(): return lax.ppermute(x, axis, [(partner(i, k, n), i) for i in range(n)])  9.85 us
    ppermute x6, waiting for transfers between devices, fetch_chip(): lax.ppermute(x, 'mp', [(there, here) for here, there in chip_pairs(k)])  7.53 us
    ppermute x6, starting transfers between devices, fetch_chip(): lax.ppermute(x, 'mp', [(there, here) for here, there in chip_pairs(k)])  7.04 us
    all_to_all x1, starting transfers between devices, shards(): lax.all_to_all(grad_in_part(grad_pre, w_in.T, n_mp, grad_pre_all[1]), 'mp...  3.59 us
    all_to_all x1, waiting for transfers between devices, shards(): lax.all_to_all(grad_in_part(grad_pre, w_in.T, n_mp, grad_pre_all[1]), 'mp...  1.7 us
  transfers between devices with their start and end apart: 15, of which 8 were waited for; matrix products, arithmetic and copies ran while one was open for 0% of the time, Pallas kernels for 16%

profile of v9, /device:TPU:0, one launch (start us, length us, event | category | flops | bytes accessed | tf_op | source)
XLA Modules:
  0.0 59.2 jit_solution(2298065249337628466)
XLA Ops:
  0.7 0.7 %copy-done.1 = bf16[4,5120]{1,0:T(4,128)(2,1)S(1)} copy-done((bf16[4,5120]{1,0:T(4,128)(2,1)S(1)}, bf16[4,5120]{1,0:T(4,128)(2,1)}, u32[]{:S(2)}) %copy-start.1) | copy-done | bytes 40984
  2.0 3.1 %collective-permute-start = (bf16[40,1728]{1,0:T(8,128)(2,1)S(1)}, bf16[40,1728]{1,0:T(8,128)(2,1)S(1)}, u32[]{:S(2)}, u32[]{:S(2)}) collective-permute-start(bf16[40,1728]{1,0:T(8,128)(2,1)S(1)} %get-tuple-element.16), channel_id=1, source_target_pairs={{1,0},{0,1},{3,2},{2,3},{5,4},{4,5},{7,6},{6,7},{9,8},{8,9},{11,10... | collective-permute-start | bytes 414728 | tf_op jit(solution)/shard_map/ppermute | solution.py:35
  5.0 1.5 %collective-permute-start.3 = (bf16[4,5120]{1,0:T(4,128)(2,1)S(1)}, bf16[4,5120]{1,0:T(4,128)(2,1)S(1)}, u32[]{:S(2)}, u32[]{:S(2)}) collective-permute-start(bf16[4,5120]{1,0:T(4,128)(2,1)S(1)} %copy-done.2), channel_id=1, source_target_pairs={{8,0},{12,4},{0,8},{4,12},{24,16},{28,20},{16,24},{20,28},{9,1},{1... | collective-permute-start | bytes 122888 | tf_op jit(solution)/shard_map/ppermute | solution.py:48
  6.5 1.5 %collective-permute-start.4 = (bf16[4,5120]{1,0:T(4,128)(2,1)S(1)}, bf16[4,5120]{1,0:T(4,128)(2,1)S(1)}, u32[]{:S(2)}, u32[]{:S(2)}) collective-permute-start(bf16[4,5120]{1,0:T(4,128)(2,1)S(1)} %copy-done.2), channel_id=1, source_target_pairs={{16,0},{20,4},{24,8},{28,12},{0,16},{4,20},{8,24},{12,28},{17,1},{... | collective-permute-start | bytes 122888 | tf_op jit(solution)/shard_map/ppermute | solution.py:48
  8.1 0.5 collective-permute-start.5
  8.5 0.5 collective-permute-done.3.refs_1_
  9.0 1.5 %collective-permute-done.4.refs_2_ = bf16[4,5120]{1,0:T(4,128)(2,1)S(1)} collective-permute-done((bf16[4,5120]{1,0:T(4,128)(2,1)S(1)}, bf16[4,5120]{1,0:T(4,128)(2,1)S(1)}, u32[]{:S(2)}, u32[]{:S(2)}) %collective-permute-start.4) | collective-permute-done | bytes 40992 | tf_op jit(solution)/shard_map/ppermute | solution.py:48
  10.5 2.4 %collective-permute-done.5.refs_3_ = bf16[4,5120]{1,0:T(4,128)(2,1)S(1)} collective-permute-done((bf16[4,5120]{1,0:T(4,128)(2,1)S(1)}, bf16[4,5120]{1,0:T(4,128)(2,1)S(1)}, u32[]{:S(2)}, u32[]{:S(2)}) %collective-permute-start.5) | collective-permute-done | bytes 40992 | tf_op jit(solution)/shard_map/ppermute | solution.py:48
  13.1 2.7 %collective-permute-start.1 = (bf16[40,1728]{1,0:T(8,128)(2,1)S(1)}, bf16[40,1728]{1,0:T(8,128)(2,1)S(1)}, u32[]{:S(2)}, u32[]{:S(2)}) collective-permute-start(bf16[40,1728]{1,0:T(8,128)(2,1)S(1)} %get-tuple-element.17), channel_id=1, source_target_pairs={{2,0},{3,1},{0,2},{1,3},{6,4},{7,5},{4,6},{5,7},{10,8},{11,9},{8,1... | collective-permute-start | bytes 414728 | tf_op jit(solution)/shard_map/ppermute | solution.py:35
  16.0 4.9 %grad_pre.1.grad_pre_ref.refs_4_ = bf16[32,1728]{1,0:T(8,128)(2,1)S(1)} custom-call(bf16[16,5120]{1,0:T(8,128)(2,1)S(1)} %join.1.own_ref, bf16[16,5120]{1,0:T(8,128)(2,1)S(1)} %collective-permute-done.6.other_ref, bf16[32,1728]{1,0:T(8,128)(2,1)S(1)} %get-tuple-element.21.pre_ref.refs_0_, bf16[1728,5120]{1,0:T(8,128)(2,1)S(1)} %bitcast.3), custom_call_target="tpu_custom_call" | custom-call | flops 1000000 | bytes 100000 | tf_op jit(solution)/shard_map/grad_pre/pallas_call | solution.py:61
  21.0 0.7 %collective-permute-start.7 = (bf16[32,1728]{1,0:T(8,128)(2,1)S(1)}, bf16[32,1728]{1,0:T(8,128)(2,1)S(1)}, u32[]{:S(2)}, u32[]{:S(2)}) collective-permute-start(bf16[32,1728]{1,0:T(8,128)(2,1)S(1)} %grad_pre.1.grad_pre_ref.refs_4_), channel_id=1, source_target_pairs={{1,0},{0,1},{3,2},{2,3},{5,4},{4,5},{7,6},{6,7},{9,8},{8,9},{11,10... | collective-permute-start | bytes 331784 | tf_op jit(solution)/shard_map/ppermute | solution.py:35
  21.7 4.6 %collective-permute-done.1.refs_1_.refs_2_ = bf16[40,1728]{1,0:T(8,128)(2,1)S(1)} collective-permute-done((bf16[40,1728]{1,0:T(8,128)(2,1)S(1)}, bf16[40,1728]{1,0:T(8,128)(2,1)S(1)}, u32[]{:S(2)}, u32[]{:S(2)}) %collective-permute-start.1) | collective-permute-done | bytes 138272 | tf_op jit(solution)/shard_map/ppermute | solution.py:35
  26.3 0.6 %collective-permute-start.10 = (bf16[2,16,1280]{2,1,0:T(8,128)(2,1)S(1)}, bf16[2,16,1280]{2,1,0:T(8,128)(2,1)S(1)}, u32[]{:S(2)}, u32[]{:S(2)}) collective-permute-start(bf16[2,16,1280]{2,1,0:T(8,128)(2,1)S(1)} %sort.1.refs_0_), channel_id=1, source_target_pairs={{8,0},{12,4},{0,8},{4,12},{24,16},{28,20},{16,24},{20,28},{9,1},{1... | collective-permute-start | bytes 245768 | tf_op jit(solution)/shard_map/ppermute | solution.py:48
  27.4 2.5 %collective-permute-start.12 = (bf16[2,16,1280]{2,1,0:T(8,128)(2,1)S(1)}, bf16[2,16,1280]{2,1,0:T(8,128)(2,1)S(1)}, u32[]{:S(2)}, u32[]{:S(2)}) collective-permute-start(bf16[2,16,1280]{2,1,0:T(8,128)(2,1)S(1)} %sort.1.refs_0_), channel_id=1, source_target_pairs={{24,0},{28,4},{16,8},{20,12},{8,16},{12,20},{0,24},{4,28},{25,1},{... | collective-permute-start | bytes 245768 | tf_op jit(solution)/shard_map/ppermute | solution.py:48
  29.9 1.4 %collective-permute-done.10.refs_1_ = bf16[2,16,1280]{2,1,0:T(8,128)(2,1)S(1)} collective-permute-done((bf16[2,16,1280]{2,1,0:T(8,128)(2,1)S(1)}, bf16[2,16,1280]{2,1,0:T(8,128)(2,1)S(1)}, u32[]{:S(2)}, u32[]{:S(2)}) %collective-permute-start.10) | collective-permute-done | bytes 81952 | tf_op jit(solution)/shard_map/ppermute | solution.py:48
  31.3 1.7 %collective-permute-done.11.refs_2_ = bf16[2,16,1280]{2,1,0:T(8,128)(2,1)S(1)} collective-permute-done((bf16[2,16,1280]{2,1,0:T(8,128)(2,1)S(1)}, bf16[2,16,1280]{2,1,0:T(8,128)(2,1)S(1)}, u32[]{:S(2)}, u32[]{:S(2)}) %collective-permute-start.11) | collective-permute-done | bytes 81952 | tf_op jit(solution)/shard_map/ppermute | solution.py:48
  33.2 3.9 %grad_in_part.1 = bf16[8,4,5120]{2,1,0:T(4,128)(2,1)} custom-call(bf16[32,1728]{1,0:T(8,128)(2,1)S(1)} %grad_pre.1.grad_pre_ref.refs_4_, bf16[1728,5120]{1,0:T(8,128)(2,1)S(1)} %bitcast.6, bf16[32,1728]{1,0:T(8,128)(2,1)S(1)} %collective-permute-done.7.after.refs_5_), custom_call_target="tpu_custom_call" | custom-call | flops 566231040 | bytes 17694720 | tf_op jit(solution)/shard_map/grad_in_part/pallas_call | solution.py:61
  37.1 3.6 %all-to-all-start = ((bf16[8,4,5120]{2,1,0:T(4,128)(2,1)}), bf16[8,4,5120]{2,1,0:T(4,128)(2,1)S(1)}, u32[]{:S(2)}, u32[]{:S(2)}) async-start(bf16[8,4,5120]{2,1,0:T(4,128)(2,1)} %grad_in_part.1), calls=%async_computation | async-start | bytes 655360 | tf_op jit(solution)/shard_map/all_to_all | solution.py:373
  40.7 4.7 %collective-permute-start.8 = (bf16[32,1728]{1,0:T(8,128)(2,1)S(1)}, bf16[32,1728]{1,0:T(8,128)(2,1)S(1)}, u32[]{:S(2)}, u32[]{:S(2)}) collective-permute-start(bf16[32,1728]{1,0:T(8,128)(2,1)S(1)} %grad_pre.1.grad_pre_ref.refs_4_), channel_id=1, source_target_pairs={{2,0},{3,1},{0,2},{1,3},{6,4},{7,5},{4,6},{5,7},{10,8},{11,9},{8,1... | collective-permute-start | bytes 331784 | tf_op jit(solution)/shard_map/ppermute | solution.py:35
  45.3 1.3 %collective-permute-start.9 = (bf16[32,1728]{1,0:T(8,128)(2,1)S(1)}, bf16[32,1728]{1,0:T(8,128)(2,1)S(1)}, u32[]{:S(2)}, u32[]{:S(2)}) collective-permute-start(bf16[32,1728]{1,0:T(8,128)(2,1)S(1)} %grad_pre.1.grad_pre_ref.refs_4_), channel_id=1, source_target_pairs={{3,0},{2,1},{1,2},{0,3},{7,4},{6,5},{5,6},{4,7},{11,8},{10,9},{9,1... | collective-permute-start | bytes 331784 | tf_op jit(solution)/shard_map/ppermute | solution.py:35
  46.6 1.7 %all-to-all-done.terms_ref = bf16[8,4,5120]{2,1,0:T(4,128)(2,1)S(1)} async-done(((bf16[8,4,5120]{2,1,0:T(4,128)(2,1)}), bf16[8,4,5120]{2,1,0:T(4,128)(2,1)S(1)}, u32[]{:S(2)}, u32[]{:S(2)}) %all-to-all-start) | async-done | bytes 327712 | tf_op jit(solution)/shard_map/all_to_all | solution.py:373
  48.3 0.7 %finish.1 = bf16[4,5120]{1,0:T(4,128)(2,1)} custom-call(bf16[8,4,5120]{2,1,0:T(4,128)(2,1)S(1)} %all-to-all-done.terms_ref), custom_call_target="tpu_custom_call" | custom-call | flops 1000000 | bytes 100000 | tf_op jit(solution)/shard_map/finish/pallas_call | solution.py:61
  49.0 5.3 %collective-permute-done.8.refs_6_ = bf16[32,1728]{1,0:T(8,128)(2,1)S(1)} collective-permute-done((bf16[32,1728]{1,0:T(8,128)(2,1)S(1)}, bf16[32,1728]{1,0:T(8,128)(2,1)S(1)}, u32[]{:S(2)}, u32[]{:S(2)}) %collective-permute-start.8) | collective-permute-done | bytes 110624 | tf_op jit(solution)/shard_map/ppermute | solution.py:35
  54.2 4.9 %grad_w.1 = (bf16[1728,1280]{1,0:T(8,128)(2,1)}, bf16[1728,1280]{1,0:T(8,128)(2,1)}) custom-call(bf16[32,1728]{1,0:T(8,128)(2,1)S(1)} %get-tuple-element.21.pre_ref.refs_0_, bf16[40,1728]{1,0:T(8,128)(2,1)S(1)} %collective-permute-done.after.refs_0_.refs_1_, bf16[40,1728]{1,0:T(8,128)(2,1)S(1)} %collective-permute-done.1.refs_1_.refs_2_, ...), custom_call_target="tpu_custom_call" | custom-call | flops 22649241600 | bytes 88473600 | tf_op jit(solution)/shard_map/grad_w/pallas_call | solution.py:61
  (43 shorter events, 1.5 us)
Async XLA Ops:
  0.7 15.3 %slice-start = ((s8[17694720]{0:T(1024)(128)(4,1)}), s8[4194304]{0:T(1024)(128)(4,1)S(1)}, s32[]{:S(2)}) async-start(s8[17694720]{0:T(1024)(128)(4,1)} %bitcast.2), calls=%async_computation.1 | async-start | bytes 8388608
  0.7 15.3 %slice-start.1 = ((s8[17694720]{0:T(1024)(128)(4,1)}), s8[4194304]{0:T(1024)(128)(4,1)S(1)}, s32[]{:S(2)}) async-start(s8[17694720]{0:T(1024)(128)(4,1)} %bitcast.2), calls=%async_computation.2 | async-start | bytes 8388608
  0.7 15.3 %slice-start.2 = ((s8[17694720]{0:T(1024)(128)(4,1)}), s8[4194304]{0:T(1024)(128)(4,1)S(1)}, s32[]{:S(2)}) async-start(s8[17694720]{0:T(1024)(128)(4,1)} %bitcast.2), calls=%async_computation.3 | async-start | bytes 8388608
  1.6 14.4 %slice-start.4 = ((s8[17694720]{0:T(1024)(128)(4,1)}), s8[917504]{0:T(1024)(128)(4,1)S(1)}, s32[]{:S(2)}) async-start(s8[17694720]{0:T(1024)(128)(4,1)} %bitcast.2), calls=%async_computation.5 | async-start | bytes 1835008
  1.6 31.5 %slice-start.5 = ((s8[17694720]{0:T(1024)(128)(4,1)}), s8[4194304]{0:T(1024)(128)(4,1)S(1)}, s32[]{:S(2)}) async-start(s8[17694720]{0:T(1024)(128)(4,1)} %bitcast.4), calls=%async_computation.6 | async-start | bytes 8388608
  1.6 31.5 %slice-start.6 = ((s8[17694720]{0:T(1024)(128)(4,1)}), s8[4194304]{0:T(1024)(128)(4,1)S(1)}, s32[]{:S(2)}) async-start(s8[17694720]{0:T(1024)(128)(4,1)} %bitcast.4), calls=%async_computation.7 | async-start | bytes 8388608
  1.6 31.5 %slice-start.7 = ((s8[17694720]{0:T(1024)(128)(4,1)}), s8[4194304]{0:T(1024)(128)(4,1)S(1)}, s32[]{:S(2)}) async-start(s8[17694720]{0:T(1024)(128)(4,1)} %bitcast.4), calls=%async_computation.8 | async-start | bytes 8388608
  1.6 31.5 %slice-start.8 = ((s8[17694720]{0:T(1024)(128)(4,1)}), s8[4194304]{0:T(1024)(128)(4,1)S(1)}, s32[]{:S(2)}) async-start(s8[17694720]{0:T(1024)(128)(4,1)} %bitcast.4), calls=%async_computation.9 | async-start | bytes 8388608
  2.0 11.0 %collective-permute-start = (bf16[40,1728]{1,0:T(8,128)(2,1)S(1)}, bf16[40,1728]{1,0:T(8,128)(2,1)S(1)}, u32[]{:S(2)}, u32[]{:S(2)}) collective-permute-start(bf16[40,1728]{1,0:T(8,128)(2,1)S(1)} %get-tuple-element.16), channel_id=1, source_target_pairs={{1,0},{0,1},{3,2},{2,3},{5,4},{4,5},{7,6},{6,7},{9,8},{8,9},{11,10... | collective-permute-start | bytes 414728 | tf_op jit(solution)/shard_map/ppermute | solution.py:35
  5.0 4.0 %collective-permute-start.3 = (bf16[4,5120]{1,0:T(4,128)(2,1)S(1)}, bf16[4,5120]{1,0:T(4,128)(2,1)S(1)}, u32[]{:S(2)}, u32[]{:S(2)}) collective-permute-start(bf16[4,5120]{1,0:T(4,128)(2,1)S(1)} %copy-done.2), channel_id=1, source_target_pairs={{8,0},{12,4},{0,8},{4,12},{24,16},{28,20},{16,24},{20,28},{9,1},{1... | collective-permute-start | bytes 122888 | tf_op jit(solution)/shard_map/ppermute | solution.py:48
  6.5 4.0 %collective-permute-start.4 = (bf16[4,5120]{1,0:T(4,128)(2,1)S(1)}, bf16[4,5120]{1,0:T(4,128)(2,1)S(1)}, u32[]{:S(2)}, u32[]{:S(2)}) collective-permute-start(bf16[4,5120]{1,0:T(4,128)(2,1)S(1)} %copy-done.2), channel_id=1, source_target_pairs={{16,0},{20,4},{24,8},{28,12},{0,16},{4,20},{8,24},{12,28},{17,1},{... | collective-permute-start | bytes 122888 | tf_op jit(solution)/shard_map/ppermute | solution.py:48
  8.1 4.9 %collective-permute-start.5 = (bf16[4,5120]{1,0:T(4,128)(2,1)S(1)}, bf16[4,5120]{1,0:T(4,128)(2,1)S(1)}, u32[]{:S(2)}, u32[]{:S(2)}) collective-permute-start(bf16[4,5120]{1,0:T(4,128)(2,1)S(1)} %copy-done.2), channel_id=1, source_target_pairs={{24,0},{28,4},{16,8},{20,12},{8,16},{12,20},{0,24},{4,28},{25,1},{... | collective-permute-start | bytes 122888 | tf_op jit(solution)/shard_map/ppermute | solution.py:48
  13.0 3.0 %collective-permute-start.6 = (bf16[16,5120]{1,0:T(8,128)(2,1)S(1)}, bf16[16,5120]{1,0:T(8,128)(2,1)S(1)}, u32[]{:S(2)}, u32[]{:S(2)}) collective-permute-start(bf16[16,5120]{1,0:T(8,128)(2,1)S(1)} %join.1.own_ref), channel_id=1, source_target_pairs={{4,0},{0,4},{12,8},{8,12},{20,16},{16,20},{28,24},{24,28},{5,1},{1... | collective-permute-start | bytes 491528 | tf_op jit(solution)/shard_map/ppermute | solution.py:39
  13.1 13.2 %collective-permute-start.1 = (bf16[40,1728]{1,0:T(8,128)(2,1)S(1)}, bf16[40,1728]{1,0:T(8,128)(2,1)S(1)}, u32[]{:S(2)}, u32[]{:S(2)}) collective-permute-start(bf16[40,1728]{1,0:T(8,128)(2,1)S(1)} %get-tuple-element.17), channel_id=1, source_target_pairs={{2,0},{3,1},{0,2},{1,3},{6,4},{7,5},{4,6},{5,7},{10,8},{11,9},{8,1... | collective-permute-start | bytes 414728 | tf_op jit(solution)/shard_map/ppermute | solution.py:35
  15.7 10.6 %collective-permute-start.2 = (bf16[40,1728]{1,0:T(8,128)(2,1)S(1)}, bf16[40,1728]{1,0:T(8,128)(2,1)S(1)}, u32[]{:S(2)}, u32[]{:S(2)}) collective-permute-start(bf16[40,1728]{1,0:T(8,128)(2,1)S(1)} %get-tuple-element.18), channel_id=1, source_target_pairs={{3,0},{2,1},{1,2},{0,3},{7,4},{6,5},{5,6},{4,7},{11,8},{10,9},{9,1... | collective-permute-start | bytes 414728 | tf_op jit(solution)/shard_map/ppermute | solution.py:35
  16.0 17.1 %slice-start.9 = ((s8[17694720]{0:T(1024)(128)(4,1)}), s8[917504]{0:T(1024)(128)(4,1)S(1)}, s32[]{:S(2)}) async-start(s8[17694720]{0:T(1024)(128)(4,1)} %bitcast.4), calls=%async_computation.10 | async-start | bytes 1835008
  21.0 12.1 %collective-permute-start.7 = (bf16[32,1728]{1,0:T(8,128)(2,1)S(1)}, bf16[32,1728]{1,0:T(8,128)(2,1)S(1)}, u32[]{:S(2)}, u32[]{:S(2)}) collective-permute-start(bf16[32,1728]{1,0:T(8,128)(2,1)S(1)} %grad_pre.1.grad_pre_ref.refs_4_), channel_id=1, source_target_pairs={{1,0},{0,1},{3,2},{2,3},{5,4},{4,5},{7,6},{6,7},{9,8},{8,9},{11,10... | collective-permute-start | bytes 331784 | tf_op jit(solution)/shard_map/ppermute | solution.py:35
  26.3 5.0 %collective-permute-start.10 = (bf16[2,16,1280]{2,1,0:T(8,128)(2,1)S(1)}, bf16[2,16,1280]{2,1,0:T(8,128)(2,1)S(1)}, u32[]{:S(2)}, u32[]{:S(2)}) collective-permute-start(bf16[2,16,1280]{2,1,0:T(8,128)(2,1)S(1)} %sort.1.refs_0_), channel_id=1, source_target_pairs={{8,0},{12,4},{0,8},{4,12},{24,16},{28,20},{16,24},{20,28},{9,1},{1... | collective-permute-start | bytes 245768 | tf_op jit(solution)/shard_map/ppermute | solution.py:48
  26.9 6.1 %collective-permute-start.11 = (bf16[2,16,1280]{2,1,0:T(8,128)(2,1)S(1)}, bf16[2,16,1280]{2,1,0:T(8,128)(2,1)S(1)}, u32[]{:S(2)}, u32[]{:S(2)}) collective-permute-start(bf16[2,16,1280]{2,1,0:T(8,128)(2,1)S(1)} %sort.1.refs_0_), channel_id=1, source_target_pairs={{16,0},{20,4},{24,8},{28,12},{0,16},{4,20},{8,24},{12,28},{17,1},{... | collective-permute-start | bytes 245768 | tf_op jit(solution)/shard_map/ppermute | solution.py:48
  27.4 5.6 %collective-permute-start.12 = (bf16[2,16,1280]{2,1,0:T(8,128)(2,1)S(1)}, bf16[2,16,1280]{2,1,0:T(8,128)(2,1)S(1)}, u32[]{:S(2)}, u32[]{:S(2)}) collective-permute-start(bf16[2,16,1280]{2,1,0:T(8,128)(2,1)S(1)} %sort.1.refs_0_), channel_id=1, source_target_pairs={{24,0},{28,4},{16,8},{20,12},{8,16},{12,20},{0,24},{4,28},{25,1},{... | collective-permute-start | bytes 245768 | tf_op jit(solution)/shard_map/ppermute | solution.py:48
  33.0 21.2 %collective-permute-start.13 = (bf16[4,2,16,1280]{3,2,1,0:T(8,128)(2,1)S(1)}, bf16[4,2,16,1280]{3,2,1,0:T(8,128)(2,1)S(1)}, u32[]{:S(2)}, u32[]{:S(2)}) collective-permute-start(bf16[4,2,16,1280]{3,2,1,0:T(8,128)(2,1)S(1)} %stack.1.refs_8_), channel_id=1, source_target_pairs={{4,0},{0,4},{12,8},{8,12},{20,16},{16,20},{28,24},{24,28},{5,1},{1... | collective-permute-start | bytes 983048 | tf_op jit(solution)/shard_map/ppermute | solution.py:39
  37.1 11.2 %all-to-all-start = ((bf16[8,4,5120]{2,1,0:T(4,128)(2,1)}), bf16[8,4,5120]{2,1,0:T(4,128)(2,1)S(1)}, u32[]{:S(2)}, u32[]{:S(2)}) async-start(bf16[8,4,5120]{2,1,0:T(4,128)(2,1)} %grad_in_part.1), calls=%async_computation | async-start | bytes 655360 | tf_op jit(solution)/shard_map/all_to_all | solution.py:373
  40.7 13.6 %collective-permute-start.8 = (bf16[32,1728]{1,0:T(8,128)(2,1)S(1)}, bf16[32,1728]{1,0:T(8,128)(2,1)S(1)}, u32[]{:S(2)}, u32[]{:S(2)}) collective-permute-start(bf16[32,1728]{1,0:T(8,128)(2,1)S(1)} %grad_pre.1.grad_pre_ref.refs_4_), channel_id=1, source_target_pairs={{2,0},{3,1},{0,2},{1,3},{6,4},{7,5},{4,6},{5,7},{10,8},{11,9},{8,1... | collective-permute-start | bytes 331784 | tf_op jit(solution)/shard_map/ppermute | solution.py:35
  45.3 8.9 %collective-permute-start.9 = (bf16[32,1728]{1,0:T(8,128)(2,1)S(1)}, bf16[32,1728]{1,0:T(8,128)(2,1)S(1)}, u32[]{:S(2)}, u32[]{:S(2)}) collective-permute-start(bf16[32,1728]{1,0:T(8,128)(2,1)S(1)} %grad_pre.1.grad_pre_ref.refs_4_), channel_id=1, source_target_pairs={{3,0},{2,1},{1,2},{0,3},{7,4},{6,5},{5,6},{4,7},{11,8},{10,9},{9,1... | collective-permute-start | bytes 331784 | tf_op jit(solution)/shard_map/ppermute | solution.py:35
  (4 other events, 16.9 us)

commit v10 on v9

--- a/solution.py
+++ b/solution.py
@@ -57,11 +57,13 @@
 
 
 def call(body, shapes, args, name, scratch=(), limit=8, flops=10**6, bytes_accessed=10**5,
-         in_space=pltpu.VMEM, out_space=pltpu.VMEM):
+         in_space=pltpu.VMEM, out_spaces=None):
     return pl.pallas_call(
         body,
         in_specs=[pl.BlockSpec(memory_space=in_space)] * len(args),
-        out_specs=[pl.BlockSpec(memory_space=out_space)] * len(shapes),
+        out_specs=[
+            pl.BlockSpec(memory_space=space) for space in out_spaces or [pltpu.VMEM] * len(shapes)
+        ],
         out_shape=[jax.ShapeDtypeStruct(*shape) for shape in shapes],
         scratch_shapes=list(scratch),
         compiler_params=pltpu.CompilerParams(vmem_limit_bytes=limit << 20),
@@ -89,7 +91,7 @@
 
 
 def pack_body(tokens_in, grad_in, pre_in, after, *refs):
-    *packed, own, pre_ref, grad_ref, slabs, tokens_ref, sems = refs
+    *pieces, own, pre_ref, grad_ref, slabs, tokens_ref, sems = refs
     copies = [
         pltpu.make_async_copy(source, target, sems.at[i])
         for i, (source, target) in enumerate(
@@ -101,7 +103,6 @@
     for copy in copies:
         copy.wait()
     places, rows, part = slabs.shape
-    hidden = pre_ref.shape[1]
     both = jnp.concatenate(
         [tokens_ref[...].astype(jnp.float32), grad_ref[...].astype(jnp.float32)], axis=0
     )
@@ -109,25 +110,15 @@
         slabs[p] = both[:, p * part : (p + 1) * part]
     t = lax.axis_index("tokens")
     own[...] = slabs[t].astype(jnp.bfloat16)
-    pre = pre_ref[...].astype(jnp.float32)
-    for k, ref in enumerate(packed, 1):
+    for k, ref in enumerate(pieces, 1):
         taker = t ^ k if places & (places - 1) == 0 else lax.rem(t - k + places, places)
-        wide = ref.shape[1]
-        ref[...] = jnp.concatenate(
-            [
-                jnp.pad(pre, ((0, 0), (0, wide - hidden))),
-                jnp.pad(slabs[taker], ((0, 0), (0, wide - part))),
-            ],
-            axis=0,
-        ).astype(jnp.bfloat16)
+        ref[...] = slabs[taker].astype(jnp.bfloat16)
 
 
 def pack(tokens_in, grad_out, pre_act, n_tok, after):
     rows, width = tokens_in.shape
-    group, hidden = pre_act.shape
     part = width // n_tok
-    shapes = [(group + 2 * rows, max(hidden, part))] * (n_tok - 1)
-    shapes += [(2 * rows, part), pre_act.shape, grad_out.shape]
+    shapes = [(2 * rows, part)] * n_tok + [pre_act.shape, grad_out.shape]
     return call(
         pack_body,
         [(shape, jnp.bfloat16) for shape in shapes],
@@ -156,22 +147,20 @@
     return call(join_body, [(shape, jnp.bfloat16)], [after, *pieces], "join")[0]
 
 
-def sort_body(own, *refs):
-    *packed, out = refs
-    rows, part = own.shape[0] // 2, own.shape[1]
-    pieces = [own[...].astype(jnp.float32)]
-    for ref in packed:
-        group = ref.shape[0] - 2 * rows
-        pieces.append(ref[...].astype(jnp.float32)[group:, :part])
+def sort_body(*refs):
+    *pieces, out = refs
+    rows = pieces[0].shape[0] // 2
+    pieces = [x[...].astype(jnp.float32) for x in pieces]
     for a in range(2):
         out[a] = jnp.concatenate([x[a * rows : (a + 1) * rows] for x in pieces], axis=0).astype(
             jnp.bfloat16
         )
 
 
-def sort(own, packed):
-    shape = (2, own.shape[0] // 2 * (len(packed) + 1), own.shape[1])
-    return call(sort_body, [(shape, jnp.bfloat16)], [own, *packed], "sort")[0]
+def sort(pieces):
+    rows, part = pieces[0].shape
+    shape = (2, rows // 2 * len(pieces), part)
+    return call(sort_body, [(shape, jnp.bfloat16)], pieces, "sort")[0]
 
 
 def stack_body(*refs):
@@ -185,7 +174,7 @@
     return call(stack_body, [(shape, jnp.bfloat16)], pieces, "stack")[0]
 
 
-def grad_pre_body(block, own_ref, other_ref, pre_ref, w_ref, out_ref, rows, total):
+def grad_pre_body(block, own_ref, other_ref, pre_ref, w_ref, after, out_ref, rows, total):
     hidden, group = total.shape
     half = own_ref.shape[0]
     rows[:half, :] = own_ref[...]
@@ -209,19 +198,22 @@
     out_ref[...] = (total[...].T * gelu_slope(pre)).astype(jnp.bfloat16)
 
 
-def grad_pre_of(own, other, pre_act, w_out):
+def grad_pre_of(own, other, pre_act, w_out, after):
     group, hidden = pre_act.shape
     width = w_out.shape[1]
     return call(
         functools.partial(grad_pre_body, block_of(hidden, 432, 16)),
         [((group, hidden), jnp.bfloat16)],
-        [own, other, pre_act, w_out],
+        [own, other, pre_act, w_out, after],
         "grad_pre",
         [pltpu.VMEM((group, width), jnp.bfloat16), pltpu.VMEM((hidden, group), jnp.float32)],
+        flops=2 * group * width * hidden,
+        bytes_accessed=2 * hidden * width,
     )[0]
 
 
-def grad_in_body(block, grad_pre_ref, w_ref, after, out_ref):
+def grad_in_body(block, grad_pre_ref, w_ref, *refs):
+    out_ref = refs[-1]
     places, rows, width = out_ref.shape
     for low in range(0, width, block):
         here = slice(low, low + block)
@@ -238,22 +230,22 @@
     return call(
         functools.partial(grad_in_body, block_of(width, 1024, 128)),
         [((places, group // places, width), jnp.bfloat16)],
-        [grad_pre, w_in_t, after],
+        [grad_pre, w_in_t, *after],
         "grad_in_part",
         flops=2 * group * width * hidden,
         bytes_accessed=2 * hidden * width,
     )[0]
 
 
-def finish_body(terms_ref, out):
+def finish_body(terms_ref, after, out):
     total = terms_ref[0].astype(jnp.float32)
     for k in range(1, terms_ref.shape[0]):
         total = total + terms_ref[k].astype(jnp.float32)
     out[...] = total.astype(jnp.bfloat16)
 
 
-def finish(terms):
-    return call(finish_body, [(terms.shape[1:], jnp.bfloat16)], [terms], "finish")[0]
+def finish(terms, after):
+    return call(finish_body, [(terms.shape[1:], jnp.bfloat16)], [terms, after], "finish")[0]
 
 
 def turn(x_ref, to_ref, unit):
@@ -273,9 +265,9 @@
 
 def grad_w_body(places, scale_back, block, *refs):
     pre_refs, grad_pre_refs = refs[:places], refs[places : 2 * places]
-    own_ref, other_ref, in_ref, out_ref, flat, sorted_rows, turned, held_in, held_out, sems = refs[
-        2 * places :
-    ]
+    own_ref, other_ref, in_ref, out_ref, end_ref = refs[2 * places : 2 * places + 5]
+    flat, sorted_rows, turned, held_in, held_out, sems = refs[2 * places + 5 :]
+    end_ref[...] = jnp.zeros_like(end_ref)
     group, hidden = grad_pre_refs[0].shape
     chips, _, each, part = own_ref.shape
     rows = each // places
@@ -315,7 +307,7 @@
             copies[-1].start()
 
     for k in range(places):
-        pre = pre_refs[k][:group, :hidden].astype(jnp.float32)
+        pre = pre_refs[k][...].astype(jnp.float32)
         flat[k * group : (k + 1) * group, :] = gelu_value(pre).astype(jnp.bfloat16)
     arrange(lambda b: place_of(b, chips))
     product(1, held_out, out_ref)
@@ -334,7 +326,7 @@
     block = block_of(part, 256, 128)
     return call(
         functools.partial(grad_w_body, places, scale_back, block),
-        [((hidden, part), jnp.bfloat16)] * 2,
+        [((hidden, part), jnp.bfloat16)] * 2 + [((8, 128), jnp.float32)],
         [*pre, *grad_pre, own, other],
         "grad_w",
         [
@@ -348,7 +340,7 @@
         limit=20,
         flops=80 * total * part * hidden,
         bytes_accessed=40 * hidden * part,
-        out_space=pltpu.HBM,
+        out_spaces=[pltpu.HBM, pltpu.HBM, pltpu.VMEM],
     )
 
 
@@ -357,27 +349,24 @@
     chips = n_mp // 2
     scale_back = 1.0 / math.sqrt(pre_act.shape[0] * n_tok)
 
+    *pieces, own_piece, pre_act, own_grad = pack(tokens_in, grad_out, pre_act, n_tok, lead())
     rows_grad = [fetch_chip(grad_out, k) for k in range(1, chips)]
-    *packed, own_piece, pre_act, grad_out = pack(tokens_in, grad_out, pre_act, n_tok, lead())
-    packed = [fetch(x, "tokens", k) for k, x in enumerate(packed, 1)]
-    own_rows = join([grad_out, *rows_grad], packed[0])
+    cols = sort([own_piece] + [fetch(x, "tokens", k) for k, x in enumerate(pieces, 1)])
+    cols_chips = [fetch_chip(cols, k) for k in range(1, chips)]
+
+    own_rows = join([own_grad, *rows_grad], cols)
     other_rows = other_core(own_rows)
-
-    grad_pre = grad_pre_of(own_rows, other_rows, pre_act, w_out)
-    grad_pre_all = [grad_pre] + [fetch(grad_pre, "tokens", k) for k in range(1, n_tok)]
-
-    packed, own_piece, grad_pre = lax.optimization_barrier((packed, own_piece, grad_pre))
-    cols = sort(own_piece, packed)
-    cols_chips = [fetch_chip(cols, k) for k in range(1, chips)]
-
-    terms = lax.all_to_all(grad_in_part(grad_pre, w_in.T, n_mp, grad_pre_all[1]), "mp", 0, 0)
-
     own_cols = stack([cols, *cols_chips])
     other_cols = other_core(own_cols)
-    grad_w_in_t, grad_w_out = grad_w_of(
-        [pre_act] + packed, grad_pre_all, own_cols, other_cols, scale_back
-    )
-    return (finish(terms), grad_w_in_t.T, grad_w_out)
+    pre = [fetch(pre_act, "tokens", k) for k in range(1, n_tok)]
+
+    grad_pre = grad_pre_of(own_rows, other_rows, pre_act, w_out, own_cols)
+    grad_pre_all = [grad_pre] + [fetch(grad_pre, "tokens", k) for k in range(1, n_tok)]
+    terms = lax.all_to_all(grad_in_part(grad_pre, w_in.T, n_mp, pre), "mp", 0, 0)
+    grad_w_in_t, grad_w_out, end = grad_w_of(
+        [pre_act] + pre, grad_pre_all, own_cols, other_cols, scale_back
+    )
+    return (finish(terms, end), grad_w_in_t.T, grad_w_out)
 
 
 def solution(mesh):

time: 59.4 us -> 56.5 us (0.951)
  the two profiles are of different devices: /device:TPU:0 before, /device:TPU:8 now
where the time goes in v10:
time: 56.5 us; the launch traced here: 56.3 us
  starting transfers between devices  25 us (44%)
  Pallas kernels  14.8 us (26%)
  waiting for transfers between devices  14.7 us (26%)
  local copies, waits for them, and re-layouts  0.92 us (2%)
  between operations  0.91 us (2%)
    pallas_call x9, Pallas kernels, call(): pl.pallas_call(body, in_specs=[pl.BlockSpec(memory_space=in_space)] * len...  14.8 us
    ppermute x9, starting transfers between devices, fetch(): return lax.ppermute(x, axis, [(partner(i, k, n), i) for i in range(n)])  12.9 us
    ppermute x9, waiting for transfers between devices, fetch(): return lax.ppermute(x, axis, [(partner(i, k, n), i) for i in range(n)])  8.62 us
    ppermute x6, starting transfers between devices, fetch_chip(): lax.ppermute(x, 'mp', [(there, here) for here, there in chip_pairs(k)])  8 us
    ppermute x6, waiting for transfers between devices, fetch_chip(): lax.ppermute(x, 'mp', [(there, here) for here, there in chip_pairs(k)])  3.48 us
    all_to_all x1, starting transfers between devices, shards(): lax.all_to_all(grad_in_part(grad_pre, w_in.T, n_mp, pre), 'mp', 0, 0)  3.43 us
    all_to_all x1, waiting for transfers between devices, shards(): lax.all_to_all(grad_in_part(grad_pre, w_in.T, n_mp, pre), 'mp', 0, 0)  2.59 us
  transfers between devices with their start and end apart: 18, of which 5 were waited for; matrix products, arithmetic and copies ran while one was open for 0% of the time, Pallas kernels for 25%

profile of v10, /device:TPU:8, one launch (start us, length us, event | category | flops | bytes accessed | tf_op | source)
XLA Modules:
  0.0 56.3 jit_solution(16260427519948049428)
XLA Ops:
  0.7 0.7 %copy-done.1 = bf16[4,5120]{1,0:T(4,128)(2,1)S(1)} copy-done((bf16[4,5120]{1,0:T(4,128)(2,1)S(1)}, bf16[4,5120]{1,0:T(4,128)(2,1)}, u32[]{:S(2)}) %copy-start.1) | copy-done | bytes 40984
  2.0 3.0 %collective-permute-start.1 = (bf16[8,1280]{1,0:T(8,128)(2,1)S(1)}, bf16[8,1280]{1,0:T(8,128)(2,1)S(1)}, u32[]{:S(2)}, u32[]{:S(2)}) collective-permute-start(bf16[8,1280]{1,0:T(8,128)(2,1)S(1)} %get-tuple-element.14), channel_id=1, source_target_pairs={{2,0},{3,1},{0,2},{1,3},{6,4},{7,5},{4,6},{5,7},{10,8},{11,9},{8,1... | collective-permute-start | bytes 61448 | tf_op jit(solution)/shard_map/ppermute | solution.py:35
  5.0 0.4 collective-permute-start.2
  5.5 1.5 %collective-permute-start.3 = (bf16[4,5120]{1,0:T(4,128)(2,1)S(1)}, bf16[4,5120]{1,0:T(4,128)(2,1)S(1)}, u32[]{:S(2)}, u32[]{:S(2)}) collective-permute-start(bf16[4,5120]{1,0:T(4,128)(2,1)S(1)} %copy-done.2), channel_id=1, source_target_pairs={{8,0},{12,4},{0,8},{4,12},{24,16},{28,20},{16,24},{20,28},{9,1},{1... | collective-permute-start | bytes 122888 | tf_op jit(solution)/shard_map/ppermute | solution.py:48
  7.0 1.8 %collective-permute-done.2.refs_3_ = bf16[8,1280]{1,0:T(8,128)(2,1)S(1)} collective-permute-done((bf16[8,1280]{1,0:T(8,128)(2,1)S(1)}, bf16[8,1280]{1,0:T(8,128)(2,1)S(1)}, u32[]{:S(2)}, u32[]{:S(2)}) %collective-permute-start.2) | collective-permute-done | bytes 20512 | tf_op jit(solution)/shard_map/ppermute | solution.py:35
  8.9 1.6 %collective-permute-start.7 = (bf16[2,16,1280]{2,1,0:T(8,128)(2,1)S(1)}, bf16[2,16,1280]{2,1,0:T(8,128)(2,1)S(1)}, u32[]{:S(2)}, u32[]{:S(2)}) collective-permute-start(bf16[2,16,1280]{2,1,0:T(8,128)(2,1)S(1)} %sort.1.after.refs_0_), channel_id=1, source_target_pairs={{8,0},{12,4},{0,8},{4,12},{24,16},{28,20},{16,24},{20,28},{9,1},{1... | collective-permute-start | bytes 245768 | tf_op jit(solution)/shard_map/ppermute | solution.py:48
  10.4 1.5 %collective-permute-start.8 = (bf16[2,16,1280]{2,1,0:T(8,128)(2,1)S(1)}, bf16[2,16,1280]{2,1,0:T(8,128)(2,1)S(1)}, u32[]{:S(2)}, u32[]{:S(2)}) collective-permute-start(bf16[2,16,1280]{2,1,0:T(8,128)(2,1)S(1)} %sort.1.after.refs_0_), channel_id=1, source_target_pairs={{16,0},{20,4},{24,8},{28,12},{0,16},{4,20},{8,24},{12,28},{17,1},{... | collective-permute-start | bytes 245768 | tf_op jit(solution)/shard_map/ppermute | solution.py:48
  11.9 0.5 collective-permute-start.9
  12.4 1.5 %collective-permute-start.4 = (bf16[4,5120]{1,0:T(4,128)(2,1)S(1)}, bf16[4,5120]{1,0:T(4,128)(2,1)S(1)}, u32[]{:S(2)}, u32[]{:S(2)}) collective-permute-start(bf16[4,5120]{1,0:T(4,128)(2,1)S(1)} %copy-done.2), channel_id=1, source_target_pairs={{16,0},{20,4},{24,8},{28,12},{0,16},{4,20},{8,24},{12,28},{17,1},{... | collective-permute-start | bytes 122888 | tf_op jit(solution)/shard_map/ppermute | solution.py:48
  13.9 1.4 %collective-permute-start.5 = (bf16[4,5120]{1,0:T(4,128)(2,1)S(1)}, bf16[4,5120]{1,0:T(4,128)(2,1)S(1)}, u32[]{:S(2)}, u32[]{:S(2)}) collective-permute-start(bf16[4,5120]{1,0:T(4,128)(2,1)S(1)} %copy-done.2), channel_id=1, source_target_pairs={{24,0},{28,4},{16,8},{20,12},{8,16},{12,20},{0,24},{4,28},{25,1},{... | collective-permute-start | bytes 122888 | tf_op jit(solution)/shard_map/ppermute | solution.py:48
  15.4 1.1 %collective-permute-done.4.refs_2_ = bf16[4,5120]{1,0:T(4,128)(2,1)S(1)} collective-permute-done((bf16[4,5120]{1,0:T(4,128)(2,1)S(1)}, bf16[4,5120]{1,0:T(4,128)(2,1)S(1)}, u32[]{:S(2)}, u32[]{:S(2)}) %collective-permute-start.4) | collective-permute-done | bytes 40992 | tf_op jit(solution)/shard_map/ppermute | solution.py:48
  16.4 2.4 %collective-permute-done.5.refs_3_ = bf16[4,5120]{1,0:T(4,128)(2,1)S(1)} collective-permute-done((bf16[4,5120]{1,0:T(4,128)(2,1)S(1)}, bf16[4,5120]{1,0:T(4,128)(2,1)S(1)}, u32[]{:S(2)}, u32[]{:S(2)}) %collective-permute-start.5) | collective-permute-done | bytes 40992 | tf_op jit(solution)/shard_map/ppermute | solution.py:48
  19.0 0.5 collective-permute-start.16
  19.6 3.4 %collective-permute-start.10 = (bf16[32,1728]{1,0:T(8,128)(2,1)S(1)}, bf16[32,1728]{1,0:T(8,128)(2,1)S(1)}, u32[]{:S(2)}, u32[]{:S(2)}) collective-permute-start(bf16[32,1728]{1,0:T(8,128)(2,1)S(1)} %get-tuple-element.17.pre_ref.refs_0_), channel_id=1, source_target_pairs={{1,0},{0,1},{3,2},{2,3},{5,4},{4,5},{7,6},{6,7},{9,8},{8,9},{11,10... | collective-permute-start | bytes 331784 | tf_op jit(solution)/shard_map/ppermute | solution.py:35
  22.9 1.5 %collective-permute-start.12 = (bf16[32,1728]{1,0:T(8,128)(2,1)S(1)}, bf16[32,1728]{1,0:T(8,128)(2,1)S(1)}, u32[]{:S(2)}, u32[]{:S(2)}) collective-permute-start(bf16[32,1728]{1,0:T(8,128)(2,1)S(1)} %get-tuple-element.17.pre_ref.refs_0_), channel_id=1, source_target_pairs={{3,0},{2,1},{1,2},{0,3},{7,4},{6,5},{5,6},{4,7},{11,8},{10,9},{9,1... | collective-permute-start | bytes 331784 | tf_op jit(solution)/shard_map/ppermute | solution.py:35
  24.5 4.9 %grad_pre.1.grad_pre_ref.refs_4_ = bf16[32,1728]{1,0:T(8,128)(2,1)S(1)} custom-call(bf16[16,5120]{1,0:T(8,128)(2,1)S(1)} %join.1.own_ref, bf16[16,5120]{1,0:T(8,128)(2,1)S(1)} %collective-permute-done.6.other_ref, bf16[32,1728]{1,0:T(8,128)(2,1)S(1)} %get-tuple-element.17.pre_ref.refs_0_, bf16[1728,5120]{1,0:T(8,128)(2,1)S(1)} %bitcast.3, ...), custom_call_target="tpu_custom_call" | custom-call | flops 566231040 | bytes 17694720 | tf_op jit(solution)/shard_map/grad_pre/pallas_call | solution.py:61
  29.4 3.0 %collective-permute-start.13 = (bf16[32,1728]{1,0:T(8,128)(2,1)S(1)}, bf16[32,1728]{1,0:T(8,128)(2,1)S(1)}, u32[]{:S(2)}, u32[]{:S(2)}) collective-permute-start(bf16[32,1728]{1,0:T(8,128)(2,1)S(1)} %grad_pre.1.grad_pre_ref.refs_4_), channel_id=1, source_target_pairs={{1,0},{0,1},{3,2},{2,3},{5,4},{4,5},{7,6},{6,7},{9,8},{8,9},{11,10... | collective-permute-start | bytes 331784 | tf_op jit(solution)/shard_map/ppermute | solution.py:35
  32.4 1.5 %collective-permute-start.15 = (bf16[32,1728]{1,0:T(8,128)(2,1)S(1)}, bf16[32,1728]{1,0:T(8,128)(2,1)S(1)}, u32[]{:S(2)}, u32[]{:S(2)}) collective-permute-start(bf16[32,1728]{1,0:T(8,128)(2,1)S(1)} %grad_pre.1.grad_pre_ref.refs_4_), channel_id=1, source_target_pairs={{3,0},{2,1},{1,2},{0,3},{7,4},{6,5},{5,6},{4,7},{11,8},{10,9},{9,1... | collective-permute-start | bytes 331784 | tf_op jit(solution)/shard_map/ppermute | solution.py:35
  33.9 6.8 %collective-permute-done.12.refs_2_.refs_3_ = bf16[32,1728]{1,0:T(8,128)(2,1)S(1)} collective-permute-done((bf16[32,1728]{1,0:T(8,128)(2,1)S(1)}, bf16[32,1728]{1,0:T(8,128)(2,1)S(1)}, u32[]{:S(2)}, u32[]{:S(2)}) %collective-permute-start.12) | collective-permute-done | bytes 110624 | tf_op jit(solution)/shard_map/ppermute | solution.py:35
  40.7 3.9 %grad_in_part.1 = bf16[8,4,5120]{2,1,0:T(4,128)(2,1)} custom-call(bf16[32,1728]{1,0:T(8,128)(2,1)S(1)} %grad_pre.1.grad_pre_ref.refs_4_, bf16[1728,5120]{1,0:T(8,128)(2,1)S(1)} %bitcast.6, bf16[32,1728]{1,0:T(8,128)(2,1)S(1)} %collective-permute-done.10.refs_0_.refs_1_, bf16[32,1728]{1,0:T(8,128)(2,1)S(1)} %collective-permute-done.11.refs_1_.refs_2_, ...), custom_call_target="tpu_custom_call" | custom-call | flops 566231040 | bytes 17694720 | tf_op jit(solution)/shard_map/grad_in_part/pallas_call | solution.py:61
  44.6 3.4 %all-to-all-start = ((bf16[8,4,5120]{2,1,0:T(4,128)(2,1)}), bf16[8,4,5120]{2,1,0:T(4,128)(2,1)S(1)}, u32[]{:S(2)}, u32[]{:S(2)}) async-start(bf16[8,4,5120]{2,1,0:T(4,128)(2,1)} %grad_in_part.1), calls=%async_computation | async-start | bytes 655360 | tf_op jit(solution)/shard_map/all_to_all | solution.py:365
  48.1 4.9 %grad_w.1 = (bf16[1728,1280]{1,0:T(8,128)(2,1)}, bf16[1728,1280]{1,0:T(8,128)(2,1)}, f32[8,128]{1,0:T(8,128)S(1)}) custom-call(bf16[32,1728]{1,0:T(8,128)(2,1)S(1)} %get-tuple-element.17.pre_ref.refs_0_, bf16[32,1728]{1,0:T(8,128)(2,1)S(1)} %collective-permute-done.10.refs_0_.refs_1_, bf16[32,1728]{1,0:T(8,128)(2,1)S(1)} %collective-permute-done.11.refs_1_.refs_2_, ...), custom_call_target="tpu_custom_call" | custom-call | flops 22649241600 | bytes 88473600 | tf_op jit(solution)/shard_map/grad_w/pallas_call | solution.py:61
  53.1 2.6 %all-to-all-done.terms_ref = bf16[8,4,5120]{2,1,0:T(4,128)(2,1)S(1)} async-done(((bf16[8,4,5120]{2,1,0:T(4,128)(2,1)}), bf16[8,4,5120]{2,1,0:T(4,128)(2,1)S(1)}, u32[]{:S(2)}, u32[]{:S(2)}) %all-to-all-start) | async-done | bytes 327712 | tf_op jit(solution)/shard_map/all_to_all | solution.py:365
  55.6 0.7 %finish.1 = bf16[4,5120]{1,0:T(4,128)(2,1)} custom-call(bf16[8,4,5120]{2,1,0:T(4,128)(2,1)S(1)} %all-to-all-done.terms_ref, f32[8,128]{1,0:T(8,128)S(1)} %get-tuple-element.18.after), custom_call_target="tpu_custom_call" | custom-call | flops 1000000 | bytes 100000 | tf_op jit(solution)/shard_map/finish/pallas_call | solution.py:61
  (49 shorter events, 0.8 us)
Async XLA Ops:
  0.7 23.8 %slice-start = ((s8[17694720]{0:T(1024)(128)(4,1)}), s8[4194304]{0:T(1024)(128)(4,1)S(1)}, s32[]{:S(2)}) async-start(s8[17694720]{0:T(1024)(128)(4,1)} %bitcast.2), calls=%async_computation.1 | async-start | bytes 8388608
  0.7 23.7 %slice-start.1 = ((s8[17694720]{0:T(1024)(128)(4,1)}), s8[4194304]{0:T(1024)(128)(4,1)S(1)}, s32[]{:S(2)}) async-start(s8[17694720]{0:T(1024)(128)(4,1)} %bitcast.2), calls=%async_computation.2 | async-start | bytes 8388608
  1.6 39.1 %slice-start.5 = ((s8[17694720]{0:T(1024)(128)(4,1)}), s8[4194304]{0:T(1024)(128)(4,1)S(1)}, s32[]{:S(2)}) async-start(s8[17694720]{0:T(1024)(128)(4,1)} %bitcast.4), calls=%async_computation.6 | async-start | bytes 8388608
  1.6 39.1 %slice-start.6 = ((s8[17694720]{0:T(1024)(128)(4,1)}), s8[4194304]{0:T(1024)(128)(4,1)S(1)}, s32[]{:S(2)}) async-start(s8[17694720]{0:T(1024)(128)(4,1)} %bitcast.4), calls=%async_computation.7 | async-start | bytes 8388608
  1.6 39.1 %slice-start.7 = ((s8[17694720]{0:T(1024)(128)(4,1)}), s8[4194304]{0:T(1024)(128)(4,1)S(1)}, s32[]{:S(2)}) async-start(s8[17694720]{0:T(1024)(128)(4,1)} %bitcast.4), calls=%async_computation.8 | async-start | bytes 8388608
  1.6 39.1 %slice-start.8 = ((s8[17694720]{0:T(1024)(128)(4,1)}), s8[4194304]{0:T(1024)(128)(4,1)S(1)}, s32[]{:S(2)}) async-start(s8[17694720]{0:T(1024)(128)(4,1)} %bitcast.4), calls=%async_computation.9 | async-start | bytes 8388608
  1.9 5.0 %collective-permute-start = (bf16[8,1280]{1,0:T(8,128)(2,1)S(1)}, bf16[8,1280]{1,0:T(8,128)(2,1)S(1)}, u32[]{:S(2)}, u32[]{:S(2)}) collective-permute-start(bf16[8,1280]{1,0:T(8,128)(2,1)S(1)} %get-tuple-element.13), channel_id=1, source_target_pairs={{1,0},{0,1},{3,2},{2,3},{5,4},{4,5},{7,6},{6,7},{9,8},{8,9},{11,10... | collective-permute-start | bytes 61448 | tf_op jit(solution)/shard_map/ppermute | solution.py:35
  2.0 5.0 %collective-permute-start.1 = (bf16[8,1280]{1,0:T(8,128)(2,1)S(1)}, bf16[8,1280]{1,0:T(8,128)(2,1)S(1)}, u32[]{:S(2)}, u32[]{:S(2)}) collective-permute-start(bf16[8,1280]{1,0:T(8,128)(2,1)S(1)} %get-tuple-element.14), channel_id=1, source_target_pairs={{2,0},{3,1},{0,2},{1,3},{6,4},{7,5},{4,6},{5,7},{10,8},{11,9},{8,1... | collective-permute-start | bytes 61448 | tf_op jit(solution)/shard_map/ppermute | solution.py:35
  5.0 3.8 %collective-permute-start.2 = (bf16[8,1280]{1,0:T(8,128)(2,1)S(1)}, bf16[8,1280]{1,0:T(8,128)(2,1)S(1)}, u32[]{:S(2)}, u32[]{:S(2)}) collective-permute-start(bf16[8,1280]{1,0:T(8,128)(2,1)S(1)} %get-tuple-element.15), channel_id=1, source_target_pairs={{3,0},{2,1},{1,2},{0,3},{7,4},{6,5},{5,6},{4,7},{11,8},{10,9},{9,1... | collective-permute-start | bytes 61448 | tf_op jit(solution)/shard_map/ppermute | solution.py:35
  5.5 8.4 %collective-permute-start.3 = (bf16[4,5120]{1,0:T(4,128)(2,1)S(1)}, bf16[4,5120]{1,0:T(4,128)(2,1)S(1)}, u32[]{:S(2)}, u32[]{:S(2)}) collective-permute-start(bf16[4,5120]{1,0:T(4,128)(2,1)S(1)} %copy-done.2), channel_id=1, source_target_pairs={{8,0},{12,4},{0,8},{4,12},{24,16},{28,20},{16,24},{20,28},{9,1},{1... | collective-permute-start | bytes 122888 | tf_op jit(solution)/shard_map/ppermute | solution.py:48
  8.9 10.1 %collective-permute-start.7 = (bf16[2,16,1280]{2,1,0:T(8,128)(2,1)S(1)}, bf16[2,16,1280]{2,1,0:T(8,128)(2,1)S(1)}, u32[]{:S(2)}, u32[]{:S(2)}) collective-permute-start(bf16[2,16,1280]{2,1,0:T(8,128)(2,1)S(1)} %sort.1.after.refs_0_), channel_id=1, source_target_pairs={{8,0},{12,4},{0,8},{4,12},{24,16},{28,20},{16,24},{20,28},{9,1},{1... | collective-permute-start | bytes 245768 | tf_op jit(solution)/shard_map/ppermute | solution.py:48
  10.4 8.6 %collective-permute-start.8 = (bf16[2,16,1280]{2,1,0:T(8,128)(2,1)S(1)}, bf16[2,16,1280]{2,1,0:T(8,128)(2,1)S(1)}, u32[]{:S(2)}, u32[]{:S(2)}) collective-permute-start(bf16[2,16,1280]{2,1,0:T(8,128)(2,1)S(1)} %sort.1.after.refs_0_), channel_id=1, source_target_pairs={{16,0},{20,4},{24,8},{28,12},{0,16},{4,20},{8,24},{12,28},{17,1},{... | collective-permute-start | bytes 245768 | tf_op jit(solution)/shard_map/ppermute | solution.py:48
  11.9 7.0 %collective-permute-start.9 = (bf16[2,16,1280]{2,1,0:T(8,128)(2,1)S(1)}, bf16[2,16,1280]{2,1,0:T(8,128)(2,1)S(1)}, u32[]{:S(2)}, u32[]{:S(2)}) collective-permute-start(bf16[2,16,1280]{2,1,0:T(8,128)(2,1)S(1)} %sort.1.after.refs_0_), channel_id=1, source_target_pairs={{24,0},{28,4},{16,8},{20,12},{8,16},{12,20},{0,24},{4,28},{25,1},{... | collective-permute-start | bytes 245768 | tf_op jit(solution)/shard_map/ppermute | solution.py:48
  12.4 4.0 %collective-permute-start.4 = (bf16[4,5120]{1,0:T(4,128)(2,1)S(1)}, bf16[4,5120]{1,0:T(4,128)(2,1)S(1)}, u32[]{:S(2)}, u32[]{:S(2)}) collective-permute-start(bf16[4,5120]{1,0:T(4,128)(2,1)S(1)} %copy-done.2), channel_id=1, source_target_pairs={{16,0},{20,4},{24,8},{28,12},{0,16},{4,20},{8,24},{12,28},{17,1},{... | collective-permute-start | bytes 122888 | tf_op jit(solution)/shard_map/ppermute | solution.py:48
  13.9 4.9 %collective-permute-start.5 = (bf16[4,5120]{1,0:T(4,128)(2,1)S(1)}, bf16[4,5120]{1,0:T(4,128)(2,1)S(1)}, u32[]{:S(2)}, u32[]{:S(2)}) collective-permute-start(bf16[4,5120]{1,0:T(4,128)(2,1)S(1)} %copy-done.2), channel_id=1, source_target_pairs={{24,0},{28,4},{16,8},{20,12},{8,16},{12,20},{0,24},{4,28},{25,1},{... | collective-permute-start | bytes 122888 | tf_op jit(solution)/shard_map/ppermute | solution.py:48
  18.9 5.5 %collective-permute-start.6 = (bf16[16,5120]{1,0:T(8,128)(2,1)S(1)}, bf16[16,5120]{1,0:T(8,128)(2,1)S(1)}, u32[]{:S(2)}, u32[]{:S(2)}) collective-permute-start(bf16[16,5120]{1,0:T(8,128)(2,1)S(1)} %join.1.own_ref), channel_id=1, source_target_pairs={{4,0},{0,4},{12,8},{8,12},{20,16},{16,20},{28,24},{24,28},{5,1},{1... | collective-permute-start | bytes 491528 | tf_op jit(solution)/shard_map/ppermute | solution.py:39
  19.0 29.1 %collective-permute-start.16 = (bf16[4,2,16,1280]{3,2,1,0:T(8,128)(2,1)S(1)}, bf16[4,2,16,1280]{3,2,1,0:T(8,128)(2,1)S(1)}, u32[]{:S(2)}, u32[]{:S(2)}) collective-permute-start(bf16[4,2,16,1280]{3,2,1,0:T(8,128)(2,1)S(1)} %stack.1.after.refs_8_), channel_id=1, source_target_pairs={{4,0},{0,4},{12,8},{8,12},{20,16},{16,20},{28,24},{24,28},{5,1},{1... | collective-permute-start | bytes 983048 | tf_op jit(solution)/shard_map/ppermute | solution.py:39
  19.6 12.8 %collective-permute-start.10 = (bf16[32,1728]{1,0:T(8,128)(2,1)S(1)}, bf16[32,1728]{1,0:T(8,128)(2,1)S(1)}, u32[]{:S(2)}, u32[]{:S(2)}) collective-permute-start(bf16[32,1728]{1,0:T(8,128)(2,1)S(1)} %get-tuple-element.17.pre_ref.refs_0_), channel_id=1, source_target_pairs={{1,0},{0,1},{3,2},{2,3},{5,4},{4,5},{7,6},{6,7},{9,8},{8,9},{11,10... | collective-permute-start | bytes 331784 | tf_op jit(solution)/shard_map/ppermute | solution.py:35
  22.9 9.4 %collective-permute-start.11 = (bf16[32,1728]{1,0:T(8,128)(2,1)S(1)}, bf16[32,1728]{1,0:T(8,128)(2,1)S(1)}, u32[]{:S(2)}, u32[]{:S(2)}) collective-permute-start(bf16[32,1728]{1,0:T(8,128)(2,1)S(1)} %get-tuple-element.17.pre_ref.refs_0_), channel_id=1, source_target_pairs={{2,0},{3,1},{0,2},{1,3},{6,4},{7,5},{4,6},{5,7},{10,8},{11,9},{8,1... | collective-permute-start | bytes 331784 | tf_op jit(solution)/shard_map/ppermute | solution.py:35
  22.9 17.8 %collective-permute-start.12 = (bf16[32,1728]{1,0:T(8,128)(2,1)S(1)}, bf16[32,1728]{1,0:T(8,128)(2,1)S(1)}, u32[]{:S(2)}, u32[]{:S(2)}) collective-permute-start(bf16[32,1728]{1,0:T(8,128)(2,1)S(1)} %get-tuple-element.17.pre_ref.refs_0_), channel_id=1, source_target_pairs={{3,0},{2,1},{1,2},{0,3},{7,4},{6,5},{5,6},{4,7},{11,8},{10,9},{9,1... | collective-permute-start | bytes 331784 | tf_op jit(solution)/shard_map/ppermute | solution.py:35
  29.4 18.7 %collective-permute-start.13 = (bf16[32,1728]{1,0:T(8,128)(2,1)S(1)}, bf16[32,1728]{1,0:T(8,128)(2,1)S(1)}, u32[]{:S(2)}, u32[]{:S(2)}) collective-permute-start(bf16[32,1728]{1,0:T(8,128)(2,1)S(1)} %grad_pre.1.grad_pre_ref.refs_4_), channel_id=1, source_target_pairs={{1,0},{0,1},{3,2},{2,3},{5,4},{4,5},{7,6},{6,7},{9,8},{8,9},{11,10... | collective-permute-start | bytes 331784 | tf_op jit(solution)/shard_map/ppermute | solution.py:35
  32.4 15.7 %collective-permute-start.14 = (bf16[32,1728]{1,0:T(8,128)(2,1)S(1)}, bf16[32,1728]{1,0:T(8,128)(2,1)S(1)}, u32[]{:S(2)}, u32[]{:S(2)}) collective-permute-start(bf16[32,1728]{1,0:T(8,128)(2,1)S(1)} %grad_pre.1.grad_pre_ref.refs_4_), channel_id=1, source_target_pairs={{2,0},{3,1},{0,2},{1,3},{6,4},{7,5},{4,6},{5,7},{10,8},{11,9},{8,1... | collective-permute-start | bytes 331784 | tf_op jit(solution)/shard_map/ppermute | solution.py:35
  32.4 15.7 %collective-permute-start.15 = (bf16[32,1728]{1,0:T(8,128)(2,1)S(1)}, bf16[32,1728]{1,0:T(8,128)(2,1)S(1)}, u32[]{:S(2)}, u32[]{:S(2)}) collective-permute-start(bf16[32,1728]{1,0:T(8,128)(2,1)S(1)} %grad_pre.1.grad_pre_ref.refs_4_), channel_id=1, source_target_pairs={{3,0},{2,1},{1,2},{0,3},{7,4},{6,5},{5,6},{4,7},{11,8},{10,9},{9,1... | collective-permute-start | bytes 331784 | tf_op jit(solution)/shard_map/ppermute | solution.py:35
  44.6 11.0 %all-to-all-start = ((bf16[8,4,5120]{2,1,0:T(4,128)(2,1)}), bf16[8,4,5120]{2,1,0:T(4,128)(2,1)S(1)}, u32[]{:S(2)}, u32[]{:S(2)}) async-start(bf16[8,4,5120]{2,1,0:T(4,128)(2,1)} %grad_in_part.1), calls=%async_computation | async-start | bytes 655360 | tf_op jit(solution)/shard_map/all_to_all | solution.py:365
  (7 other events, 93.1 us)

commit v11 on v10

--- a/solution.py
+++ b/solution.py
@@ -135,20 +135,20 @@
     )
 
 
-def join_body(after, *refs):
+def join_body(*refs):
     *pieces, out = refs
     out[...] = jnp.concatenate([x[...].astype(jnp.float32) for x in pieces], axis=0).astype(
         jnp.bfloat16
     )
 
 
-def join(pieces, after):
+def join(pieces):
     shape = (sum(x.shape[0] for x in pieces), pieces[0].shape[1])
-    return call(join_body, [(shape, jnp.bfloat16)], [after, *pieces], "join")[0]
-
-
-def sort_body(*refs):
-    *pieces, out = refs
+    return call(join_body, [(shape, jnp.bfloat16)], pieces, "join")[0]
+
+
+def sort_body(count, *refs):
+    pieces, out = refs[:count], refs[-1]
     rows = pieces[0].shape[0] // 2
     pieces = [x[...].astype(jnp.float32) for x in pieces]
     for a in range(2):
@@ -157,24 +157,47 @@
         )
 
 
-def sort(pieces):
+def sort(pieces, after):
     rows, part = pieces[0].shape
     shape = (2, rows // 2 * len(pieces), part)
-    return call(sort_body, [(shape, jnp.bfloat16)], pieces, "sort")[0]
-
-
-def stack_body(*refs):
-    *pieces, out = refs
+    body = functools.partial(sort_body, len(pieces))
+    return call(body, [(shape, jnp.bfloat16)], [*pieces, *after], "sort")[0]
+
+
+def stack_body(count, *refs):
+    pieces, out = refs[:count], refs[-1]
     for k, x in enumerate(pieces):
         out[k] = x[...]
 
 
-def stack(pieces):
+def stack(pieces, after=()):
     shape = (len(pieces),) + pieces[0].shape
-    return call(stack_body, [(shape, jnp.bfloat16)], pieces, "stack")[0]
-
-
-def grad_pre_body(block, own_ref, other_ref, pre_ref, w_ref, after, out_ref, rows, total):
+    body = functools.partial(stack_body, len(pieces))
+    return call(body, [(shape, jnp.bfloat16)], [*pieces, *after], "stack")[0]
+
+
+def pile_body(low, high, out):
+    count = low.shape[0]
+    out[:count] = low[...]
+    out[count:] = high[...]
+
+
+def spread(x, masks):
+    held, got, order = stack([x]), [], [0]
+    where = {}
+    n = lax.axis_size("tokens")
+    for mask in masks:
+        if got:
+            shape = (2 * held.shape[0],) + held.shape[1:]
+            held = call(pile_body, [(shape, jnp.bfloat16)], [held, got[-1]], "pile")[0]
+        got.append(lax.ppermute(held, "tokens", [(i ^ mask, i) for i in range(n)]))
+        for j, k in enumerate(order):
+            where[k ^ mask] = (len(got), j)
+        order = order + [k ^ mask for k in order]
+    return held, got, where
+
+
+def grad_pre_body(block, own_ref, other_ref, pre_ref, w_ref, out_ref, rows, total):
     hidden, group = total.shape
     half = own_ref.shape[0]
     rows[:half, :] = own_ref[...]
@@ -198,13 +221,13 @@
     out_ref[...] = (total[...].T * gelu_slope(pre)).astype(jnp.bfloat16)
 
 
-def grad_pre_of(own, other, pre_act, w_out, after):
+def grad_pre_of(own, other, pre_act, w_out):
     group, hidden = pre_act.shape
     width = w_out.shape[1]
     return call(
         functools.partial(grad_pre_body, block_of(hidden, 432, 16)),
         [((group, hidden), jnp.bfloat16)],
-        [own, other, pre_act, w_out, after],
+        [own, other, pre_act, w_out],
         "grad_pre",
         [pltpu.VMEM((group, width), jnp.bfloat16), pltpu.VMEM((hidden, group), jnp.float32)],
         flops=2 * group * width * hidden,
@@ -263,10 +286,10 @@
         ).astype(jnp.bfloat16)
 
 
-def grad_w_body(places, scale_back, block, *refs):
-    pre_refs, grad_pre_refs = refs[:places], refs[places : 2 * places]
-    own_ref, other_ref, in_ref, out_ref, end_ref = refs[2 * places : 2 * places + 5]
-    flat, sorted_rows, turned, held_in, held_out, sems = refs[2 * places + 5 :]
+def grad_w_body(places, arrays, where, scale_back, block, *refs):
+    pre_refs, grad_pre_refs = refs[:arrays], refs[arrays : arrays + places]
+    own_ref, other_ref, in_ref, out_ref, end_ref = refs[arrays + places : arrays + places + 5]
+    flat, sorted_rows, turned, held_in, held_out, sems = refs[arrays + places + 5 :]
     end_ref[...] = jnp.zeros_like(end_ref)
     group, hidden = grad_pre_refs[0].shape
     chips, _, each, part = own_ref.shape
@@ -307,7 +330,8 @@
             copies[-1].start()
 
     for k in range(places):
-        pre = pre_refs[k][...].astype(jnp.float32)
+        array, j = where[k]
+        pre = (pre_refs[array][j] if array else pre_refs[0][...]).astype(jnp.float32)
         flat[k * group : (k + 1) * group, :] = gelu_value(pre).astype(jnp.bfloat16)
     arrange(lambda b: place_of(b, chips))
     product(1, held_out, out_ref)
@@ -319,13 +343,13 @@
         copy.wait()
 
 
-def grad_w_of(pre, grad_pre, own, other, scale_back):
-    places = len(pre)
+def grad_w_of(pre, where, grad_pre, own, other, scale_back):
+    places = len(grad_pre)
     group, hidden = grad_pre[0].shape
     total, part = places * group, own.shape[3]
     block = block_of(part, 256, 128)
     return call(
-        functools.partial(grad_w_body, places, scale_back, block),
+        functools.partial(grad_w_body, places, len(pre), where, scale_back, block),
         [((hidden, part), jnp.bfloat16)] * 2 + [((8, 128), jnp.float32)],
         [*pre, *grad_pre, own, other],
         "grad_w",
@@ -350,21 +374,20 @@
     scale_back = 1.0 / math.sqrt(pre_act.shape[0] * n_tok)
 
     *pieces, own_piece, pre_act, own_grad = pack(tokens_in, grad_out, pre_act, n_tok, lead())
-    rows_grad = [fetch_chip(grad_out, k) for k in range(1, chips)]
-    cols = sort([own_piece] + [fetch(x, "tokens", k) for k, x in enumerate(pieces, 1)])
-    cols_chips = [fetch_chip(cols, k) for k in range(1, chips)]
-
-    own_rows = join([own_grad, *rows_grad], cols)
+    own_rows = join([own_grad] + [fetch_chip(grad_out, k) for k in range(1, chips)])
     other_rows = other_core(own_rows)
-    own_cols = stack([cols, *cols_chips])
+    masks = (3, 1) if n_tok == 4 else [1 << i for i in range(n_tok.bit_length() - 1)]
+    held, pre, where = spread(pre_act, masks)
+    where[0] = (0, 0)
+    pieces = [fetch(x, "tokens", k) for k, x in enumerate(pieces, 1)]
+    grad_pre = grad_pre_of(own_rows, other_rows, pre_act, w_out)
+    cols = sort([own_piece, *pieces], [grad_pre])
+    own_cols = stack([cols] + [fetch_chip(cols, k) for k in range(1, chips)])
     other_cols = other_core(own_cols)
-    pre = [fetch(pre_act, "tokens", k) for k in range(1, n_tok)]
-
-    grad_pre = grad_pre_of(own_rows, other_rows, pre_act, w_out, own_cols)
     grad_pre_all = [grad_pre] + [fetch(grad_pre, "tokens", k) for k in range(1, n_tok)]
-    terms = lax.all_to_all(grad_in_part(grad_pre, w_in.T, n_mp, pre), "mp", 0, 0)
+    terms = lax.all_to_all(grad_in_part(grad_pre, w_in.T, n_mp, [pre[-1]]), "mp", 0, 0)
     grad_w_in_t, grad_w_out, end = grad_w_of(
-        [pre_act] + pre, grad_pre_all, own_cols, other_cols, scale_back
+        [pre_act, *pre], where, grad_pre_all, own_cols, other_cols, scale_back
     )
     return (finish(terms, end), grad_w_in_t.T, grad_w_out)
 

time: 56.5 us -> 55.5 us (0.982)
  the two profiles are of different devices: /device:TPU:8 before, /device:TPU:0 now
where the time goes in v11:
time: 55.5 us; the launch traced here: 55.3 us
  starting transfers between devices  24.7 us (45%)
  Pallas kernels  14.9 us (27%)
  waiting for transfers between devices  14.7 us (26%)
  between operations  0.94 us (2%)
    pallas_call x11, Pallas kernels, call(): pl.pallas_call(body, in_specs=[pl.BlockSpec(memory_space=in_space)] * len...  14.9 us
    ppermute x6, starting transfers between devices, fetch(): return lax.ppermute(x, axis, [(partner(i, k, n), i) for i in range(n)])  8.62 us
    ppermute x6, starting transfers between devices, fetch_chip(): lax.ppermute(x, 'mp', [(there, here) for here, there in chip_pairs(k)])  8.1 us
    ppermute x2, waiting for transfers between devices, spread(): got.append(lax.ppermute(held, 'tokens', [(i ^ mask, i) for i in range(n)]))  7.38 us
    ppermute x6, waiting for transfers between devices, fetch_chip(): lax.ppermute(x, 'mp', [(there, here) for here, there in chip_pairs(k)])  4.73 us
    ppermute x2, starting transfers between devices, spread(): got.append(lax.ppermute(held, 'tokens', [(i ^ mask, i) for i in range(n)]))  4.42 us
    all_to_all x1, starting transfers between devices, shards(): lax.all_to_all(grad_in_part(grad_pre, w_in.T, n_mp, [pre[-1]]), 'mp', 0, 0)  3.43 us
    all_to_all x1, waiting for transfers between devices, shards(): lax.all_to_all(grad_in_part(grad_pre, w_in.T, n_mp, [pre[-1]]), 'mp', 0, 0)  2.59 us
  transfers between devices with their start and end apart: 17, of which 7 were waited for; matrix products, arithmetic and copies ran while one was open for 0% of the time, Pallas kernels for 26%

profile of v11, /device:TPU:0, one launch (start us, length us, event | category | flops | bytes accessed | tf_op | source)
XLA Modules:
  0.0 55.3 jit_solution(2592371028028128730)
XLA Ops:
  0.7 3.0 %collective-permute-start = (bf16[4,5120]{1,0:T(4,128)(2,1)}, bf16[4,5120]{1,0:T(4,128)(2,1)S(1)}, u32[]{:S(2)}, u32[]{:S(2)}) collective-permute-start(bf16[4,5120]{1,0:T(4,128)(2,1)} %grad_in.1), channel_id=1, source_target_pairs={{8,0},{12,4},{0,8},{4,12},{24,16},{28,20},{16,24},{20,28},{9,1},{1... | collective-permute-start | bytes 122888 | tf_op jit(solution)/shard_map/ppermute | solution.py:48
  3.7 1.5 %collective-permute-start.1 = (bf16[4,5120]{1,0:T(4,128)(2,1)}, bf16[4,5120]{1,0:T(4,128)(2,1)S(1)}, u32[]{:S(2)}, u32[]{:S(2)}) collective-permute-start(bf16[4,5120]{1,0:T(4,128)(2,1)} %grad_in.1), channel_id=1, source_target_pairs={{16,0},{20,4},{24,8},{28,12},{0,16},{4,20},{8,24},{12,28},{17,1},{... | collective-permute-start | bytes 122888 | tf_op jit(solution)/shard_map/ppermute | solution.py:48
  5.3 0.3 pack.1
  5.9 2.0 %collective-permute-done.1.refs_2_ = bf16[4,5120]{1,0:T(4,128)(2,1)S(1)} collective-permute-done((bf16[4,5120]{1,0:T(4,128)(2,1)}, bf16[4,5120]{1,0:T(4,128)(2,1)S(1)}, u32[]{:S(2)}, u32[]{:S(2)}) %collective-permute-start.1) | collective-permute-done | bytes 40992 | tf_op jit(solution)/shard_map/ppermute | solution.py:48
  7.9 2.4 %collective-permute-done.2.refs_3_ = bf16[4,5120]{1,0:T(4,128)(2,1)S(1)} collective-permute-done((bf16[4,5120]{1,0:T(4,128)(2,1)}, bf16[4,5120]{1,0:T(4,128)(2,1)S(1)}, u32[]{:S(2)}, u32[]{:S(2)}) %collective-permute-start.2) | collective-permute-done | bytes 40992 | tf_op jit(solution)/shard_map/ppermute | solution.py:48
  10.4 2.7 %collective-permute-start.10 = (bf16[8,1280]{1,0:T(8,128)(2,1)S(1)}, bf16[8,1280]{1,0:T(8,128)(2,1)S(1)}, u32[]{:S(2)}, u32[]{:S(2)}) collective-permute-start(bf16[8,1280]{1,0:T(8,128)(2,1)S(1)} %get-tuple-element.16), channel_id=1, source_target_pairs={{2,0},{3,1},{0,2},{1,3},{6,4},{7,5},{4,6},{5,7},{10,8},{11,9},{8,1... | collective-permute-start | bytes 61448 | tf_op jit(solution)/shard_map/ppermute | solution.py:35
  13.1 1.3 %collective-permute-start.11 = (bf16[8,1280]{1,0:T(8,128)(2,1)S(1)}, bf16[8,1280]{1,0:T(8,128)(2,1)S(1)}, u32[]{:S(2)}, u32[]{:S(2)}) collective-permute-start(bf16[8,1280]{1,0:T(8,128)(2,1)S(1)} %get-tuple-element.17), channel_id=1, source_target_pairs={{3,0},{2,1},{1,2},{0,3},{7,4},{6,5},{5,6},{4,7},{11,8},{10,9},{9,1... | collective-permute-start | bytes 61448 | tf_op jit(solution)/shard_map/ppermute | solution.py:35
  14.4 0.2 collective-permute-start.9
  14.7 4.9 %grad_pre.1.grad_pre_ref.refs_4_.refs_3_ = bf16[32,1728]{1,0:T(8,128)(2,1)S(1)} custom-call(bf16[16,5120]{1,0:T(8,128)(2,1)S(1)} %join.1.own_ref, bf16[16,5120]{1,0:T(8,128)(2,1)S(1)} %collective-permute-done.3.other_ref, bf16[32,1728]{1,0:T(8,128)(2,1)S(1)} %get-tuple-element.13.pre_ref.refs_0_, bf16[1728,5120]{1,0:T(8,128)(2,1)S(1)} %bitcast.3), custom_call_target="tpu_custom_call" | custom-call | flops 566231040 | bytes 17694720 | tf_op jit(solution)/shard_map/grad_pre/pallas_call | solution.py:61
  19.7 0.6 %collective-permute-start.12 = (bf16[2,16,1280]{2,1,0:T(8,128)(2,1)S(1)}, bf16[2,16,1280]{2,1,0:T(8,128)(2,1)S(1)}, u32[]{:S(2)}, u32[]{:S(2)}) collective-permute-start(bf16[2,16,1280]{2,1,0:T(8,128)(2,1)S(1)} %sort.1.refs_0_), channel_id=1, source_target_pairs={{8,0},{12,4},{0,8},{4,12},{24,16},{28,20},{16,24},{20,28},{9,1},{1... | collective-permute-start | bytes 245768 | tf_op jit(solution)/shard_map/ppermute | solution.py:48
  20.3 0.5 collective-permute-start.13
  20.8 2.4 %collective-permute-start.14 = (bf16[2,16,1280]{2,1,0:T(8,128)(2,1)S(1)}, bf16[2,16,1280]{2,1,0:T(8,128)(2,1)S(1)}, u32[]{:S(2)}, u32[]{:S(2)}) collective-permute-start(bf16[2,16,1280]{2,1,0:T(8,128)(2,1)S(1)} %sort.1.refs_0_), channel_id=1, source_target_pairs={{24,0},{28,4},{16,8},{20,12},{8,16},{12,20},{0,24},{4,28},{25,1},{... | collective-permute-start | bytes 245768 | tf_op jit(solution)/shard_map/ppermute | solution.py:48
  23.3 3.0 %collective-permute-start.4 = (bf16[1,32,1728]{2,1,0:T(8,128)(2,1)S(1)}, bf16[1,32,1728]{2,1,0:T(8,128)(2,1)S(1)}, u32[]{:S(2)}, u32[]{:S(2)}) collective-permute-start(bf16[1,32,1728]{2,1,0:T(8,128)(2,1)S(1)} %stack.2.low), channel_id=1, source_target_pairs={{3,0},{2,1},{1,2},{0,3},{7,4},{6,5},{5,6},{4,7},{11,8},{10,9},{9,1... | collective-permute-start | bytes 331784 | tf_op jit(solution)/shard_map/ppermute | solution.py:193
  26.5 3.6 %collective-permute-done.4.high.refs_1_ = bf16[1,32,1728]{2,1,0:T(8,128)(2,1)S(1)} collective-permute-done((bf16[1,32,1728]{2,1,0:T(8,128)(2,1)S(1)}, bf16[1,32,1728]{2,1,0:T(8,128)(2,1)S(1)}, u32[]{:S(2)}, u32[]{:S(2)}) %collective-permute-start.4) | collective-permute-done | bytes 110624 | tf_op jit(solution)/shard_map/ppermute | solution.py:193
  30.1 1.4 %collective-permute-start.5 = (bf16[2,32,1728]{2,1,0:T(8,128)(2,1)S(1)}, bf16[2,32,1728]{2,1,0:T(8,128)(2,1)S(1)}, u32[]{:S(2)}, u32[]{:S(2)}) collective-permute-start(bf16[2,32,1728]{2,1,0:T(8,128)(2,1)S(1)} %pile.1), channel_id=1, source_target_pairs={{1,0},{0,1},{3,2},{2,3},{5,4},{4,5},{7,6},{6,7},{9,8},{8,9},{11,10... | collective-permute-start | bytes 663560 | tf_op jit(solution)/shard_map/ppermute | solution.py:193
  31.5 0.7 %collective-permute-start.6 = (bf16[32,1728]{1,0:T(8,128)(2,1)S(1)}, bf16[32,1728]{1,0:T(8,128)(2,1)S(1)}, u32[]{:S(2)}, u32[]{:S(2)}) collective-permute-start(bf16[32,1728]{1,0:T(8,128)(2,1)S(1)} %grad_pre.1.grad_pre_ref.refs_4_.refs_3_), channel_id=1, source_target_pairs={{1,0},{0,1},{3,2},{2,3},{5,4},{4,5},{7,6},{6,7},{9,8},{8,9},{11,10... | collective-permute-start | bytes 331784 | tf_op jit(solution)/shard_map/ppermute | solution.py:35
  32.2 2.4 %collective-permute-start.7 = (bf16[32,1728]{1,0:T(8,128)(2,1)S(1)}, bf16[32,1728]{1,0:T(8,128)(2,1)S(1)}, u32[]{:S(2)}, u32[]{:S(2)}) collective-permute-start(bf16[32,1728]{1,0:T(8,128)(2,1)S(1)} %grad_pre.1.grad_pre_ref.refs_4_.refs_3_), channel_id=1, source_target_pairs={{2,0},{3,1},{0,2},{1,3},{6,4},{7,5},{4,6},{5,7},{10,8},{11,9},{8,1... | collective-permute-start | bytes 331784 | tf_op jit(solution)/shard_map/ppermute | solution.py:35
  34.5 1.3 %collective-permute-start.8 = (bf16[32,1728]{1,0:T(8,128)(2,1)S(1)}, bf16[32,1728]{1,0:T(8,128)(2,1)S(1)}, u32[]{:S(2)}, u32[]{:S(2)}) collective-permute-start(bf16[32,1728]{1,0:T(8,128)(2,1)S(1)} %grad_pre.1.grad_pre_ref.refs_4_.refs_3_), channel_id=1, source_target_pairs={{3,0},{2,1},{1,2},{0,3},{7,4},{6,5},{5,6},{4,7},{11,8},{10,9},{9,1... | collective-permute-start | bytes 331784 | tf_op jit(solution)/shard_map/ppermute | solution.py:35
  35.9 3.8 %collective-permute-done.5.refs_0_.refs_2_ = bf16[2,32,1728]{2,1,0:T(8,128)(2,1)S(1)} collective-permute-done((bf16[2,32,1728]{2,1,0:T(8,128)(2,1)S(1)}, bf16[2,32,1728]{2,1,0:T(8,128)(2,1)S(1)}, u32[]{:S(2)}, u32[]{:S(2)}) %collective-permute-start.5) | collective-permute-done | bytes 221216 | tf_op jit(solution)/shard_map/ppermute | solution.py:193
  39.7 3.9 %grad_in_part.1 = bf16[8,4,5120]{2,1,0:T(4,128)(2,1)} custom-call(bf16[32,1728]{1,0:T(8,128)(2,1)S(1)} %grad_pre.1.grad_pre_ref.refs_4_.refs_3_, bf16[1728,5120]{1,0:T(8,128)(2,1)S(1)} %bitcast.6, bf16[2,32,1728]{2,1,0:T(8,128)(2,1)S(1)} %collective-permute-done.5.refs_0_.refs_2_), custom_call_target="tpu_custom_call" | custom-call | flops 566231040 | bytes 17694720 | tf_op jit(solution)/shard_map/grad_in_part/pallas_call | solution.py:61
  43.6 3.4 %all-to-all-start = ((bf16[8,4,5120]{2,1,0:T(4,128)(2,1)}), bf16[8,4,5120]{2,1,0:T(4,128)(2,1)S(1)}, u32[]{:S(2)}, u32[]{:S(2)}) async-start(bf16[8,4,5120]{2,1,0:T(4,128)(2,1)} %grad_in_part.1), calls=%async_computation | async-start | bytes 655360 | tf_op jit(solution)/shard_map/all_to_all | solution.py:388
  47.1 4.9 %grad_w.1 = (bf16[1728,1280]{1,0:T(8,128)(2,1)}, bf16[1728,1280]{1,0:T(8,128)(2,1)}, f32[8,128]{1,0:T(8,128)S(1)}) custom-call(bf16[32,1728]{1,0:T(8,128)(2,1)S(1)} %get-tuple-element.13.pre_ref.refs_0_, bf16[1,32,1728]{2,1,0:T(8,128)(2,1)S(1)} %collective-permute-done.4.high.refs_1_, bf16[2,32,1728]{2,1,0:T(8,128)(2,1)S(1)} %collective-permute-done.5.refs_0_.refs_2_, ...), custom_call_target="tpu_custom_call" | custom-call | flops 22649241600 | bytes 88473600 | tf_op jit(solution)/shard_map/grad_w/pallas_call | solution.py:61
  52.1 2.6 %all-to-all-done.terms_ref = bf16[8,4,5120]{2,1,0:T(4,128)(2,1)S(1)} async-done(((bf16[8,4,5120]{2,1,0:T(4,128)(2,1)}), bf16[8,4,5120]{2,1,0:T(4,128)(2,1)S(1)}, u32[]{:S(2)}, u32[]{:S(2)}) %all-to-all-start) | async-done | bytes 327712 | tf_op jit(solution)/shard_map/all_to_all | solution.py:388
  54.6 0.7 %finish.1 = bf16[4,5120]{1,0:T(4,128)(2,1)} custom-call(bf16[8,4,5120]{2,1,0:T(4,128)(2,1)S(1)} %all-to-all-done.terms_ref, f32[8,128]{1,0:T(8,128)S(1)} %get-tuple-element.18.after), custom_call_target="tpu_custom_call" | custom-call | flops 1000000 | bytes 100000 | tf_op jit(solution)/shard_map/finish/pallas_call | solution.py:61
  (49 shorter events, 0.7 us)
Async XLA Ops:
  0.7 5.2 %collective-permute-start = (bf16[4,5120]{1,0:T(4,128)(2,1)}, bf16[4,5120]{1,0:T(4,128)(2,1)S(1)}, u32[]{:S(2)}, u32[]{:S(2)}) collective-permute-start(bf16[4,5120]{1,0:T(4,128)(2,1)} %grad_in.1), channel_id=1, source_target_pairs={{8,0},{12,4},{0,8},{4,12},{24,16},{28,20},{16,24},{20,28},{9,1},{1... | collective-permute-start | bytes 122888 | tf_op jit(solution)/shard_map/ppermute | solution.py:48
  3.7 4.2 %collective-permute-start.1 = (bf16[4,5120]{1,0:T(4,128)(2,1)}, bf16[4,5120]{1,0:T(4,128)(2,1)S(1)}, u32[]{:S(2)}, u32[]{:S(2)}) collective-permute-start(bf16[4,5120]{1,0:T(4,128)(2,1)} %grad_in.1), channel_id=1, source_target_pairs={{16,0},{20,4},{24,8},{28,12},{0,16},{4,20},{8,24},{12,28},{17,1},{... | collective-permute-start | bytes 122888 | tf_op jit(solution)/shard_map/ppermute | solution.py:48
  5.2 5.1 %collective-permute-start.2 = (bf16[4,5120]{1,0:T(4,128)(2,1)}, bf16[4,5120]{1,0:T(4,128)(2,1)S(1)}, u32[]{:S(2)}, u32[]{:S(2)}) collective-permute-start(bf16[4,5120]{1,0:T(4,128)(2,1)} %grad_in.1), channel_id=1, source_target_pairs={{24,0},{28,4},{16,8},{20,12},{8,16},{12,20},{0,24},{4,28},{25,1},{... | collective-permute-start | bytes 122888 | tf_op jit(solution)/shard_map/ppermute | solution.py:48
  5.2 9.5 %slice-start.1 = ((s8[17694720]{0:T(1024)(128)(4,1)}), s8[4194304]{0:T(1024)(128)(4,1)S(1)}, s32[]{:S(2)}) async-start(s8[17694720]{0:T(1024)(128)(4,1)} %bitcast.2), calls=%async_computation.2 | async-start | bytes 8388608
  5.2 9.5 %slice-start.2 = ((s8[17694720]{0:T(1024)(128)(4,1)}), s8[4194304]{0:T(1024)(128)(4,1)S(1)}, s32[]{:S(2)}) async-start(s8[17694720]{0:T(1024)(128)(4,1)} %bitcast.2), calls=%async_computation.3 | async-start | bytes 8388608
  5.3 34.4 %slice-start.5 = ((s8[17694720]{0:T(1024)(128)(4,1)}), s8[4194304]{0:T(1024)(128)(4,1)S(1)}, s32[]{:S(2)}) async-start(s8[17694720]{0:T(1024)(128)(4,1)} %bitcast.4), calls=%async_computation.6 | async-start | bytes 8388608
  5.3 34.4 %slice-start.6 = ((s8[17694720]{0:T(1024)(128)(4,1)}), s8[4194304]{0:T(1024)(128)(4,1)S(1)}, s32[]{:S(2)}) async-start(s8[17694720]{0:T(1024)(128)(4,1)} %bitcast.4), calls=%async_computation.7 | async-start | bytes 8388608
  5.3 34.4 %slice-start.7 = ((s8[17694720]{0:T(1024)(128)(4,1)}), s8[4194304]{0:T(1024)(128)(4,1)S(1)}, s32[]{:S(2)}) async-start(s8[17694720]{0:T(1024)(128)(4,1)} %bitcast.4), calls=%async_computation.8 | async-start | bytes 8388608
  5.3 34.4 %slice-start.8 = ((s8[17694720]{0:T(1024)(128)(4,1)}), s8[4194304]{0:T(1024)(128)(4,1)S(1)}, s32[]{:S(2)}) async-start(s8[17694720]{0:T(1024)(128)(4,1)} %bitcast.4), calls=%async_computation.9 | async-start | bytes 8388608
  10.3 4.3 %collective-permute-start.3 = (bf16[16,5120]{1,0:T(8,128)(2,1)S(1)}, bf16[16,5120]{1,0:T(8,128)(2,1)S(1)}, u32[]{:S(2)}, u32[]{:S(2)}) collective-permute-start(bf16[16,5120]{1,0:T(8,128)(2,1)S(1)} %join.1.own_ref), channel_id=1, source_target_pairs={{4,0},{0,4},{12,8},{8,12},{20,16},{16,20},{28,24},{24,28},{5,1},{1... | collective-permute-start | bytes 491528 | tf_op jit(solution)/shard_map/ppermute | solution.py:39
  10.4 9.2 %collective-permute-start.10 = (bf16[8,1280]{1,0:T(8,128)(2,1)S(1)}, bf16[8,1280]{1,0:T(8,128)(2,1)S(1)}, u32[]{:S(2)}, u32[]{:S(2)}) collective-permute-start(bf16[8,1280]{1,0:T(8,128)(2,1)S(1)} %get-tuple-element.16), channel_id=1, source_target_pairs={{2,0},{3,1},{0,2},{1,3},{6,4},{7,5},{4,6},{5,7},{10,8},{11,9},{8,1... | collective-permute-start | bytes 61448 | tf_op jit(solution)/shard_map/ppermute | solution.py:35
  13.1 6.6 %collective-permute-start.11 = (bf16[8,1280]{1,0:T(8,128)(2,1)S(1)}, bf16[8,1280]{1,0:T(8,128)(2,1)S(1)}, u32[]{:S(2)}, u32[]{:S(2)}) collective-permute-start(bf16[8,1280]{1,0:T(8,128)(2,1)S(1)} %get-tuple-element.17), channel_id=1, source_target_pairs={{3,0},{2,1},{1,2},{0,3},{7,4},{6,5},{5,6},{4,7},{11,8},{10,9},{9,1... | collective-permute-start | bytes 61448 | tf_op jit(solution)/shard_map/ppermute | solution.py:35
  14.4 5.3 %collective-permute-start.9 = (bf16[8,1280]{1,0:T(8,128)(2,1)S(1)}, bf16[8,1280]{1,0:T(8,128)(2,1)S(1)}, u32[]{:S(2)}, u32[]{:S(2)}) collective-permute-start(bf16[8,1280]{1,0:T(8,128)(2,1)S(1)} %get-tuple-element.15), channel_id=1, source_target_pairs={{1,0},{0,1},{3,2},{2,3},{5,4},{4,5},{7,6},{6,7},{9,8},{8,9},{11,10... | collective-permute-start | bytes 61448 | tf_op jit(solution)/shard_map/ppermute | solution.py:35
  14.7 25.0 %slice-start.9 = ((s8[17694720]{0:T(1024)(128)(4,1)}), s8[917504]{0:T(1024)(128)(4,1)S(1)}, s32[]{:S(2)}) async-start(s8[17694720]{0:T(1024)(128)(4,1)} %bitcast.4), calls=%async_computation.10 | async-start | bytes 1835008
  19.7 6.6 %collective-permute-start.12 = (bf16[2,16,1280]{2,1,0:T(8,128)(2,1)S(1)}, bf16[2,16,1280]{2,1,0:T(8,128)(2,1)S(1)}, u32[]{:S(2)}, u32[]{:S(2)}) collective-permute-start(bf16[2,16,1280]{2,1,0:T(8,128)(2,1)S(1)} %sort.1.refs_0_), channel_id=1, source_target_pairs={{8,0},{12,4},{0,8},{4,12},{24,16},{28,20},{16,24},{20,28},{9,1},{1... | collective-permute-start | bytes 245768 | tf_op jit(solution)/shard_map/ppermute | solution.py:48
  20.3 6.0 %collective-permute-start.13 = (bf16[2,16,1280]{2,1,0:T(8,128)(2,1)S(1)}, bf16[2,16,1280]{2,1,0:T(8,128)(2,1)S(1)}, u32[]{:S(2)}, u32[]{:S(2)}) collective-permute-start(bf16[2,16,1280]{2,1,0:T(8,128)(2,1)S(1)} %sort.1.refs_0_), channel_id=1, source_target_pairs={{16,0},{20,4},{24,8},{28,12},{0,16},{4,20},{8,24},{12,28},{17,1},{... | collective-permute-start | bytes 245768 | tf_op jit(solution)/shard_map/ppermute | solution.py:48
  20.8 5.5 %collective-permute-start.14 = (bf16[2,16,1280]{2,1,0:T(8,128)(2,1)S(1)}, bf16[2,16,1280]{2,1,0:T(8,128)(2,1)S(1)}, u32[]{:S(2)}, u32[]{:S(2)}) collective-permute-start(bf16[2,16,1280]{2,1,0:T(8,128)(2,1)S(1)} %sort.1.refs_0_), channel_id=1, source_target_pairs={{24,0},{28,4},{16,8},{20,12},{8,16},{12,20},{0,24},{4,28},{25,1},{... | collective-permute-start | bytes 245768 | tf_op jit(solution)/shard_map/ppermute | solution.py:48
  23.3 6.8 %collective-permute-start.4 = (bf16[1,32,1728]{2,1,0:T(8,128)(2,1)S(1)}, bf16[1,32,1728]{2,1,0:T(8,128)(2,1)S(1)}, u32[]{:S(2)}, u32[]{:S(2)}) collective-permute-start(bf16[1,32,1728]{2,1,0:T(8,128)(2,1)S(1)} %stack.2.low), channel_id=1, source_target_pairs={{3,0},{2,1},{1,2},{0,3},{7,4},{6,5},{5,6},{4,7},{11,8},{10,9},{9,1... | collective-permute-start | bytes 331784 | tf_op jit(solution)/shard_map/ppermute | solution.py:193
  26.4 20.7 %collective-permute-start.15 = (bf16[4,2,16,1280]{3,2,1,0:T(8,128)(2,1)S(1)}, bf16[4,2,16,1280]{3,2,1,0:T(8,128)(2,1)S(1)}, u32[]{:S(2)}, u32[]{:S(2)}) collective-permute-start(bf16[4,2,16,1280]{3,2,1,0:T(8,128)(2,1)S(1)} %stack.3.refs_7_), channel_id=1, source_target_pairs={{4,0},{0,4},{12,8},{8,12},{20,16},{16,20},{28,24},{24,28},{5,1},{1... | collective-permute-start | bytes 983048 | tf_op jit(solution)/shard_map/ppermute | solution.py:39
  30.1 9.6 %collective-permute-start.5 = (bf16[2,32,1728]{2,1,0:T(8,128)(2,1)S(1)}, bf16[2,32,1728]{2,1,0:T(8,128)(2,1)S(1)}, u32[]{:S(2)}, u32[]{:S(2)}) collective-permute-start(bf16[2,32,1728]{2,1,0:T(8,128)(2,1)S(1)} %pile.1), channel_id=1, source_target_pairs={{1,0},{0,1},{3,2},{2,3},{5,4},{4,5},{7,6},{6,7},{9,8},{8,9},{11,10... | collective-permute-start | bytes 663560 | tf_op jit(solution)/shard_map/ppermute | solution.py:193
  31.5 15.6 %collective-permute-start.6 = (bf16[32,1728]{1,0:T(8,128)(2,1)S(1)}, bf16[32,1728]{1,0:T(8,128)(2,1)S(1)}, u32[]{:S(2)}, u32[]{:S(2)}) collective-permute-start(bf16[32,1728]{1,0:T(8,128)(2,1)S(1)} %grad_pre.1.grad_pre_ref.refs_4_.refs_3_), channel_id=1, source_target_pairs={{1,0},{0,1},{3,2},{2,3},{5,4},{4,5},{7,6},{6,7},{9,8},{8,9},{11,10... | collective-permute-start | bytes 331784 | tf_op jit(solution)/shard_map/ppermute | solution.py:35
  32.2 14.9 %collective-permute-start.7 = (bf16[32,1728]{1,0:T(8,128)(2,1)S(1)}, bf16[32,1728]{1,0:T(8,128)(2,1)S(1)}, u32[]{:S(2)}, u32[]{:S(2)}) collective-permute-start(bf16[32,1728]{1,0:T(8,128)(2,1)S(1)} %grad_pre.1.grad_pre_ref.refs_4_.refs_3_), channel_id=1, source_target_pairs={{2,0},{3,1},{0,2},{1,3},{6,4},{7,5},{4,6},{5,7},{10,8},{11,9},{8,1... | collective-permute-start | bytes 331784 | tf_op jit(solution)/shard_map/ppermute | solution.py:35
  34.5 12.5 %collective-permute-start.8 = (bf16[32,1728]{1,0:T(8,128)(2,1)S(1)}, bf16[32,1728]{1,0:T(8,128)(2,1)S(1)}, u32[]{:S(2)}, u32[]{:S(2)}) collective-permute-start(bf16[32,1728]{1,0:T(8,128)(2,1)S(1)} %grad_pre.1.grad_pre_ref.refs_4_.refs_3_), channel_id=1, source_target_pairs={{3,0},{2,1},{1,2},{0,3},{7,4},{6,5},{5,6},{4,7},{11,8},{10,9},{9,1... | collective-permute-start | bytes 331784 | tf_op jit(solution)/shard_map/ppermute | solution.py:35
  43.6 11.0 %all-to-all-start = ((bf16[8,4,5120]{2,1,0:T(4,128)(2,1)}), bf16[8,4,5120]{2,1,0:T(4,128)(2,1)S(1)}, u32[]{:S(2)}, u32[]{:S(2)}) async-start(bf16[8,4,5120]{2,1,0:T(4,128)(2,1)} %grad_in_part.1), calls=%async_computation | async-start | bytes 655360 | tf_op jit(solution)/shard_map/all_to_all | solution.py:388
  (6 other events, 42.1 us)

commit v12 on v11

--- a/solution.py
+++ b/solution.py
@@ -135,16 +135,16 @@
     )
 
 
-def join_body(*refs):
+def join_body(after, *refs):
     *pieces, out = refs
     out[...] = jnp.concatenate([x[...].astype(jnp.float32) for x in pieces], axis=0).astype(
         jnp.bfloat16
     )
 
 
-def join(pieces):
+def join(pieces, after):
     shape = (sum(x.shape[0] for x in pieces), pieces[0].shape[1])
-    return call(join_body, [(shape, jnp.bfloat16)], pieces, "join")[0]
+    return call(join_body, [(shape, jnp.bfloat16)], [after, *pieces], "join")[0]
 
 
 def sort_body(count, *refs):
@@ -177,18 +177,21 @@
 
 
 def pile_body(low, high, out):
-    count = low.shape[0]
-    out[:count] = low[...]
-    out[count:] = high[...]
+    count = out.shape[0] // 2
+    if count == 1:
+        out[0] = low[...]
+        out[1] = high[...]
+    else:
+        out[:count] = low[...]
+        out[count:] = high[...]
 
 
 def spread(x, masks):
-    held, got, order = stack([x]), [], [0]
-    where = {}
+    held, got, order, where = x, [], [0], {0: (0, 0)}
     n = lax.axis_size("tokens")
     for mask in masks:
         if got:
-            shape = (2 * held.shape[0],) + held.shape[1:]
+            shape = (len(order),) + x.shape
             held = call(pile_body, [(shape, jnp.bfloat16)], [held, got[-1]], "pile")[0]
         got.append(lax.ppermute(held, "tokens", [(i ^ mask, i) for i in range(n)]))
         for j, k in enumerate(order):
@@ -331,7 +334,8 @@
 
     for k in range(places):
         array, j = where[k]
-        pre = (pre_refs[array][j] if array else pre_refs[0][...]).astype(jnp.float32)
+        ref = pre_refs[array]
+        pre = (ref[...] if len(ref.shape) == 2 else ref[j]).astype(jnp.float32)
         flat[k * group : (k + 1) * group, :] = gelu_value(pre).astype(jnp.bfloat16)
     arrange(lambda b: place_of(b, chips))
     product(1, held_out, out_ref)
@@ -373,19 +377,18 @@
     chips = n_mp // 2
     scale_back = 1.0 / math.sqrt(pre_act.shape[0] * n_tok)
 
-    *pieces, own_piece, pre_act, own_grad = pack(tokens_in, grad_out, pre_act, n_tok, lead())
-    own_rows = join([own_grad] + [fetch_chip(grad_out, k) for k in range(1, chips)])
-    other_rows = other_core(own_rows)
     masks = (3, 1) if n_tok == 4 else [1 << i for i in range(n_tok.bit_length() - 1)]
     held, pre, where = spread(pre_act, masks)
-    where[0] = (0, 0)
+    *pieces, own_piece, pre_act, own_grad = pack(tokens_in, grad_out, pre_act, n_tok, lead())
+    own_rows = join([own_grad] + [fetch_chip(grad_out, k) for k in range(1, chips)], held)
+    other_rows = other_core(own_rows)
     pieces = [fetch(x, "tokens", k) for k, x in enumerate(pieces, 1)]
     grad_pre = grad_pre_of(own_rows, other_rows, pre_act, w_out)
     cols = sort([own_piece, *pieces], [grad_pre])
     own_cols = stack([cols] + [fetch_chip(cols, k) for k in range(1, chips)])
     other_cols = other_core(own_cols)
     grad_pre_all = [grad_pre] + [fetch(grad_pre, "tokens", k) for k in range(1, n_tok)]
-    terms = lax.all_to_all(grad_in_part(grad_pre, w_in.T, n_mp, [pre[-1]]), "mp", 0, 0)
+    terms = lax.all_to_all(grad_in_part(grad_pre, w_in.T, n_mp, []), "mp", 0, 0)
     grad_w_in_t, grad_w_out, end = grad_w_of(
         [pre_act, *pre], where, grad_pre_all, own_cols, other_cols, scale_back
     )

time: 55.5 us -> 54.5 us (0.982)
  waiting for transfers between devices: 14.7 us -> 12.2 us
  starting transfers between devices: 24.7 us -> 26.3 us
    ppermute x2, waiting for transfers between devices: 7.38 us -> 2.61 us  [spread(): got.append(lax.ppermute(held, 'tokens', [(i ^ mask, i) for i in range(n)]))]
    ppermute x6, waiting for transfers between devices: 0.02 us -> 4.68 us  [fetch(): return lax.ppermute(x, axis, [(partner(i, k, n), i) for i in range(n)])]
    all_to_all x1, waiting for transfers between devices: 2.59 us -> 0.01 us  [shards(): terms = lax.all_to_all(grad_in_part(grad_pre, w_in.T, n_mp, []), 'mp', 0, 0)]
    ppermute x2, starting transfers between devices: 4.42 us -> 5.72 us  [spread(): got.append(lax.ppermute(held, 'tokens', [(i ^ mask, i) for i in range(n)]))]
    pallas_call x11 -> x10, Pallas kernels: 14.9 us -> 14.9 us  [call(): pl.pallas_call(body, in_specs=[pl.BlockSpec(memory_space=in_space)] * len...]
  transfers between devices with their start and end apart: 17 -> 17, of which waited for: 7 -> 5; matrix products, arithmetic and copies ran while one was open for 0% -> 0% of each run, Pallas kernels for 26% -> 26%
where the time goes in v12:
time: 54.5 us; the launch traced here: 54.3 us
  starting transfers between devices  26.3 us (48%)
  Pallas kernels  14.9 us (27%)
  waiting for transfers between devices  12.2 us (22%)
  between operations  0.95 us (2%)
    pallas_call x10, Pallas kernels, call(): pl.pallas_call(body, in_specs=[pl.BlockSpec(memory_space=in_space)] * len...  14.9 us
    ppermute x6, starting transfers between devices, fetch(): return lax.ppermute(x, axis, [(partner(i, k, n), i) for i in range(n)])  8.89 us
    ppermute x6, starting transfers between devices, fetch_chip(): lax.ppermute(x, 'mp', [(there, here) for here, there in chip_pairs(k)])  8.1 us
    ppermute x2, starting transfers between devices, spread(): got.append(lax.ppermute(held, 'tokens', [(i ^ mask, i) for i in range(n)]))  5.72 us
    ppermute x6, waiting for transfers between devices, fetch_chip(): lax.ppermute(x, 'mp', [(there, here) for here, there in chip_pairs(k)])  4.87 us
    ppermute x6, waiting for transfers between devices, fetch(): return lax.ppermute(x, axis, [(partner(i, k, n), i) for i in range(n)])  4.68 us
    all_to_all x1, starting transfers between devices, shards(): terms = lax.all_to_all(grad_in_part(grad_pre, w_in.T, n_mp, []), 'mp', 0, 0)  3.43 us
    ppermute x2, waiting for transfers between devices, spread(): got.append(lax.ppermute(held, 'tokens', [(i ^ mask, i) for i in range(n)]))  2.61 us
  transfers between devices with their start and end apart: 17, of which 5 were waited for; matrix products, arithmetic and copies ran while one was open for 0% of the time, Pallas kernels for 26%

profile of v12, /device:TPU:0, one launch (start us, length us, event | category | flops | bytes accessed | tf_op | source)
XLA Modules:
  0.0 54.3 jit_solution(16630379287296220428)
XLA Ops:
  0.7 3.0 %collective-permute-start.1 = (bf16[4,5120]{1,0:T(4,128)(2,1)}, bf16[4,5120]{1,0:T(4,128)(2,1)S(1)}, u32[]{:S(2)}, u32[]{:S(2)}) collective-permute-start(bf16[4,5120]{1,0:T(4,128)(2,1)} %grad_in.1), channel_id=1, source_target_pairs={{8,0},{12,4},{0,8},{4,12},{24,16},{28,20},{16,24},{20,28},{9,1},{1... | collective-permute-start | bytes 122888 | tf_op jit(solution)/shard_map/ppermute | solution.py:48
  3.7 1.5 %collective-permute-start.2 = (bf16[4,5120]{1,0:T(4,128)(2,1)}, bf16[4,5120]{1,0:T(4,128)(2,1)S(1)}, u32[]{:S(2)}, u32[]{:S(2)}) collective-permute-start(bf16[4,5120]{1,0:T(4,128)(2,1)} %grad_in.1), channel_id=1, source_target_pairs={{16,0},{20,4},{24,8},{28,12},{0,16},{4,20},{8,24},{12,28},{17,1},{... | collective-permute-start | bytes 122888 | tf_op jit(solution)/shard_map/ppermute | solution.py:48
  5.2 4.1 %collective-permute-start = (bf16[32,1728]{1,0:T(8,128)(2,1)}, bf16[32,1728]{1,0:T(8,128)(2,1)S(1)}, u32[]{:S(2)}, u32[]{:S(2)}) collective-permute-start(bf16[32,1728]{1,0:T(8,128)(2,1)} %pre_in.1), channel_id=1, source_target_pairs={{3,0},{2,1},{1,2},{0,3},{7,4},{6,5},{5,6},{4,7},{11,8},{10,9},{9,1... | collective-permute-start | bytes 331784 | tf_op jit(solution)/shard_map/ppermute | solution.py:196
  9.4 0.3 pack.1
  9.7 2.6 %collective-permute-done.high.refs_1_ = bf16[32,1728]{1,0:T(8,128)(2,1)S(1)} collective-permute-done((bf16[32,1728]{1,0:T(8,128)(2,1)}, bf16[32,1728]{1,0:T(8,128)(2,1)S(1)}, u32[]{:S(2)}, u32[]{:S(2)}) %collective-permute-start) | collective-permute-done | bytes 110624 | tf_op jit(solution)/shard_map/ppermute | solution.py:196
  12.5 3.4 %collective-permute-start.10 = (bf16[8,1280]{1,0:T(8,128)(2,1)S(1)}, bf16[8,1280]{1,0:T(8,128)(2,1)S(1)}, u32[]{:S(2)}, u32[]{:S(2)}) collective-permute-start(bf16[8,1280]{1,0:T(8,128)(2,1)S(1)} %get-tuple-element.16), channel_id=1, source_target_pairs={{2,0},{3,1},{0,2},{1,3},{6,4},{7,5},{4,6},{5,7},{10,8},{11,9},{8,1... | collective-permute-start | bytes 61448 | tf_op jit(solution)/shard_map/ppermute | solution.py:35
  15.9 0.7 %collective-permute-start.11 = (bf16[8,1280]{1,0:T(8,128)(2,1)S(1)}, bf16[8,1280]{1,0:T(8,128)(2,1)S(1)}, u32[]{:S(2)}, u32[]{:S(2)}) collective-permute-start(bf16[8,1280]{1,0:T(8,128)(2,1)S(1)} %get-tuple-element.17), channel_id=1, source_target_pairs={{3,0},{2,1},{1,2},{0,3},{7,4},{6,5},{5,6},{4,7},{11,8},{10,9},{9,1... | collective-permute-start | bytes 61448 | tf_op jit(solution)/shard_map/ppermute | solution.py:35
  16.6 0.4 collective-permute-start.9
  17.1 4.9 %grad_pre.1.grad_pre_ref.refs_4_.refs_3_ = bf16[32,1728]{1,0:T(8,128)(2,1)S(1)} custom-call(bf16[16,5120]{1,0:T(8,128)(2,1)S(1)} %join.1.own_ref, bf16[16,5120]{1,0:T(8,128)(2,1)S(1)} %collective-permute-done.4.other_ref, bf16[32,1728]{1,0:T(8,128)(2,1)S(1)} %get-tuple-element.13.pre_ref.refs_0_, bf16[1728,5120]{1,0:T(8,128)(2,1)S(1)} %bitcast.6), custom_call_target="tpu_custom_call" | custom-call | flops 566231040 | bytes 17694720 | tf_op jit(solution)/shard_map/grad_pre/pallas_call | solution.py:61
  22.1 1.6 %collective-permute-start.12 = (bf16[2,16,1280]{2,1,0:T(8,128)(2,1)S(1)}, bf16[2,16,1280]{2,1,0:T(8,128)(2,1)S(1)}, u32[]{:S(2)}, u32[]{:S(2)}) collective-permute-start(bf16[2,16,1280]{2,1,0:T(8,128)(2,1)S(1)} %sort.1.refs_0_), channel_id=1, source_target_pairs={{8,0},{12,4},{0,8},{4,12},{24,16},{28,20},{16,24},{20,28},{9,1},{1... | collective-permute-start | bytes 245768 | tf_op jit(solution)/shard_map/ppermute | solution.py:48
  23.6 1.5 %collective-permute-start.13 = (bf16[2,16,1280]{2,1,0:T(8,128)(2,1)S(1)}, bf16[2,16,1280]{2,1,0:T(8,128)(2,1)S(1)}, u32[]{:S(2)}, u32[]{:S(2)}) collective-permute-start(bf16[2,16,1280]{2,1,0:T(8,128)(2,1)S(1)} %sort.1.refs_0_), channel_id=1, source_target_pairs={{16,0},{20,4},{24,8},{28,12},{0,16},{4,20},{8,24},{12,28},{17,1},{... | collective-permute-start | bytes 245768 | tf_op jit(solution)/shard_map/ppermute | solution.py:48
  25.1 0.5 collective-permute-start.14
  25.6 1.0 %collective-permute-done.12.refs_1_ = bf16[2,16,1280]{2,1,0:T(8,128)(2,1)S(1)} collective-permute-done((bf16[2,16,1280]{2,1,0:T(8,128)(2,1)S(1)}, bf16[2,16,1280]{2,1,0:T(8,128)(2,1)S(1)}, u32[]{:S(2)}, u32[]{:S(2)}) %collective-permute-start.12) | collective-permute-done | bytes 81952 | tf_op jit(solution)/shard_map/ppermute | solution.py:48
  26.6 1.5 %collective-permute-done.13.refs_2_ = bf16[2,16,1280]{2,1,0:T(8,128)(2,1)S(1)} collective-permute-done((bf16[2,16,1280]{2,1,0:T(8,128)(2,1)S(1)}, bf16[2,16,1280]{2,1,0:T(8,128)(2,1)S(1)}, u32[]{:S(2)}, u32[]{:S(2)}) %collective-permute-start.13) | collective-permute-done | bytes 81952 | tf_op jit(solution)/shard_map/ppermute | solution.py:48
  28.1 2.4 %collective-permute-done.14.refs_3_ = bf16[2,16,1280]{2,1,0:T(8,128)(2,1)S(1)} collective-permute-done((bf16[2,16,1280]{2,1,0:T(8,128)(2,1)S(1)}, bf16[2,16,1280]{2,1,0:T(8,128)(2,1)S(1)}, u32[]{:S(2)}, u32[]{:S(2)}) %collective-permute-start.14) | collective-permute-done | bytes 81952 | tf_op jit(solution)/shard_map/ppermute | solution.py:48
  30.6 1.7 %collective-permute-start.5 = (bf16[2,32,1728]{2,1,0:T(8,128)(2,1)S(1)}, bf16[2,32,1728]{2,1,0:T(8,128)(2,1)S(1)}, u32[]{:S(2)}, u32[]{:S(2)}) collective-permute-start(bf16[2,32,1728]{2,1,0:T(8,128)(2,1)S(1)} %pile.1.after), channel_id=1, source_target_pairs={{1,0},{0,1},{3,2},{2,3},{5,4},{4,5},{7,6},{6,7},{9,8},{8,9},{11,10... | collective-permute-start | bytes 663560 | tf_op jit(solution)/shard_map/ppermute | solution.py:196
  32.2 0.4 collective-permute-start.6
  32.7 3.3 %collective-permute-start.7 = (bf16[32,1728]{1,0:T(8,128)(2,1)S(1)}, bf16[32,1728]{1,0:T(8,128)(2,1)S(1)}, u32[]{:S(2)}, u32[]{:S(2)}) collective-permute-start(bf16[32,1728]{1,0:T(8,128)(2,1)S(1)} %grad_pre.1.grad_pre_ref.refs_4_.refs_3_), channel_id=1, source_target_pairs={{2,0},{3,1},{0,2},{1,3},{6,4},{7,5},{4,6},{5,7},{10,8},{11,9},{8,1... | collective-permute-start | bytes 331784 | tf_op jit(solution)/shard_map/ppermute | solution.py:35
  36.0 0.7 %collective-permute-start.8 = (bf16[32,1728]{1,0:T(8,128)(2,1)S(1)}, bf16[32,1728]{1,0:T(8,128)(2,1)S(1)}, u32[]{:S(2)}, u32[]{:S(2)}) collective-permute-start(bf16[32,1728]{1,0:T(8,128)(2,1)S(1)} %grad_pre.1.grad_pre_ref.refs_4_.refs_3_), channel_id=1, source_target_pairs={{3,0},{2,1},{1,2},{0,3},{7,4},{6,5},{5,6},{4,7},{11,8},{10,9},{9,1... | collective-permute-start | bytes 331784 | tf_op jit(solution)/shard_map/ppermute | solution.py:35
  36.7 3.9 %grad_in_part.1 = bf16[8,4,5120]{2,1,0:T(4,128)(2,1)} custom-call(bf16[32,1728]{1,0:T(8,128)(2,1)S(1)} %grad_pre.1.grad_pre_ref.refs_4_.refs_3_, bf16[1728,5120]{1,0:T(8,128)(2,1)S(1)} %bitcast.4), custom_call_target="tpu_custom_call" | custom-call | flops 566231040 | bytes 17694720 | tf_op jit(solution)/shard_map/grad_in_part/pallas_call | solution.py:61
  40.6 3.4 %all-to-all-start = ((bf16[8,4,5120]{2,1,0:T(4,128)(2,1)}), bf16[8,4,5120]{2,1,0:T(4,128)(2,1)S(1)}, u32[]{:S(2)}, u32[]{:S(2)}) async-start(bf16[8,4,5120]{2,1,0:T(4,128)(2,1)} %grad_in_part.1), calls=%async_computation | async-start | bytes 655360 | tf_op jit(solution)/shard_map/all_to_all | solution.py:391
  44.0 4.7 %collective-permute-done.8.refs_6_ = bf16[32,1728]{1,0:T(8,128)(2,1)S(1)} collective-permute-done((bf16[32,1728]{1,0:T(8,128)(2,1)S(1)}, bf16[32,1728]{1,0:T(8,128)(2,1)S(1)}, u32[]{:S(2)}, u32[]{:S(2)}) %collective-permute-start.8) | collective-permute-done | bytes 110624 | tf_op jit(solution)/shard_map/ppermute | solution.py:35
  48.7 4.9 %grad_w.1 = (bf16[1728,1280]{1,0:T(8,128)(2,1)}, bf16[1728,1280]{1,0:T(8,128)(2,1)}, f32[8,128]{1,0:T(8,128)S(1)}) custom-call(bf16[32,1728]{1,0:T(8,128)(2,1)S(1)} %get-tuple-element.13.pre_ref.refs_0_, bf16[32,1728]{1,0:T(8,128)(2,1)S(1)} %collective-permute-done.high.refs_1_, bf16[2,32,1728]{2,1,0:T(8,128)(2,1)S(1)} %collective-permute-done.5.refs_2_, ...), custom_call_target="tpu_custom_call" | custom-call | flops 22649241600 | bytes 88473600 | tf_op jit(solution)/shard_map/grad_w/pallas_call | solution.py:61
  53.7 0.7 %finish.1 = bf16[4,5120]{1,0:T(4,128)(2,1)} custom-call(bf16[8,4,5120]{2,1,0:T(4,128)(2,1)S(1)} %all-to-all-done.terms_ref, f32[8,128]{1,0:T(8,128)S(1)} %get-tuple-element.18.after), custom_call_target="tpu_custom_call" | custom-call | flops 1000000 | bytes 100000 | tf_op jit(solution)/shard_map/finish/pallas_call | solution.py:61
  (48 shorter events, 0.4 us)
Async XLA Ops:
  0.6 8.6 %copy-start.2 = (bf16[4,5120]{1,0:T(4,128)(2,1)S(1)}, bf16[4,5120]{1,0:T(4,128)(2,1)}, u32[]{:S(2)}) copy-start(bf16[4,5120]{1,0:T(4,128)(2,1)} %grad_in.1) | copy-start | bytes 122884
  0.6 8.6 %copy-start = (bf16[32,1728]{1,0:T(8,128)(2,1)S(1)}, bf16[32,1728]{1,0:T(8,128)(2,1)}, u32[]{:S(2)}) copy-start(bf16[32,1728]{1,0:T(8,128)(2,1)} %pre_in.1) | copy-start | bytes 331780
  0.7 11.7 %collective-permute-start.1 = (bf16[4,5120]{1,0:T(4,128)(2,1)}, bf16[4,5120]{1,0:T(4,128)(2,1)S(1)}, u32[]{:S(2)}, u32[]{:S(2)}) collective-permute-start(bf16[4,5120]{1,0:T(4,128)(2,1)} %grad_in.1), channel_id=1, source_target_pairs={{8,0},{12,4},{0,8},{4,12},{24,16},{28,20},{16,24},{20,28},{9,1},{1... | collective-permute-start | bytes 122888 | tf_op jit(solution)/shard_map/ppermute | solution.py:48
  3.7 8.7 %collective-permute-start.2 = (bf16[4,5120]{1,0:T(4,128)(2,1)}, bf16[4,5120]{1,0:T(4,128)(2,1)S(1)}, u32[]{:S(2)}, u32[]{:S(2)}) collective-permute-start(bf16[4,5120]{1,0:T(4,128)(2,1)} %grad_in.1), channel_id=1, source_target_pairs={{16,0},{20,4},{24,8},{28,12},{0,16},{4,20},{8,24},{12,28},{17,1},{... | collective-permute-start | bytes 122888 | tf_op jit(solution)/shard_map/ppermute | solution.py:48
  5.2 7.2 %collective-permute-start.3 = (bf16[4,5120]{1,0:T(4,128)(2,1)}, bf16[4,5120]{1,0:T(4,128)(2,1)S(1)}, u32[]{:S(2)}, u32[]{:S(2)}) collective-permute-start(bf16[4,5120]{1,0:T(4,128)(2,1)} %grad_in.1), channel_id=1, source_target_pairs={{24,0},{28,4},{16,8},{20,12},{8,16},{12,20},{0,24},{4,28},{25,1},{... | collective-permute-start | bytes 122888 | tf_op jit(solution)/shard_map/ppermute | solution.py:48
  5.2 7.1 %collective-permute-start = (bf16[32,1728]{1,0:T(8,128)(2,1)}, bf16[32,1728]{1,0:T(8,128)(2,1)S(1)}, u32[]{:S(2)}, u32[]{:S(2)}) collective-permute-start(bf16[32,1728]{1,0:T(8,128)(2,1)} %pre_in.1), channel_id=1, source_target_pairs={{3,0},{2,1},{1,2},{0,3},{7,4},{6,5},{5,6},{4,7},{11,8},{10,9},{9,1... | collective-permute-start | bytes 331784 | tf_op jit(solution)/shard_map/ppermute | solution.py:196
  9.3 27.3 %slice-start = ((s8[17694720]{0:T(1024)(128)(4,1)}), s8[4194304]{0:T(1024)(128)(4,1)S(1)}, s32[]{:S(2)}) async-start(s8[17694720]{0:T(1024)(128)(4,1)} %bitcast.2), calls=%async_computation.1 | async-start | bytes 8388608
  9.3 27.3 %slice-start.1 = ((s8[17694720]{0:T(1024)(128)(4,1)}), s8[4194304]{0:T(1024)(128)(4,1)S(1)}, s32[]{:S(2)}) async-start(s8[17694720]{0:T(1024)(128)(4,1)} %bitcast.2), calls=%async_computation.2 | async-start | bytes 8388608
  9.4 27.3 %slice-start.2 = ((s8[17694720]{0:T(1024)(128)(4,1)}), s8[4194304]{0:T(1024)(128)(4,1)S(1)}, s32[]{:S(2)}) async-start(s8[17694720]{0:T(1024)(128)(4,1)} %bitcast.2), calls=%async_computation.3 | async-start | bytes 8388608
  9.4 27.3 %slice-start.3 = ((s8[17694720]{0:T(1024)(128)(4,1)}), s8[4194304]{0:T(1024)(128)(4,1)S(1)}, s32[]{:S(2)}) async-start(s8[17694720]{0:T(1024)(128)(4,1)} %bitcast.2), calls=%async_computation.4 | async-start | bytes 8388608
  12.4 4.6 %collective-permute-start.4 = (bf16[16,5120]{1,0:T(8,128)(2,1)S(1)}, bf16[16,5120]{1,0:T(8,128)(2,1)S(1)}, u32[]{:S(2)}, u32[]{:S(2)}) collective-permute-start(bf16[16,5120]{1,0:T(8,128)(2,1)S(1)} %join.1.own_ref), channel_id=1, source_target_pairs={{4,0},{0,4},{12,8},{8,12},{20,16},{16,20},{28,24},{24,28},{5,1},{1... | collective-permute-start | bytes 491528 | tf_op jit(solution)/shard_map/ppermute | solution.py:39
  12.5 9.5 %collective-permute-start.10 = (bf16[8,1280]{1,0:T(8,128)(2,1)S(1)}, bf16[8,1280]{1,0:T(8,128)(2,1)S(1)}, u32[]{:S(2)}, u32[]{:S(2)}) collective-permute-start(bf16[8,1280]{1,0:T(8,128)(2,1)S(1)} %get-tuple-element.16), channel_id=1, source_target_pairs={{2,0},{3,1},{0,2},{1,3},{6,4},{7,5},{4,6},{5,7},{10,8},{11,9},{8,1... | collective-permute-start | bytes 61448 | tf_op jit(solution)/shard_map/ppermute | solution.py:35
  15.9 6.1 %collective-permute-start.11 = (bf16[8,1280]{1,0:T(8,128)(2,1)S(1)}, bf16[8,1280]{1,0:T(8,128)(2,1)S(1)}, u32[]{:S(2)}, u32[]{:S(2)}) collective-permute-start(bf16[8,1280]{1,0:T(8,128)(2,1)S(1)} %get-tuple-element.17), channel_id=1, source_target_pairs={{3,0},{2,1},{1,2},{0,3},{7,4},{6,5},{5,6},{4,7},{11,8},{10,9},{9,1... | collective-permute-start | bytes 61448 | tf_op jit(solution)/shard_map/ppermute | solution.py:35
  16.6 5.5 %collective-permute-start.9 = (bf16[8,1280]{1,0:T(8,128)(2,1)S(1)}, bf16[8,1280]{1,0:T(8,128)(2,1)S(1)}, u32[]{:S(2)}, u32[]{:S(2)}) collective-permute-start(bf16[8,1280]{1,0:T(8,128)(2,1)S(1)} %get-tuple-element.15), channel_id=1, source_target_pairs={{1,0},{0,1},{3,2},{2,3},{5,4},{4,5},{7,6},{6,7},{9,8},{8,9},{11,10... | collective-permute-start | bytes 61448 | tf_op jit(solution)/shard_map/ppermute | solution.py:35
  17.0 19.6 %slice-start.4 = ((s8[17694720]{0:T(1024)(128)(4,1)}), s8[917504]{0:T(1024)(128)(4,1)S(1)}, s32[]{:S(2)}) async-start(s8[17694720]{0:T(1024)(128)(4,1)} %bitcast.2), calls=%async_computation.5 | async-start | bytes 1835008
  22.1 4.5 %collective-permute-start.12 = (bf16[2,16,1280]{2,1,0:T(8,128)(2,1)S(1)}, bf16[2,16,1280]{2,1,0:T(8,128)(2,1)S(1)}, u32[]{:S(2)}, u32[]{:S(2)}) collective-permute-start(bf16[2,16,1280]{2,1,0:T(8,128)(2,1)S(1)} %sort.1.refs_0_), channel_id=1, source_target_pairs={{8,0},{12,4},{0,8},{4,12},{24,16},{28,20},{16,24},{20,28},{9,1},{1... | collective-permute-start | bytes 245768 | tf_op jit(solution)/shard_map/ppermute | solution.py:48
  23.6 4.5 %collective-permute-start.13 = (bf16[2,16,1280]{2,1,0:T(8,128)(2,1)S(1)}, bf16[2,16,1280]{2,1,0:T(8,128)(2,1)S(1)}, u32[]{:S(2)}, u32[]{:S(2)}) collective-permute-start(bf16[2,16,1280]{2,1,0:T(8,128)(2,1)S(1)} %sort.1.refs_0_), channel_id=1, source_target_pairs={{16,0},{20,4},{24,8},{28,12},{0,16},{4,20},{8,24},{12,28},{17,1},{... | collective-permute-start | bytes 245768 | tf_op jit(solution)/shard_map/ppermute | solution.py:48
  25.1 5.3 %collective-permute-start.14 = (bf16[2,16,1280]{2,1,0:T(8,128)(2,1)S(1)}, bf16[2,16,1280]{2,1,0:T(8,128)(2,1)S(1)}, u32[]{:S(2)}, u32[]{:S(2)}) collective-permute-start(bf16[2,16,1280]{2,1,0:T(8,128)(2,1)S(1)} %sort.1.refs_0_), channel_id=1, source_target_pairs={{24,0},{28,4},{16,8},{20,12},{8,16},{12,20},{0,24},{4,28},{25,1},{... | collective-permute-start | bytes 245768 | tf_op jit(solution)/shard_map/ppermute | solution.py:48
  30.5 18.2 %collective-permute-start.15 = (bf16[4,2,16,1280]{3,2,1,0:T(8,128)(2,1)S(1)}, bf16[4,2,16,1280]{3,2,1,0:T(8,128)(2,1)S(1)}, u32[]{:S(2)}, u32[]{:S(2)}) collective-permute-start(bf16[4,2,16,1280]{3,2,1,0:T(8,128)(2,1)S(1)} %stack.1.refs_7_), channel_id=1, source_target_pairs={{4,0},{0,4},{12,8},{8,12},{20,16},{16,20},{28,24},{24,28},{5,1},{1... | collective-permute-start | bytes 983048 | tf_op jit(solution)/shard_map/ppermute | solution.py:39
  30.6 13.4 %collective-permute-start.5 = (bf16[2,32,1728]{2,1,0:T(8,128)(2,1)S(1)}, bf16[2,32,1728]{2,1,0:T(8,128)(2,1)S(1)}, u32[]{:S(2)}, u32[]{:S(2)}) collective-permute-start(bf16[2,32,1728]{2,1,0:T(8,128)(2,1)S(1)} %pile.1.after), channel_id=1, source_target_pairs={{1,0},{0,1},{3,2},{2,3},{5,4},{4,5},{7,6},{6,7},{9,8},{8,9},{11,10... | collective-permute-start | bytes 663560 | tf_op jit(solution)/shard_map/ppermute | solution.py:196
  32.2 11.8 %collective-permute-start.6 = (bf16[32,1728]{1,0:T(8,128)(2,1)S(1)}, bf16[32,1728]{1,0:T(8,128)(2,1)S(1)}, u32[]{:S(2)}, u32[]{:S(2)}) collective-permute-start(bf16[32,1728]{1,0:T(8,128)(2,1)S(1)} %grad_pre.1.grad_pre_ref.refs_4_.refs_3_), channel_id=1, source_target_pairs={{1,0},{0,1},{3,2},{2,3},{5,4},{4,5},{7,6},{6,7},{9,8},{8,9},{11,10... | collective-permute-start | bytes 331784 | tf_op jit(solution)/shard_map/ppermute | solution.py:35
  32.7 11.4 %collective-permute-start.7 = (bf16[32,1728]{1,0:T(8,128)(2,1)S(1)}, bf16[32,1728]{1,0:T(8,128)(2,1)S(1)}, u32[]{:S(2)}, u32[]{:S(2)}) collective-permute-start(bf16[32,1728]{1,0:T(8,128)(2,1)S(1)} %grad_pre.1.grad_pre_ref.refs_4_.refs_3_), channel_id=1, source_target_pairs={{2,0},{3,1},{0,2},{1,3},{6,4},{7,5},{4,6},{5,7},{10,8},{11,9},{8,1... | collective-permute-start | bytes 331784 | tf_op jit(solution)/shard_map/ppermute | solution.py:35
  36.0 12.7 %collective-permute-start.8 = (bf16[32,1728]{1,0:T(8,128)(2,1)S(1)}, bf16[32,1728]{1,0:T(8,128)(2,1)S(1)}, u32[]{:S(2)}, u32[]{:S(2)}) collective-permute-start(bf16[32,1728]{1,0:T(8,128)(2,1)S(1)} %grad_pre.1.grad_pre_ref.refs_4_.refs_3_), channel_id=1, source_target_pairs={{3,0},{2,1},{1,2},{0,3},{7,4},{6,5},{5,6},{4,7},{11,8},{10,9},{9,1... | collective-permute-start | bytes 331784 | tf_op jit(solution)/shard_map/ppermute | solution.py:35
  40.6 13.1 %all-to-all-start = ((bf16[8,4,5120]{2,1,0:T(4,128)(2,1)}), bf16[8,4,5120]{2,1,0:T(4,128)(2,1)S(1)}, u32[]{:S(2)}, u32[]{:S(2)}) async-start(bf16[8,4,5120]{2,1,0:T(4,128)(2,1)} %grad_in_part.1), calls=%async_computation | async-start | bytes 655360 | tf_op jit(solution)/shard_map/all_to_all | solution.py:391
  (6 other events, 47.2 us)

commit v13 on v12

--- a/solution.py
+++ b/solution.py
@@ -90,8 +90,7 @@
     )[0]
 
 
-def pack_body(tokens_in, grad_in, pre_in, after, *refs):
-    *pieces, own, pre_ref, grad_ref, slabs, tokens_ref, sems = refs
+def pack_body(tokens_in, grad_in, pre_in, after, both, pre_ref, tokens_ref, grad_ref, sems):
     copies = [
         pltpu.make_async_copy(source, target, sems.at[i])
         for i, (source, target) in enumerate(
@@ -102,30 +101,21 @@
         copy.start()
     for copy in copies:
         copy.wait()
-    places, rows, part = slabs.shape
-    both = jnp.concatenate(
+    both[...] = jnp.concatenate(
         [tokens_ref[...].astype(jnp.float32), grad_ref[...].astype(jnp.float32)], axis=0
-    )
-    for p in range(places):
-        slabs[p] = both[:, p * part : (p + 1) * part]
-    t = lax.axis_index("tokens")
-    own[...] = slabs[t].astype(jnp.bfloat16)
-    for k, ref in enumerate(pieces, 1):
-        taker = t ^ k if places & (places - 1) == 0 else lax.rem(t - k + places, places)
-        ref[...] = slabs[taker].astype(jnp.bfloat16)
-
-
-def pack(tokens_in, grad_out, pre_act, n_tok, after):
+    ).astype(jnp.bfloat16)
+
+
+def pack(tokens_in, grad_out, pre_act, after):
     rows, width = tokens_in.shape
-    part = width // n_tok
-    shapes = [(2 * rows, part)] * n_tok + [pre_act.shape, grad_out.shape]
+    shapes = [(2 * rows, width), pre_act.shape]
     return call(
         pack_body,
         [(shape, jnp.bfloat16) for shape in shapes],
         [tokens_in, grad_out, pre_act, after],
         "pack",
         [
-            pltpu.VMEM((n_tok, 2 * rows, part), jnp.float32),
+            pltpu.VMEM(tokens_in.shape, jnp.bfloat16),
             pltpu.VMEM(tokens_in.shape, jnp.bfloat16),
             pltpu.SemaphoreType.DMA((3,)),
         ],
@@ -135,33 +125,37 @@
     )
 
 
-def join_body(after, *refs):
-    *pieces, out = refs
-    out[...] = jnp.concatenate([x[...].astype(jnp.float32) for x in pieces], axis=0).astype(
-        jnp.bfloat16
-    )
-
-
-def join(pieces, after):
-    shape = (sum(x.shape[0] for x in pieces), pieces[0].shape[1])
-    return call(join_body, [(shape, jnp.bfloat16)], [after, *pieces], "join")[0]
-
-
-def sort_body(count, *refs):
-    pieces, out = refs[:count], refs[-1]
-    rows = pieces[0].shape[0] // 2
-    pieces = [x[...].astype(jnp.float32) for x in pieces]
-    for a in range(2):
-        out[a] = jnp.concatenate([x[a * rows : (a + 1) * rows] for x in pieces], axis=0).astype(
-            jnp.bfloat16
-        )
-
-
-def sort(pieces, after):
-    rows, part = pieces[0].shape
-    shape = (2, rows // 2 * len(pieces), part)
-    body = functools.partial(sort_body, len(pieces))
-    return call(body, [(shape, jnp.bfloat16)], [*pieces, *after], "sort")[0]
+def join_body(count, after, *refs):
+    rows_in = refs[:count]
+    *pieces, grad_ref, slabs = refs[count:]
+    places, _, _, part = slabs.shape
+    parts = [x[...].astype(jnp.float32) for x in rows_in]
+    each = parts[0].shape[0] // 2
+    tokens = jnp.concatenate([x[:each] for x in parts], axis=0)
+    grad = jnp.concatenate([x[each:] for x in parts], axis=0)
+    grad_ref[...] = grad.astype(jnp.bfloat16)
+    for p in range(places):
+        here = slice(p * part, (p + 1) * part)
+        slabs[p, 0] = tokens[:, here]
+        slabs[p, 1] = grad[:, here]
+    t = lax.axis_index("tokens")
+    for k, ref in enumerate(pieces):
+        taker = t ^ k if places & (places - 1) == 0 else lax.rem(t - k + places, places)
+        ref[...] = slabs[taker].astype(jnp.bfloat16)
+
+
+def join(rows_in, n_tok, after):
+    count, (both, width) = len(rows_in), rows_in[0].shape
+    rows, part = count * both // 2, width // n_tok
+    shapes = [(2, rows, part)] * n_tok + [(rows, width)]
+    return call(
+        functools.partial(join_body, count),
+        [(shape, jnp.bfloat16) for shape in shapes],
+        [after, *rows_in],
+        "join",
+        [pltpu.VMEM((n_tok, 2, rows, part), jnp.float32)],
+        limit=16,
+    )
 
 
 def stack_body(count, *refs):
@@ -295,22 +289,23 @@
     flat, sorted_rows, turned, held_in, held_out, sems = refs[arrays + places + 5 :]
     end_ref[...] = jnp.zeros_like(end_ref)
     group, hidden = grad_pre_refs[0].shape
-    chips, _, each, part = own_ref.shape
-    rows = each // places
-    total = places * group
+    part = own_ref.shape[3]
+    half, total = group // 2, places * group
+    chips = lax.axis_size("mp") // 2
+    rows = half // chips
     copies = []
 
     def arrange(place):
-        size = block_of(total, 128, each)
+        size = block_of(total, 128, rows)
+        blocks = [(core, k, chip) for core in range(2) for k in range(places) for chip in range(chips)]
         for low in range(0, total, size):
             row = low + lax.broadcasted_iota(jnp.int32, (size, 1), 0)
             from_row = row
-            for b in range(low // each, (low + size) // each):
-                for k in range(places):
-                    first = b * each + k * rows
-                    inside = (row >= first) & (row < first + rows)
-                    shift = k * group + place(b) * rows - first
-                    from_row = jnp.where(inside, row + shift, from_row)
+            for core, k, chip in blocks[low // rows : (low + size) // rows]:
+                first = core * places * half + k * half + chip * rows
+                inside = (row >= first) & (row < first + rows)
+                shift = k * group + place(core * chips + chip) * rows - first
+                from_row = jnp.where(inside, row + shift, from_row)
             pick = from_row == lax.broadcasted_iota(jnp.int32, (size, total), 1)
             sorted_rows[low : low + size, :] = jnp.dot(
                 pick.astype(jnp.float32).astype(jnp.bfloat16),
@@ -323,7 +318,7 @@
         for low in range(0, part, block):
             here = slice(low, low + block)
             cols = jnp.concatenate(
-                [ref[k, right, :, here] for ref in (own_ref, other_ref) for k in range(chips)], axis=0
+                [ref[k, right, :, here] for ref in (own_ref, other_ref) for k in range(places)], axis=0
             )
             term = jnp.dot(turned[...], cols, preferred_element_type=jnp.float32)
             held[:, here] = (term * scale_back).astype(jnp.bfloat16)
@@ -379,13 +374,14 @@
 
     masks = (3, 1) if n_tok == 4 else [1 << i for i in range(n_tok.bit_length() - 1)]
     held, pre, where = spread(pre_act, masks)
-    *pieces, own_piece, pre_act, own_grad = pack(tokens_in, grad_out, pre_act, n_tok, lead())
-    own_rows = join([own_grad] + [fetch_chip(grad_out, k) for k in range(1, chips)], held)
-    other_rows = other_core(own_rows)
-    pieces = [fetch(x, "tokens", k) for k, x in enumerate(pieces, 1)]
-    grad_pre = grad_pre_of(own_rows, other_rows, pre_act, w_out)
-    cols = sort([own_piece, *pieces], [grad_pre])
-    own_cols = stack([cols] + [fetch_chip(cols, k) for k in range(1, chips)])
+    both, pre_act = pack(tokens_in, grad_out, pre_act, lead())
+    *pieces, own_rows = join(
+        [both] + [fetch_chip(both, k) for k in range(1, chips)], n_tok, held
+    )
+    pieces = [x if k == 0 else fetch(x, "tokens", k) for k, x in enumerate(pieces)]
+
+    grad_pre = grad_pre_of(own_rows, other_core(own_rows), pre_act, w_out)
+    own_cols = stack(pieces, [grad_pre])
     other_cols = other_core(own_cols)
     grad_pre_all = [grad_pre] + [fetch(grad_pre, "tokens", k) for k in range(1, n_tok)]
     terms = lax.all_to_all(grad_in_part(grad_pre, w_in.T, n_mp, []), "mp", 0, 0)

time: 54.5 us -> 46.6 us (0.86)
  starting transfers between devices: 26.3 us -> 21.2 us
  waiting for transfers between devices: 12.2 us -> 9.27 us
    ppermute x6 -> x3, starting transfers between devices: 8.1 us -> 3.55 us  [fetch_chip(): lax.ppermute(x, 'mp', [(there, here) for here, there in chip_pairs(k)])]
    ppermute x2, waiting for transfers between devices: 2.61 us -> 0.01 us  [spread(): got.append(lax.ppermute(held, 'tokens', [(i ^ mask, i) for i in range(n)]))]
    ppermute x6, starting transfers between devices: 8.89 us -> 7.93 us  [fetch(): return lax.ppermute(x, axis, [(partner(i, k, n), i) for i in range(n)])]
    pallas_call x10 -> x9, Pallas kernels: 14.9 us -> 14.9 us  [call(): pl.pallas_call(body, in_specs=[pl.BlockSpec(memory_space=in_space)] * len...]
    ppermute x6 -> x3, waiting for transfers between devices: 4.87 us -> 4.84 us  [fetch_chip(): lax.ppermute(x, 'mp', [(there, here) for here, there in chip_pairs(k)])]
  transfers between devices with their start and end apart: 17 -> 14, of which waited for: 5 -> 6; matrix products, arithmetic and copies ran while one was open for 0% -> 0% of each run, Pallas kernels for 26% -> 30%
where the time goes in v13:
time: 46.6 us; the launch traced here: 46.3 us
  starting transfers between devices  21.2 us (45%)
  Pallas kernels  14.9 us (32%)
  waiting for transfers between devices  9.27 us (20%)
  between operations  0.9 us (2%)
    pallas_call x9, Pallas kernels, call(): pl.pallas_call(body, in_specs=[pl.BlockSpec(memory_space=in_space)] * len...  14.9 us
    ppermute x6, starting transfers between devices, fetch(): return lax.ppermute(x, axis, [(partner(i, k, n), i) for i in range(n)])  7.93 us
    ppermute x2, starting transfers between devices, spread(): got.append(lax.ppermute(held, 'tokens', [(i ^ mask, i) for i in range(n)]))  6.12 us
    ppermute x3, waiting for transfers between devices, fetch_chip(): lax.ppermute(x, 'mp', [(there, here) for here, there in chip_pairs(k)])  4.84 us
    ppermute x6, waiting for transfers between devices, fetch(): return lax.ppermute(x, axis, [(partner(i, k, n), i) for i in range(n)])  4.42 us
    ppermute x3, starting transfers between devices, fetch_chip(): lax.ppermute(x, 'mp', [(there, here) for here, there in chip_pairs(k)])  3.55 us
    all_to_all x1, starting transfers between devices, shards(): terms = lax.all_to_all(grad_in_part(grad_pre, w_in.T, n_mp, []), 'mp', 0, 0)  3.43 us
  transfers between devices with their start and end apart: 14, of which 6 were waited for; matrix products, arithmetic and copies ran while one was open for 0% of the time, Pallas kernels for 30%

profile of v13, /device:TPU:0, one launch (start us, length us, event | category | flops | bytes accessed | tf_op | source)
XLA Modules:
  0.0 46.3 jit_solution(3139828514210637499)
XLA Ops:
  0.7 5.1 %collective-permute-start = (bf16[32,1728]{1,0:T(8,128)(2,1)}, bf16[32,1728]{1,0:T(8,128)(2,1)S(1)}, u32[]{:S(2)}, u32[]{:S(2)}) collective-permute-start(bf16[32,1728]{1,0:T(8,128)(2,1)} %pre_in.1), channel_id=1, source_target_pairs={{3,0},{2,1},{1,2},{0,3},{7,4},{6,5},{5,6},{4,7},{11,8},{10,9},{9,1... | collective-permute-start | bytes 331784 | tf_op jit(solution)/shard_map/ppermute | solution.py:190
  5.9 0.3 pack.1
  6.2 1.6 %collective-permute-start.1 = (bf16[8,5120]{1,0:T(8,128)(2,1)S(1)}, bf16[8,5120]{1,0:T(8,128)(2,1)S(1)}, u32[]{:S(2)}, u32[]{:S(2)}) collective-permute-start(bf16[8,5120]{1,0:T(8,128)(2,1)S(1)} %get-tuple-element.13.refs_0_), channel_id=1, source_target_pairs={{8,0},{12,4},{0,8},{4,12},{24,16},{28,20},{16,24},{20,28},{9,1},{1... | collective-permute-start | bytes 245768 | tf_op jit(solution)/shard_map/ppermute | solution.py:48
  7.8 1.5 %collective-permute-start.2 = (bf16[8,5120]{1,0:T(8,128)(2,1)S(1)}, bf16[8,5120]{1,0:T(8,128)(2,1)S(1)}, u32[]{:S(2)}, u32[]{:S(2)}) collective-permute-start(bf16[8,5120]{1,0:T(8,128)(2,1)S(1)} %get-tuple-element.13.refs_0_), channel_id=1, source_target_pairs={{16,0},{20,4},{24,8},{28,12},{0,16},{4,20},{8,24},{12,28},{17,1},{... | collective-permute-start | bytes 245768 | tf_op jit(solution)/shard_map/ppermute | solution.py:48
  9.3 0.5 %collective-permute-start.3 = (bf16[8,5120]{1,0:T(8,128)(2,1)S(1)}, bf16[8,5120]{1,0:T(8,128)(2,1)S(1)}, u32[]{:S(2)}, u32[]{:S(2)}) collective-permute-start(bf16[8,5120]{1,0:T(8,128)(2,1)S(1)} %get-tuple-element.13.refs_0_), channel_id=1, source_target_pairs={{24,0},{28,4},{16,8},{20,12},{8,16},{12,20},{0,24},{4,28},{25,1},{... | collective-permute-start | bytes 245768 | tf_op jit(solution)/shard_map/ppermute | solution.py:48
  9.8 0.9 %collective-permute-done.1.refs_1_ = bf16[8,5120]{1,0:T(8,128)(2,1)S(1)} collective-permute-done((bf16[8,5120]{1,0:T(8,128)(2,1)S(1)}, bf16[8,5120]{1,0:T(8,128)(2,1)S(1)}, u32[]{:S(2)}, u32[]{:S(2)}) %collective-permute-start.1) | collective-permute-done | bytes 81952 | tf_op jit(solution)/shard_map/ppermute | solution.py:48
  10.7 2.4 %collective-permute-done.2.refs_2_ = bf16[8,5120]{1,0:T(8,128)(2,1)S(1)} collective-permute-done((bf16[8,5120]{1,0:T(8,128)(2,1)S(1)}, bf16[8,5120]{1,0:T(8,128)(2,1)S(1)}, u32[]{:S(2)}, u32[]{:S(2)}) %collective-permute-start.2) | collective-permute-done | bytes 81952 | tf_op jit(solution)/shard_map/ppermute | solution.py:48
  13.1 1.5 %collective-permute-done.3.refs_3_ = bf16[8,5120]{1,0:T(8,128)(2,1)S(1)} collective-permute-done((bf16[8,5120]{1,0:T(8,128)(2,1)S(1)}, bf16[8,5120]{1,0:T(8,128)(2,1)S(1)}, u32[]{:S(2)}, u32[]{:S(2)}) %collective-permute-start.3) | collective-permute-done | bytes 81952 | tf_op jit(solution)/shard_map/ppermute | solution.py:48
  14.6 0.2 join.1
  14.8 0.1 collective-permute-start.4
  14.9 1.9 %collective-permute-start.11 = (bf16[2,16,1280]{2,1,0:T(8,128)(2,1)S(1)}, bf16[2,16,1280]{2,1,0:T(8,128)(2,1)S(1)}, u32[]{:S(2)}, u32[]{:S(2)}) collective-permute-start(bf16[2,16,1280]{2,1,0:T(8,128)(2,1)S(1)} %get-tuple-element.19), channel_id=1, source_target_pairs={{3,0},{2,1},{1,2},{0,3},{7,4},{6,5},{5,6},{4,7},{11,8},{10,9},{9,1... | collective-permute-start | bytes 245768 | tf_op jit(solution)/shard_map/ppermute | solution.py:35
  16.8 1.6 %collective-permute-start.9 = (bf16[2,16,1280]{2,1,0:T(8,128)(2,1)S(1)}, bf16[2,16,1280]{2,1,0:T(8,128)(2,1)S(1)}, u32[]{:S(2)}, u32[]{:S(2)}) collective-permute-start(bf16[2,16,1280]{2,1,0:T(8,128)(2,1)S(1)} %get-tuple-element.17), channel_id=1, source_target_pairs={{1,0},{0,1},{3,2},{2,3},{5,4},{4,5},{7,6},{6,7},{9,8},{8,9},{11,10... | collective-permute-start | bytes 245768 | tf_op jit(solution)/shard_map/ppermute | solution.py:35
  18.5 4.9 %grad_pre.1.grad_pre_ref.refs_4_.refs_3_ = bf16[32,1728]{1,0:T(8,128)(2,1)S(1)} custom-call(bf16[16,5120]{1,0:T(8,128)(2,1)S(1)} %get-tuple-element.14.own_ref, bf16[16,5120]{1,0:T(8,128)(2,1)S(1)} %collective-permute-done.4.other_ref, bf16[32,1728]{1,0:T(8,128)(2,1)S(1)} %get-tuple-element.15.pre_ref.refs_0_, bf16[1728,5120]{1,0:T(8,128)(2,1)S(1)} %bitcast.6), custom_call_target="tpu_custom_call" | custom-call | flops 566231040 | bytes 17694720 | tf_op jit(solution)/shard_map/grad_pre/pallas_call | solution.py:61
  23.4 1.1 %collective-permute-done.9.refs_1_ = bf16[2,16,1280]{2,1,0:T(8,128)(2,1)S(1)} collective-permute-done((bf16[2,16,1280]{2,1,0:T(8,128)(2,1)S(1)}, bf16[2,16,1280]{2,1,0:T(8,128)(2,1)S(1)}, u32[]{:S(2)}, u32[]{:S(2)}) %collective-permute-start.9) | collective-permute-done | bytes 81952 | tf_op jit(solution)/shard_map/ppermute | solution.py:35
  24.6 1.0 %collective-permute-start.5 = (bf16[2,32,1728]{2,1,0:T(8,128)(2,1)S(1)}, bf16[2,32,1728]{2,1,0:T(8,128)(2,1)S(1)}, u32[]{:S(2)}, u32[]{:S(2)}) collective-permute-start(bf16[2,32,1728]{2,1,0:T(8,128)(2,1)S(1)} %pile.1.after), channel_id=1, source_target_pairs={{1,0},{0,1},{3,2},{2,3},{5,4},{4,5},{7,6},{6,7},{9,8},{8,9},{11,10... | collective-permute-start | bytes 663560 | tf_op jit(solution)/shard_map/ppermute | solution.py:190
  25.7 1.1 %collective-permute-start.6 = (bf16[32,1728]{1,0:T(8,128)(2,1)S(1)}, bf16[32,1728]{1,0:T(8,128)(2,1)S(1)}, u32[]{:S(2)}, u32[]{:S(2)}) collective-permute-start(bf16[32,1728]{1,0:T(8,128)(2,1)S(1)} %grad_pre.1.grad_pre_ref.refs_4_.refs_3_), channel_id=1, source_target_pairs={{1,0},{0,1},{3,2},{2,3},{5,4},{4,5},{7,6},{6,7},{9,8},{8,9},{11,10... | collective-permute-start | bytes 331784 | tf_op jit(solution)/shard_map/ppermute | solution.py:35
  26.7 1.2 %collective-permute-start.7 = (bf16[32,1728]{1,0:T(8,128)(2,1)S(1)}, bf16[32,1728]{1,0:T(8,128)(2,1)S(1)}, u32[]{:S(2)}, u32[]{:S(2)}) collective-permute-start(bf16[32,1728]{1,0:T(8,128)(2,1)S(1)} %grad_pre.1.grad_pre_ref.refs_4_.refs_3_), channel_id=1, source_target_pairs={{2,0},{3,1},{0,2},{1,3},{6,4},{7,5},{4,6},{5,7},{10,8},{11,9},{8,1... | collective-permute-start | bytes 331784 | tf_op jit(solution)/shard_map/ppermute | solution.py:35
  28.0 2.1 %collective-permute-start.8 = (bf16[32,1728]{1,0:T(8,128)(2,1)S(1)}, bf16[32,1728]{1,0:T(8,128)(2,1)S(1)}, u32[]{:S(2)}, u32[]{:S(2)}) collective-permute-start(bf16[32,1728]{1,0:T(8,128)(2,1)S(1)} %grad_pre.1.grad_pre_ref.refs_4_.refs_3_), channel_id=1, source_target_pairs={{3,0},{2,1},{1,2},{0,3},{7,4},{6,5},{5,6},{4,7},{11,8},{10,9},{9,1... | collective-permute-start | bytes 331784 | tf_op jit(solution)/shard_map/ppermute | solution.py:35
  30.1 3.9 %grad_in_part.1 = bf16[8,4,5120]{2,1,0:T(4,128)(2,1)} custom-call(bf16[32,1728]{1,0:T(8,128)(2,1)S(1)} %grad_pre.1.grad_pre_ref.refs_4_.refs_3_, bf16[1728,5120]{1,0:T(8,128)(2,1)S(1)} %bitcast.4), custom_call_target="tpu_custom_call" | custom-call | flops 566231040 | bytes 17694720 | tf_op jit(solution)/shard_map/grad_in_part/pallas_call | solution.py:61
  34.0 3.4 %all-to-all-start = ((bf16[8,4,5120]{2,1,0:T(4,128)(2,1)}), bf16[8,4,5120]{2,1,0:T(4,128)(2,1)S(1)}, u32[]{:S(2)}, u32[]{:S(2)}) async-start(bf16[8,4,5120]{2,1,0:T(4,128)(2,1)} %grad_in_part.1), calls=%async_computation | async-start | bytes 655360 | tf_op jit(solution)/shard_map/all_to_all | solution.py:387
  37.4 0.2 collective-permute-done.6.refs_4_
  37.6 3.1 %collective-permute-done.8.refs_6_ = bf16[32,1728]{1,0:T(8,128)(2,1)S(1)} collective-permute-done((bf16[32,1728]{1,0:T(8,128)(2,1)S(1)}, bf16[32,1728]{1,0:T(8,128)(2,1)S(1)}, u32[]{:S(2)}, u32[]{:S(2)}) %collective-permute-start.8) | collective-permute-done | bytes 110624 | tf_op jit(solution)/shard_map/ppermute | solution.py:35
  40.7 4.9 %grad_w.1 = (bf16[1728,1280]{1,0:T(8,128)(2,1)}, bf16[1728,1280]{1,0:T(8,128)(2,1)}, f32[8,128]{1,0:T(8,128)S(1)}) custom-call(bf16[32,1728]{1,0:T(8,128)(2,1)S(1)} %get-tuple-element.15.pre_ref.refs_0_, bf16[32,1728]{1,0:T(8,128)(2,1)S(1)} %collective-permute-done.high.refs_1_, bf16[2,32,1728]{2,1,0:T(8,128)(2,1)S(1)} %collective-permute-done.5.refs_2_, ...), custom_call_target="tpu_custom_call" | custom-call | flops 22649241600 | bytes 88473600 | tf_op jit(solution)/shard_map/grad_w/pallas_call | solution.py:61
  45.7 0.7 %finish.1 = bf16[4,5120]{1,0:T(4,128)(2,1)} custom-call(bf16[8,4,5120]{2,1,0:T(4,128)(2,1)S(1)} %all-to-all-done.terms_ref, f32[8,128]{1,0:T(8,128)S(1)} %get-tuple-element.20.after), custom_call_target="tpu_custom_call" | custom-call | flops 1000000 | bytes 100000 | tf_op jit(solution)/shard_map/finish/pallas_call | solution.py:61
  (41 shorter events, 0.3 us)
Async XLA Ops:
  0.7 9.1 %collective-permute-start = (bf16[32,1728]{1,0:T(8,128)(2,1)}, bf16[32,1728]{1,0:T(8,128)(2,1)S(1)}, u32[]{:S(2)}, u32[]{:S(2)}) collective-permute-start(bf16[32,1728]{1,0:T(8,128)(2,1)} %pre_in.1), channel_id=1, source_target_pairs={{3,0},{2,1},{1,2},{0,3},{7,4},{6,5},{5,6},{4,7},{11,8},{10,9},{9,1... | collective-permute-start | bytes 331784 | tf_op jit(solution)/shard_map/ppermute | solution.py:190
  5.8 12.7 %slice-start.5 = ((s8[17694720]{0:T(1024)(128)(4,1)}), s8[4194304]{0:T(1024)(128)(4,1)S(1)}, s32[]{:S(2)}) async-start(s8[17694720]{0:T(1024)(128)(4,1)} %bitcast.5), calls=%async_computation.6 | async-start | bytes 8388608
  5.8 12.7 %slice-start.6 = ((s8[17694720]{0:T(1024)(128)(4,1)}), s8[4194304]{0:T(1024)(128)(4,1)S(1)}, s32[]{:S(2)}) async-start(s8[17694720]{0:T(1024)(128)(4,1)} %bitcast.5), calls=%async_computation.7 | async-start | bytes 8388608
  5.8 12.7 %slice-start.7 = ((s8[17694720]{0:T(1024)(128)(4,1)}), s8[4194304]{0:T(1024)(128)(4,1)S(1)}, s32[]{:S(2)}) async-start(s8[17694720]{0:T(1024)(128)(4,1)} %bitcast.5), calls=%async_computation.8 | async-start | bytes 8388608
  5.8 12.6 %slice-start.8 = ((s8[17694720]{0:T(1024)(128)(4,1)}), s8[4194304]{0:T(1024)(128)(4,1)S(1)}, s32[]{:S(2)}) async-start(s8[17694720]{0:T(1024)(128)(4,1)} %bitcast.5), calls=%async_computation.9 | async-start | bytes 8388608
  5.8 12.6 %slice-start.9 = ((s8[17694720]{0:T(1024)(128)(4,1)}), s8[917504]{0:T(1024)(128)(4,1)S(1)}, s32[]{:S(2)}) async-start(s8[17694720]{0:T(1024)(128)(4,1)} %bitcast.5), calls=%async_computation.10 | async-start | bytes 1835008
  5.8 24.2 %slice-start = ((s8[17694720]{0:T(1024)(128)(4,1)}), s8[4194304]{0:T(1024)(128)(4,1)S(1)}, s32[]{:S(2)}) async-start(s8[17694720]{0:T(1024)(128)(4,1)} %bitcast.2), calls=%async_computation.1 | async-start | bytes 8388608
  5.9 24.2 %slice-start.1 = ((s8[17694720]{0:T(1024)(128)(4,1)}), s8[4194304]{0:T(1024)(128)(4,1)S(1)}, s32[]{:S(2)}) async-start(s8[17694720]{0:T(1024)(128)(4,1)} %bitcast.2), calls=%async_computation.2 | async-start | bytes 8388608
  5.9 24.2 %slice-start.2 = ((s8[17694720]{0:T(1024)(128)(4,1)}), s8[4194304]{0:T(1024)(128)(4,1)S(1)}, s32[]{:S(2)}) async-start(s8[17694720]{0:T(1024)(128)(4,1)} %bitcast.2), calls=%async_computation.3 | async-start | bytes 8388608
  5.9 24.2 %slice-start.3 = ((s8[17694720]{0:T(1024)(128)(4,1)}), s8[4194304]{0:T(1024)(128)(4,1)S(1)}, s32[]{:S(2)}) async-start(s8[17694720]{0:T(1024)(128)(4,1)} %bitcast.2), calls=%async_computation.4 | async-start | bytes 8388608
  6.2 4.5 %collective-permute-start.1 = (bf16[8,5120]{1,0:T(8,128)(2,1)S(1)}, bf16[8,5120]{1,0:T(8,128)(2,1)S(1)}, u32[]{:S(2)}, u32[]{:S(2)}) collective-permute-start(bf16[8,5120]{1,0:T(8,128)(2,1)S(1)} %get-tuple-element.13.refs_0_), channel_id=1, source_target_pairs={{8,0},{12,4},{0,8},{4,12},{24,16},{28,20},{16,24},{20,28},{9,1},{1... | collective-permute-start | bytes 245768 | tf_op jit(solution)/shard_map/ppermute | solution.py:48
  7.8 5.3 %collective-permute-start.2 = (bf16[8,5120]{1,0:T(8,128)(2,1)S(1)}, bf16[8,5120]{1,0:T(8,128)(2,1)S(1)}, u32[]{:S(2)}, u32[]{:S(2)}) collective-permute-start(bf16[8,5120]{1,0:T(8,128)(2,1)S(1)} %get-tuple-element.13.refs_0_), channel_id=1, source_target_pairs={{16,0},{20,4},{24,8},{28,12},{0,16},{4,20},{8,24},{12,28},{17,1},{... | collective-permute-start | bytes 245768 | tf_op jit(solution)/shard_map/ppermute | solution.py:48
  9.3 5.3 %collective-permute-start.3 = (bf16[8,5120]{1,0:T(8,128)(2,1)S(1)}, bf16[8,5120]{1,0:T(8,128)(2,1)S(1)}, u32[]{:S(2)}, u32[]{:S(2)}) collective-permute-start(bf16[8,5120]{1,0:T(8,128)(2,1)S(1)} %get-tuple-element.13.refs_0_), channel_id=1, source_target_pairs={{24,0},{28,4},{16,8},{20,12},{8,16},{12,20},{0,24},{4,28},{25,1},{... | collective-permute-start | bytes 245768 | tf_op jit(solution)/shard_map/ppermute | solution.py:48
  14.8 3.6 %collective-permute-start.4 = (bf16[16,5120]{1,0:T(8,128)(2,1)S(1)}, bf16[16,5120]{1,0:T(8,128)(2,1)S(1)}, u32[]{:S(2)}, u32[]{:S(2)}) collective-permute-start(bf16[16,5120]{1,0:T(8,128)(2,1)S(1)} %get-tuple-element.14.own_ref), channel_id=1, source_target_pairs={{4,0},{0,4},{12,8},{8,12},{20,16},{16,20},{28,24},{24,28},{5,1},{1... | collective-permute-start | bytes 491528 | tf_op jit(solution)/shard_map/ppermute | solution.py:39
  14.9 8.6 %collective-permute-start.10 = (bf16[2,16,1280]{2,1,0:T(8,128)(2,1)S(1)}, bf16[2,16,1280]{2,1,0:T(8,128)(2,1)S(1)}, u32[]{:S(2)}, u32[]{:S(2)}) collective-permute-start(bf16[2,16,1280]{2,1,0:T(8,128)(2,1)S(1)} %get-tuple-element.18), channel_id=1, source_target_pairs={{2,0},{3,1},{0,2},{1,3},{6,4},{7,5},{4,6},{5,7},{10,8},{11,9},{8,1... | collective-permute-start | bytes 245768 | tf_op jit(solution)/shard_map/ppermute | solution.py:35
  14.9 8.5 %collective-permute-start.11 = (bf16[2,16,1280]{2,1,0:T(8,128)(2,1)S(1)}, bf16[2,16,1280]{2,1,0:T(8,128)(2,1)S(1)}, u32[]{:S(2)}, u32[]{:S(2)}) collective-permute-start(bf16[2,16,1280]{2,1,0:T(8,128)(2,1)S(1)} %get-tuple-element.19), channel_id=1, source_target_pairs={{3,0},{2,1},{1,2},{0,3},{7,4},{6,5},{5,6},{4,7},{11,8},{10,9},{9,1... | collective-permute-start | bytes 245768 | tf_op jit(solution)/shard_map/ppermute | solution.py:35
  16.8 7.7 %collective-permute-start.9 = (bf16[2,16,1280]{2,1,0:T(8,128)(2,1)S(1)}, bf16[2,16,1280]{2,1,0:T(8,128)(2,1)S(1)}, u32[]{:S(2)}, u32[]{:S(2)}) collective-permute-start(bf16[2,16,1280]{2,1,0:T(8,128)(2,1)S(1)} %get-tuple-element.17), channel_id=1, source_target_pairs={{1,0},{0,1},{3,2},{2,3},{5,4},{4,5},{7,6},{6,7},{9,8},{8,9},{11,10... | collective-permute-start | bytes 245768 | tf_op jit(solution)/shard_map/ppermute | solution.py:35
  18.5 11.6 %slice-start.4 = ((s8[17694720]{0:T(1024)(128)(4,1)}), s8[917504]{0:T(1024)(128)(4,1)S(1)}, s32[]{:S(2)}) async-start(s8[17694720]{0:T(1024)(128)(4,1)} %bitcast.2), calls=%async_computation.5 | async-start | bytes 1835008
  24.6 16.2 %collective-permute-start.12 = (bf16[4,2,16,1280]{3,2,1,0:T(8,128)(2,1)S(1)}, bf16[4,2,16,1280]{3,2,1,0:T(8,128)(2,1)S(1)}, u32[]{:S(2)}, u32[]{:S(2)}) collective-permute-start(bf16[4,2,16,1280]{3,2,1,0:T(8,128)(2,1)S(1)} %stack.1.refs_7_), channel_id=1, source_target_pairs={{4,0},{0,4},{12,8},{8,12},{20,16},{16,20},{28,24},{24,28},{5,1},{1... | collective-permute-start | bytes 983048 | tf_op jit(solution)/shard_map/ppermute | solution.py:39
  24.6 12.8 %collective-permute-start.5 = (bf16[2,32,1728]{2,1,0:T(8,128)(2,1)S(1)}, bf16[2,32,1728]{2,1,0:T(8,128)(2,1)S(1)}, u32[]{:S(2)}, u32[]{:S(2)}) collective-permute-start(bf16[2,32,1728]{2,1,0:T(8,128)(2,1)S(1)} %pile.1.after), channel_id=1, source_target_pairs={{1,0},{0,1},{3,2},{2,3},{5,4},{4,5},{7,6},{6,7},{9,8},{8,9},{11,10... | collective-permute-start | bytes 663560 | tf_op jit(solution)/shard_map/ppermute | solution.py:190
  25.7 11.9 %collective-permute-start.6 = (bf16[32,1728]{1,0:T(8,128)(2,1)S(1)}, bf16[32,1728]{1,0:T(8,128)(2,1)S(1)}, u32[]{:S(2)}, u32[]{:S(2)}) collective-permute-start(bf16[32,1728]{1,0:T(8,128)(2,1)S(1)} %grad_pre.1.grad_pre_ref.refs_4_.refs_3_), channel_id=1, source_target_pairs={{1,0},{0,1},{3,2},{2,3},{5,4},{4,5},{7,6},{6,7},{9,8},{8,9},{11,10... | collective-permute-start | bytes 331784 | tf_op jit(solution)/shard_map/ppermute | solution.py:35
  26.7 10.8 %collective-permute-start.7 = (bf16[32,1728]{1,0:T(8,128)(2,1)S(1)}, bf16[32,1728]{1,0:T(8,128)(2,1)S(1)}, u32[]{:S(2)}, u32[]{:S(2)}) collective-permute-start(bf16[32,1728]{1,0:T(8,128)(2,1)S(1)} %grad_pre.1.grad_pre_ref.refs_4_.refs_3_), channel_id=1, source_target_pairs={{2,0},{3,1},{0,2},{1,3},{6,4},{7,5},{4,6},{5,7},{10,8},{11,9},{8,1... | collective-permute-start | bytes 331784 | tf_op jit(solution)/shard_map/ppermute | solution.py:35
  28.0 12.7 %collective-permute-start.8 = (bf16[32,1728]{1,0:T(8,128)(2,1)S(1)}, bf16[32,1728]{1,0:T(8,128)(2,1)S(1)}, u32[]{:S(2)}, u32[]{:S(2)}) collective-permute-start(bf16[32,1728]{1,0:T(8,128)(2,1)S(1)} %grad_pre.1.grad_pre_ref.refs_4_.refs_3_), channel_id=1, source_target_pairs={{3,0},{2,1},{1,2},{0,3},{7,4},{6,5},{5,6},{4,7},{11,8},{10,9},{9,1... | collective-permute-start | bytes 331784 | tf_op jit(solution)/shard_map/ppermute | solution.py:35
  34.0 11.7 %all-to-all-start = ((bf16[8,4,5120]{2,1,0:T(4,128)(2,1)}), bf16[8,4,5120]{2,1,0:T(4,128)(2,1)S(1)}, u32[]{:S(2)}, u32[]{:S(2)}) async-start(bf16[8,4,5120]{2,1,0:T(4,128)(2,1)} %grad_in_part.1), calls=%async_computation | async-start | bytes 655360 | tf_op jit(solution)/shard_map/all_to_all | solution.py:387
  (3 other events, 15.5 us)

commit v14 on v13

--- a/solution.py
+++ b/solution.py
@@ -283,87 +283,85 @@
         ).astype(jnp.bfloat16)
 
 
-def grad_w_body(places, arrays, where, scale_back, block, *refs):
-    pre_refs, grad_pre_refs = refs[:arrays], refs[arrays : arrays + places]
-    own_ref, other_ref, in_ref, out_ref, end_ref = refs[arrays + places : arrays + places + 5]
-    flat, sorted_rows, turned, held_in, held_out, sems = refs[arrays + places + 5 :]
+def grad_w_body(count, places, slab, act, scale_back, block, *refs):
+    row_refs = refs[:count]
+    own_ref, other_ref = refs[count : count + 2]
+    to_ref, end_ref, flat, sorted_rows, turned, held, sems = refs[-7:]
     end_ref[...] = jnp.zeros_like(end_ref)
-    group, hidden = grad_pre_refs[0].shape
+    total, hidden = flat.shape
+    group = total // places
     part = own_ref.shape[3]
-    half, total = group // 2, places * group
+    half = group // 2
     chips = lax.axis_size("mp") // 2
     rows = half // chips
+
+    for k in range(places):
+        here = slice(k * group, (k + 1) * group)
+        if act is None:
+            flat[here, :] = row_refs[k][...]
+        else:
+            array, j = act[k]
+            ref = row_refs[array]
+            pre = (ref[...] if len(ref.shape) == 2 else ref[j]).astype(jnp.float32)
+            flat[here, :] = gelu_value(pre).astype(jnp.bfloat16)
+
+    size = block_of(total, 128, rows)
+    blocks = [(core, k, chip) for core in range(2) for k in range(places) for chip in range(chips)]
+    for low in range(0, total, size):
+        row = low + lax.broadcasted_iota(jnp.int32, (size, 1), 0)
+        from_row = row
+        for core, k, chip in blocks[low // rows : (low + size) // rows]:
+            first = core * places * half + k * half + chip * rows
+            inside = (row >= first) & (row < first + rows)
+            b = core * chips + chip
+            place = b if act is None else place_of(b, chips)
+            from_row = jnp.where(inside, row + (k * group + place * rows - first), from_row)
+        pick = from_row == lax.broadcasted_iota(jnp.int32, (size, total), 1)
+        sorted_rows[low : low + size, :] = jnp.dot(
+            pick.astype(jnp.float32).astype(jnp.bfloat16),
+            flat[...],
+            preferred_element_type=jnp.float32,
+        ).astype(jnp.bfloat16)
+    turn(sorted_rows, turned, 256)
+
     copies = []
-
-    def arrange(place):
-        size = block_of(total, 128, rows)
-        blocks = [(core, k, chip) for core in range(2) for k in range(places) for chip in range(chips)]
-        for low in range(0, total, size):
-            row = low + lax.broadcasted_iota(jnp.int32, (size, 1), 0)
-            from_row = row
-            for core, k, chip in blocks[low // rows : (low + size) // rows]:
-                first = core * places * half + k * half + chip * rows
-                inside = (row >= first) & (row < first + rows)
-                shift = k * group + place(core * chips + chip) * rows - first
-                from_row = jnp.where(inside, row + shift, from_row)
-            pick = from_row == lax.broadcasted_iota(jnp.int32, (size, total), 1)
-            sorted_rows[low : low + size, :] = jnp.dot(
-                pick.astype(jnp.float32).astype(jnp.bfloat16),
-                flat[...],
-                preferred_element_type=jnp.float32,
-            ).astype(jnp.bfloat16)
-        turn(sorted_rows, turned, 256)
-
-    def product(right, held, to_ref):
-        for low in range(0, part, block):
-            here = slice(low, low + block)
-            cols = jnp.concatenate(
-                [ref[k, right, :, here] for ref in (own_ref, other_ref) for k in range(places)], axis=0
-            )
-            term = jnp.dot(turned[...], cols, preferred_element_type=jnp.float32)
-            held[:, here] = (term * scale_back).astype(jnp.bfloat16)
-            copies.append(
-                pltpu.make_async_copy(held.at[:, here], to_ref.at[:, here], sems.at[len(copies)])
-            )
-            copies[-1].start()
-
-    for k in range(places):
-        array, j = where[k]
-        ref = pre_refs[array]
-        pre = (ref[...] if len(ref.shape) == 2 else ref[j]).astype(jnp.float32)
-        flat[k * group : (k + 1) * group, :] = gelu_value(pre).astype(jnp.bfloat16)
-    arrange(lambda b: place_of(b, chips))
-    product(1, held_out, out_ref)
-    for k in range(places):
-        flat[k * group : (k + 1) * group, :] = grad_pre_refs[k][...]
-    arrange(lambda b: b)
-    product(0, held_in, in_ref)
+    for low in range(0, part, block):
+        here = slice(low, low + block)
+        cols = jnp.concatenate(
+            [ref[k, slab, :, here] for ref in (own_ref, other_ref) for k in range(places)], axis=0
+        )
+        term = jnp.dot(turned[...], cols, preferred_element_type=jnp.float32)
+        held[:, here] = (term * scale_back).astype(jnp.bfloat16)
+        copies.append(
+            pltpu.make_async_copy(held.at[:, here], to_ref.at[:, here], sems.at[len(copies)])
+        )
+        copies[-1].start()
     for copy in copies:
         copy.wait()
 
 
-def grad_w_of(pre, where, grad_pre, own, other, scale_back):
-    places = len(grad_pre)
-    group, hidden = grad_pre[0].shape
-    total, part = places * group, own.shape[3]
+def grad_w_of(row_arrays, act, own, other, slab, scale_back, name, flops, after=()):
+    group, hidden = row_arrays[0].shape
+    places, _, _, part = own.shape
+    total = places * group
     block = block_of(part, 256, 128)
-    return call(
-        functools.partial(grad_w_body, places, len(pre), where, scale_back, block),
-        [((hidden, part), jnp.bfloat16)] * 2 + [((8, 128), jnp.float32)],
-        [*pre, *grad_pre, own, other],
-        "grad_w",
+    body = functools.partial(grad_w_body, len(row_arrays), places, slab, act, scale_back, block)
+    return call(
+        body,
+        [((hidden, part), jnp.bfloat16), ((8, 128), jnp.float32)],
+        [*row_arrays, own, other, *after],
+        name,
         [
             pltpu.VMEM((total, hidden), jnp.bfloat16),
             pltpu.VMEM((total, hidden), jnp.bfloat16),
             pltpu.VMEM((hidden, total), jnp.bfloat16),
             pltpu.VMEM((hidden, part), jnp.bfloat16),
-            pltpu.VMEM((hidden, part), jnp.bfloat16),
-            pltpu.SemaphoreType.DMA((2 * (part // block),)),
+            pltpu.SemaphoreType.DMA((part // block,)),
         ],
         limit=20,
-        flops=80 * total * part * hidden,
-        bytes_accessed=40 * hidden * part,
-        out_spaces=[pltpu.HBM, pltpu.HBM, pltpu.VMEM],
+        flops=flops,
+        bytes_accessed=2 * hidden * part,
+        out_spaces=[pltpu.HBM, pltpu.VMEM],
     )
 
 
@@ -381,12 +379,16 @@
     pieces = [x if k == 0 else fetch(x, "tokens", k) for k, x in enumerate(pieces)]
 
     grad_pre = grad_pre_of(own_rows, other_core(own_rows), pre_act, w_out)
+    grad_pre_all = [grad_pre] + [fetch(grad_pre, "tokens", k) for k in range(1, n_tok)]
     own_cols = stack(pieces, [grad_pre])
     other_cols = other_core(own_cols)
-    grad_pre_all = [grad_pre] + [fetch(grad_pre, "tokens", k) for k in range(1, n_tok)]
-    terms = lax.all_to_all(grad_in_part(grad_pre, w_in.T, n_mp, []), "mp", 0, 0)
-    grad_w_in_t, grad_w_out, end = grad_w_of(
-        [pre_act, *pre], where, grad_pre_all, own_cols, other_cols, scale_back
+    blocks = grad_in_part(grad_pre, w_in.T, n_mp, [pre[-1]])
+    terms = lax.all_to_all(blocks, "mp", 0, 0)
+    grad_w_out, mid = grad_w_of(
+        [pre_act, *pre], where, own_cols, other_cols, 1, scale_back, "grad_w_out", 10**9
+    )
+    grad_w_in_t, end = grad_w_of(
+        grad_pre_all, None, own_cols, other_cols, 0, scale_back, "grad_w_in", 5 * 10**10, [mid]
     )
     return (finish(terms, end), grad_w_in_t.T, grad_w_out)
 

time: 46.6 us -> 51.4 us (1.10)
  waiting for transfers between devices: 9.27 us -> 12.6 us
  Pallas kernels: 14.9 us -> 16.4 us
    ppermute x2, waiting for transfers between devices: 0.01 us -> 5.53 us  [spread(): got.append(lax.ppermute(held, 'tokens', [(i ^ mask, i) for i in range(n)]))]
    ppermute x6, waiting for transfers between devices: 4.42 us -> 1.12 us  [fetch(): return lax.ppermute(x, axis, [(partner(i, k, n), i) for i in range(n)])]
    pallas_call x9 -> x10, Pallas kernels: 14.9 us -> 16.4 us  [call(): pl.pallas_call(body, in_specs=[pl.BlockSpec(memory_space=in_space)] * len...]
    all_to_all x1, waiting for transfers between devices: 0.01 us -> 1.1 us  [shards(): terms = lax.all_to_all(blocks, 'mp', 0, 0)]
where the time goes in v14:
time: 51.4 us; the launch traced here: 51.2 us
  starting transfers between devices  21.2 us (41%)
  Pallas kernels  16.4 us (32%)
  waiting for transfers between devices  12.6 us (25%)
  between operations  0.93 us (2%)
    pallas_call x10, Pallas kernels, call(): pl.pallas_call(body, in_specs=[pl.BlockSpec(memory_space=in_space)] * len...  16.4 us
    ppermute x6, starting transfers between devices, fetch(): return lax.ppermute(x, axis, [(partner(i, k, n), i) for i in range(n)])  7.93 us
    ppermute x2, starting transfers between devices, spread(): got.append(lax.ppermute(held, 'tokens', [(i ^ mask, i) for i in range(n)]))  6.12 us
    ppermute x2, waiting for transfers between devices, spread(): got.append(lax.ppermute(held, 'tokens', [(i ^ mask, i) for i in range(n)]))  5.53 us
    ppermute x3, waiting for transfers between devices, fetch_chip(): lax.ppermute(x, 'mp', [(there, here) for here, there in chip_pairs(k)])  4.84 us
    ppermute x3, starting transfers between devices, fetch_chip(): lax.ppermute(x, 'mp', [(there, here) for here, there in chip_pairs(k)])  3.55 us
    all_to_all x1, starting transfers between devices, shards(): terms = lax.all_to_all(blocks, 'mp', 0, 0)  3.43 us
    ppermute x6, waiting for transfers between devices, fetch(): return lax.ppermute(x, axis, [(partner(i, k, n), i) for i in range(n)])  1.12 us
  transfers between devices with their start and end apart: 14, of which 6 were waited for; matrix products, arithmetic and copies ran while one was open for 0% of the time, Pallas kernels for 30%

profile of v14, /device:TPU:0, one launch (start us, length us, event | category | flops | bytes accessed | tf_op | source)
XLA Modules:
  0.0 51.2 jit_solution(13576792415027218265)
XLA Ops:
  0.7 5.1 %collective-permute-start = (bf16[32,1728]{1,0:T(8,128)(2,1)}, bf16[32,1728]{1,0:T(8,128)(2,1)S(1)}, u32[]{:S(2)}, u32[]{:S(2)}) collective-permute-start(bf16[32,1728]{1,0:T(8,128)(2,1)} %pre_in.1), channel_id=1, source_target_pairs={{3,0},{2,1},{1,2},{0,3},{7,4},{6,5},{5,6},{4,7},{11,8},{10,9},{9,1... | collective-permute-start | bytes 331784 | tf_op jit(solution)/shard_map/ppermute | solution.py:190
  5.9 0.3 pack.1
  6.2 1.6 %collective-permute-start.1 = (bf16[8,5120]{1,0:T(8,128)(2,1)S(1)}, bf16[8,5120]{1,0:T(8,128)(2,1)S(1)}, u32[]{:S(2)}, u32[]{:S(2)}) collective-permute-start(bf16[8,5120]{1,0:T(8,128)(2,1)S(1)} %get-tuple-element.14.refs_0_), channel_id=1, source_target_pairs={{8,0},{12,4},{0,8},{4,12},{24,16},{28,20},{16,24},{20,28},{9,1},{1... | collective-permute-start | bytes 245768 | tf_op jit(solution)/shard_map/ppermute | solution.py:48
  7.8 1.5 %collective-permute-start.2 = (bf16[8,5120]{1,0:T(8,128)(2,1)S(1)}, bf16[8,5120]{1,0:T(8,128)(2,1)S(1)}, u32[]{:S(2)}, u32[]{:S(2)}) collective-permute-start(bf16[8,5120]{1,0:T(8,128)(2,1)S(1)} %get-tuple-element.14.refs_0_), channel_id=1, source_target_pairs={{16,0},{20,4},{24,8},{28,12},{0,16},{4,20},{8,24},{12,28},{17,1},{... | collective-permute-start | bytes 245768 | tf_op jit(solution)/shard_map/ppermute | solution.py:48
  9.3 0.5 collective-permute-start.3
  9.8 0.9 %collective-permute-done.1.refs_1_ = bf16[8,5120]{1,0:T(8,128)(2,1)S(1)} collective-permute-done((bf16[8,5120]{1,0:T(8,128)(2,1)S(1)}, bf16[8,5120]{1,0:T(8,128)(2,1)S(1)}, u32[]{:S(2)}, u32[]{:S(2)}) %collective-permute-start.1) | collective-permute-done | bytes 81952 | tf_op jit(solution)/shard_map/ppermute | solution.py:48
  10.7 2.4 %collective-permute-done.2.refs_2_ = bf16[8,5120]{1,0:T(8,128)(2,1)S(1)} collective-permute-done((bf16[8,5120]{1,0:T(8,128)(2,1)S(1)}, bf16[8,5120]{1,0:T(8,128)(2,1)S(1)}, u32[]{:S(2)}, u32[]{:S(2)}) %collective-permute-start.2) | collective-permute-done | bytes 81952 | tf_op jit(solution)/shard_map/ppermute | solution.py:48
  13.1 1.5 %collective-permute-done.3.refs_3_ = bf16[8,5120]{1,0:T(8,128)(2,1)S(1)} collective-permute-done((bf16[8,5120]{1,0:T(8,128)(2,1)S(1)}, bf16[8,5120]{1,0:T(8,128)(2,1)S(1)}, u32[]{:S(2)}, u32[]{:S(2)}) %collective-permute-start.3) | collective-permute-done | bytes 81952 | tf_op jit(solution)/shard_map/ppermute | solution.py:48
  14.6 0.2 join.1
  14.9 1.9 %collective-permute-start.11 = (bf16[2,16,1280]{2,1,0:T(8,128)(2,1)S(1)}, bf16[2,16,1280]{2,1,0:T(8,128)(2,1)S(1)}, u32[]{:S(2)}, u32[]{:S(2)}) collective-permute-start(bf16[2,16,1280]{2,1,0:T(8,128)(2,1)S(1)} %get-tuple-element.20), channel_id=1, source_target_pairs={{3,0},{2,1},{1,2},{0,3},{7,4},{6,5},{5,6},{4,7},{11,8},{10,9},{9,1... | collective-permute-start | bytes 245768 | tf_op jit(solution)/shard_map/ppermute | solution.py:35
  16.8 1.6 %collective-permute-start.9 = (bf16[2,16,1280]{2,1,0:T(8,128)(2,1)S(1)}, bf16[2,16,1280]{2,1,0:T(8,128)(2,1)S(1)}, u32[]{:S(2)}, u32[]{:S(2)}) collective-permute-start(bf16[2,16,1280]{2,1,0:T(8,128)(2,1)S(1)} %get-tuple-element.18), channel_id=1, source_target_pairs={{1,0},{0,1},{3,2},{2,3},{5,4},{4,5},{7,6},{6,7},{9,8},{8,9},{11,10... | collective-permute-start | bytes 245768 | tf_op jit(solution)/shard_map/ppermute | solution.py:35
  18.5 4.9 %grad_pre.1.grad_pre_ref.refs_4_.refs_0_ = bf16[32,1728]{1,0:T(8,128)(2,1)S(1)} custom-call(bf16[16,5120]{1,0:T(8,128)(2,1)S(1)} %get-tuple-element.15.own_ref, bf16[16,5120]{1,0:T(8,128)(2,1)S(1)} %collective-permute-done.4.other_ref, bf16[32,1728]{1,0:T(8,128)(2,1)S(1)} %get-tuple-element.16.pre_ref.refs_0_, bf16[1728,5120]{1,0:T(8,128)(2,1)S(1)} %bitcast.3), custom_call_target="tpu_custom_call" | custom-call | flops 566231040 | bytes 17694720 | tf_op jit(solution)/shard_map/grad_pre/pallas_call | solution.py:61
  23.4 1.1 %collective-permute-done.9.refs_1_ = bf16[2,16,1280]{2,1,0:T(8,128)(2,1)S(1)} collective-permute-done((bf16[2,16,1280]{2,1,0:T(8,128)(2,1)S(1)}, bf16[2,16,1280]{2,1,0:T(8,128)(2,1)S(1)}, u32[]{:S(2)}, u32[]{:S(2)}) %collective-permute-start.9) | collective-permute-done | bytes 81952 | tf_op jit(solution)/shard_map/ppermute | solution.py:35
  24.6 1.0 %collective-permute-start.5 = (bf16[2,32,1728]{2,1,0:T(8,128)(2,1)S(1)}, bf16[2,32,1728]{2,1,0:T(8,128)(2,1)S(1)}, u32[]{:S(2)}, u32[]{:S(2)}) collective-permute-start(bf16[2,32,1728]{2,1,0:T(8,128)(2,1)S(1)} %pile.1.after), channel_id=1, source_target_pairs={{1,0},{0,1},{3,2},{2,3},{5,4},{4,5},{7,6},{6,7},{9,8},{8,9},{11,10... | collective-permute-start | bytes 663560 | tf_op jit(solution)/shard_map/ppermute | solution.py:190
  25.7 1.1 %collective-permute-start.6 = (bf16[32,1728]{1,0:T(8,128)(2,1)S(1)}, bf16[32,1728]{1,0:T(8,128)(2,1)S(1)}, u32[]{:S(2)}, u32[]{:S(2)}) collective-permute-start(bf16[32,1728]{1,0:T(8,128)(2,1)S(1)} %grad_pre.1.grad_pre_ref.refs_4_.refs_0_), channel_id=1, source_target_pairs={{1,0},{0,1},{3,2},{2,3},{5,4},{4,5},{7,6},{6,7},{9,8},{8,9},{11,10... | collective-permute-start | bytes 331784 | tf_op jit(solution)/shard_map/ppermute | solution.py:35
  26.7 1.2 %collective-permute-start.7 = (bf16[32,1728]{1,0:T(8,128)(2,1)S(1)}, bf16[32,1728]{1,0:T(8,128)(2,1)S(1)}, u32[]{:S(2)}, u32[]{:S(2)}) collective-permute-start(bf16[32,1728]{1,0:T(8,128)(2,1)S(1)} %grad_pre.1.grad_pre_ref.refs_4_.refs_0_), channel_id=1, source_target_pairs={{2,0},{3,1},{0,2},{1,3},{6,4},{7,5},{4,6},{5,7},{10,8},{11,9},{8,1... | collective-permute-start | bytes 331784 | tf_op jit(solution)/shard_map/ppermute | solution.py:35
  28.0 2.1 %collective-permute-start.8 = (bf16[32,1728]{1,0:T(8,128)(2,1)S(1)}, bf16[32,1728]{1,0:T(8,128)(2,1)S(1)}, u32[]{:S(2)}, u32[]{:S(2)}) collective-permute-start(bf16[32,1728]{1,0:T(8,128)(2,1)S(1)} %grad_pre.1.grad_pre_ref.refs_4_.refs_0_), channel_id=1, source_target_pairs={{3,0},{2,1},{1,2},{0,3},{7,4},{6,5},{5,6},{4,7},{11,8},{10,9},{9,1... | collective-permute-start | bytes 331784 | tf_op jit(solution)/shard_map/ppermute | solution.py:35
  30.0 5.5 %collective-permute-done.5.refs_0_.refs_2_ = bf16[2,32,1728]{2,1,0:T(8,128)(2,1)S(1)} collective-permute-done((bf16[2,32,1728]{2,1,0:T(8,128)(2,1)S(1)}, bf16[2,32,1728]{2,1,0:T(8,128)(2,1)S(1)}, u32[]{:S(2)}, u32[]{:S(2)}) %collective-permute-start.5) | collective-permute-done | bytes 221216 | tf_op jit(solution)/shard_map/ppermute | solution.py:190
  35.6 3.9 %grad_in_part.1 = bf16[8,4,5120]{2,1,0:T(4,128)(2,1)} custom-call(bf16[32,1728]{1,0:T(8,128)(2,1)S(1)} %grad_pre.1.grad_pre_ref.refs_4_.refs_0_, bf16[1728,5120]{1,0:T(8,128)(2,1)S(1)} %bitcast.6, bf16[2,32,1728]{2,1,0:T(8,128)(2,1)S(1)} %collective-permute-done.5.refs_0_.refs_2_), custom_call_target="tpu_custom_call" | custom-call | flops 566231040 | bytes 17694720 | tf_op jit(solution)/shard_map/grad_in_part/pallas_call | solution.py:61
  39.5 3.4 %all-to-all-start = ((bf16[8,4,5120]{2,1,0:T(4,128)(2,1)}), bf16[8,4,5120]{2,1,0:T(4,128)(2,1)S(1)}, u32[]{:S(2)}, u32[]{:S(2)}) async-start(bf16[8,4,5120]{2,1,0:T(4,128)(2,1)} %grad_in_part.1), calls=%async_computation | async-start | bytes 655360 | tf_op jit(solution)/shard_map/all_to_all | solution.py:386
  43.0 3.3 %grad_w_out.1 = (bf16[1728,1280]{1,0:T(8,128)(2,1)}, f32[8,128]{1,0:T(8,128)S(1)}) custom-call(bf16[32,1728]{1,0:T(8,128)(2,1)S(1)} %get-tuple-element.16.pre_ref.refs_0_, bf16[32,1728]{1,0:T(8,128)(2,1)S(1)} %collective-permute-done.high.refs_1_, bf16[2,32,1728]{2,1,0:T(8,128)(2,1)S(1)} %collective-permute-done.5.refs_0_.refs_2_, ...), custom_call_target="tpu_custom_call" | custom-call | flops 1000000000 | bytes 4423680 | tf_op jit(solution)/shard_map/grad_w_out/pallas_call | solution.py:61
  46.3 3.1 %grad_w_in.1 = (bf16[1728,1280]{1,0:T(8,128)(2,1)}, f32[8,128]{1,0:T(8,128)S(1)}) custom-call(bf16[32,1728]{1,0:T(8,128)(2,1)S(1)} %grad_pre.1.grad_pre_ref.refs_4_.refs_0_, bf16[32,1728]{1,0:T(8,128)(2,1)S(1)} %collective-permute-done.6.refs_1_, bf16[32,1728]{1,0:T(8,128)(2,1)S(1)} %collective-permute-done.7.refs_2_, ...), custom_call_target="tpu_custom_call" | custom-call | flops 49999998976 | bytes 4423680 | tf_op jit(solution)/shard_map/grad_w_in/pallas_call | solution.py:61
  49.4 1.1 %all-to-all-done.terms_ref = bf16[8,4,5120]{2,1,0:T(4,128)(2,1)S(1)} async-done(((bf16[8,4,5120]{2,1,0:T(4,128)(2,1)}), bf16[8,4,5120]{2,1,0:T(4,128)(2,1)S(1)}, u32[]{:S(2)}, u32[]{:S(2)}) %all-to-all-start) | async-done | bytes 327712 | tf_op jit(solution)/shard_map/all_to_all | solution.py:386
  50.5 0.7 %finish.1 = bf16[4,5120]{1,0:T(4,128)(2,1)} custom-call(bf16[8,4,5120]{2,1,0:T(4,128)(2,1)S(1)} %all-to-all-done.terms_ref, f32[8,128]{1,0:T(8,128)S(1)} %get-tuple-element.22.after), custom_call_target="tpu_custom_call" | custom-call | flops 1000000 | bytes 100000 | tf_op jit(solution)/shard_map/finish/pallas_call | solution.py:61
  (42 shorter events, 0.3 us)
Async XLA Ops:
  0.7 9.1 %collective-permute-start = (bf16[32,1728]{1,0:T(8,128)(2,1)}, bf16[32,1728]{1,0:T(8,128)(2,1)S(1)}, u32[]{:S(2)}, u32[]{:S(2)}) collective-permute-start(bf16[32,1728]{1,0:T(8,128)(2,1)} %pre_in.1), channel_id=1, source_target_pairs={{3,0},{2,1},{1,2},{0,3},{7,4},{6,5},{5,6},{4,7},{11,8},{10,9},{9,1... | collective-permute-start | bytes 331784 | tf_op jit(solution)/shard_map/ppermute | solution.py:190
  5.8 12.7 %slice-start = ((s8[17694720]{0:T(1024)(128)(4,1)}), s8[4194304]{0:T(1024)(128)(4,1)S(1)}, s32[]{:S(2)}) async-start(s8[17694720]{0:T(1024)(128)(4,1)} %bitcast.2), calls=%async_computation.1 | async-start | bytes 8388608
  5.8 12.7 %slice-start.1 = ((s8[17694720]{0:T(1024)(128)(4,1)}), s8[4194304]{0:T(1024)(128)(4,1)S(1)}, s32[]{:S(2)}) async-start(s8[17694720]{0:T(1024)(128)(4,1)} %bitcast.2), calls=%async_computation.2 | async-start | bytes 8388608
  5.8 12.7 %slice-start.2 = ((s8[17694720]{0:T(1024)(128)(4,1)}), s8[4194304]{0:T(1024)(128)(4,1)S(1)}, s32[]{:S(2)}) async-start(s8[17694720]{0:T(1024)(128)(4,1)} %bitcast.2), calls=%async_computation.3 | async-start | bytes 8388608
  5.8 12.6 %slice-start.3 = ((s8[17694720]{0:T(1024)(128)(4,1)}), s8[4194304]{0:T(1024)(128)(4,1)S(1)}, s32[]{:S(2)}) async-start(s8[17694720]{0:T(1024)(128)(4,1)} %bitcast.2), calls=%async_computation.4 | async-start | bytes 8388608
  5.8 12.6 %slice-start.4 = ((s8[17694720]{0:T(1024)(128)(4,1)}), s8[917504]{0:T(1024)(128)(4,1)S(1)}, s32[]{:S(2)}) async-start(s8[17694720]{0:T(1024)(128)(4,1)} %bitcast.2), calls=%async_computation.5 | async-start | bytes 1835008
  5.8 29.7 %slice-start.5 = ((s8[17694720]{0:T(1024)(128)(4,1)}), s8[4194304]{0:T(1024)(128)(4,1)S(1)}, s32[]{:S(2)}) async-start(s8[17694720]{0:T(1024)(128)(4,1)} %bitcast.4), calls=%async_computation.6 | async-start | bytes 8388608
  5.9 29.7 %slice-start.6 = ((s8[17694720]{0:T(1024)(128)(4,1)}), s8[4194304]{0:T(1024)(128)(4,1)S(1)}, s32[]{:S(2)}) async-start(s8[17694720]{0:T(1024)(128)(4,1)} %bitcast.4), calls=%async_computation.7 | async-start | bytes 8388608
  5.9 29.7 %slice-start.7 = ((s8[17694720]{0:T(1024)(128)(4,1)}), s8[4194304]{0:T(1024)(128)(4,1)S(1)}, s32[]{:S(2)}) async-start(s8[17694720]{0:T(1024)(128)(4,1)} %bitcast.4), calls=%async_computation.8 | async-start | bytes 8388608
  5.9 29.7 %slice-start.8 = ((s8[17694720]{0:T(1024)(128)(4,1)}), s8[4194304]{0:T(1024)(128)(4,1)S(1)}, s32[]{:S(2)}) async-start(s8[17694720]{0:T(1024)(128)(4,1)} %bitcast.4), calls=%async_computation.9 | async-start | bytes 8388608
  6.2 4.5 %collective-permute-start.1 = (bf16[8,5120]{1,0:T(8,128)(2,1)S(1)}, bf16[8,5120]{1,0:T(8,128)(2,1)S(1)}, u32[]{:S(2)}, u32[]{:S(2)}) collective-permute-start(bf16[8,5120]{1,0:T(8,128)(2,1)S(1)} %get-tuple-element.14.refs_0_), channel_id=1, source_target_pairs={{8,0},{12,4},{0,8},{4,12},{24,16},{28,20},{16,24},{20,28},{9,1},{1... | collective-permute-start | bytes 245768 | tf_op jit(solution)/shard_map/ppermute | solution.py:48
  7.8 5.3 %collective-permute-start.2 = (bf16[8,5120]{1,0:T(8,128)(2,1)S(1)}, bf16[8,5120]{1,0:T(8,128)(2,1)S(1)}, u32[]{:S(2)}, u32[]{:S(2)}) collective-permute-start(bf16[8,5120]{1,0:T(8,128)(2,1)S(1)} %get-tuple-element.14.refs_0_), channel_id=1, source_target_pairs={{16,0},{20,4},{24,8},{28,12},{0,16},{4,20},{8,24},{12,28},{17,1},{... | collective-permute-start | bytes 245768 | tf_op jit(solution)/shard_map/ppermute | solution.py:48
  9.3 5.3 %collective-permute-start.3 = (bf16[8,5120]{1,0:T(8,128)(2,1)S(1)}, bf16[8,5120]{1,0:T(8,128)(2,1)S(1)}, u32[]{:S(2)}, u32[]{:S(2)}) collective-permute-start(bf16[8,5120]{1,0:T(8,128)(2,1)S(1)} %get-tuple-element.14.refs_0_), channel_id=1, source_target_pairs={{24,0},{28,4},{16,8},{20,12},{8,16},{12,20},{0,24},{4,28},{25,1},{... | collective-permute-start | bytes 245768 | tf_op jit(solution)/shard_map/ppermute | solution.py:48
  14.8 3.6 %collective-permute-start.4 = (bf16[16,5120]{1,0:T(8,128)(2,1)S(1)}, bf16[16,5120]{1,0:T(8,128)(2,1)S(1)}, u32[]{:S(2)}, u32[]{:S(2)}) collective-permute-start(bf16[16,5120]{1,0:T(8,128)(2,1)S(1)} %get-tuple-element.15.own_ref), channel_id=1, source_target_pairs={{4,0},{0,4},{12,8},{8,12},{20,16},{16,20},{28,24},{24,28},{5,1},{1... | collective-permute-start | bytes 491528 | tf_op jit(solution)/shard_map/ppermute | solution.py:39
  14.9 8.6 %collective-permute-start.10 = (bf16[2,16,1280]{2,1,0:T(8,128)(2,1)S(1)}, bf16[2,16,1280]{2,1,0:T(8,128)(2,1)S(1)}, u32[]{:S(2)}, u32[]{:S(2)}) collective-permute-start(bf16[2,16,1280]{2,1,0:T(8,128)(2,1)S(1)} %get-tuple-element.19), channel_id=1, source_target_pairs={{2,0},{3,1},{0,2},{1,3},{6,4},{7,5},{4,6},{5,7},{10,8},{11,9},{8,1... | collective-permute-start | bytes 245768 | tf_op jit(solution)/shard_map/ppermute | solution.py:35
  14.9 8.5 %collective-permute-start.11 = (bf16[2,16,1280]{2,1,0:T(8,128)(2,1)S(1)}, bf16[2,16,1280]{2,1,0:T(8,128)(2,1)S(1)}, u32[]{:S(2)}, u32[]{:S(2)}) collective-permute-start(bf16[2,16,1280]{2,1,0:T(8,128)(2,1)S(1)} %get-tuple-element.20), channel_id=1, source_target_pairs={{3,0},{2,1},{1,2},{0,3},{7,4},{6,5},{5,6},{4,7},{11,8},{10,9},{9,1... | collective-permute-start | bytes 245768 | tf_op jit(solution)/shard_map/ppermute | solution.py:35
  16.8 7.7 %collective-permute-start.9 = (bf16[2,16,1280]{2,1,0:T(8,128)(2,1)S(1)}, bf16[2,16,1280]{2,1,0:T(8,128)(2,1)S(1)}, u32[]{:S(2)}, u32[]{:S(2)}) collective-permute-start(bf16[2,16,1280]{2,1,0:T(8,128)(2,1)S(1)} %get-tuple-element.18), channel_id=1, source_target_pairs={{1,0},{0,1},{3,2},{2,3},{5,4},{4,5},{7,6},{6,7},{9,8},{8,9},{11,10... | collective-permute-start | bytes 245768 | tf_op jit(solution)/shard_map/ppermute | solution.py:35
  18.5 17.1 %slice-start.9 = ((s8[17694720]{0:T(1024)(128)(4,1)}), s8[917504]{0:T(1024)(128)(4,1)S(1)}, s32[]{:S(2)}) async-start(s8[17694720]{0:T(1024)(128)(4,1)} %bitcast.4), calls=%async_computation.10 | async-start | bytes 1835008
  24.6 18.4 %collective-permute-start.12 = (bf16[4,2,16,1280]{3,2,1,0:T(8,128)(2,1)S(1)}, bf16[4,2,16,1280]{3,2,1,0:T(8,128)(2,1)S(1)}, u32[]{:S(2)}, u32[]{:S(2)}) collective-permute-start(bf16[4,2,16,1280]{3,2,1,0:T(8,128)(2,1)S(1)} %stack.1.refs_3_.refs_4_), channel_id=1, source_target_pairs={{4,0},{0,4},{12,8},{8,12},{20,16},{16,20},{28,24},{24,28},{5,1},{1... | collective-permute-start | bytes 983048 | tf_op jit(solution)/shard_map/ppermute | solution.py:39
  24.6 10.9 %collective-permute-start.5 = (bf16[2,32,1728]{2,1,0:T(8,128)(2,1)S(1)}, bf16[2,32,1728]{2,1,0:T(8,128)(2,1)S(1)}, u32[]{:S(2)}, u32[]{:S(2)}) collective-permute-start(bf16[2,32,1728]{2,1,0:T(8,128)(2,1)S(1)} %pile.1.after), channel_id=1, source_target_pairs={{1,0},{0,1},{3,2},{2,3},{5,4},{4,5},{7,6},{6,7},{9,8},{8,9},{11,10... | collective-permute-start | bytes 663560 | tf_op jit(solution)/shard_map/ppermute | solution.py:190
  25.7 20.6 %collective-permute-start.6 = (bf16[32,1728]{1,0:T(8,128)(2,1)S(1)}, bf16[32,1728]{1,0:T(8,128)(2,1)S(1)}, u32[]{:S(2)}, u32[]{:S(2)}) collective-permute-start(bf16[32,1728]{1,0:T(8,128)(2,1)S(1)} %grad_pre.1.grad_pre_ref.refs_4_.refs_0_), channel_id=1, source_target_pairs={{1,0},{0,1},{3,2},{2,3},{5,4},{4,5},{7,6},{6,7},{9,8},{8,9},{11,10... | collective-permute-start | bytes 331784 | tf_op jit(solution)/shard_map/ppermute | solution.py:35
  26.7 19.5 %collective-permute-start.7 = (bf16[32,1728]{1,0:T(8,128)(2,1)S(1)}, bf16[32,1728]{1,0:T(8,128)(2,1)S(1)}, u32[]{:S(2)}, u32[]{:S(2)}) collective-permute-start(bf16[32,1728]{1,0:T(8,128)(2,1)S(1)} %grad_pre.1.grad_pre_ref.refs_4_.refs_0_), channel_id=1, source_target_pairs={{2,0},{3,1},{0,2},{1,3},{6,4},{7,5},{4,6},{5,7},{10,8},{11,9},{8,1... | collective-permute-start | bytes 331784 | tf_op jit(solution)/shard_map/ppermute | solution.py:35
  28.0 18.3 %collective-permute-start.8 = (bf16[32,1728]{1,0:T(8,128)(2,1)S(1)}, bf16[32,1728]{1,0:T(8,128)(2,1)S(1)}, u32[]{:S(2)}, u32[]{:S(2)}) collective-permute-start(bf16[32,1728]{1,0:T(8,128)(2,1)S(1)} %grad_pre.1.grad_pre_ref.refs_4_.refs_0_), channel_id=1, source_target_pairs={{3,0},{2,1},{1,2},{0,3},{7,4},{6,5},{5,6},{4,7},{11,8},{10,9},{9,1... | collective-permute-start | bytes 331784 | tf_op jit(solution)/shard_map/ppermute | solution.py:35
  39.5 11.0 %all-to-all-start = ((bf16[8,4,5120]{2,1,0:T(4,128)(2,1)}), bf16[8,4,5120]{2,1,0:T(4,128)(2,1)S(1)}, u32[]{:S(2)}, u32[]{:S(2)}) async-start(bf16[8,4,5120]{2,1,0:T(4,128)(2,1)} %grad_in_part.1), calls=%async_computation | async-start | bytes 655360 | tf_op jit(solution)/shard_map/all_to_all | solution.py:386
  (3 other events, 15.5 us)

commit v15 on v14

--- a/solution.py
+++ b/solution.py
@@ -90,20 +90,11 @@
     )[0]
 
 
-def pack_body(tokens_in, grad_in, pre_in, after, both, pre_ref, tokens_ref, grad_ref, sems):
-    copies = [
-        pltpu.make_async_copy(source, target, sems.at[i])
-        for i, (source, target) in enumerate(
-            ((tokens_in, tokens_ref), (grad_in, grad_ref), (pre_in, pre_ref))
-        )
-    ]
-    for copy in copies:
-        copy.start()
-    for copy in copies:
-        copy.wait()
+def pack_body(tokens_ref, grad_ref, pre_in, after, both, pre_ref):
     both[...] = jnp.concatenate(
         [tokens_ref[...].astype(jnp.float32), grad_ref[...].astype(jnp.float32)], axis=0
     ).astype(jnp.bfloat16)
+    pre_ref[...] = pre_in[...]
 
 
 def pack(tokens_in, grad_out, pre_act, after):
@@ -114,14 +105,8 @@
         [(shape, jnp.bfloat16) for shape in shapes],
         [tokens_in, grad_out, pre_act, after],
         "pack",
-        [
-            pltpu.VMEM(tokens_in.shape, jnp.bfloat16),
-            pltpu.VMEM(tokens_in.shape, jnp.bfloat16),
-            pltpu.SemaphoreType.DMA((3,)),
-        ],
         flops=10**10,
         bytes_accessed=36 * 10**6,
-        in_space=pltpu.HBM,
     )
 
 
@@ -170,7 +155,8 @@
     return call(body, [(shape, jnp.bfloat16)], [*pieces, *after], "stack")[0]
 
 
-def pile_body(low, high, out):
+def pile_body(low, high, *refs):
+    out = refs[-1]
     count = out.shape[0] // 2
     if count == 1:
         out[0] = low[...]
@@ -180,18 +166,20 @@
         out[count:] = high[...]
 
 
-def spread(x, masks):
-    held, got, order, where = x, [], [0], {0: (0, 0)}
-    n = lax.axis_size("tokens")
-    for mask in masks:
-        if got:
-            shape = (len(order),) + x.shape
-            held = call(pile_body, [(shape, jnp.bfloat16)], [held, got[-1]], "pile")[0]
-        got.append(lax.ppermute(held, "tokens", [(i ^ mask, i) for i in range(n)]))
+def swap(x, mask):
+    return lax.ppermute(x, "tokens", [(i ^ mask, i) for i in range(lax.axis_size("tokens"))])
+
+
+def spread(x, first, masks, after):
+    held, got, order, where = x, [first], [0, masks[0]], {0: (0, 0), masks[0]: (1, 0)}
+    for mask in masks[1:]:
+        shape = (len(order),) + x.shape
+        held = call(pile_body, [(shape, jnp.bfloat16)], [held, got[-1], *after], "pile")[0]
+        got.append(swap(held, mask))
         for j, k in enumerate(order):
             where[k ^ mask] = (len(got), j)
         order = order + [k ^ mask for k in order]
-    return held, got, where
+    return got, where
 
 
 def grad_pre_body(block, own_ref, other_ref, pre_ref, w_ref, out_ref, rows, total):
@@ -360,7 +348,6 @@
         ],
         limit=20,
         flops=flops,
-        bytes_accessed=2 * hidden * part,
         out_spaces=[pltpu.HBM, pltpu.VMEM],
     )
 
@@ -371,10 +358,10 @@
     scale_back = 1.0 / math.sqrt(pre_act.shape[0] * n_tok)
 
     masks = (3, 1) if n_tok == 4 else [1 << i for i in range(n_tok.bit_length() - 1)]
-    held, pre, where = spread(pre_act, masks)
+    first = swap(pre_act, masks[0])
     both, pre_act = pack(tokens_in, grad_out, pre_act, lead())
     *pieces, own_rows = join(
-        [both] + [fetch_chip(both, k) for k in range(1, chips)], n_tok, held
+        [both] + [fetch_chip(both, k) for k in range(1, chips)], n_tok, first
     )
     pieces = [x if k == 0 else fetch(x, "tokens", k) for k, x in enumerate(pieces)]
 
@@ -382,13 +369,14 @@
     grad_pre_all = [grad_pre] + [fetch(grad_pre, "tokens", k) for k in range(1, n_tok)]
     own_cols = stack(pieces, [grad_pre])
     other_cols = other_core(own_cols)
-    blocks = grad_in_part(grad_pre, w_in.T, n_mp, [pre[-1]])
+    blocks = grad_in_part(grad_pre, w_in.T, n_mp, [])
     terms = lax.all_to_all(blocks, "mp", 0, 0)
-    grad_w_out, mid = grad_w_of(
-        [pre_act, *pre], where, own_cols, other_cols, 1, scale_back, "grad_w_out", 10**9
-    )
-    grad_w_in_t, end = grad_w_of(
-        grad_pre_all, None, own_cols, other_cols, 0, scale_back, "grad_w_in", 5 * 10**10, [mid]
+    pre, where = spread(pre_act, first, masks, [grad_pre])
+    grad_w_in_t, mid = grad_w_of(
+        grad_pre_all, None, own_cols, other_cols, 0, scale_back, "grad_w_in", 10**6
+    )
+    grad_w_out, end = grad_w_of(
+        [pre_act, *pre], where, own_cols, other_cols, 1, scale_back, "grad_w_out", 5 * 10**10, [mid]
     )
     return (finish(terms, end), grad_w_in_t.T, grad_w_out)
 

time: 51.4 us -> 48.6 us (0.946)
  waiting for transfers between devices: 12.6 us -> 8.33 us
  starting transfers between devices: 21.2 us -> 22.9 us
    ppermute x2, waiting for transfers between devices: 5.53 us -> 0.01 us  [swap(): lax.ppermute(x, 'tokens', [(i ^ mask, i) for i in range(lax.axis_size('to...]
    ppermute x6, waiting for transfers between devices: 1.12 us -> 3.46 us  [fetch(): return lax.ppermute(x, axis, [(partner(i, k, n), i) for i in range(n)])]
    all_to_all x1, waiting for transfers between devices: 1.1 us -> 0.01 us  [shards(): terms = lax.all_to_all(blocks, 'mp', 0, 0)]
    ppermute x6, starting transfers between devices: 7.93 us -> 8.83 us  [fetch(): return lax.ppermute(x, axis, [(partner(i, k, n), i) for i in range(n)])]
    ppermute x2, starting transfers between devices: 6.12 us -> 6.94 us  [swap(): lax.ppermute(x, 'tokens', [(i ^ mask, i) for i in range(lax.axis_size('to...]
  transfers between devices with their start and end apart: 14 -> 14, of which waited for: 6 -> 5; matrix products, arithmetic and copies ran while one was open for 0% -> 0% of each run, Pallas kernels for 30% -> 32%
where the time goes in v15:
time: 48.6 us; the launch traced here: 48.4 us
  starting transfers between devices  22.9 us (47%)
  Pallas kernels  16.1 us (33%)
  waiting for transfers between devices  8.33 us (17%)
  between operations  0.92 us (2%)
    pallas_call x10, Pallas kernels, call(): pl.pallas_call(body, in_specs=[pl.BlockSpec(memory_space=in_space)] * len...  16.1 us
    ppermute x6, starting transfers between devices, fetch(): return lax.ppermute(x, axis, [(partner(i, k, n), i) for i in range(n)])  8.83 us
    ppermute x2, starting transfers between devices, swap(): lax.ppermute(x, 'tokens', [(i ^ mask, i) for i in range(lax.axis_size('to...  6.94 us
    ppermute x3, waiting for transfers between devices, fetch_chip(): lax.ppermute(x, 'mp', [(there, here) for here, there in chip_pairs(k)])  4.86 us
    ppermute x3, starting transfers between devices, fetch_chip(): lax.ppermute(x, 'mp', [(there, here) for here, there in chip_pairs(k)])  3.55 us
    ppermute x6, waiting for transfers between devices, fetch(): return lax.ppermute(x, axis, [(partner(i, k, n), i) for i in range(n)])  3.46 us
    all_to_all x1, starting transfers between devices, shards(): terms = lax.all_to_all(blocks, 'mp', 0, 0)  3.43 us
  transfers between devices with their start and end apart: 14, of which 5 were waited for; matrix products, arithmetic and copies ran while one was open for 0% of the time, Pallas kernels for 32%

profile of v15, /device:TPU:0, one launch (start us, length us, event | category | flops | bytes accessed | tf_op | source)
XLA Modules:
  0.0 48.4 jit_solution(9615656892145504070)
XLA Ops:
  0.7 5.1 %collective-permute-start = (bf16[32,1728]{1,0:T(8,128)(2,1)}, bf16[32,1728]{1,0:T(8,128)(2,1)S(1)}, u32[]{:S(2)}, u32[]{:S(2)}) collective-permute-start(bf16[32,1728]{1,0:T(8,128)(2,1)} %pre_in.1), channel_id=1, source_target_pairs={{3,0},{2,1},{1,2},{0,3},{7,4},{6,5},{5,6},{4,7},{11,8},{10,9},{9,1... | collective-permute-start | bytes 331784 | tf_op jit(solution)/shard_map/ppermute | solution.py:170
  5.9 1.6 %collective-permute-start.1 = (bf16[8,5120]{1,0:T(8,128)(2,1)S(1)}, bf16[8,5120]{1,0:T(8,128)(2,1)S(1)}, u32[]{:S(2)}, u32[]{:S(2)}) collective-permute-start(bf16[8,5120]{1,0:T(8,128)(2,1)S(1)} %get-tuple-element.14.refs_0_), channel_id=1, source_target_pairs={{8,0},{12,4},{0,8},{4,12},{24,16},{28,20},{16,24},{20,28},{9,1},{1... | collective-permute-start | bytes 245768 | tf_op jit(solution)/shard_map/ppermute | solution.py:48
  7.5 1.5 %collective-permute-start.2 = (bf16[8,5120]{1,0:T(8,128)(2,1)S(1)}, bf16[8,5120]{1,0:T(8,128)(2,1)S(1)}, u32[]{:S(2)}, u32[]{:S(2)}) collective-permute-start(bf16[8,5120]{1,0:T(8,128)(2,1)S(1)} %get-tuple-element.14.refs_0_), channel_id=1, source_target_pairs={{16,0},{20,4},{24,8},{28,12},{0,16},{4,20},{8,24},{12,28},{17,1},{... | collective-permute-start | bytes 245768 | tf_op jit(solution)/shard_map/ppermute | solution.py:48
  9.0 0.5 collective-permute-start.3
  9.5 1.0 %collective-permute-done.1.refs_1_ = bf16[8,5120]{1,0:T(8,128)(2,1)S(1)} collective-permute-done((bf16[8,5120]{1,0:T(8,128)(2,1)S(1)}, bf16[8,5120]{1,0:T(8,128)(2,1)S(1)}, u32[]{:S(2)}, u32[]{:S(2)}) %collective-permute-start.1) | collective-permute-done | bytes 81952 | tf_op jit(solution)/shard_map/ppermute | solution.py:48
  10.4 2.4 %collective-permute-done.2.refs_2_ = bf16[8,5120]{1,0:T(8,128)(2,1)S(1)} collective-permute-done((bf16[8,5120]{1,0:T(8,128)(2,1)S(1)}, bf16[8,5120]{1,0:T(8,128)(2,1)S(1)}, u32[]{:S(2)}, u32[]{:S(2)}) %collective-permute-start.2) | collective-permute-done | bytes 81952 | tf_op jit(solution)/shard_map/ppermute | solution.py:48
  12.8 1.5 %collective-permute-done.3.refs_3_ = bf16[8,5120]{1,0:T(8,128)(2,1)S(1)} collective-permute-done((bf16[8,5120]{1,0:T(8,128)(2,1)S(1)}, bf16[8,5120]{1,0:T(8,128)(2,1)S(1)}, u32[]{:S(2)}, u32[]{:S(2)}) %collective-permute-start.3) | collective-permute-done | bytes 81952 | tf_op jit(solution)/shard_map/ppermute | solution.py:48
  14.3 0.2 join.1
  14.5 0.1 collective-permute-start.4
  14.7 1.3 %collective-permute-start.7 = (bf16[2,16,1280]{2,1,0:T(8,128)(2,1)S(1)}, bf16[2,16,1280]{2,1,0:T(8,128)(2,1)S(1)}, u32[]{:S(2)}, u32[]{:S(2)}) collective-permute-start(bf16[2,16,1280]{2,1,0:T(8,128)(2,1)S(1)} %get-tuple-element.19), channel_id=1, source_target_pairs={{2,0},{3,1},{0,2},{1,3},{6,4},{7,5},{4,6},{5,7},{10,8},{11,9},{8,1... | collective-permute-start | bytes 245768 | tf_op jit(solution)/shard_map/ppermute | solution.py:35
  16.0 3.1 %collective-permute-start.8 = (bf16[2,16,1280]{2,1,0:T(8,128)(2,1)S(1)}, bf16[2,16,1280]{2,1,0:T(8,128)(2,1)S(1)}, u32[]{:S(2)}, u32[]{:S(2)}) collective-permute-start(bf16[2,16,1280]{2,1,0:T(8,128)(2,1)S(1)} %get-tuple-element.20), channel_id=1, source_target_pairs={{3,0},{2,1},{1,2},{0,3},{7,4},{6,5},{5,6},{4,7},{11,8},{10,9},{9,1... | collective-permute-start | bytes 245768 | tf_op jit(solution)/shard_map/ppermute | solution.py:35
  19.1 4.9 %grad_pre.1.grad_pre_ref.refs_0_.refs_4_ = bf16[32,1728]{1,0:T(8,128)(2,1)S(1)} custom-call(bf16[16,5120]{1,0:T(8,128)(2,1)S(1)} %get-tuple-element.15.own_ref, bf16[16,5120]{1,0:T(8,128)(2,1)S(1)} %collective-permute-done.4.other_ref, bf16[32,1728]{1,0:T(8,128)(2,1)S(1)} %get-tuple-element.16.pre_ref.low.refs_0_, bf16[1728,5120]{1,0:T(8,128)(2,1)S(1)} %bitcast.6), custom_call_target="tpu_custom_call" | custom-call | flops 566231040 | bytes 17694720 | tf_op jit(solution)/shard_map/grad_pre/pallas_call | solution.py:61
  24.1 0.4 collective-permute-done.7.refs_2_
  24.5 0.1 collective-permute-start.9
  24.6 1.8 %collective-permute-start.5 = (bf16[2,32,1728]{2,1,0:T(8,128)(2,1)S(1)}, bf16[2,32,1728]{2,1,0:T(8,128)(2,1)S(1)}, u32[]{:S(2)}, u32[]{:S(2)}) collective-permute-start(bf16[2,32,1728]{2,1,0:T(8,128)(2,1)S(1)} %pile.1), channel_id=1, source_target_pairs={{1,0},{0,1},{3,2},{2,3},{5,4},{4,5},{7,6},{6,7},{9,8},{8,9},{11,10... | collective-permute-start | bytes 663560 | tf_op jit(solution)/shard_map/ppermute | solution.py:170
  26.4 0.3 collective-permute-start.10
  26.7 1.8 %collective-permute-start.11 = (bf16[32,1728]{1,0:T(8,128)(2,1)S(1)}, bf16[32,1728]{1,0:T(8,128)(2,1)S(1)}, u32[]{:S(2)}, u32[]{:S(2)}) collective-permute-start(bf16[32,1728]{1,0:T(8,128)(2,1)S(1)} %grad_pre.1.grad_pre_ref.refs_0_.refs_4_), channel_id=1, source_target_pairs={{2,0},{3,1},{0,2},{1,3},{6,4},{7,5},{4,6},{5,7},{10,8},{11,9},{8,1... | collective-permute-start | bytes 331784 | tf_op jit(solution)/shard_map/ppermute | solution.py:35
  28.4 2.3 %collective-permute-start.12 = (bf16[32,1728]{1,0:T(8,128)(2,1)S(1)}, bf16[32,1728]{1,0:T(8,128)(2,1)S(1)}, u32[]{:S(2)}, u32[]{:S(2)}) collective-permute-start(bf16[32,1728]{1,0:T(8,128)(2,1)S(1)} %grad_pre.1.grad_pre_ref.refs_0_.refs_4_), channel_id=1, source_target_pairs={{3,0},{2,1},{1,2},{0,3},{7,4},{6,5},{5,6},{4,7},{11,8},{10,9},{9,1... | collective-permute-start | bytes 331784 | tf_op jit(solution)/shard_map/ppermute | solution.py:35
  30.8 3.9 %grad_in_part.1 = bf16[8,4,5120]{2,1,0:T(4,128)(2,1)} custom-call(bf16[32,1728]{1,0:T(8,128)(2,1)S(1)} %grad_pre.1.grad_pre_ref.refs_0_.refs_4_, bf16[1728,5120]{1,0:T(8,128)(2,1)S(1)} %bitcast.4), custom_call_target="tpu_custom_call" | custom-call | flops 566231040 | bytes 17694720 | tf_op jit(solution)/shard_map/grad_in_part/pallas_call | solution.py:61
  34.7 3.4 %all-to-all-start = ((bf16[8,4,5120]{2,1,0:T(4,128)(2,1)}), bf16[8,4,5120]{2,1,0:T(4,128)(2,1)S(1)}, u32[]{:S(2)}, u32[]{:S(2)}) async-start(bf16[8,4,5120]{2,1,0:T(4,128)(2,1)} %grad_in_part.1), calls=%async_computation | async-start | bytes 655360 | tf_op jit(solution)/shard_map/all_to_all | solution.py:373
  38.2 3.1 %collective-permute-done.12.refs_3_ = bf16[32,1728]{1,0:T(8,128)(2,1)S(1)} collective-permute-done((bf16[32,1728]{1,0:T(8,128)(2,1)S(1)}, bf16[32,1728]{1,0:T(8,128)(2,1)S(1)}, u32[]{:S(2)}, u32[]{:S(2)}) %collective-permute-start.12) | collective-permute-done | bytes 110624 | tf_op jit(solution)/shard_map/ppermute | solution.py:35
  41.2 3.1 %grad_w_in.1 = (bf16[1728,1280]{1,0:T(8,128)(2,1)}, f32[8,128]{1,0:T(8,128)S(1)}) custom-call(bf16[32,1728]{1,0:T(8,128)(2,1)S(1)} %grad_pre.1.grad_pre_ref.refs_0_.refs_4_, bf16[32,1728]{1,0:T(8,128)(2,1)S(1)} %collective-permute-done.10.refs_1_, bf16[32,1728]{1,0:T(8,128)(2,1)S(1)} %collective-permute-done.11.refs_2_, ...), custom_call_target="tpu_custom_call" | custom-call | flops 1000000 | bytes 100000 | tf_op jit(solution)/shard_map/grad_w_in/pallas_call | solution.py:61
  44.4 3.3 %grad_w_out.1 = (bf16[1728,1280]{1,0:T(8,128)(2,1)}, f32[8,128]{1,0:T(8,128)S(1)}) custom-call(bf16[32,1728]{1,0:T(8,128)(2,1)S(1)} %get-tuple-element.16.pre_ref.low.refs_0_, bf16[32,1728]{1,0:T(8,128)(2,1)S(1)} %collective-permute-done.after.high.refs_1_, bf16[2,32,1728]{2,1,0:T(8,128)(2,1)S(1)} %collective-permute-done.5.refs_2_, ...), custom_call_target="tpu_custom_call" | custom-call | flops 49999998976 | bytes 100000 | tf_op jit(solution)/shard_map/grad_w_out/pallas_call | solution.py:61
  47.7 0.7 %finish.1 = bf16[4,5120]{1,0:T(4,128)(2,1)} custom-call(bf16[8,4,5120]{2,1,0:T(4,128)(2,1)S(1)} %all-to-all-done.terms_ref, f32[8,128]{1,0:T(8,128)S(1)} %get-tuple-element.22.after), custom_call_target="tpu_custom_call" | custom-call | flops 1000000 | bytes 100000 | tf_op jit(solution)/shard_map/finish/pallas_call | solution.py:61
  (42 shorter events, 0.2 us)
Async XLA Ops:
  0.7 13.7 %collective-permute-start = (bf16[32,1728]{1,0:T(8,128)(2,1)}, bf16[32,1728]{1,0:T(8,128)(2,1)S(1)}, u32[]{:S(2)}, u32[]{:S(2)}) collective-permute-start(bf16[32,1728]{1,0:T(8,128)(2,1)} %pre_in.1), channel_id=1, source_target_pairs={{3,0},{2,1},{1,2},{0,3},{7,4},{6,5},{5,6},{4,7},{11,8},{10,9},{9,1... | collective-permute-start | bytes 331784 | tf_op jit(solution)/shard_map/ppermute | solution.py:170
  5.8 13.3 %slice-start.5 = ((s8[17694720]{0:T(1024)(128)(4,1)}), s8[4194304]{0:T(1024)(128)(4,1)S(1)}, s32[]{:S(2)}) async-start(s8[17694720]{0:T(1024)(128)(4,1)} %bitcast.5), calls=%async_computation.6 | async-start | bytes 8388608
  5.8 13.3 %slice-start.6 = ((s8[17694720]{0:T(1024)(128)(4,1)}), s8[4194304]{0:T(1024)(128)(4,1)S(1)}, s32[]{:S(2)}) async-start(s8[17694720]{0:T(1024)(128)(4,1)} %bitcast.5), calls=%async_computation.7 | async-start | bytes 8388608
  5.8 13.3 %slice-start.7 = ((s8[17694720]{0:T(1024)(128)(4,1)}), s8[4194304]{0:T(1024)(128)(4,1)S(1)}, s32[]{:S(2)}) async-start(s8[17694720]{0:T(1024)(128)(4,1)} %bitcast.5), calls=%async_computation.8 | async-start | bytes 8388608
  5.8 13.2 %slice-start.8 = ((s8[17694720]{0:T(1024)(128)(4,1)}), s8[4194304]{0:T(1024)(128)(4,1)S(1)}, s32[]{:S(2)}) async-start(s8[17694720]{0:T(1024)(128)(4,1)} %bitcast.5), calls=%async_computation.9 | async-start | bytes 8388608
  5.8 13.2 %slice-start.9 = ((s8[17694720]{0:T(1024)(128)(4,1)}), s8[917504]{0:T(1024)(128)(4,1)S(1)}, s32[]{:S(2)}) async-start(s8[17694720]{0:T(1024)(128)(4,1)} %bitcast.5), calls=%async_computation.10 | async-start | bytes 1835008
  5.8 25.0 %slice-start = ((s8[17694720]{0:T(1024)(128)(4,1)}), s8[4194304]{0:T(1024)(128)(4,1)S(1)}, s32[]{:S(2)}) async-start(s8[17694720]{0:T(1024)(128)(4,1)} %bitcast.2), calls=%async_computation.1 | async-start | bytes 8388608
  5.9 24.9 %slice-start.1 = ((s8[17694720]{0:T(1024)(128)(4,1)}), s8[4194304]{0:T(1024)(128)(4,1)S(1)}, s32[]{:S(2)}) async-start(s8[17694720]{0:T(1024)(128)(4,1)} %bitcast.2), calls=%async_computation.2 | async-start | bytes 8388608
  5.9 24.9 %slice-start.2 = ((s8[17694720]{0:T(1024)(128)(4,1)}), s8[4194304]{0:T(1024)(128)(4,1)S(1)}, s32[]{:S(2)}) async-start(s8[17694720]{0:T(1024)(128)(4,1)} %bitcast.2), calls=%async_computation.3 | async-start | bytes 8388608
  5.9 24.9 %slice-start.3 = ((s8[17694720]{0:T(1024)(128)(4,1)}), s8[4194304]{0:T(1024)(128)(4,1)S(1)}, s32[]{:S(2)}) async-start(s8[17694720]{0:T(1024)(128)(4,1)} %bitcast.2), calls=%async_computation.4 | async-start | bytes 8388608
  5.9 4.5 %collective-permute-start.1 = (bf16[8,5120]{1,0:T(8,128)(2,1)S(1)}, bf16[8,5120]{1,0:T(8,128)(2,1)S(1)}, u32[]{:S(2)}, u32[]{:S(2)}) collective-permute-start(bf16[8,5120]{1,0:T(8,128)(2,1)S(1)} %get-tuple-element.14.refs_0_), channel_id=1, source_target_pairs={{8,0},{12,4},{0,8},{4,12},{24,16},{28,20},{16,24},{20,28},{9,1},{1... | collective-permute-start | bytes 245768 | tf_op jit(solution)/shard_map/ppermute | solution.py:48
  7.5 5.3 %collective-permute-start.2 = (bf16[8,5120]{1,0:T(8,128)(2,1)S(1)}, bf16[8,5120]{1,0:T(8,128)(2,1)S(1)}, u32[]{:S(2)}, u32[]{:S(2)}) collective-permute-start(bf16[8,5120]{1,0:T(8,128)(2,1)S(1)} %get-tuple-element.14.refs_0_), channel_id=1, source_target_pairs={{16,0},{20,4},{24,8},{28,12},{0,16},{4,20},{8,24},{12,28},{17,1},{... | collective-permute-start | bytes 245768 | tf_op jit(solution)/shard_map/ppermute | solution.py:48
  9.0 5.3 %collective-permute-start.3 = (bf16[8,5120]{1,0:T(8,128)(2,1)S(1)}, bf16[8,5120]{1,0:T(8,128)(2,1)S(1)}, u32[]{:S(2)}, u32[]{:S(2)}) collective-permute-start(bf16[8,5120]{1,0:T(8,128)(2,1)S(1)} %get-tuple-element.14.refs_0_), channel_id=1, source_target_pairs={{24,0},{28,4},{16,8},{20,12},{8,16},{12,20},{0,24},{4,28},{25,1},{... | collective-permute-start | bytes 245768 | tf_op jit(solution)/shard_map/ppermute | solution.py:48
  14.5 4.5 %collective-permute-start.4 = (bf16[16,5120]{1,0:T(8,128)(2,1)S(1)}, bf16[16,5120]{1,0:T(8,128)(2,1)S(1)}, u32[]{:S(2)}, u32[]{:S(2)}) collective-permute-start(bf16[16,5120]{1,0:T(8,128)(2,1)S(1)} %get-tuple-element.15.own_ref), channel_id=1, source_target_pairs={{4,0},{0,4},{12,8},{8,12},{20,16},{16,20},{28,24},{24,28},{5,1},{1... | collective-permute-start | bytes 491528 | tf_op jit(solution)/shard_map/ppermute | solution.py:39
  14.6 9.5 %collective-permute-start.6 = (bf16[2,16,1280]{2,1,0:T(8,128)(2,1)S(1)}, bf16[2,16,1280]{2,1,0:T(8,128)(2,1)S(1)}, u32[]{:S(2)}, u32[]{:S(2)}) collective-permute-start(bf16[2,16,1280]{2,1,0:T(8,128)(2,1)S(1)} %get-tuple-element.18), channel_id=1, source_target_pairs={{1,0},{0,1},{3,2},{2,3},{5,4},{4,5},{7,6},{6,7},{9,8},{8,9},{11,10... | collective-permute-start | bytes 245768 | tf_op jit(solution)/shard_map/ppermute | solution.py:35
  14.7 9.8 %collective-permute-start.7 = (bf16[2,16,1280]{2,1,0:T(8,128)(2,1)S(1)}, bf16[2,16,1280]{2,1,0:T(8,128)(2,1)S(1)}, u32[]{:S(2)}, u32[]{:S(2)}) collective-permute-start(bf16[2,16,1280]{2,1,0:T(8,128)(2,1)S(1)} %get-tuple-element.19), channel_id=1, source_target_pairs={{2,0},{3,1},{0,2},{1,3},{6,4},{7,5},{4,6},{5,7},{10,8},{11,9},{8,1... | collective-permute-start | bytes 245768 | tf_op jit(solution)/shard_map/ppermute | solution.py:35
  16.0 8.5 %collective-permute-start.8 = (bf16[2,16,1280]{2,1,0:T(8,128)(2,1)S(1)}, bf16[2,16,1280]{2,1,0:T(8,128)(2,1)S(1)}, u32[]{:S(2)}, u32[]{:S(2)}) collective-permute-start(bf16[2,16,1280]{2,1,0:T(8,128)(2,1)S(1)} %get-tuple-element.20), channel_id=1, source_target_pairs={{3,0},{2,1},{1,2},{0,3},{7,4},{6,5},{5,6},{4,7},{11,8},{10,9},{9,1... | collective-permute-start | bytes 245768 | tf_op jit(solution)/shard_map/ppermute | solution.py:35
  19.1 11.7 %slice-start.4 = ((s8[17694720]{0:T(1024)(128)(4,1)}), s8[917504]{0:T(1024)(128)(4,1)S(1)}, s32[]{:S(2)}) async-start(s8[17694720]{0:T(1024)(128)(4,1)} %bitcast.2), calls=%async_computation.5 | async-start | bytes 1835008
  24.5 16.8 %collective-permute-start.9 = (bf16[4,2,16,1280]{3,2,1,0:T(8,128)(2,1)S(1)}, bf16[4,2,16,1280]{3,2,1,0:T(8,128)(2,1)S(1)}, u32[]{:S(2)}, u32[]{:S(2)}) collective-permute-start(bf16[4,2,16,1280]{3,2,1,0:T(8,128)(2,1)S(1)} %stack.1.refs_4_.refs_3_), channel_id=1, source_target_pairs={{4,0},{0,4},{12,8},{8,12},{20,16},{16,20},{28,24},{24,28},{5,1},{1... | collective-permute-start | bytes 983048 | tf_op jit(solution)/shard_map/ppermute | solution.py:39
  24.6 19.8 %collective-permute-start.5 = (bf16[2,32,1728]{2,1,0:T(8,128)(2,1)S(1)}, bf16[2,32,1728]{2,1,0:T(8,128)(2,1)S(1)}, u32[]{:S(2)}, u32[]{:S(2)}) collective-permute-start(bf16[2,32,1728]{2,1,0:T(8,128)(2,1)S(1)} %pile.1), channel_id=1, source_target_pairs={{1,0},{0,1},{3,2},{2,3},{5,4},{4,5},{7,6},{6,7},{9,8},{8,9},{11,10... | collective-permute-start | bytes 663560 | tf_op jit(solution)/shard_map/ppermute | solution.py:170
  26.4 11.7 %collective-permute-start.10 = (bf16[32,1728]{1,0:T(8,128)(2,1)S(1)}, bf16[32,1728]{1,0:T(8,128)(2,1)S(1)}, u32[]{:S(2)}, u32[]{:S(2)}) collective-permute-start(bf16[32,1728]{1,0:T(8,128)(2,1)S(1)} %grad_pre.1.grad_pre_ref.refs_0_.refs_4_), channel_id=1, source_target_pairs={{1,0},{0,1},{3,2},{2,3},{5,4},{4,5},{7,6},{6,7},{9,8},{8,9},{11,10... | collective-permute-start | bytes 331784 | tf_op jit(solution)/shard_map/ppermute | solution.py:35
  26.7 11.5 %collective-permute-start.11 = (bf16[32,1728]{1,0:T(8,128)(2,1)S(1)}, bf16[32,1728]{1,0:T(8,128)(2,1)S(1)}, u32[]{:S(2)}, u32[]{:S(2)}) collective-permute-start(bf16[32,1728]{1,0:T(8,128)(2,1)S(1)} %grad_pre.1.grad_pre_ref.refs_0_.refs_4_), channel_id=1, source_target_pairs={{2,0},{3,1},{0,2},{1,3},{6,4},{7,5},{4,6},{5,7},{10,8},{11,9},{8,1... | collective-permute-start | bytes 331784 | tf_op jit(solution)/shard_map/ppermute | solution.py:35
  28.4 12.8 %collective-permute-start.12 = (bf16[32,1728]{1,0:T(8,128)(2,1)S(1)}, bf16[32,1728]{1,0:T(8,128)(2,1)S(1)}, u32[]{:S(2)}, u32[]{:S(2)}) collective-permute-start(bf16[32,1728]{1,0:T(8,128)(2,1)S(1)} %grad_pre.1.grad_pre_ref.refs_0_.refs_4_), channel_id=1, source_target_pairs={{3,0},{2,1},{1,2},{0,3},{7,4},{6,5},{5,6},{4,7},{11,8},{10,9},{9,1... | collective-permute-start | bytes 331784 | tf_op jit(solution)/shard_map/ppermute | solution.py:35
  34.7 13.0 %all-to-all-start = ((bf16[8,4,5120]{2,1,0:T(4,128)(2,1)}), bf16[8,4,5120]{2,1,0:T(4,128)(2,1)S(1)}, u32[]{:S(2)}, u32[]{:S(2)}) async-start(bf16[8,4,5120]{2,1,0:T(4,128)(2,1)} %grad_in_part.1), calls=%async_computation | async-start | bytes 655360 | tf_op jit(solution)/shard_map/all_to_all | solution.py:373
  (3 other events, 15.5 us)

commit v16 on v13

--- a/solution.py
+++ b/solution.py
@@ -90,20 +90,11 @@
     )[0]
 
 
-def pack_body(tokens_in, grad_in, pre_in, after, both, pre_ref, tokens_ref, grad_ref, sems):
-    copies = [
-        pltpu.make_async_copy(source, target, sems.at[i])
-        for i, (source, target) in enumerate(
-            ((tokens_in, tokens_ref), (grad_in, grad_ref), (pre_in, pre_ref))
-        )
-    ]
-    for copy in copies:
-        copy.start()
-    for copy in copies:
-        copy.wait()
+def pack_body(tokens_ref, grad_ref, pre_in, after, both, pre_ref):
     both[...] = jnp.concatenate(
         [tokens_ref[...].astype(jnp.float32), grad_ref[...].astype(jnp.float32)], axis=0
     ).astype(jnp.bfloat16)
+    pre_ref[...] = pre_in[...]
 
 
 def pack(tokens_in, grad_out, pre_act, after):
@@ -114,21 +105,15 @@
         [(shape, jnp.bfloat16) for shape in shapes],
         [tokens_in, grad_out, pre_act, after],
         "pack",
-        [
-            pltpu.VMEM(tokens_in.shape, jnp.bfloat16),
-            pltpu.VMEM(tokens_in.shape, jnp.bfloat16),
-            pltpu.SemaphoreType.DMA((3,)),
-        ],
         flops=10**10,
         bytes_accessed=36 * 10**6,
-        in_space=pltpu.HBM,
-    )
-
-
-def join_body(count, after, *refs):
+    )
+
+
+def join_body(count, places, *refs):
     rows_in = refs[:count]
-    *pieces, grad_ref, slabs = refs[count:]
-    places, _, _, part = slabs.shape
+    *pieces, grad_ref, slabs = refs[-places - 2 :]
+    part = slabs.shape[3]
     parts = [x[...].astype(jnp.float32) for x in rows_in]
     each = parts[0].shape[0] // 2
     tokens = jnp.concatenate([x[:each] for x in parts], axis=0)
@@ -149,9 +134,9 @@
     rows, part = count * both // 2, width // n_tok
     shapes = [(2, rows, part)] * n_tok + [(rows, width)]
     return call(
-        functools.partial(join_body, count),
+        functools.partial(join_body, count, n_tok),
         [(shape, jnp.bfloat16) for shape in shapes],
-        [after, *rows_in],
+        [*rows_in, *after],
         "join",
         [pltpu.VMEM((n_tok, 2, rows, part), jnp.float32)],
         limit=16,
@@ -170,31 +155,7 @@
     return call(body, [(shape, jnp.bfloat16)], [*pieces, *after], "stack")[0]
 
 
-def pile_body(low, high, out):
-    count = out.shape[0] // 2
-    if count == 1:
-        out[0] = low[...]
-        out[1] = high[...]
-    else:
-        out[:count] = low[...]
-        out[count:] = high[...]
-
-
-def spread(x, masks):
-    held, got, order, where = x, [], [0], {0: (0, 0)}
-    n = lax.axis_size("tokens")
-    for mask in masks:
-        if got:
-            shape = (len(order),) + x.shape
-            held = call(pile_body, [(shape, jnp.bfloat16)], [held, got[-1]], "pile")[0]
-        got.append(lax.ppermute(held, "tokens", [(i ^ mask, i) for i in range(n)]))
-        for j, k in enumerate(order):
-            where[k ^ mask] = (len(got), j)
-        order = order + [k ^ mask for k in order]
-    return held, got, where
-
-
-def grad_pre_body(block, own_ref, other_ref, pre_ref, w_ref, out_ref, rows, total):
+def grad_pre_body(block, own_ref, other_ref, pre_ref, w_ref, rider_ref, out_ref, duo_ref, rows, total):
     hidden, group = total.shape
     half = own_ref.shape[0]
     rows[:half, :] = own_ref[...]
@@ -215,21 +176,24 @@
     pre = jnp.dot(
         pick.astype(jnp.float32).astype(jnp.bfloat16), pre_ref[...], preferred_element_type=jnp.float32
     )
-    out_ref[...] = (total[...].T * gelu_slope(pre)).astype(jnp.bfloat16)
-
-
-def grad_pre_of(own, other, pre_act, w_out):
+    grad_pre = (total[...].T * gelu_slope(pre)).astype(jnp.bfloat16)
+    out_ref[...] = grad_pre
+    duo_ref[0] = grad_pre
+    duo_ref[1] = rider_ref[...]
+
+
+def grad_pre_of(own, other, pre_act, w_out, rider):
     group, hidden = pre_act.shape
     width = w_out.shape[1]
     return call(
         functools.partial(grad_pre_body, block_of(hidden, 432, 16)),
-        [((group, hidden), jnp.bfloat16)],
-        [own, other, pre_act, w_out],
+        [((group, hidden), jnp.bfloat16), ((2, group, hidden), jnp.bfloat16)],
+        [own, other, pre_act, w_out, rider],
         "grad_pre",
         [pltpu.VMEM((group, width), jnp.bfloat16), pltpu.VMEM((hidden, group), jnp.float32)],
         flops=2 * group * width * hidden,
         bytes_accessed=2 * hidden * width,
-    )[0]
+    )
 
 
 def grad_in_body(block, grad_pre_ref, w_ref, *refs):
@@ -283,13 +247,17 @@
         ).astype(jnp.bfloat16)
 
 
-def grad_w_body(places, arrays, where, scale_back, block, *refs):
-    pre_refs, grad_pre_refs = refs[:arrays], refs[arrays : arrays + places]
-    own_ref, other_ref, in_ref, out_ref, end_ref = refs[arrays + places : arrays + places + 5]
-    flat, sorted_rows, turned, held_in, held_out, sems = refs[arrays + places + 5 :]
+def grad_w_body(arrays, pre_at, grad_pre_at, scale_back, block, *refs):
+    own_ref, other_ref, in_ref, out_ref, end_ref = refs[arrays : arrays + 5]
+    flat, sorted_rows, turned, held_in, held_out, sems = refs[arrays + 5 :]
+    places = len(pre_at)
+
+    def rows_of(at):
+        ref = refs[at[0]]
+        return ref[...] if len(ref.shape) == 2 else ref[at[1]]
+
     end_ref[...] = jnp.zeros_like(end_ref)
-    group, hidden = grad_pre_refs[0].shape
-    part = own_ref.shape[3]
+    group, part = flat.shape[0] // places, own_ref.shape[3]
     half, total = group // 2, places * group
     chips = lax.axis_size("mp") // 2
     rows = half // chips
@@ -328,29 +296,27 @@
             copies[-1].start()
 
     for k in range(places):
-        array, j = where[k]
-        ref = pre_refs[array]
-        pre = (ref[...] if len(ref.shape) == 2 else ref[j]).astype(jnp.float32)
+        pre = rows_of(pre_at[k]).astype(jnp.float32)
         flat[k * group : (k + 1) * group, :] = gelu_value(pre).astype(jnp.bfloat16)
     arrange(lambda b: place_of(b, chips))
     product(1, held_out, out_ref)
     for k in range(places):
-        flat[k * group : (k + 1) * group, :] = grad_pre_refs[k][...]
+        flat[k * group : (k + 1) * group, :] = rows_of(grad_pre_at[k])
     arrange(lambda b: b)
     product(0, held_in, in_ref)
     for copy in copies:
         copy.wait()
 
 
-def grad_w_of(pre, where, grad_pre, own, other, scale_back):
-    places = len(grad_pre)
-    group, hidden = grad_pre[0].shape
+def grad_w_of(arrays, pre_at, grad_pre_at, own, other, scale_back):
+    places = len(pre_at)
+    group, hidden = arrays[0].shape
     total, part = places * group, own.shape[3]
     block = block_of(part, 256, 128)
     return call(
-        functools.partial(grad_w_body, places, len(pre), where, scale_back, block),
+        functools.partial(grad_w_body, len(arrays), pre_at, grad_pre_at, scale_back, block),
         [((hidden, part), jnp.bfloat16)] * 2 + [((8, 128), jnp.float32)],
-        [*pre, *grad_pre, own, other],
+        [*arrays, own, other],
         "grad_w",
         [
             pltpu.VMEM((total, hidden), jnp.bfloat16),
@@ -372,21 +338,32 @@
     chips = n_mp // 2
     scale_back = 1.0 / math.sqrt(pre_act.shape[0] * n_tok)
 
-    masks = (3, 1) if n_tok == 4 else [1 << i for i in range(n_tok.bit_length() - 1)]
-    held, pre, where = spread(pre_act, masks)
+    relay = n_tok == 4
+    early = [k for k in range(1, n_tok) if not (relay and k == 2)]
+    pre = {k: fetch(pre_act, "tokens", k) for k in reversed(early)}
     both, pre_act = pack(tokens_in, grad_out, pre_act, lead())
     *pieces, own_rows = join(
-        [both] + [fetch_chip(both, k) for k in range(1, chips)], n_tok, held
+        [both] + [fetch_chip(both, k) for k in range(1, chips)],
+        n_tok,
+        [pre[k] for k in early] if relay else [],
     )
     pieces = [x if k == 0 else fetch(x, "tokens", k) for k, x in enumerate(pieces)]
 
-    grad_pre = grad_pre_of(own_rows, other_core(own_rows), pre_act, w_out)
+    rider = pre[3] if relay else pre_act
+    grad_pre, duo = grad_pre_of(own_rows, other_core(own_rows), pre_act, w_out, rider)
+    grad_pre_all = [grad_pre] + [
+        fetch(duo if relay and k == 1 else grad_pre, "tokens", k) for k in range(1, n_tok)
+    ]
     own_cols = stack(pieces, [grad_pre])
     other_cols = other_core(own_cols)
-    grad_pre_all = [grad_pre] + [fetch(grad_pre, "tokens", k) for k in range(1, n_tok)]
     terms = lax.all_to_all(grad_in_part(grad_pre, w_in.T, n_mp, []), "mp", 0, 0)
+    arrays = [pre_act] + [pre[k] for k in early] + grad_pre_all
+    pre_at = {k: (i, 0) for i, k in enumerate([0] + early)}
+    grad_pre_at = [(len(pre_at) + k, 0) for k in range(n_tok)]
+    if relay:
+        pre_at[2] = (grad_pre_at[1][0], 1)
     grad_w_in_t, grad_w_out, end = grad_w_of(
-        [pre_act, *pre], where, grad_pre_all, own_cols, other_cols, scale_back
+        arrays, pre_at, grad_pre_at, own_cols, other_cols, scale_back
     )
     return (finish(terms, end), grad_w_in_t.T, grad_w_out)
 

time: 46.6 us -> 45.7 us (0.981)
  waiting for transfers between devices: 9.27 us -> 8.77 us
    ppermute x2 -> x0, starting transfers between devices: 6.12 us -> none  [spread(): got.append(lax.ppermute(held, 'tokens', [(i ^ mask, i) for i in range(n)]))]
    ppermute x6 -> x8, starting transfers between devices: 7.93 us -> 14 us  [fetch(): return lax.ppermute(x, axis, [(partner(i, k, n), i) for i in range(n)])]
    ppermute x6 -> x8, waiting for transfers between devices: 4.42 us -> 3.07 us  [fetch(): return lax.ppermute(x, axis, [(partner(i, k, n), i) for i in range(n)])]
    all_to_all x1, waiting for transfers between devices: 0.01 us -> 0.84 us  [shards(): terms = lax.all_to_all(grad_in_part(grad_pre, w_in.T, n_mp, []), 'mp', 0, 0)]
    pallas_call x9 -> x8, Pallas kernels: 14.9 us -> 14.6 us  [call(): pl.pallas_call(body, in_specs=[pl.BlockSpec(memory_space=in_space)] * len...]
  transfers between devices with their start and end apart: 14 -> 14, of which waited for: 6 -> 7; matrix products, arithmetic and copies ran while one was open for 0% -> 0% of each run, Pallas kernels for 30% -> 30%
where the time goes in v16:
time: 45.7 us; the launch traced here: 45.5 us
  starting transfers between devices  21.1 us (46%)
  Pallas kernels  14.6 us (32%)
  waiting for transfers between devices  8.77 us (19%)
  between operations  0.89 us (2%)
    pallas_call x8, Pallas kernels, call(): pl.pallas_call(body, in_specs=[pl.BlockSpec(memory_space=in_space)] * len...  14.6 us
    ppermute x8, starting transfers between devices, fetch(): return lax.ppermute(x, axis, [(partner(i, k, n), i) for i in range(n)])  14 us
    ppermute x3, waiting for transfers between devices, fetch_chip(): lax.ppermute(x, 'mp', [(there, here) for here, there in chip_pairs(k)])  4.86 us
    ppermute x3, starting transfers between devices, fetch_chip(): lax.ppermute(x, 'mp', [(there, here) for here, there in chip_pairs(k)])  3.55 us
    all_to_all x1, starting transfers between devices, shards(): terms = lax.all_to_all(grad_in_part(grad_pre, w_in.T, n_mp, []), 'mp', 0, 0)  3.43 us
    ppermute x8, waiting for transfers between devices, fetch(): return lax.ppermute(x, axis, [(partner(i, k, n), i) for i in range(n)])  3.07 us
  transfers between devices with their start and end apart: 14, of which 7 were waited for; matrix products, arithmetic and copies ran while one was open for 0% of the time, Pallas kernels for 30%

profile of v16, /device:TPU:0, one launch (start us, length us, event | category | flops | bytes accessed | tf_op | source)
XLA Modules:
  0.0 45.5 jit_solution(11078836030218769001)
XLA Ops:
  0.7 5.1 %collective-permute-start.4 = (bf16[32,1728]{1,0:T(8,128)(2,1)}, bf16[32,1728]{1,0:T(8,128)(2,1)S(1)}, u32[]{:S(2)}, u32[]{:S(2)}) collective-permute-start(bf16[32,1728]{1,0:T(8,128)(2,1)} %pre_in.1), channel_id=1, source_target_pairs={{3,0},{2,1},{1,2},{0,3},{7,4},{6,5},{5,6},{4,7},{11,8},{10,9},{9,1... | collective-permute-start | bytes 331784 | tf_op jit(solution)/shard_map/ppermute | solution.py:35
  5.9 1.6 %collective-permute-start = (bf16[8,5120]{1,0:T(8,128)(2,1)S(1)}, bf16[8,5120]{1,0:T(8,128)(2,1)S(1)}, u32[]{:S(2)}, u32[]{:S(2)}) collective-permute-start(bf16[8,5120]{1,0:T(8,128)(2,1)S(1)} %get-tuple-element.15.refs_0_), channel_id=1, source_target_pairs={{8,0},{12,4},{0,8},{4,12},{24,16},{28,20},{16,24},{20,28},{9,1},{1... | collective-permute-start | bytes 245768 | tf_op jit(solution)/shard_map/ppermute | solution.py:48
  7.5 1.5 %collective-permute-start.1 = (bf16[8,5120]{1,0:T(8,128)(2,1)S(1)}, bf16[8,5120]{1,0:T(8,128)(2,1)S(1)}, u32[]{:S(2)}, u32[]{:S(2)}) collective-permute-start(bf16[8,5120]{1,0:T(8,128)(2,1)S(1)} %get-tuple-element.15.refs_0_), channel_id=1, source_target_pairs={{16,0},{20,4},{24,8},{28,12},{0,16},{4,20},{8,24},{12,28},{17,1},{... | collective-permute-start | bytes 245768 | tf_op jit(solution)/shard_map/ppermute | solution.py:48
  9.0 0.5 %collective-permute-start.2 = (bf16[8,5120]{1,0:T(8,128)(2,1)S(1)}, bf16[8,5120]{1,0:T(8,128)(2,1)S(1)}, u32[]{:S(2)}, u32[]{:S(2)}) collective-permute-start(bf16[8,5120]{1,0:T(8,128)(2,1)S(1)} %get-tuple-element.15.refs_0_), channel_id=1, source_target_pairs={{24,0},{28,4},{16,8},{20,12},{8,16},{12,20},{0,24},{4,28},{25,1},{... | collective-permute-start | bytes 245768 | tf_op jit(solution)/shard_map/ppermute | solution.py:48
  9.5 1.0 %collective-permute-done.refs_1_ = bf16[8,5120]{1,0:T(8,128)(2,1)S(1)} collective-permute-done((bf16[8,5120]{1,0:T(8,128)(2,1)S(1)}, bf16[8,5120]{1,0:T(8,128)(2,1)S(1)}, u32[]{:S(2)}, u32[]{:S(2)}) %collective-permute-start) | collective-permute-done | bytes 81952 | tf_op jit(solution)/shard_map/ppermute | solution.py:48
  10.4 2.4 %collective-permute-done.1.refs_2_ = bf16[8,5120]{1,0:T(8,128)(2,1)S(1)} collective-permute-done((bf16[8,5120]{1,0:T(8,128)(2,1)S(1)}, bf16[8,5120]{1,0:T(8,128)(2,1)S(1)}, u32[]{:S(2)}, u32[]{:S(2)}) %collective-permute-start.1) | collective-permute-done | bytes 81952 | tf_op jit(solution)/shard_map/ppermute | solution.py:48
  12.8 1.5 %collective-permute-done.2.refs_3_ = bf16[8,5120]{1,0:T(8,128)(2,1)S(1)} collective-permute-done((bf16[8,5120]{1,0:T(8,128)(2,1)S(1)}, bf16[8,5120]{1,0:T(8,128)(2,1)S(1)}, u32[]{:S(2)}, u32[]{:S(2)}) %collective-permute-start.2) | collective-permute-done | bytes 81952 | tf_op jit(solution)/shard_map/ppermute | solution.py:48
  14.4 0.2 join.1
  14.5 0.1 collective-permute-start.5
  14.6 0.8 %collective-permute-start.10 = (bf16[2,16,1280]{2,1,0:T(8,128)(2,1)S(1)}, bf16[2,16,1280]{2,1,0:T(8,128)(2,1)S(1)}, u32[]{:S(2)}, u32[]{:S(2)}) collective-permute-start(bf16[2,16,1280]{2,1,0:T(8,128)(2,1)S(1)} %get-tuple-element.22), channel_id=1, source_target_pairs={{2,0},{3,1},{0,2},{1,3},{6,4},{7,5},{4,6},{5,7},{10,8},{11,9},{8,1... | collective-permute-start | bytes 245768 | tf_op jit(solution)/shard_map/ppermute | solution.py:35
  15.4 3.6 %collective-permute-start.11 = (bf16[2,16,1280]{2,1,0:T(8,128)(2,1)S(1)}, bf16[2,16,1280]{2,1,0:T(8,128)(2,1)S(1)}, u32[]{:S(2)}, u32[]{:S(2)}) collective-permute-start(bf16[2,16,1280]{2,1,0:T(8,128)(2,1)S(1)} %get-tuple-element.23), channel_id=1, source_target_pairs={{3,0},{2,1},{1,2},{0,3},{7,4},{6,5},{5,6},{4,7},{11,8},{10,9},{9,1... | collective-permute-start | bytes 245768 | tf_op jit(solution)/shard_map/ppermute | solution.py:35
  19.1 4.9 %grad_pre.1 = (bf16[32,1728]{1,0:T(8,128)(2,1)S(1)}, bf16[2,32,1728]{2,1,0:T(8,128)(2,1)S(1)}) custom-call(bf16[16,5120]{1,0:T(8,128)(2,1)S(1)} %get-tuple-element.16.own_ref, bf16[16,5120]{1,0:T(8,128)(2,1)S(1)} %collective-permute-done.5.other_ref, bf16[32,1728]{1,0:T(8,128)(2,1)S(1)} %get-tuple-element.17.pre_ref.refs_0_, bf16[1728,5120]{1,0:T(8,128)(2,1)S(1)} %bitcast.6, ...), custom_call_target="tpu_custom_call" | custom-call | flops 566231040 | bytes 17694720 | tf_op jit(solution)/shard_map/grad_pre/pallas_call | solution.py:61
  24.1 0.3 collective-permute-done.10.refs_2_
  24.3 1.0 %collective-permute-done.9.refs_1_ = bf16[2,16,1280]{2,1,0:T(8,128)(2,1)S(1)} collective-permute-done((bf16[2,16,1280]{2,1,0:T(8,128)(2,1)S(1)}, bf16[2,16,1280]{2,1,0:T(8,128)(2,1)S(1)}, u32[]{:S(2)}, u32[]{:S(2)}) %collective-permute-start.9) | collective-permute-done | bytes 81952 | tf_op jit(solution)/shard_map/ppermute | solution.py:35
  25.4 0.1 collective-permute-start.12
  25.4 1.0 %collective-permute-start.6 = (bf16[2,32,1728]{2,1,0:T(8,128)(2,1)S(1)}, bf16[2,32,1728]{2,1,0:T(8,128)(2,1)S(1)}, u32[]{:S(2)}, u32[]{:S(2)}) collective-permute-start(bf16[2,32,1728]{2,1,0:T(8,128)(2,1)S(1)} %get-tuple-element.19), channel_id=1, source_target_pairs={{1,0},{0,1},{3,2},{2,3},{5,4},{4,5},{7,6},{6,7},{9,8},{8,9},{11,10... | collective-permute-start | bytes 663560 | tf_op jit(solution)/shard_map/ppermute | solution.py:35
  26.4 1.3 %collective-permute-start.7 = (bf16[32,1728]{1,0:T(8,128)(2,1)S(1)}, bf16[32,1728]{1,0:T(8,128)(2,1)S(1)}, u32[]{:S(2)}, u32[]{:S(2)}) collective-permute-start(bf16[32,1728]{1,0:T(8,128)(2,1)S(1)} %get-tuple-element.18.grad_pre_ref.refs_4_.refs_3_), channel_id=1, source_target_pairs={{2,0},{3,1},{0,2},{1,3},{6,4},{7,5},{4,6},{5,7},{10,8},{11,9},{8,1... | collective-permute-start | bytes 331784 | tf_op jit(solution)/shard_map/ppermute | solution.py:35
  27.7 2.2 %collective-permute-start.8 = (bf16[32,1728]{1,0:T(8,128)(2,1)S(1)}, bf16[32,1728]{1,0:T(8,128)(2,1)S(1)}, u32[]{:S(2)}, u32[]{:S(2)}) collective-permute-start(bf16[32,1728]{1,0:T(8,128)(2,1)S(1)} %get-tuple-element.18.grad_pre_ref.refs_4_.refs_3_), channel_id=1, source_target_pairs={{3,0},{2,1},{1,2},{0,3},{7,4},{6,5},{5,6},{4,7},{11,8},{10,9},{9,1... | collective-permute-start | bytes 331784 | tf_op jit(solution)/shard_map/ppermute | solution.py:35
  29.9 3.9 %grad_in_part.1 = bf16[8,4,5120]{2,1,0:T(4,128)(2,1)} custom-call(bf16[32,1728]{1,0:T(8,128)(2,1)S(1)} %get-tuple-element.18.grad_pre_ref.refs_4_.refs_3_, bf16[1728,5120]{1,0:T(8,128)(2,1)S(1)} %bitcast.4), custom_call_target="tpu_custom_call" | custom-call | flops 566231040 | bytes 17694720 | tf_op jit(solution)/shard_map/grad_in_part/pallas_call | solution.py:61
  33.8 3.4 %all-to-all-start = ((bf16[8,4,5120]{2,1,0:T(4,128)(2,1)}), bf16[8,4,5120]{2,1,0:T(4,128)(2,1)S(1)}, u32[]{:S(2)}, u32[]{:S(2)}) async-start(bf16[8,4,5120]{2,1,0:T(4,128)(2,1)} %grad_in_part.1), calls=%async_computation | async-start | bytes 655360 | tf_op jit(solution)/shard_map/all_to_all | solution.py:359
  37.3 1.8 %collective-permute-done.8.refs_6_ = bf16[32,1728]{1,0:T(8,128)(2,1)S(1)} collective-permute-done((bf16[32,1728]{1,0:T(8,128)(2,1)S(1)}, bf16[32,1728]{1,0:T(8,128)(2,1)S(1)}, u32[]{:S(2)}, u32[]{:S(2)}) %collective-permute-start.8) | collective-permute-done | bytes 110624 | tf_op jit(solution)/shard_map/ppermute | solution.py:35
  39.0 4.9 %grad_w.1 = (bf16[1728,1280]{1,0:T(8,128)(2,1)}, bf16[1728,1280]{1,0:T(8,128)(2,1)}, f32[8,128]{1,0:T(8,128)S(1)}) custom-call(bf16[32,1728]{1,0:T(8,128)(2,1)S(1)} %get-tuple-element.17.pre_ref.refs_0_, bf16[32,1728]{1,0:T(8,128)(2,1)S(1)} %collective-permute-done.3.refs_4_.refs_1_, bf16[32,1728]{1,0:T(8,128)(2,1)S(1)} %collective-permute-done.4.refs_5_.rider_ref.refs_2_, ...), custom_call_target="tpu_custom_call" | custom-call | flops 22649241600 | bytes 88473600 | tf_op jit(solution)/shard_map/grad_w/pallas_call | solution.py:61
  44.0 0.8 %all-to-all-done.terms_ref = bf16[8,4,5120]{2,1,0:T(4,128)(2,1)S(1)} async-done(((bf16[8,4,5120]{2,1,0:T(4,128)(2,1)}), bf16[8,4,5120]{2,1,0:T(4,128)(2,1)S(1)}, u32[]{:S(2)}, u32[]{:S(2)}) %all-to-all-start) | async-done | bytes 327712 | tf_op jit(solution)/shard_map/all_to_all | solution.py:359
  44.8 0.7 %finish.1 = bf16[4,5120]{1,0:T(4,128)(2,1)} custom-call(bf16[8,4,5120]{2,1,0:T(4,128)(2,1)S(1)} %all-to-all-done.terms_ref, f32[8,128]{1,0:T(8,128)S(1)} %get-tuple-element.24.after), custom_call_target="tpu_custom_call" | custom-call | flops 1000000 | bytes 100000 | tf_op jit(solution)/shard_map/finish/pallas_call | solution.py:61
  (40 shorter events, 0.1 us)
Async XLA Ops:
  0.7 13.7 %collective-permute-start.4 = (bf16[32,1728]{1,0:T(8,128)(2,1)}, bf16[32,1728]{1,0:T(8,128)(2,1)S(1)}, u32[]{:S(2)}, u32[]{:S(2)}) collective-permute-start(bf16[32,1728]{1,0:T(8,128)(2,1)} %pre_in.1), channel_id=1, source_target_pairs={{3,0},{2,1},{1,2},{0,3},{7,4},{6,5},{5,6},{4,7},{11,8},{10,9},{9,1... | collective-permute-start | bytes 331784 | tf_op jit(solution)/shard_map/ppermute | solution.py:35
  5.8 8.6 %collective-permute-start.3 = (bf16[32,1728]{1,0:T(8,128)(2,1)}, bf16[32,1728]{1,0:T(8,128)(2,1)S(1)}, u32[]{:S(2)}, u32[]{:S(2)}) collective-permute-start(bf16[32,1728]{1,0:T(8,128)(2,1)} %pre_in.1), channel_id=1, source_target_pairs={{1,0},{0,1},{3,2},{2,3},{5,4},{4,5},{7,6},{6,7},{9,8},{8,9},{11,10... | collective-permute-start | bytes 331784 | tf_op jit(solution)/shard_map/ppermute | solution.py:35
  5.8 13.3 %slice-start.5 = ((s8[17694720]{0:T(1024)(128)(4,1)}), s8[4194304]{0:T(1024)(128)(4,1)S(1)}, s32[]{:S(2)}) async-start(s8[17694720]{0:T(1024)(128)(4,1)} %bitcast.5), calls=%async_computation.6 | async-start | bytes 8388608
  5.8 13.3 %slice-start.6 = ((s8[17694720]{0:T(1024)(128)(4,1)}), s8[4194304]{0:T(1024)(128)(4,1)S(1)}, s32[]{:S(2)}) async-start(s8[17694720]{0:T(1024)(128)(4,1)} %bitcast.5), calls=%async_computation.7 | async-start | bytes 8388608
  5.8 13.3 %slice-start.7 = ((s8[17694720]{0:T(1024)(128)(4,1)}), s8[4194304]{0:T(1024)(128)(4,1)S(1)}, s32[]{:S(2)}) async-start(s8[17694720]{0:T(1024)(128)(4,1)} %bitcast.5), calls=%async_computation.8 | async-start | bytes 8388608
  5.8 13.2 %slice-start.8 = ((s8[17694720]{0:T(1024)(128)(4,1)}), s8[4194304]{0:T(1024)(128)(4,1)S(1)}, s32[]{:S(2)}) async-start(s8[17694720]{0:T(1024)(128)(4,1)} %bitcast.5), calls=%async_computation.9 | async-start | bytes 8388608
  5.8 13.2 %slice-start.9 = ((s8[17694720]{0:T(1024)(128)(4,1)}), s8[917504]{0:T(1024)(128)(4,1)S(1)}, s32[]{:S(2)}) async-start(s8[17694720]{0:T(1024)(128)(4,1)} %bitcast.5), calls=%async_computation.10 | async-start | bytes 1835008
  5.9 24.0 %slice-start = ((s8[17694720]{0:T(1024)(128)(4,1)}), s8[4194304]{0:T(1024)(128)(4,1)S(1)}, s32[]{:S(2)}) async-start(s8[17694720]{0:T(1024)(128)(4,1)} %bitcast.2), calls=%async_computation.1 | async-start | bytes 8388608
  5.9 24.0 %slice-start.1 = ((s8[17694720]{0:T(1024)(128)(4,1)}), s8[4194304]{0:T(1024)(128)(4,1)S(1)}, s32[]{:S(2)}) async-start(s8[17694720]{0:T(1024)(128)(4,1)} %bitcast.2), calls=%async_computation.2 | async-start | bytes 8388608
  5.9 24.0 %slice-start.2 = ((s8[17694720]{0:T(1024)(128)(4,1)}), s8[4194304]{0:T(1024)(128)(4,1)S(1)}, s32[]{:S(2)}) async-start(s8[17694720]{0:T(1024)(128)(4,1)} %bitcast.2), calls=%async_computation.3 | async-start | bytes 8388608
  5.9 24.0 %slice-start.3 = ((s8[17694720]{0:T(1024)(128)(4,1)}), s8[4194304]{0:T(1024)(128)(4,1)S(1)}, s32[]{:S(2)}) async-start(s8[17694720]{0:T(1024)(128)(4,1)} %bitcast.2), calls=%async_computation.4 | async-start | bytes 8388608
  5.9 4.5 %collective-permute-start = (bf16[8,5120]{1,0:T(8,128)(2,1)S(1)}, bf16[8,5120]{1,0:T(8,128)(2,1)S(1)}, u32[]{:S(2)}, u32[]{:S(2)}) collective-permute-start(bf16[8,5120]{1,0:T(8,128)(2,1)S(1)} %get-tuple-element.15.refs_0_), channel_id=1, source_target_pairs={{8,0},{12,4},{0,8},{4,12},{24,16},{28,20},{16,24},{20,28},{9,1},{1... | collective-permute-start | bytes 245768 | tf_op jit(solution)/shard_map/ppermute | solution.py:48
  7.5 5.3 %collective-permute-start.1 = (bf16[8,5120]{1,0:T(8,128)(2,1)S(1)}, bf16[8,5120]{1,0:T(8,128)(2,1)S(1)}, u32[]{:S(2)}, u32[]{:S(2)}) collective-permute-start(bf16[8,5120]{1,0:T(8,128)(2,1)S(1)} %get-tuple-element.15.refs_0_), channel_id=1, source_target_pairs={{16,0},{20,4},{24,8},{28,12},{0,16},{4,20},{8,24},{12,28},{17,1},{... | collective-permute-start | bytes 245768 | tf_op jit(solution)/shard_map/ppermute | solution.py:48
  9.0 5.3 %collective-permute-start.2 = (bf16[8,5120]{1,0:T(8,128)(2,1)S(1)}, bf16[8,5120]{1,0:T(8,128)(2,1)S(1)}, u32[]{:S(2)}, u32[]{:S(2)}) collective-permute-start(bf16[8,5120]{1,0:T(8,128)(2,1)S(1)} %get-tuple-element.15.refs_0_), channel_id=1, source_target_pairs={{24,0},{28,4},{16,8},{20,12},{8,16},{12,20},{0,24},{4,28},{25,1},{... | collective-permute-start | bytes 245768 | tf_op jit(solution)/shard_map/ppermute | solution.py:48
  14.5 4.5 %collective-permute-start.5 = (bf16[16,5120]{1,0:T(8,128)(2,1)S(1)}, bf16[16,5120]{1,0:T(8,128)(2,1)S(1)}, u32[]{:S(2)}, u32[]{:S(2)}) collective-permute-start(bf16[16,5120]{1,0:T(8,128)(2,1)S(1)} %get-tuple-element.16.own_ref), channel_id=1, source_target_pairs={{4,0},{0,4},{12,8},{8,12},{20,16},{16,20},{28,24},{24,28},{5,1},{1... | collective-permute-start | bytes 491528 | tf_op jit(solution)/shard_map/ppermute | solution.py:39
  14.6 9.7 %collective-permute-start.10 = (bf16[2,16,1280]{2,1,0:T(8,128)(2,1)S(1)}, bf16[2,16,1280]{2,1,0:T(8,128)(2,1)S(1)}, u32[]{:S(2)}, u32[]{:S(2)}) collective-permute-start(bf16[2,16,1280]{2,1,0:T(8,128)(2,1)S(1)} %get-tuple-element.22), channel_id=1, source_target_pairs={{2,0},{3,1},{0,2},{1,3},{6,4},{7,5},{4,6},{5,7},{10,8},{11,9},{8,1... | collective-permute-start | bytes 245768 | tf_op jit(solution)/shard_map/ppermute | solution.py:35
  15.4 8.9 %collective-permute-start.11 = (bf16[2,16,1280]{2,1,0:T(8,128)(2,1)S(1)}, bf16[2,16,1280]{2,1,0:T(8,128)(2,1)S(1)}, u32[]{:S(2)}, u32[]{:S(2)}) collective-permute-start(bf16[2,16,1280]{2,1,0:T(8,128)(2,1)S(1)} %get-tuple-element.23), channel_id=1, source_target_pairs={{3,0},{2,1},{1,2},{0,3},{7,4},{6,5},{5,6},{4,7},{11,8},{10,9},{9,1... | collective-permute-start | bytes 245768 | tf_op jit(solution)/shard_map/ppermute | solution.py:35
  19.0 6.3 %collective-permute-start.9 = (bf16[2,16,1280]{2,1,0:T(8,128)(2,1)S(1)}, bf16[2,16,1280]{2,1,0:T(8,128)(2,1)S(1)}, u32[]{:S(2)}, u32[]{:S(2)}) collective-permute-start(bf16[2,16,1280]{2,1,0:T(8,128)(2,1)S(1)} %get-tuple-element.21), channel_id=1, source_target_pairs={{1,0},{0,1},{3,2},{2,3},{5,4},{4,5},{7,6},{6,7},{9,8},{8,9},{11,10... | collective-permute-start | bytes 245768 | tf_op jit(solution)/shard_map/ppermute | solution.py:35
  19.1 10.8 %slice-start.4 = ((s8[17694720]{0:T(1024)(128)(4,1)}), s8[917504]{0:T(1024)(128)(4,1)S(1)}, s32[]{:S(2)}) async-start(s8[17694720]{0:T(1024)(128)(4,1)} %bitcast.2), calls=%async_computation.5 | async-start | bytes 1835008
  25.4 13.7 %collective-permute-start.12 = (bf16[4,2,16,1280]{3,2,1,0:T(8,128)(2,1)S(1)}, bf16[4,2,16,1280]{3,2,1,0:T(8,128)(2,1)S(1)}, u32[]{:S(2)}, u32[]{:S(2)}) collective-permute-start(bf16[4,2,16,1280]{3,2,1,0:T(8,128)(2,1)S(1)} %stack.1.refs_7_), channel_id=1, source_target_pairs={{4,0},{0,4},{12,8},{8,12},{20,16},{16,20},{28,24},{24,28},{5,1},{1... | collective-permute-start | bytes 983048 | tf_op jit(solution)/shard_map/ppermute | solution.py:39
  25.4 13.6 %collective-permute-start.6 = (bf16[2,32,1728]{2,1,0:T(8,128)(2,1)S(1)}, bf16[2,32,1728]{2,1,0:T(8,128)(2,1)S(1)}, u32[]{:S(2)}, u32[]{:S(2)}) collective-permute-start(bf16[2,32,1728]{2,1,0:T(8,128)(2,1)S(1)} %get-tuple-element.19), channel_id=1, source_target_pairs={{1,0},{0,1},{3,2},{2,3},{5,4},{4,5},{7,6},{6,7},{9,8},{8,9},{11,10... | collective-permute-start | bytes 663560 | tf_op jit(solution)/shard_map/ppermute | solution.py:35
  26.4 10.9 %collective-permute-start.7 = (bf16[32,1728]{1,0:T(8,128)(2,1)S(1)}, bf16[32,1728]{1,0:T(8,128)(2,1)S(1)}, u32[]{:S(2)}, u32[]{:S(2)}) collective-permute-start(bf16[32,1728]{1,0:T(8,128)(2,1)S(1)} %get-tuple-element.18.grad_pre_ref.refs_4_.refs_3_), channel_id=1, source_target_pairs={{2,0},{3,1},{0,2},{1,3},{6,4},{7,5},{4,6},{5,7},{10,8},{11,9},{8,1... | collective-permute-start | bytes 331784 | tf_op jit(solution)/shard_map/ppermute | solution.py:35
  27.7 11.3 %collective-permute-start.8 = (bf16[32,1728]{1,0:T(8,128)(2,1)S(1)}, bf16[32,1728]{1,0:T(8,128)(2,1)S(1)}, u32[]{:S(2)}, u32[]{:S(2)}) collective-permute-start(bf16[32,1728]{1,0:T(8,128)(2,1)S(1)} %get-tuple-element.18.grad_pre_ref.refs_4_.refs_3_), channel_id=1, source_target_pairs={{3,0},{2,1},{1,2},{0,3},{7,4},{6,5},{5,6},{4,7},{11,8},{10,9},{9,1... | collective-permute-start | bytes 331784 | tf_op jit(solution)/shard_map/ppermute | solution.py:35
  33.8 11.0 %all-to-all-start = ((bf16[8,4,5120]{2,1,0:T(4,128)(2,1)}), bf16[8,4,5120]{2,1,0:T(4,128)(2,1)S(1)}, u32[]{:S(2)}, u32[]{:S(2)}) async-start(bf16[8,4,5120]{2,1,0:T(4,128)(2,1)} %grad_in_part.1), calls=%async_computation | async-start | bytes 655360 | tf_op jit(solution)/shard_map/all_to_all | solution.py:359
  (3 other events, 15.5 us)

commit v17 on v16

--- a/solution.py
+++ b/solution.py
@@ -155,16 +155,11 @@
     return call(body, [(shape, jnp.bfloat16)], [*pieces, *after], "stack")[0]
 
 
-def grad_pre_body(block, own_ref, other_ref, pre_ref, w_ref, rider_ref, out_ref, duo_ref, rows, total):
-    hidden, group = total.shape
+def grad_pre_body(block, own_ref, other_ref, pre_ref, w_ref, rider_ref, out_ref, duo_ref, rows, slope):
+    group, hidden = slope.shape
     half = own_ref.shape[0]
     rows[:half, :] = own_ref[...]
     rows[half:, :] = other_ref[...]
-    for low in range(0, hidden, block):
-        here = slice(low, low + block)
-        total[here, :] = lax.dot_general(
-            w_ref[here, :], rows[...], (((1,), (1,)), ((), ())), preferred_element_type=jnp.float32
-        )
     each = group // lax.axis_size("mp")
     chips = half // each
     row = lax.broadcasted_iota(jnp.int32, (group, 1), 0)
@@ -176,21 +171,27 @@
     pre = jnp.dot(
         pick.astype(jnp.float32).astype(jnp.bfloat16), pre_ref[...], preferred_element_type=jnp.float32
     )
-    grad_pre = (total[...].T * gelu_slope(pre)).astype(jnp.bfloat16)
-    out_ref[...] = grad_pre
-    duo_ref[0] = grad_pre
+    slope[...] = gelu_slope(pre)
     duo_ref[1] = rider_ref[...]
+    for low in range(0, hidden, block):
+        here = slice(low, min(low + block, hidden))
+        term = lax.dot_general(
+            w_ref[here, :], rows[...], (((1,), (1,)), ((), ())), preferred_element_type=jnp.float32
+        )
+        grad_pre = (term.T * slope[:, here]).astype(jnp.bfloat16)
+        out_ref[:, here] = grad_pre
+        duo_ref[0, :, here] = grad_pre
 
 
 def grad_pre_of(own, other, pre_act, w_out, rider):
     group, hidden = pre_act.shape
     width = w_out.shape[1]
     return call(
-        functools.partial(grad_pre_body, block_of(hidden, 432, 16)),
+        functools.partial(grad_pre_body, 384),
         [((group, hidden), jnp.bfloat16), ((2, group, hidden), jnp.bfloat16)],
         [own, other, pre_act, w_out, rider],
         "grad_pre",
-        [pltpu.VMEM((group, width), jnp.bfloat16), pltpu.VMEM((hidden, group), jnp.float32)],
+        [pltpu.VMEM((group, width), jnp.bfloat16), pltpu.VMEM((group, hidden), jnp.float32)],
         flops=2 * group * width * hidden,
         bytes_accessed=2 * hidden * width,
     )

time: 45.7 us -> 45.7 us (level)
  no operation moved by 1% of the time
where the time goes in v17:
time: 45.7 us; the launch traced here: 45.5 us
  starting transfers between devices  21.1 us (46%)
  Pallas kernels  14.5 us (32%)
  waiting for transfers between devices  8.9 us (19%)
  between operations  0.88 us (2%)
    pallas_call x8, Pallas kernels, call(): pl.pallas_call(body, in_specs=[pl.BlockSpec(memory_space=in_space)] * len...  14.5 us
    ppermute x8, starting transfers between devices, fetch(): return lax.ppermute(x, axis, [(partner(i, k, n), i) for i in range(n)])  14 us
    ppermute x3, waiting for transfers between devices, fetch_chip(): lax.ppermute(x, 'mp', [(there, here) for here, there in chip_pairs(k)])  4.86 us
    ppermute x3, starting transfers between devices, fetch_chip(): lax.ppermute(x, 'mp', [(there, here) for here, there in chip_pairs(k)])  3.55 us
    all_to_all x1, starting transfers between devices, shards(): terms = lax.all_to_all(grad_in_part(grad_pre, w_in.T, n_mp, []), 'mp', 0, 0)  3.43 us
    ppermute x8, waiting for transfers between devices, fetch(): return lax.ppermute(x, axis, [(partner(i, k, n), i) for i in range(n)])  3.19 us
  transfers between devices with their start and end apart: 14, of which 7 were waited for; matrix products, arithmetic and copies ran while one was open for 0% of the time, Pallas kernels for 30%

profile of v17, /device:TPU:0, one launch (start us, length us, event | category | flops | bytes accessed | tf_op | source)
XLA Modules:
  0.0 45.5 jit_solution(16175422217356374556)
XLA Ops:
  0.7 5.1 %collective-permute-start.4 = (bf16[32,1728]{1,0:T(8,128)(2,1)}, bf16[32,1728]{1,0:T(8,128)(2,1)S(1)}, u32[]{:S(2)}, u32[]{:S(2)}) collective-permute-start(bf16[32,1728]{1,0:T(8,128)(2,1)} %pre_in.1), channel_id=1, source_target_pairs={{3,0},{2,1},{1,2},{0,3},{7,4},{6,5},{5,6},{4,7},{11,8},{10,9},{9,1... | collective-permute-start | bytes 331784 | tf_op jit(solution)/shard_map/ppermute | solution.py:35
  5.9 1.6 %collective-permute-start = (bf16[8,5120]{1,0:T(8,128)(2,1)S(1)}, bf16[8,5120]{1,0:T(8,128)(2,1)S(1)}, u32[]{:S(2)}, u32[]{:S(2)}) collective-permute-start(bf16[8,5120]{1,0:T(8,128)(2,1)S(1)} %get-tuple-element.15.refs_0_), channel_id=1, source_target_pairs={{8,0},{12,4},{0,8},{4,12},{24,16},{28,20},{16,24},{20,28},{9,1},{1... | collective-permute-start | bytes 245768 | tf_op jit(solution)/shard_map/ppermute | solution.py:48
  7.5 1.5 %collective-permute-start.1 = (bf16[8,5120]{1,0:T(8,128)(2,1)S(1)}, bf16[8,5120]{1,0:T(8,128)(2,1)S(1)}, u32[]{:S(2)}, u32[]{:S(2)}) collective-permute-start(bf16[8,5120]{1,0:T(8,128)(2,1)S(1)} %get-tuple-element.15.refs_0_), channel_id=1, source_target_pairs={{16,0},{20,4},{24,8},{28,12},{0,16},{4,20},{8,24},{12,28},{17,1},{... | collective-permute-start | bytes 245768 | tf_op jit(solution)/shard_map/ppermute | solution.py:48
  9.0 0.5 %collective-permute-start.2 = (bf16[8,5120]{1,0:T(8,128)(2,1)S(1)}, bf16[8,5120]{1,0:T(8,128)(2,1)S(1)}, u32[]{:S(2)}, u32[]{:S(2)}) collective-permute-start(bf16[8,5120]{1,0:T(8,128)(2,1)S(1)} %get-tuple-element.15.refs_0_), channel_id=1, source_target_pairs={{24,0},{28,4},{16,8},{20,12},{8,16},{12,20},{0,24},{4,28},{25,1},{... | collective-permute-start | bytes 245768 | tf_op jit(solution)/shard_map/ppermute | solution.py:48
  9.5 1.0 %collective-permute-done.refs_1_ = bf16[8,5120]{1,0:T(8,128)(2,1)S(1)} collective-permute-done((bf16[8,5120]{1,0:T(8,128)(2,1)S(1)}, bf16[8,5120]{1,0:T(8,128)(2,1)S(1)}, u32[]{:S(2)}, u32[]{:S(2)}) %collective-permute-start) | collective-permute-done | bytes 81952 | tf_op jit(solution)/shard_map/ppermute | solution.py:48
  10.4 2.4 %collective-permute-done.1.refs_2_ = bf16[8,5120]{1,0:T(8,128)(2,1)S(1)} collective-permute-done((bf16[8,5120]{1,0:T(8,128)(2,1)S(1)}, bf16[8,5120]{1,0:T(8,128)(2,1)S(1)}, u32[]{:S(2)}, u32[]{:S(2)}) %collective-permute-start.1) | collective-permute-done | bytes 81952 | tf_op jit(solution)/shard_map/ppermute | solution.py:48
  12.8 1.5 %collective-permute-done.2.refs_3_ = bf16[8,5120]{1,0:T(8,128)(2,1)S(1)} collective-permute-done((bf16[8,5120]{1,0:T(8,128)(2,1)S(1)}, bf16[8,5120]{1,0:T(8,128)(2,1)S(1)}, u32[]{:S(2)}, u32[]{:S(2)}) %collective-permute-start.2) | collective-permute-done | bytes 81952 | tf_op jit(solution)/shard_map/ppermute | solution.py:48
  14.4 0.2 join.1
  14.5 0.1 collective-permute-start.5
  14.6 0.8 %collective-permute-start.10 = (bf16[2,16,1280]{2,1,0:T(8,128)(2,1)S(1)}, bf16[2,16,1280]{2,1,0:T(8,128)(2,1)S(1)}, u32[]{:S(2)}, u32[]{:S(2)}) collective-permute-start(bf16[2,16,1280]{2,1,0:T(8,128)(2,1)S(1)} %get-tuple-element.22), channel_id=1, source_target_pairs={{2,0},{3,1},{0,2},{1,3},{6,4},{7,5},{4,6},{5,7},{10,8},{11,9},{8,1... | collective-permute-start | bytes 245768 | tf_op jit(solution)/shard_map/ppermute | solution.py:35
  15.4 3.6 %collective-permute-start.11 = (bf16[2,16,1280]{2,1,0:T(8,128)(2,1)S(1)}, bf16[2,16,1280]{2,1,0:T(8,128)(2,1)S(1)}, u32[]{:S(2)}, u32[]{:S(2)}) collective-permute-start(bf16[2,16,1280]{2,1,0:T(8,128)(2,1)S(1)} %get-tuple-element.23), channel_id=1, source_target_pairs={{3,0},{2,1},{1,2},{0,3},{7,4},{6,5},{5,6},{4,7},{11,8},{10,9},{9,1... | collective-permute-start | bytes 245768 | tf_op jit(solution)/shard_map/ppermute | solution.py:35
  19.1 4.8 %grad_pre.1 = (bf16[32,1728]{1,0:T(8,128)(2,1)S(1)}, bf16[2,32,1728]{2,1,0:T(8,128)(2,1)S(1)}) custom-call(bf16[16,5120]{1,0:T(8,128)(2,1)S(1)} %get-tuple-element.16.own_ref, bf16[16,5120]{1,0:T(8,128)(2,1)S(1)} %collective-permute-done.5.other_ref, bf16[32,1728]{1,0:T(8,128)(2,1)S(1)} %get-tuple-element.17.pre_ref.refs_0_, bf16[1728,5120]{1,0:T(8,128)(2,1)S(1)} %bitcast.6, ...), custom_call_target="tpu_custom_call" | custom-call | flops 566231040 | bytes 17694720 | tf_op jit(solution)/shard_map/grad_pre/pallas_call | solution.py:61
  23.9 0.4 collective-permute-done.10.refs_2_
  24.3 1.0 %collective-permute-done.9.refs_1_ = bf16[2,16,1280]{2,1,0:T(8,128)(2,1)S(1)} collective-permute-done((bf16[2,16,1280]{2,1,0:T(8,128)(2,1)S(1)}, bf16[2,16,1280]{2,1,0:T(8,128)(2,1)S(1)}, u32[]{:S(2)}, u32[]{:S(2)}) %collective-permute-start.9) | collective-permute-done | bytes 81952 | tf_op jit(solution)/shard_map/ppermute | solution.py:35
  25.4 0.1 collective-permute-start.12
  25.4 1.0 %collective-permute-start.6 = (bf16[2,32,1728]{2,1,0:T(8,128)(2,1)S(1)}, bf16[2,32,1728]{2,1,0:T(8,128)(2,1)S(1)}, u32[]{:S(2)}, u32[]{:S(2)}) collective-permute-start(bf16[2,32,1728]{2,1,0:T(8,128)(2,1)S(1)} %get-tuple-element.19), channel_id=1, source_target_pairs={{1,0},{0,1},{3,2},{2,3},{5,4},{4,5},{7,6},{6,7},{9,8},{8,9},{11,10... | collective-permute-start | bytes 663560 | tf_op jit(solution)/shard_map/ppermute | solution.py:35
  26.4 1.3 %collective-permute-start.7 = (bf16[32,1728]{1,0:T(8,128)(2,1)S(1)}, bf16[32,1728]{1,0:T(8,128)(2,1)S(1)}, u32[]{:S(2)}, u32[]{:S(2)}) collective-permute-start(bf16[32,1728]{1,0:T(8,128)(2,1)S(1)} %get-tuple-element.18.grad_pre_ref.refs_4_.refs_3_), channel_id=1, source_target_pairs={{2,0},{3,1},{0,2},{1,3},{6,4},{7,5},{4,6},{5,7},{10,8},{11,9},{8,1... | collective-permute-start | bytes 331784 | tf_op jit(solution)/shard_map/ppermute | solution.py:35
  27.7 2.2 %collective-permute-start.8 = (bf16[32,1728]{1,0:T(8,128)(2,1)S(1)}, bf16[32,1728]{1,0:T(8,128)(2,1)S(1)}, u32[]{:S(2)}, u32[]{:S(2)}) collective-permute-start(bf16[32,1728]{1,0:T(8,128)(2,1)S(1)} %get-tuple-element.18.grad_pre_ref.refs_4_.refs_3_), channel_id=1, source_target_pairs={{3,0},{2,1},{1,2},{0,3},{7,4},{6,5},{5,6},{4,7},{11,8},{10,9},{9,1... | collective-permute-start | bytes 331784 | tf_op jit(solution)/shard_map/ppermute | solution.py:35
  29.9 3.9 %grad_in_part.1 = bf16[8,4,5120]{2,1,0:T(4,128)(2,1)} custom-call(bf16[32,1728]{1,0:T(8,128)(2,1)S(1)} %get-tuple-element.18.grad_pre_ref.refs_4_.refs_3_, bf16[1728,5120]{1,0:T(8,128)(2,1)S(1)} %bitcast.4), custom_call_target="tpu_custom_call" | custom-call | flops 566231040 | bytes 17694720 | tf_op jit(solution)/shard_map/grad_in_part/pallas_call | solution.py:61
  33.8 3.4 %all-to-all-start = ((bf16[8,4,5120]{2,1,0:T(4,128)(2,1)}), bf16[8,4,5120]{2,1,0:T(4,128)(2,1)S(1)}, u32[]{:S(2)}, u32[]{:S(2)}) async-start(bf16[8,4,5120]{2,1,0:T(4,128)(2,1)} %grad_in_part.1), calls=%async_computation | async-start | bytes 655360 | tf_op jit(solution)/shard_map/all_to_all | solution.py:360
  37.3 1.8 %collective-permute-done.8.refs_6_ = bf16[32,1728]{1,0:T(8,128)(2,1)S(1)} collective-permute-done((bf16[32,1728]{1,0:T(8,128)(2,1)S(1)}, bf16[32,1728]{1,0:T(8,128)(2,1)S(1)}, u32[]{:S(2)}, u32[]{:S(2)}) %collective-permute-start.8) | collective-permute-done | bytes 110624 | tf_op jit(solution)/shard_map/ppermute | solution.py:35
  39.0 4.9 %grad_w.1 = (bf16[1728,1280]{1,0:T(8,128)(2,1)}, bf16[1728,1280]{1,0:T(8,128)(2,1)}, f32[8,128]{1,0:T(8,128)S(1)}) custom-call(bf16[32,1728]{1,0:T(8,128)(2,1)S(1)} %get-tuple-element.17.pre_ref.refs_0_, bf16[32,1728]{1,0:T(8,128)(2,1)S(1)} %collective-permute-done.3.refs_4_.refs_1_, bf16[32,1728]{1,0:T(8,128)(2,1)S(1)} %collective-permute-done.4.refs_5_.rider_ref.refs_2_, ...), custom_call_target="tpu_custom_call" | custom-call | flops 22649241600 | bytes 88473600 | tf_op jit(solution)/shard_map/grad_w/pallas_call | solution.py:61
  44.0 0.8 %all-to-all-done.terms_ref = bf16[8,4,5120]{2,1,0:T(4,128)(2,1)S(1)} async-done(((bf16[8,4,5120]{2,1,0:T(4,128)(2,1)}), bf16[8,4,5120]{2,1,0:T(4,128)(2,1)S(1)}, u32[]{:S(2)}, u32[]{:S(2)}) %all-to-all-start) | async-done | bytes 327712 | tf_op jit(solution)/shard_map/all_to_all | solution.py:360
  44.8 0.7 %finish.1 = bf16[4,5120]{1,0:T(4,128)(2,1)} custom-call(bf16[8,4,5120]{2,1,0:T(4,128)(2,1)S(1)} %all-to-all-done.terms_ref, f32[8,128]{1,0:T(8,128)S(1)} %get-tuple-element.24.after), custom_call_target="tpu_custom_call" | custom-call | flops 1000000 | bytes 100000 | tf_op jit(solution)/shard_map/finish/pallas_call | solution.py:61
  (40 shorter events, 0.1 us)
Async XLA Ops:
  0.7 13.7 %collective-permute-start.4 = (bf16[32,1728]{1,0:T(8,128)(2,1)}, bf16[32,1728]{1,0:T(8,128)(2,1)S(1)}, u32[]{:S(2)}, u32[]{:S(2)}) collective-permute-start(bf16[32,1728]{1,0:T(8,128)(2,1)} %pre_in.1), channel_id=1, source_target_pairs={{3,0},{2,1},{1,2},{0,3},{7,4},{6,5},{5,6},{4,7},{11,8},{10,9},{9,1... | collective-permute-start | bytes 331784 | tf_op jit(solution)/shard_map/ppermute | solution.py:35
  5.8 8.6 %collective-permute-start.3 = (bf16[32,1728]{1,0:T(8,128)(2,1)}, bf16[32,1728]{1,0:T(8,128)(2,1)S(1)}, u32[]{:S(2)}, u32[]{:S(2)}) collective-permute-start(bf16[32,1728]{1,0:T(8,128)(2,1)} %pre_in.1), channel_id=1, source_target_pairs={{1,0},{0,1},{3,2},{2,3},{5,4},{4,5},{7,6},{6,7},{9,8},{8,9},{11,10... | collective-permute-start | bytes 331784 | tf_op jit(solution)/shard_map/ppermute | solution.py:35
  5.8 13.3 %slice-start.5 = ((s8[17694720]{0:T(1024)(128)(4,1)}), s8[4194304]{0:T(1024)(128)(4,1)S(1)}, s32[]{:S(2)}) async-start(s8[17694720]{0:T(1024)(128)(4,1)} %bitcast.5), calls=%async_computation.6 | async-start | bytes 8388608
  5.8 13.3 %slice-start.6 = ((s8[17694720]{0:T(1024)(128)(4,1)}), s8[4194304]{0:T(1024)(128)(4,1)S(1)}, s32[]{:S(2)}) async-start(s8[17694720]{0:T(1024)(128)(4,1)} %bitcast.5), calls=%async_computation.7 | async-start | bytes 8388608
  5.8 13.3 %slice-start.7 = ((s8[17694720]{0:T(1024)(128)(4,1)}), s8[4194304]{0:T(1024)(128)(4,1)S(1)}, s32[]{:S(2)}) async-start(s8[17694720]{0:T(1024)(128)(4,1)} %bitcast.5), calls=%async_computation.8 | async-start | bytes 8388608
  5.8 13.2 %slice-start.8 = ((s8[17694720]{0:T(1024)(128)(4,1)}), s8[4194304]{0:T(1024)(128)(4,1)S(1)}, s32[]{:S(2)}) async-start(s8[17694720]{0:T(1024)(128)(4,1)} %bitcast.5), calls=%async_computation.9 | async-start | bytes 8388608
  5.8 13.2 %slice-start.9 = ((s8[17694720]{0:T(1024)(128)(4,1)}), s8[917504]{0:T(1024)(128)(4,1)S(1)}, s32[]{:S(2)}) async-start(s8[17694720]{0:T(1024)(128)(4,1)} %bitcast.5), calls=%async_computation.10 | async-start | bytes 1835008
  5.9 24.0 %slice-start = ((s8[17694720]{0:T(1024)(128)(4,1)}), s8[4194304]{0:T(1024)(128)(4,1)S(1)}, s32[]{:S(2)}) async-start(s8[17694720]{0:T(1024)(128)(4,1)} %bitcast.2), calls=%async_computation.1 | async-start | bytes 8388608
  5.9 24.0 %slice-start.1 = ((s8[17694720]{0:T(1024)(128)(4,1)}), s8[4194304]{0:T(1024)(128)(4,1)S(1)}, s32[]{:S(2)}) async-start(s8[17694720]{0:T(1024)(128)(4,1)} %bitcast.2), calls=%async_computation.2 | async-start | bytes 8388608
  5.9 24.0 %slice-start.2 = ((s8[17694720]{0:T(1024)(128)(4,1)}), s8[4194304]{0:T(1024)(128)(4,1)S(1)}, s32[]{:S(2)}) async-start(s8[17694720]{0:T(1024)(128)(4,1)} %bitcast.2), calls=%async_computation.3 | async-start | bytes 8388608
  5.9 24.0 %slice-start.3 = ((s8[17694720]{0:T(1024)(128)(4,1)}), s8[4194304]{0:T(1024)(128)(4,1)S(1)}, s32[]{:S(2)}) async-start(s8[17694720]{0:T(1024)(128)(4,1)} %bitcast.2), calls=%async_computation.4 | async-start | bytes 8388608
  5.9 4.5 %collective-permute-start = (bf16[8,5120]{1,0:T(8,128)(2,1)S(1)}, bf16[8,5120]{1,0:T(8,128)(2,1)S(1)}, u32[]{:S(2)}, u32[]{:S(2)}) collective-permute-start(bf16[8,5120]{1,0:T(8,128)(2,1)S(1)} %get-tuple-element.15.refs_0_), channel_id=1, source_target_pairs={{8,0},{12,4},{0,8},{4,12},{24,16},{28,20},{16,24},{20,28},{9,1},{1... | collective-permute-start | bytes 245768 | tf_op jit(solution)/shard_map/ppermute | solution.py:48
  7.5 5.3 %collective-permute-start.1 = (bf16[8,5120]{1,0:T(8,128)(2,1)S(1)}, bf16[8,5120]{1,0:T(8,128)(2,1)S(1)}, u32[]{:S(2)}, u32[]{:S(2)}) collective-permute-start(bf16[8,5120]{1,0:T(8,128)(2,1)S(1)} %get-tuple-element.15.refs_0_), channel_id=1, source_target_pairs={{16,0},{20,4},{24,8},{28,12},{0,16},{4,20},{8,24},{12,28},{17,1},{... | collective-permute-start | bytes 245768 | tf_op jit(solution)/shard_map/ppermute | solution.py:48
  9.0 5.3 %collective-permute-start.2 = (bf16[8,5120]{1,0:T(8,128)(2,1)S(1)}, bf16[8,5120]{1,0:T(8,128)(2,1)S(1)}, u32[]{:S(2)}, u32[]{:S(2)}) collective-permute-start(bf16[8,5120]{1,0:T(8,128)(2,1)S(1)} %get-tuple-element.15.refs_0_), channel_id=1, source_target_pairs={{24,0},{28,4},{16,8},{20,12},{8,16},{12,20},{0,24},{4,28},{25,1},{... | collective-permute-start | bytes 245768 | tf_op jit(solution)/shard_map/ppermute | solution.py:48
  14.5 4.5 %collective-permute-start.5 = (bf16[16,5120]{1,0:T(8,128)(2,1)S(1)}, bf16[16,5120]{1,0:T(8,128)(2,1)S(1)}, u32[]{:S(2)}, u32[]{:S(2)}) collective-permute-start(bf16[16,5120]{1,0:T(8,128)(2,1)S(1)} %get-tuple-element.16.own_ref), channel_id=1, source_target_pairs={{4,0},{0,4},{12,8},{8,12},{20,16},{16,20},{28,24},{24,28},{5,1},{1... | collective-permute-start | bytes 491528 | tf_op jit(solution)/shard_map/ppermute | solution.py:39
  14.6 9.7 %collective-permute-start.10 = (bf16[2,16,1280]{2,1,0:T(8,128)(2,1)S(1)}, bf16[2,16,1280]{2,1,0:T(8,128)(2,1)S(1)}, u32[]{:S(2)}, u32[]{:S(2)}) collective-permute-start(bf16[2,16,1280]{2,1,0:T(8,128)(2,1)S(1)} %get-tuple-element.22), channel_id=1, source_target_pairs={{2,0},{3,1},{0,2},{1,3},{6,4},{7,5},{4,6},{5,7},{10,8},{11,9},{8,1... | collective-permute-start | bytes 245768 | tf_op jit(solution)/shard_map/ppermute | solution.py:35
  15.4 8.9 %collective-permute-start.11 = (bf16[2,16,1280]{2,1,0:T(8,128)(2,1)S(1)}, bf16[2,16,1280]{2,1,0:T(8,128)(2,1)S(1)}, u32[]{:S(2)}, u32[]{:S(2)}) collective-permute-start(bf16[2,16,1280]{2,1,0:T(8,128)(2,1)S(1)} %get-tuple-element.23), channel_id=1, source_target_pairs={{3,0},{2,1},{1,2},{0,3},{7,4},{6,5},{5,6},{4,7},{11,8},{10,9},{9,1... | collective-permute-start | bytes 245768 | tf_op jit(solution)/shard_map/ppermute | solution.py:35
  19.0 6.3 %collective-permute-start.9 = (bf16[2,16,1280]{2,1,0:T(8,128)(2,1)S(1)}, bf16[2,16,1280]{2,1,0:T(8,128)(2,1)S(1)}, u32[]{:S(2)}, u32[]{:S(2)}) collective-permute-start(bf16[2,16,1280]{2,1,0:T(8,128)(2,1)S(1)} %get-tuple-element.21), channel_id=1, source_target_pairs={{1,0},{0,1},{3,2},{2,3},{5,4},{4,5},{7,6},{6,7},{9,8},{8,9},{11,10... | collective-permute-start | bytes 245768 | tf_op jit(solution)/shard_map/ppermute | solution.py:35
  19.1 10.8 %slice-start.4 = ((s8[17694720]{0:T(1024)(128)(4,1)}), s8[917504]{0:T(1024)(128)(4,1)S(1)}, s32[]{:S(2)}) async-start(s8[17694720]{0:T(1024)(128)(4,1)} %bitcast.2), calls=%async_computation.5 | async-start | bytes 1835008
  25.4 13.7 %collective-permute-start.12 = (bf16[4,2,16,1280]{3,2,1,0:T(8,128)(2,1)S(1)}, bf16[4,2,16,1280]{3,2,1,0:T(8,128)(2,1)S(1)}, u32[]{:S(2)}, u32[]{:S(2)}) collective-permute-start(bf16[4,2,16,1280]{3,2,1,0:T(8,128)(2,1)S(1)} %stack.1.refs_7_), channel_id=1, source_target_pairs={{4,0},{0,4},{12,8},{8,12},{20,16},{16,20},{28,24},{24,28},{5,1},{1... | collective-permute-start | bytes 983048 | tf_op jit(solution)/shard_map/ppermute | solution.py:39
  25.4 13.6 %collective-permute-start.6 = (bf16[2,32,1728]{2,1,0:T(8,128)(2,1)S(1)}, bf16[2,32,1728]{2,1,0:T(8,128)(2,1)S(1)}, u32[]{:S(2)}, u32[]{:S(2)}) collective-permute-start(bf16[2,32,1728]{2,1,0:T(8,128)(2,1)S(1)} %get-tuple-element.19), channel_id=1, source_target_pairs={{1,0},{0,1},{3,2},{2,3},{5,4},{4,5},{7,6},{6,7},{9,8},{8,9},{11,10... | collective-permute-start | bytes 663560 | tf_op jit(solution)/shard_map/ppermute | solution.py:35
  26.4 10.9 %collective-permute-start.7 = (bf16[32,1728]{1,0:T(8,128)(2,1)S(1)}, bf16[32,1728]{1,0:T(8,128)(2,1)S(1)}, u32[]{:S(2)}, u32[]{:S(2)}) collective-permute-start(bf16[32,1728]{1,0:T(8,128)(2,1)S(1)} %get-tuple-element.18.grad_pre_ref.refs_4_.refs_3_), channel_id=1, source_target_pairs={{2,0},{3,1},{0,2},{1,3},{6,4},{7,5},{4,6},{5,7},{10,8},{11,9},{8,1... | collective-permute-start | bytes 331784 | tf_op jit(solution)/shard_map/ppermute | solution.py:35
  27.7 11.3 %collective-permute-start.8 = (bf16[32,1728]{1,0:T(8,128)(2,1)S(1)}, bf16[32,1728]{1,0:T(8,128)(2,1)S(1)}, u32[]{:S(2)}, u32[]{:S(2)}) collective-permute-start(bf16[32,1728]{1,0:T(8,128)(2,1)S(1)} %get-tuple-element.18.grad_pre_ref.refs_4_.refs_3_), channel_id=1, source_target_pairs={{3,0},{2,1},{1,2},{0,3},{7,4},{6,5},{5,6},{4,7},{11,8},{10,9},{9,1... | collective-permute-start | bytes 331784 | tf_op jit(solution)/shard_map/ppermute | solution.py:35
  33.8 11.0 %all-to-all-start = ((bf16[8,4,5120]{2,1,0:T(4,128)(2,1)}), bf16[8,4,5120]{2,1,0:T(4,128)(2,1)S(1)}, u32[]{:S(2)}, u32[]{:S(2)}) async-start(bf16[8,4,5120]{2,1,0:T(4,128)(2,1)} %grad_in_part.1), calls=%async_computation | async-start | bytes 655360 | tf_op jit(solution)/shard_map/all_to_all | solution.py:360
  (3 other events, 15.5 us)
